TPU v7x, 32 devices: a whole 2x2x4 slice. The times are simulated.
32 devices in a mesh: groups: 2 (over x), seq: 8 (over z, y), chan: 2 (over core).
Axes of the slice: x: 2, y: 2, z: 4, core: 2. Of those that a mesh axis runs over, the one named last changes fastest.
Arguments:
- query_proj: bfloat16 [16384, 256], P(('groups', 'seq'), 'chan'), parts along dimension 0, may hold values from -6 to 6
- key_proj: bfloat16 [16384, 256], P(('groups', 'seq'), 'chan'), parts along dimension 0, may hold values from -6 to 6
- value_proj: bfloat16 [16384, 256], P(('groups', 'seq'), 'chan'), parts along dimension 0, may hold values from -6 to 6
- long_filter: float32 [8192, 256], P('seq', 'chan'), may hold values from -4 to 4
- skip_bias: float32 [256], P('chan'), may hold values from -4 to 4
Outputs:
- gated_out: bfloat16 [16384, 256], P(('groups', 'seq'), 'chan'), parts along dimension 0
There are 2 independent parts, one for each index of `groups`. A program takes and returns all parts, laid end to end along the dimension named above; an argument that names none is the same for every part. Nothing has to cross between parts.
All inputs are finite; a program needn't handle non-finite values.
Results may differ from a plain program's by a relative error of at most 0.001.
Values sent between devices are 32-bit elements; how exact they have to be, the bound alone decides.
No kernel may reach another device: no remote copies, remote signals or barrier semaphores. Data moves between devices by JAX's collectives and lax.ppermute only.
A program may use at most 64 MiB of HBM per device.

v0:
```python
import functools

import jax
import jax.numpy as jnp
import ml_dtypes
import numpy as np
from jax import lax
from jax.experimental import pallas as pl
from jax.experimental.pallas import tpu as pltpu
from jax.sharding import PartitionSpec as P

LANES = 128
BF16 = jnp.bfloat16
F32 = jnp.float32
VMEM_LIMIT = 48 * 2**20


def split_np(table):
    high = table.astype(np.float32).astype(ml_dtypes.bfloat16)
    low = (table - high.astype(np.float64)).astype(np.float32).astype(ml_dtypes.bfloat16)
    return high, low


def make_tables(seq_len):
    outer = seq_len // LANES
    n_out, k_out = np.meshgrid(np.arange(outer), np.arange(outer), indexing="ij")
    head = np.exp(-2j * np.pi * (n_out * (4 * k_out + 1) % (4 * outer)) / (4 * outer))
    n_in = np.arange(LANES)
    twist = np.exp(-2j * np.pi * np.outer(4 * np.arange(outer) + 1, n_in) / (4 * seq_len))
    tail = np.exp(-2j * np.pi * (np.outer(n_in, n_in) % LANES) / LANES)

    def block(mat):
        return np.block([[mat.real, mat.imag], [-mat.imag, mat.real]])

    fwd_head = np.concatenate([head.real.T, head.imag.T], axis=0)
    high, low = split_np(fwd_head)
    head_tab = np.concatenate([high, high, low], axis=1)
    high, low = split_np(block(tail))
    tail_tab = np.concatenate([high, high, low], axis=0)
    high, low = split_np(block(tail.conj()))
    back_tail_tab = np.concatenate([high, high, low], axis=0)
    high, low = split_np(np.concatenate([head.real, head.imag], axis=1))
    back_head_tab = np.concatenate([high, high, low], axis=1)
    twist_tab = np.concatenate([twist.real, twist.imag], axis=1).astype(np.float32)
    return head_tab, twist_tab, tail_tab, back_tail_tab, back_head_tab


def halves(values):
    high = values.astype(BF16)
    return high, (values - high.astype(F32)).astype(BF16)


def by_rows(values):
    high, low = halves(values)
    return jnp.concatenate([high, low, high], axis=0)


def by_lanes(values):
    high, low = halves(values)
    return jnp.concatenate([high, low, high], axis=1)


def mat(left, right):
    return jnp.dot(left, right, preferred_element_type=F32)


def forward(signals, head, twist, tail):
    outer = signals[0].shape[0]
    mixed = mat(head, by_rows(jnp.concatenate(signals, axis=1)))
    cos, sin = twist[:, :LANES], twist[:, LANES:]
    rows = []
    for idx in range(len(signals)):
        real = mixed[:outer, idx * LANES : (idx + 1) * LANES]
        imag = mixed[outer:, idx * LANES : (idx + 1) * LANES]
        rows.append(jnp.concatenate([real * cos - imag * sin, real * sin + imag * cos], axis=1))
    return mat(by_lanes(jnp.concatenate(rows, axis=0)), tail)


def pack_kernel(rows, key_ref, value_ref, out_ref):
    for row in range(rows):
        span = pl.ds(row * LANES, LANES)
        driver = key_ref[span, :].astype(F32) * value_ref[span, :].astype(F32)
        out_ref[pl.ds(row, LANES, stride=rows), :] = driver.T


def pack_filter_kernel(rows, which_ref, filter_ref, out_ref, scratch):
    for row in range(rows):
        scratch[pl.ds(row, LANES, stride=rows), :] = filter_ref[pl.ds(row * LANES, LANES), :].T
    size = out_ref.shape[0]
    start = pl.multiple_of(which_ref[0] * size, size)
    out_ref[...] = scratch[pl.ds(start, size), :]


def filter_kernel(own, filter_ref, head_ref, twist_ref, tail_ref, out_ref):
    blocks, rows = filter_ref.shape[0], filter_ref.shape[2]
    signals = [filter_ref[:, chan].reshape(blocks * rows, LANES) for chan in range(own)]
    out_ref[...] = forward(signals, head_ref[...], twist_ref[...], tail_ref[...])


def conv_kernel(own, driver_ref, spec_ref, head_ref, twist_ref, tail_ref, back_tail_ref, back_head_ref, out_ref):
    groups, blocks, _, rows = driver_ref.shape[:4]
    outer = blocks * rows
    scale = 1.0 / (outer * LANES)
    signals = [
        driver_ref[group, :, chan].reshape(outer, LANES) for chan in range(own) for group in range(groups)
    ]
    spec = forward(signals, head_ref[...], twist_ref[...], tail_ref[...])
    prods = []
    for idx in range(len(signals)):
        own_spec = spec_ref[pl.ds(idx // groups * outer, outer), :]
        f_re, f_im = own_spec[:, :LANES], own_spec[:, LANES:]
        mine = spec[idx * outer : (idx + 1) * outer]
        d_re, d_im = mine[:, :LANES], mine[:, LANES:]
        prods.append(jnp.concatenate([d_re * f_re - d_im * f_im, d_re * f_im + d_im * f_re], axis=1))
    back = mat(by_lanes(jnp.concatenate(prods, axis=0)), back_tail_ref[...])
    cos, sin = twist_ref[:, :LANES] * scale, twist_ref[:, LANES:] * scale
    reals, imags = [], []
    for idx in range(len(signals)):
        mine = back[idx * outer : (idx + 1) * outer]
        real, imag = mine[:, :LANES], mine[:, LANES:]
        reals.append(real * cos + imag * sin)
        imags.append(imag * cos - real * sin)
    mixed = jnp.concatenate([jnp.concatenate(reals, axis=1), jnp.concatenate(imags, axis=1)], axis=0)
    result = mat(back_head_ref[...], by_rows(mixed))
    for idx in range(len(signals)):
        chan, group = divmod(idx, groups)
        out_ref[group, :, chan] = result[:, idx * LANES : (idx + 1) * LANES].reshape(blocks, rows, LANES)


def gate_kernel(rows, conv_ref, query_ref, key_ref, value_ref, bias_ref, out_ref):
    bias = bias_ref[...]
    for row in range(rows):
        span = pl.ds(row * LANES, LANES)
        driver = key_ref[span, :].astype(F32) * value_ref[span, :].astype(F32)
        convolved = conv_ref[pl.ds(row, LANES, stride=rows), :].T
        out_ref[span, :] = (query_ref[span, :].astype(F32) * (convolved + bias * driver)).astype(BF16)


VMEM = pl.BlockSpec(memory_space=pltpu.VMEM)
SMEM = pl.BlockSpec(memory_space=pltpu.SMEM)


def call(kernel, shape, dtype, specs, flops, moved, scratch=()):
    return pl.pallas_call(
        kernel,
        out_shape=jax.ShapeDtypeStruct(shape, dtype),
        in_specs=specs,
        out_specs=VMEM,
        scratch_shapes=scratch,
        compiler_params=pltpu.CompilerParams(vmem_limit_bytes=VMEM_LIMIT),
        cost_estimate=pl.CostEstimate(flops=flops, bytes_accessed=moved, transcendentals=0),
    )


def shards(groups, blocks, query_proj, key_proj, value_proj, long_filter, skip_bias):
    tokens, chans = key_proj.shape
    rows = tokens // LANES
    own = chans // (groups * blocks)
    outer = blocks * rows
    seq_len = blocks * tokens
    tables = make_tables(seq_len)
    head, twist, tail, back_tail, back_head = (jnp.asarray(table) for table in tables)
    size = tokens * chans * 4

    packed_filter = call(
        functools.partial(pack_filter_kernel, rows),
        (blocks * own * rows, LANES), F32, [SMEM, VMEM], 0, size * 2,
        [pltpu.VMEM((chans * rows, LANES), F32)],
    )(lax.axis_index("groups").reshape(1).astype(jnp.int32), long_filter)
    packed = call(functools.partial(pack_kernel, rows), (chans * rows, LANES), F32, [VMEM, VMEM], size // 4, size * 2)(
        key_proj, value_proj
    )
    moved_filter = lax.all_to_all(packed_filter, "seq", 0, 0, tiled=True)
    moved = lax.all_to_all(packed, ("groups", "seq"), 0, 0, tiled=True)
    macs = 2 * 3 * own * seq_len * (2 * outer + 4 * LANES)
    spec = call(
        functools.partial(filter_kernel, own), (own * outer, 2 * LANES), F32, [VMEM] * 4, macs, size
    )(moved_filter.reshape(blocks, own, rows, LANES), head, twist, tail)
    local = call(
        functools.partial(conv_kernel, own),
        (groups, blocks, own, rows, LANES), F32, [VMEM] * 7, 4 * macs, 3 * size,
    )(moved.reshape(groups, blocks, own, rows, LANES), spec, head, twist, tail, back_tail, back_head)
    convolved = lax.all_to_all(local.reshape(chans * rows, LANES), ("groups", "seq"), 0, 0, tiled=True)
    return call(functools.partial(gate_kernel, rows), (tokens, chans), BF16, [VMEM] * 5, size, 3 * size)(
        convolved, query_proj, key_proj, value_proj, skip_bias.reshape(1, chans)
    )


def solution(mesh):
    placed = (
        P(("groups", "seq"), "chan"),
        P(("groups", "seq"), "chan"),
        P(("groups", "seq"), "chan"),
        P("seq", "chan"),
        P("chan"),
    )
    body = functools.partial(shards, mesh.shape["groups"], mesh.shape["seq"])
    return jax.shard_map(
        body, mesh=mesh, in_specs=placed, out_specs=P(("groups", "seq"), "chan"), check_vma=False
    )
```

profile of v0, /device:TPU:0, one launch (start us, length us, event | category | flops | bytes accessed | tf_op | source)
XLA Modules:
  0.0 59.4 jit_solution(7836521200629407388)
XLA Ops:
  0.0 0.0 copy-start.2
  0.0 1.0 %copy-done.2 = f32[1024,128]{1,0:T(8,128)S(1)} copy-done((f32[1024,128]{1,0:T(8,128)S(1)}, f32[1024,128]{1,0:T(8,128)}, u32[]{:S(2)}) %copy-start.2) | copy-done | bytes 524312
  1.0 0.9 %shard_map.101 = f32[512,128]{1,0:T(8,128)} custom-call(s32[1]{0:T(128)} %bitcast.2.which_ref, f32[1024,128]{1,0:T(8,128)S(1)} %copy-done.2), custom_call_target="tpu_custom_call" | custom-call | bytes 1048576 | tf_op jit(solution)/shard_map/pallas_call | solution.py:165
  2.0 0.0 copy-start
  2.0 0.0 copy-start.1
  2.0 7.4 %all-to-all-start.1 = ((f32[8,64,128]{2,1,0:T(8,128)}), f32[8,64,128]{2,1,0:T(8,128)S(1)}, u32[]{:S(2)}, u32[]{:S(2)}) async-start(f32[8,64,128]{2,1,0:T(8,128)} %bitcast.3), calls=%async_computation.1 | async-start | bytes 524288 | tf_op jit(solution)/shard_map/all_to_all | solution.py:173
  9.4 0.0 copy-done
  9.4 0.0 copy-done.1
  9.4 1.0 %shard_map.100 = f32[1024,128]{1,0:T(8,128)} custom-call(bf16[1024,128]{1,0:T(8,128)(2,1)S(1)} %copy-done, bf16[1024,128]{1,0:T(8,128)(2,1)S(1)} %copy-done.1), custom_call_target="tpu_custom_call" | custom-call | flops 131072 | bytes 1048576 | tf_op jit(solution)/shard_map/pallas_call | solution.py:170
  10.4 7.9 %all-to-all-done.1 = f32[8,64,128]{2,1,0:T(8,128)S(1)} async-done(((f32[8,64,128]{2,1,0:T(8,128)}), f32[8,64,128]{2,1,0:T(8,128)S(1)}, u32[]{:S(2)}, u32[]{:S(2)}) %all-to-all-start.1) | async-done | bytes 262176 | tf_op jit(solution)/shard_map/all_to_all | solution.py:173
  18.3 0.0 copy-start.3
  18.3 0.0 copy-start.5
  18.3 0.0 copy-start.6
  18.3 4.8 %all-to-all-start = ((f32[16,64,128]{2,1,0:T(8,128)}), f32[16,64,128]{2,1,0:T(8,128)S(1)}, u32[]{:S(2)}, u32[]{:S(2)}) async-start(f32[16,64,128]{2,1,0:T(8,128)} %bitcast), calls=%async_computation | async-start | bytes 1048576 | tf_op jit(solution)/shard_map/all_to_all | solution.py:174
  23.1 0.0 copy-done.3
  23.1 0.0 copy-done.5
  23.1 0.0 copy-done.6
  23.1 0.0 copy-start.8
  23.1 0.0 copy-start.9
  23.1 0.5 shard_map.102.spec_ref
  23.6 14.4 %all-to-all-done = f32[16,64,128]{2,1,0:T(8,128)S(1)} async-done(((f32[16,64,128]{2,1,0:T(8,128)}), f32[16,64,128]{2,1,0:T(8,128)S(1)}, u32[]{:S(2)}, u32[]{:S(2)}) %all-to-all-start) | async-done | bytes 524320 | tf_op jit(solution)/shard_map/all_to_all | solution.py:174
  38.0 0.0 copy-done.8
  38.0 0.0 copy-done.9
  38.0 2.0 %shard_map.103 = f32[2,8,8,8,128]{4,3,2,1,0:T(8,128)S(1)} custom-call(f32[2,8,8,8,128]{4,3,2,1,0:T(8,128)S(1)} %bitcast.10, f32[512,256]{1,0:T(8,128)S(1)} %shard_map.102.spec_ref, bf16[128,192]{1,0:T(8,128)(2,1)S(1)} %copy-done.5, f32[64,256]{1,0:T(8,128)S(1)} %copy-done.6, bf16[768,256]{1,0:T(8,128)(2,1)S(1)} %copy-done.3, bf16[768,256]{1,0:T(8,128)(2,1)S(1)} %copy-done.8, ...), custom_call_target="tpu_custom_call" | custom-call | flops 1006632960 | bytes 1572864 | tf_op jit(solution)/shard_map/pallas_call | solution.py:179
  40.0 0.0 copy-start.4
  40.0 17.8 %all_to_all.29 = f32[16,64,128]{2,1,0:T(8,128)S(1)} all-to-all(f32[16,64,128]{2,1,0:T(8,128)S(1)} %bitcast.11), channel_id=1, replica_groups=mesh['groups'=2,'seq'=8,'chan'=2] {'groups','seq'}, dimensions={0} | all-to-all | bytes 1048576 | tf_op jit(solution)/shard_map/all_to_all | solution.py:183
  57.9 0.0 copy-start.7
  57.9 0.0 copy-done.4
  57.9 0.7 %copy-done.7 = f32[128]{0:T(128)S(1)} copy-done((f32[128]{0:T(128)S(1)}, f32[128]{0:T(128)}, u32[]{:S(2)}) %copy-start.7) | copy-done | bytes 536
  58.5 0.9 %shard_map.104 = bf16[1024,128]{1,0:T(8,128)(2,1)} custom-call(f32[1024,128]{1,0:T(8,128)S(1)} %bitcast.8, bf16[1024,128]{1,0:T(8,128)(2,1)S(1)} %copy-done.4, bf16[1024,128]{1,0:T(8,128)(2,1)S(1)} %copy-done, bf16[1024,128]{1,0:T(8,128)(2,1)S(1)} %copy-done.1, f32[1,128]{1,0:T(1,128)S(1)} %bitcast.12), custom_call_target="tpu_custom_call" | custom-call | flops 524288 | bytes 1572864 | tf_op jit(solution)/shard_map/pallas_call | solution.py:184
Async XLA Ops:
  0.0 1.0 %copy-start.2 = (f32[1024,128]{1,0:T(8,128)S(1)}, f32[1024,128]{1,0:T(8,128)}, u32[]{:S(2)}) copy-start(f32[1024,128]{1,0:T(8,128)} %filter_ref.1) | copy-start | bytes 1572868
  2.0 7.4 %copy-start = (bf16[1024,128]{1,0:T(8,128)(2,1)S(1)}, bf16[1024,128]{1,0:T(8,128)(2,1)}, u32[]{:S(2)}) copy-start(bf16[1024,128]{1,0:T(8,128)(2,1)} %key_ref.3) | copy-start | bytes 786436
  2.0 7.4 %copy-start.1 = (bf16[1024,128]{1,0:T(8,128)(2,1)S(1)}, bf16[1024,128]{1,0:T(8,128)(2,1)}, u32[]{:S(2)}) copy-start(bf16[1024,128]{1,0:T(8,128)(2,1)} %value_ref.3) | copy-start | bytes 786436
  2.0 16.3 %all-to-all-start.1 = ((f32[8,64,128]{2,1,0:T(8,128)}), f32[8,64,128]{2,1,0:T(8,128)S(1)}, u32[]{:S(2)}, u32[]{:S(2)}) async-start(f32[8,64,128]{2,1,0:T(8,128)} %bitcast.3), calls=%async_computation.1 | async-start | bytes 524288 | tf_op jit(solution)/shard_map/all_to_all | solution.py:173
  18.3 4.8 %copy-start.3 = (bf16[768,256]{1,0:T(8,128)(2,1)S(1)}, bf16[768,256]{1,0:T(8,128)(2,1)}, u32[]{:S(2)}) copy-start(bf16[768,256]{1,0:T(8,128)(2,1)} %constant.18.clone.tail_ref) | copy-start | bytes 1179652
  18.3 4.8 %copy-start.5 = (bf16[128,192]{1,0:T(8,128)(2,1)S(1)}, bf16[128,192]{1,0:T(8,128)(2,1)}, u32[]{:S(2)}) copy-start(bf16[128,192]{1,0:T(8,128)(2,1)} %constant.16.clone.head_ref) | copy-start | bytes 147460
  18.3 4.8 %copy-start.6 = (f32[64,256]{1,0:T(8,128)S(1)}, f32[64,256]{1,0:T(8,128)}, u32[]{:S(2)}) copy-start(f32[64,256]{1,0:T(8,128)} %constant.17.clone.twist_ref) | copy-start | bytes 196612
  18.3 19.7 %all-to-all-start = ((f32[16,64,128]{2,1,0:T(8,128)}), f32[16,64,128]{2,1,0:T(8,128)S(1)}, u32[]{:S(2)}, u32[]{:S(2)}) async-start(f32[16,64,128]{2,1,0:T(8,128)} %bitcast), calls=%async_computation | async-start | bytes 1048576 | tf_op jit(solution)/shard_map/all_to_all | solution.py:174
  23.1 14.9 %copy-start.8 = (bf16[768,256]{1,0:T(8,128)(2,1)S(1)}, bf16[768,256]{1,0:T(8,128)(2,1)}, u32[]{:S(2)}) copy-start(bf16[768,256]{1,0:T(8,128)(2,1)} %constant.19.clone.back_tail_ref) | copy-start | bytes 1179652
  23.1 14.9 %copy-start.9 = (bf16[64,384]{1,0:T(8,128)(2,1)S(1)}, bf16[64,384]{1,0:T(8,128)(2,1)}, u32[]{:S(2)}) copy-start(bf16[64,384]{1,0:T(8,128)(2,1)} %constant.20.clone.back_head_ref) | copy-start | bytes 147460
  40.0 17.8 %copy-start.4 = (bf16[1024,128]{1,0:T(8,128)(2,1)S(1)}, bf16[1024,128]{1,0:T(8,128)(2,1)}, u32[]{:S(2)}) copy-start(bf16[1024,128]{1,0:T(8,128)(2,1)} %query_ref.1) | copy-start | bytes 786436
  57.9 0.7 %copy-start.7 = (f32[128]{0:T(128)S(1)}, f32[128]{0:T(128)}, u32[]{:S(2)}) copy-start(f32[128]{0:T(128)} %param.14) | copy-start | bytes 1540
where the time goes:
time: 59.9 us; the launch traced here: 59.4 us
  waiting for transfers between devices  22.3 us (37%)
  blocking collectives  17.8 us (30%)
  starting transfers between devices  12.2 us (20%)
  Pallas kernels  5.38 us (9%)
  local copies, waits for them, and re-layouts  1.73 us (3%)
    all_to_all x1, blocking collectives, shards(): lax.all_to_all(local.reshape(chans * rows, LANES), ('groups', 'seq'), 0,...  17.8 us
    all_to_all x1, waiting for transfers between devices, shards(): moved = lax.all_to_all(packed, ('groups', 'seq'), 0, 0, tiled=True)  14.4 us
    all_to_all x1, waiting for transfers between devices, shards(): moved_filter = lax.all_to_all(packed_filter, 'seq', 0, 0, tiled=True)  7.9 us
    all_to_all x1, starting transfers between devices, shards(): moved_filter = lax.all_to_all(packed_filter, 'seq', 0, 0, tiled=True)  7.41 us
    all_to_all x1, starting transfers between devices, shards(): moved = lax.all_to_all(packed, ('groups', 'seq'), 0, 0, tiled=True)  4.75 us
    pallas_call x1, Pallas kernels, shards(): call(functools.partial(conv_kernel, own), (groups, blocks, own, rows, LAN...  2.03 us
    unnamed x20, local copies, waits for them, and re-layouts  1.73 us
  transfers between devices with their start and end apart: 2, of which 2 were waited for; matrix products, arithmetic and copies ran while one was open for 0% of the time, Pallas kernels for 3%

commit v1 on v0

--- a/solution.py
+++ b/solution.py
@@ -76,53 +76,50 @@
     return mat(by_lanes(jnp.concatenate(rows, axis=0)), tail)
 
 
-def pack_kernel(rows, key_ref, value_ref, out_ref):
+def pack_kernel(rows, own, share, which_ref, key_ref, value_ref, filter_ref, out_ref, turned):
     for row in range(rows):
         span = pl.ds(row * LANES, LANES)
-        driver = key_ref[span, :].astype(F32) * value_ref[span, :].astype(F32)
-        out_ref[pl.ds(row, LANES, stride=rows), :] = driver.T
+        turned[0, pl.ds(row, LANES, stride=rows), :] = (
+            key_ref[span, :].astype(F32) * value_ref[span, :].astype(F32)
+        ).T
+        turned[1, pl.ds(row, LANES, stride=rows), :] = filter_ref[span, :].T
+    first = which_ref[0] * (share * rows if share < own else 0)
+    for peer in range(out_ref.shape[0]):
+        start = peer * own * rows
+        out_ref[peer, : own * rows] = turned[0, pl.ds(start, own * rows), :]
+        taken = pl.ds(pl.multiple_of(start + first, rows), share * rows)
+        out_ref[peer, own * rows :] = turned[1, taken, :]
 
 
-def pack_filter_kernel(rows, which_ref, filter_ref, out_ref, scratch):
-    for row in range(rows):
-        scratch[pl.ds(row, LANES, stride=rows), :] = filter_ref[pl.ds(row * LANES, LANES), :].T
-    size = out_ref.shape[0]
-    start = pl.multiple_of(which_ref[0] * size, size)
-    out_ref[...] = scratch[pl.ds(start, size), :]
-
-
-def filter_kernel(own, filter_ref, head_ref, twist_ref, tail_ref, out_ref):
-    blocks, rows = filter_ref.shape[0], filter_ref.shape[2]
-    signals = [filter_ref[:, chan].reshape(blocks * rows, LANES) for chan in range(own)]
-    out_ref[...] = forward(signals, head_ref[...], twist_ref[...], tail_ref[...])
-
-
-def conv_kernel(own, driver_ref, spec_ref, head_ref, twist_ref, tail_ref, back_tail_ref, back_head_ref, out_ref):
-    groups, blocks, _, rows = driver_ref.shape[:4]
+def conv_kernel(rows, own, share, moved_ref, head_ref, twist_ref, tail_ref, back_tail_ref, back_head_ref, out_ref):
+    groups, blocks = moved_ref.shape[:2]
     outer = blocks * rows
     scale = 1.0 / (outer * LANES)
-    signals = [
-        driver_ref[group, :, chan].reshape(outer, LANES) for chan in range(own) for group in range(groups)
-    ]
+
+    def signal(group, place):
+        return moved_ref[group, :, place * rows : (place + 1) * rows].reshape(outer, LANES)
+
+    signals = [signal(chan // share, own + chan % share) for chan in range(own)]
+    signals += [signal(group, chan) for chan in range(own) for group in range(groups)]
     spec = forward(signals, head_ref[...], twist_ref[...], tail_ref[...])
+    pieces = [spec[idx * outer : (idx + 1) * outer] for idx in range(len(signals))]
     prods = []
-    for idx in range(len(signals)):
-        own_spec = spec_ref[pl.ds(idx // groups * outer, outer), :]
-        f_re, f_im = own_spec[:, :LANES], own_spec[:, LANES:]
-        mine = spec[idx * outer : (idx + 1) * outer]
+    for idx, mine in enumerate(pieces[own:]):
+        other = pieces[idx // groups]
+        f_re, f_im = other[:, :LANES], other[:, LANES:]
         d_re, d_im = mine[:, :LANES], mine[:, LANES:]
         prods.append(jnp.concatenate([d_re * f_re - d_im * f_im, d_re * f_im + d_im * f_re], axis=1))
     back = mat(by_lanes(jnp.concatenate(prods, axis=0)), back_tail_ref[...])
     cos, sin = twist_ref[:, :LANES] * scale, twist_ref[:, LANES:] * scale
     reals, imags = [], []
-    for idx in range(len(signals)):
+    for idx in range(len(prods)):
         mine = back[idx * outer : (idx + 1) * outer]
         real, imag = mine[:, :LANES], mine[:, LANES:]
         reals.append(real * cos + imag * sin)
         imags.append(imag * cos - real * sin)
     mixed = jnp.concatenate([jnp.concatenate(reals, axis=1), jnp.concatenate(imags, axis=1)], axis=0)
     result = mat(back_head_ref[...], by_rows(mixed))
-    for idx in range(len(signals)):
+    for idx in range(len(prods)):
         chan, group = divmod(idx, groups)
         out_ref[group, :, chan] = result[:, idx * LANES : (idx + 1) * LANES].reshape(blocks, rows, LANES)
 
@@ -162,24 +159,18 @@
     head, twist, tail, back_tail, back_head = (jnp.asarray(table) for table in tables)
     size = tokens * chans * 4
 
-    packed_filter = call(
-        functools.partial(pack_filter_kernel, rows),
-        (blocks * own * rows, LANES), F32, [SMEM, VMEM], 0, size * 2,
-        [pltpu.VMEM((chans * rows, LANES), F32)],
-    )(lax.axis_index("groups").reshape(1).astype(jnp.int32), long_filter)
-    packed = call(functools.partial(pack_kernel, rows), (chans * rows, LANES), F32, [VMEM, VMEM], size // 4, size * 2)(
-        key_proj, value_proj
-    )
-    moved_filter = lax.all_to_all(packed_filter, "seq", 0, 0, tiled=True)
+    share = own // groups if own % groups == 0 else own
+    packed = call(
+        functools.partial(pack_kernel, rows, own, share),
+        (groups * blocks, (own + share) * rows, LANES), F32, [SMEM, VMEM, VMEM, VMEM], size // 4, size * 4,
+        [pltpu.VMEM((2, chans * rows, LANES), F32)],
+    )(lax.axis_index("groups").reshape(1).astype(jnp.int32), key_proj, value_proj, long_filter)
     moved = lax.all_to_all(packed, ("groups", "seq"), 0, 0, tiled=True)
     macs = 2 * 3 * own * seq_len * (2 * outer + 4 * LANES)
-    spec = call(
-        functools.partial(filter_kernel, own), (own * outer, 2 * LANES), F32, [VMEM] * 4, macs, size
-    )(moved_filter.reshape(blocks, own, rows, LANES), head, twist, tail)
     local = call(
-        functools.partial(conv_kernel, own),
-        (groups, blocks, own, rows, LANES), F32, [VMEM] * 7, 4 * macs, 3 * size,
-    )(moved.reshape(groups, blocks, own, rows, LANES), spec, head, twist, tail, back_tail, back_head)
+        functools.partial(conv_kernel, rows, own, share),
+        (groups, blocks, own, rows, LANES), F32, [VMEM] * 6, 5 * macs, 3 * size,
+    )(moved.reshape(groups, blocks, (own + share) * rows, LANES), head, twist, tail, back_tail, back_head)
     convolved = lax.all_to_all(local.reshape(chans * rows, LANES), ("groups", "seq"), 0, 0, tiled=True)
     return call(functools.partial(gate_kernel, rows), (tokens, chans), BF16, [VMEM] * 5, size, 3 * size)(
         convolved, query_proj, key_proj, value_proj, skip_bias.reshape(1, chans)

time: 59.9 us -> 55.5 us (0.927)
  blocking collectives: 17.8 us -> 47.3 us
  waiting for transfers between devices: 22.3 us -> 0 us
  starting transfers between devices: 12.2 us -> 0 us
  local copies, waits for them, and re-layouts: 1.73 us -> 3.64 us
  Pallas kernels: 5.38 us -> 4.07 us
    all_to_all x0 -> x1, blocking collectives: none -> 29.5 us  [shards(): moved = lax.all_to_all(packed, ('groups', 'seq'), 0, 0, tiled=True)]
    all_to_all x2 -> x0, waiting for transfers between devices: 22.3 us -> none  [the longest x1 14.4 us: shards(): moved = lax.all_to_all(packed, ('groups', 'seq'), 0, 0, tiled=True)]
    all_to_all x2 -> x0, starting transfers between devices: 12.2 us -> none  [the longest x1 7.41 us: shards(): moved_filter = lax.all_to_all(packed_filter, 'seq', 0, 0, tiled=True)]
    unnamed x20 -> x24, local copies, waits for them, and re-layouts: 1.73 us -> 3.64 us
    pallas_call x4 -> x2, Pallas kernels: 4.47 us -> 3.16 us  [the longest x1 2.77 us: shards(): call(functools.partial(conv_kernel, rows, own, share), (groups, blocks, o...]
  transfers between devices with their start and end apart: 2 -> 0, of which waited for: 2 -> 0; matrix products, arithmetic and copies ran while one was open for 0% -> 0% of each run, Pallas kernels for 3% -> 0%
where the time goes in v1:
time: 55.5 us; the launch traced here: 55.1 us
  blocking collectives  47.3 us (85%)
  Pallas kernels  4.07 us (7%)
  local copies, waits for them, and re-layouts  3.64 us (7%)
    all_to_all x1, blocking collectives, shards(): moved = lax.all_to_all(packed, ('groups', 'seq'), 0, 0, tiled=True)  29.5 us
    all_to_all x1, blocking collectives, shards(): lax.all_to_all(local.reshape(chans * rows, LANES), ('groups', 'seq'), 0,...  17.8 us
    unnamed x24, local copies, waits for them, and re-layouts  3.64 us
    pallas_call x1, Pallas kernels, shards(): call(functools.partial(conv_kernel, rows, own, share), (groups, blocks, o...  2.77 us

profile of v1, /device:TPU:0, one launch (start us, length us, event | category | flops | bytes accessed | tf_op | source)
XLA Modules:
  0.0 55.1 jit_solution(16052613097703540991)
XLA Ops:
  0.0 0.0 copy-start
  0.0 0.9 %copy-done = bf16[1024,128]{1,0:T(8,128)(2,1)S(1)} copy-done((bf16[1024,128]{1,0:T(8,128)(2,1)S(1)}, bf16[1024,128]{1,0:T(8,128)(2,1)}, u32[]{:S(2)}) %copy-start) | copy-done | bytes 262168
  1.0 0.0 copy-start.2
  1.0 0.9 %copy-done.2 = bf16[1024,128]{1,0:T(8,128)(2,1)S(1)} copy-done((bf16[1024,128]{1,0:T(8,128)(2,1)S(1)}, bf16[1024,128]{1,0:T(8,128)(2,1)}, u32[]{:S(2)}) %copy-start.2) | copy-done | bytes 262168
  1.9 0.0 copy-start.4
  1.9 1.0 %copy-done.4 = f32[1024,128]{1,0:T(8,128)S(1)} copy-done((f32[1024,128]{1,0:T(8,128)S(1)}, f32[1024,128]{1,0:T(8,128)}, u32[]{:S(2)}) %copy-start.4) | copy-done | bytes 524312
  2.9 0.4 shard_map.100
  3.3 0.0 copy-start.7
  3.4 0.0 copy-start.8
  3.4 0.0 copy-start.9
  3.4 0.0 copy-start.10
  3.4 0.0 copy-start.11
  3.4 29.5 %all_to_all.16 = f32[16,96,128]{2,1,0:T(8,128)S(1)} all-to-all(f32[16,96,128]{2,1,0:T(8,128)S(1)} %shard_map.100), channel_id=1, replica_groups=mesh['groups'=2,'seq'=8,'chan'=2] {'groups','seq'}, dimensions={0} | all-to-all | bytes 1572864 | tf_op jit(solution)/shard_map/all_to_all | solution.py:168
  32.9 0.0 copy-done.7
  32.9 0.0 copy-done.8
  32.9 0.0 copy-done.9
  32.9 0.0 copy-done.10
  33.0 0.0 copy-done.11
  33.0 2.8 %shard_map.101 = f32[2,8,8,8,128]{4,3,2,1,0:T(8,128)S(1)} custom-call(f32[2,8,96,128]{3,2,1,0:T(8,128)S(1)} %bitcast.6, bf16[128,192]{1,0:T(8,128)(2,1)S(1)} %copy-done.10, f32[64,256]{1,0:T(8,128)S(1)} %copy-done.9, bf16[768,256]{1,0:T(8,128)(2,1)S(1)} %copy-done.8, bf16[768,256]{1,0:T(8,128)(2,1)S(1)} %copy-done.7, bf16[64,384]{1,0:T(8,128)(2,1)S(1)} %copy-done.11), custom_call_target="tpu_custom_call" | custom-call | flops 1258291200 | bytes 1572864 | tf_op jit(solution)/shard_map/pallas_call | solution.py:170
  35.7 0.0 copy-start.1
  35.7 0.0 copy-start.3
  35.8 0.0 copy-start.5
  35.8 17.8 %all_to_all.17 = f32[16,64,128]{2,1,0:T(8,128)S(1)} all-to-all(f32[16,64,128]{2,1,0:T(8,128)S(1)} %bitcast.7), channel_id=1, replica_groups=mesh['groups'=2,'seq'=8,'chan'=2] {'groups','seq'}, dimensions={0} | all-to-all | bytes 1048576 | tf_op jit(solution)/shard_map/all_to_all | solution.py:174
  53.6 0.0 copy-start.6
  53.6 0.0 copy-done.1
  53.6 0.0 copy-done.3
  53.6 0.0 copy-done.5
  53.6 0.6 %copy-done.6 = f32[128]{0:T(128)S(1)} copy-done((f32[128]{0:T(128)S(1)}, f32[128]{0:T(128)}, u32[]{:S(2)}) %copy-start.6) | copy-done | bytes 536
  54.2 0.9 %shard_map.102 = bf16[1024,128]{1,0:T(8,128)(2,1)} custom-call(f32[1024,128]{1,0:T(8,128)S(1)} %bitcast.5, bf16[1024,128]{1,0:T(8,128)(2,1)S(1)} %copy-done.5, bf16[1024,128]{1,0:T(8,128)(2,1)S(1)} %copy-done.1, bf16[1024,128]{1,0:T(8,128)(2,1)S(1)} %copy-done.3, f32[1,128]{1,0:T(1,128)S(1)} %bitcast.8), custom_call_target="tpu_custom_call" | custom-call | flops 524288 | bytes 1572864 | tf_op jit(solution)/shard_map/pallas_call | solution.py:175
Async XLA Ops:
  0.0 0.9 %copy-start = (bf16[1024,128]{1,0:T(8,128)(2,1)S(1)}, bf16[1024,128]{1,0:T(8,128)(2,1)}, u32[]{:S(2)}) copy-start(bf16[1024,128]{1,0:T(8,128)(2,1)} %key_ref.3) | copy-start | bytes 786436
  1.0 0.9 %copy-start.2 = (bf16[1024,128]{1,0:T(8,128)(2,1)S(1)}, bf16[1024,128]{1,0:T(8,128)(2,1)}, u32[]{:S(2)}) copy-start(bf16[1024,128]{1,0:T(8,128)(2,1)} %value_ref.3) | copy-start | bytes 786436
  1.9 1.0 %copy-start.4 = (f32[1024,128]{1,0:T(8,128)S(1)}, f32[1024,128]{1,0:T(8,128)}, u32[]{:S(2)}) copy-start(f32[1024,128]{1,0:T(8,128)} %filter_ref.1) | copy-start | bytes 1572868
  3.3 29.6 %copy-start.7 = (bf16[768,256]{1,0:T(8,128)(2,1)S(1)}, bf16[768,256]{1,0:T(8,128)(2,1)}, u32[]{:S(2)}) copy-start(bf16[768,256]{1,0:T(8,128)(2,1)} %constant.19.clone.back_tail_ref) | copy-start | bytes 1179652
  3.4 29.6 %copy-start.8 = (bf16[768,256]{1,0:T(8,128)(2,1)S(1)}, bf16[768,256]{1,0:T(8,128)(2,1)}, u32[]{:S(2)}) copy-start(bf16[768,256]{1,0:T(8,128)(2,1)} %constant.18.clone.tail_ref) | copy-start | bytes 1179652
  3.4 29.6 %copy-start.9 = (f32[64,256]{1,0:T(8,128)S(1)}, f32[64,256]{1,0:T(8,128)}, u32[]{:S(2)}) copy-start(f32[64,256]{1,0:T(8,128)} %constant.17.clone.twist_ref) | copy-start | bytes 196612
  3.4 29.6 %copy-start.10 = (bf16[128,192]{1,0:T(8,128)(2,1)S(1)}, bf16[128,192]{1,0:T(8,128)(2,1)}, u32[]{:S(2)}) copy-start(bf16[128,192]{1,0:T(8,128)(2,1)} %constant.16.clone.head_ref) | copy-start | bytes 147460
  3.4 29.6 %copy-start.11 = (bf16[64,384]{1,0:T(8,128)(2,1)S(1)}, bf16[64,384]{1,0:T(8,128)(2,1)}, u32[]{:S(2)}) copy-start(bf16[64,384]{1,0:T(8,128)(2,1)} %constant.20.clone.back_head_ref) | copy-start | bytes 147460
  35.7 17.9 %copy-start.1 = (bf16[1024,128]{1,0:T(8,128)(2,1)S(1)}, bf16[1024,128]{1,0:T(8,128)(2,1)}, u32[]{:S(2)}) copy-start(bf16[1024,128]{1,0:T(8,128)(2,1)} %key_ref.3) | copy-start | bytes 786436
  35.7 17.8 %copy-start.3 = (bf16[1024,128]{1,0:T(8,128)(2,1)S(1)}, bf16[1024,128]{1,0:T(8,128)(2,1)}, u32[]{:S(2)}) copy-start(bf16[1024,128]{1,0:T(8,128)(2,1)} %value_ref.3) | copy-start | bytes 786436
  35.8 17.8 %copy-start.5 = (bf16[1024,128]{1,0:T(8,128)(2,1)S(1)}, bf16[1024,128]{1,0:T(8,128)(2,1)}, u32[]{:S(2)}) copy-start(bf16[1024,128]{1,0:T(8,128)(2,1)} %query_ref.1) | copy-start | bytes 786436
  53.6 0.7 %copy-start.6 = (f32[128]{0:T(128)S(1)}, f32[128]{0:T(128)}, u32[]{:S(2)}) copy-start(f32[128]{0:T(128)} %param.14) | copy-start | bytes 1540

commit v2 on v1

--- a/solution.py
+++ b/solution.py
@@ -76,13 +76,26 @@
     return mat(by_lanes(jnp.concatenate(rows, axis=0)), tail)
 
 
-def pack_kernel(rows, own, share, which_ref, key_ref, value_ref, filter_ref, out_ref, turned):
+def pack_kernel(rows, own, share, which_ref, *refs):
+    sources, bias_ref, out_ref, bias_out = refs[:3], refs[3], refs[4], refs[5]
+    held, turned, sems = refs[6:9], refs[9], refs[10]
+
+    def fetch(place, row):
+        span = pl.ds(row * LANES, LANES)
+        return pltpu.make_async_copy(sources[place].at[span], held[place].at[span], sems.at[place, row])
+
+    for row in range(rows):
+        for place in range(3):
+            fetch(place, row).start()
+    bias_out[...] = bias_ref[...]
     for row in range(rows):
         span = pl.ds(row * LANES, LANES)
-        turned[0, pl.ds(row, LANES, stride=rows), :] = (
-            key_ref[span, :].astype(F32) * value_ref[span, :].astype(F32)
-        ).T
-        turned[1, pl.ds(row, LANES, stride=rows), :] = filter_ref[span, :].T
+        fetch(0, row).wait()
+        fetch(1, row).wait()
+        driver = held[0][span, :].astype(F32) * held[1][span, :].astype(F32)
+        turned[0, pl.ds(row, LANES, stride=rows), :] = driver.T
+        fetch(2, row).wait()
+        turned[1, pl.ds(row, LANES, stride=rows), :] = held[2][span, :].T
     first = which_ref[0] * (share * rows if share < own else 0)
     for peer in range(out_ref.shape[0]):
         start = peer * own * rows
@@ -134,15 +147,16 @@
 
 
 VMEM = pl.BlockSpec(memory_space=pltpu.VMEM)
+ANY = pl.BlockSpec(memory_space=pl.ANY)
 SMEM = pl.BlockSpec(memory_space=pltpu.SMEM)
 
 
-def call(kernel, shape, dtype, specs, flops, moved, scratch=()):
+def call(kernel, outs, specs, flops, moved, scratch=()):
     return pl.pallas_call(
         kernel,
-        out_shape=jax.ShapeDtypeStruct(shape, dtype),
+        out_shape=[jax.ShapeDtypeStruct(*out) for out in outs],
         in_specs=specs,
-        out_specs=VMEM,
+        out_specs=[VMEM] * len(outs),
         scratch_shapes=scratch,
         compiler_params=pltpu.CompilerParams(vmem_limit_bytes=VMEM_LIMIT),
         cost_estimate=pl.CostEstimate(flops=flops, bytes_accessed=moved, transcendentals=0),
@@ -160,21 +174,24 @@
     size = tokens * chans * 4
 
     share = own // groups if own % groups == 0 else own
-    packed = call(
+    packed, bias = call(
         functools.partial(pack_kernel, rows, own, share),
-        (groups * blocks, (own + share) * rows, LANES), F32, [SMEM, VMEM, VMEM, VMEM], size // 4, size * 4,
-        [pltpu.VMEM((2, chans * rows, LANES), F32)],
-    )(lax.axis_index("groups").reshape(1).astype(jnp.int32), key_proj, value_proj, long_filter)
+        [((groups * blocks, (own + share) * rows, LANES), F32), ((1, chans), F32)],
+        [SMEM, ANY, ANY, ANY, VMEM], size // 4, size * 4,
+        [pltpu.VMEM((tokens, chans), BF16), pltpu.VMEM((tokens, chans), BF16), pltpu.VMEM((tokens, chans), F32),
+         pltpu.VMEM((2, chans * rows, LANES), F32), pltpu.SemaphoreType.DMA((3, rows))],
+    )(lax.axis_index("groups").reshape(1).astype(jnp.int32), key_proj, value_proj, long_filter,
+      skip_bias.reshape(1, chans))
     moved = lax.all_to_all(packed, ("groups", "seq"), 0, 0, tiled=True)
     macs = 2 * 3 * own * seq_len * (2 * outer + 4 * LANES)
     local = call(
         functools.partial(conv_kernel, rows, own, share),
-        (groups, blocks, own, rows, LANES), F32, [VMEM] * 6, 5 * macs, 3 * size,
-    )(moved.reshape(groups, blocks, (own + share) * rows, LANES), head, twist, tail, back_tail, back_head)
+        [((groups, blocks, own, rows, LANES), F32)], [VMEM] * 6, 5 * macs, 3 * size,
+    )(moved.reshape(groups, blocks, (own + share) * rows, LANES), head, twist, tail, back_tail, back_head)[0]
     convolved = lax.all_to_all(local.reshape(chans * rows, LANES), ("groups", "seq"), 0, 0, tiled=True)
-    return call(functools.partial(gate_kernel, rows), (tokens, chans), BF16, [VMEM] * 5, size, 3 * size)(
-        convolved, query_proj, key_proj, value_proj, skip_bias.reshape(1, chans)
-    )
+    return call(functools.partial(gate_kernel, rows), [((tokens, chans), BF16)], [VMEM] * 5, size, 3 * size)(
+        convolved, query_proj, key_proj, value_proj, bias
+    )[0]
 
 
 def solution(mesh):

time: 55.5 us -> 58.3 us (1.050)
  Pallas kernels: 4.07 us -> 6.93 us
    pallas_call x3, Pallas kernels: 4.07 us -> 6.93 us  [the longest x1 3.24 us: shards(): call(functools.partial(pack_kernel, rows, own, share), [((groups * blocks...]
where the time goes in v2:
time: 58.3 us; the launch traced here: 58 us
  blocking collectives  47.3 us (81%)
  Pallas kernels  6.93 us (12%)
  local copies, waits for them, and re-layouts  3.65 us (6%)
    all_to_all x1, blocking collectives, shards(): moved = lax.all_to_all(packed, ('groups', 'seq'), 0, 0, tiled=True)  29.5 us
    all_to_all x1, blocking collectives, shards(): lax.all_to_all(local.reshape(chans * rows, LANES), ('groups', 'seq'), 0,...  17.8 us
    unnamed x24, local copies, waits for them, and re-layouts  3.65 us
    pallas_call x1, Pallas kernels, shards(): call(functools.partial(pack_kernel, rows, own, share), [((groups * blocks...  3.24 us
    pallas_call x1, Pallas kernels, shards(): call(functools.partial(conv_kernel, rows, own, share), [((groups, blocks,...  2.77 us

profile of v2, /device:TPU:0, one launch (start us, length us, event | category | flops | bytes accessed | tf_op | source)
XLA Modules:
  0.0 58.0 jit_solution(3318802113680644033)
XLA Ops:
  0.0 0.0 copy-start.6
  0.0 0.7 %copy-done.6 = f32[128]{0:T(128)S(1)} copy-done((f32[128]{0:T(128)S(1)}, f32[128]{0:T(128)}, u32[]{:S(2)}) %copy-start.6) | copy-done | bytes 536
  0.7 0.0 copy-start
  0.7 0.9 %copy-done = bf16[1024,128]{1,0:T(8,128)(2,1)S(1)} copy-done((bf16[1024,128]{1,0:T(8,128)(2,1)S(1)}, bf16[1024,128]{1,0:T(8,128)(2,1)}, u32[]{:S(2)}) %copy-start) | copy-done | bytes 262168
  1.6 0.0 copy-start.2
  1.6 0.9 %copy-done.2 = bf16[1024,128]{1,0:T(8,128)(2,1)S(1)} copy-done((bf16[1024,128]{1,0:T(8,128)(2,1)S(1)}, bf16[1024,128]{1,0:T(8,128)(2,1)}, u32[]{:S(2)}) %copy-start.2) | copy-done | bytes 262168
  2.6 0.0 copy-start.4
  2.6 1.0 %copy-done.4 = f32[1024,128]{1,0:T(8,128)S(1)} copy-done((f32[1024,128]{1,0:T(8,128)S(1)}, f32[1024,128]{1,0:T(8,128)}, u32[]{:S(2)}) %copy-start.4) | copy-done | bytes 524312
  3.6 3.2 %shard_map.100 = (f32[16,96,128]{2,1,0:T(8,128)S(1)}, f32[1,128]{1,0:T(1,128)S(1)}) custom-call(s32[1]{0:T(128)} %bitcast.which_ref, bf16[1024,128]{1,0:T(8,128)(2,1)S(1)} %copy-done, bf16[1024,128]{1,0:T(8,128)(2,1)S(1)} %copy-done.2, f32[1024,128]{1,0:T(8,128)S(1)} %copy-done.4, f32[1,128]{1,0:T(1,128)S(1)} %bitcast.8), custom_call_target="tpu_custom_call" | custom-call | flops 131072 | bytes 2097152 | tf_op jit(solution)/shard_map/pallas_call | solution.py:177
  6.8 0.0 copy-start.7
  6.9 0.0 copy-start.8
  6.9 0.0 copy-start.9
  6.9 0.0 copy-start.10
  6.9 0.0 copy-start.11
  6.9 29.5 %all_to_all.16 = f32[16,96,128]{2,1,0:T(8,128)S(1)} all-to-all(f32[16,96,128]{2,1,0:T(8,128)S(1)} %get-tuple-element.7), channel_id=1, replica_groups=mesh['groups'=2,'seq'=8,'chan'=2] {'groups','seq'}, dimensions={0} | all-to-all | bytes 1572864 | tf_op jit(solution)/shard_map/all_to_all | solution.py:185
  36.4 0.0 copy-done.7
  36.4 0.0 copy-done.8
  36.4 0.0 copy-done.9
  36.4 0.0 copy-done.10
  36.5 0.0 copy-done.11
  36.5 2.8 %shard_map.101 = f32[2,8,8,8,128]{4,3,2,1,0:T(8,128)S(1)} custom-call(f32[2,8,96,128]{3,2,1,0:T(8,128)S(1)} %bitcast.6, bf16[128,192]{1,0:T(8,128)(2,1)S(1)} %copy-done.10, f32[64,256]{1,0:T(8,128)S(1)} %copy-done.9, bf16[768,256]{1,0:T(8,128)(2,1)S(1)} %copy-done.8, bf16[768,256]{1,0:T(8,128)(2,1)S(1)} %copy-done.7, bf16[64,384]{1,0:T(8,128)(2,1)S(1)} %copy-done.11), custom_call_target="tpu_custom_call" | custom-call | flops 1258291200 | bytes 1572864 | tf_op jit(solution)/shard_map/pallas_call | solution.py:187
  39.2 0.0 copy-start.1
  39.2 0.0 copy-start.3
  39.3 0.0 copy-start.5
  39.3 17.8 %all_to_all.17 = f32[16,64,128]{2,1,0:T(8,128)S(1)} all-to-all(f32[16,64,128]{2,1,0:T(8,128)S(1)} %bitcast.7), channel_id=1, replica_groups=mesh['groups'=2,'seq'=8,'chan'=2] {'groups','seq'}, dimensions={0} | all-to-all | bytes 1048576 | tf_op jit(solution)/shard_map/all_to_all | solution.py:191
  57.1 0.0 copy-done.1
  57.1 0.0 copy-done.3
  57.1 0.0 copy-done.5
  57.1 0.9 %shard_map.102 = bf16[1024,128]{1,0:T(8,128)(2,1)} custom-call(f32[1024,128]{1,0:T(8,128)S(1)} %bitcast.5, bf16[1024,128]{1,0:T(8,128)(2,1)S(1)} %copy-done.5, bf16[1024,128]{1,0:T(8,128)(2,1)S(1)} %copy-done.1, bf16[1024,128]{1,0:T(8,128)(2,1)S(1)} %copy-done.3, f32[1,128]{1,0:T(1,128)S(1)} %get-tuple-element.8.bias_ref), custom_call_target="tpu_custom_call" | custom-call | flops 524288 | bytes 1572864 | tf_op jit(solution)/shard_map/pallas_call | solution.py:192
Async XLA Ops:
  0.0 0.7 %copy-start.6 = (f32[128]{0:T(128)S(1)}, f32[128]{0:T(128)}, u32[]{:S(2)}) copy-start(f32[128]{0:T(128)} %param.14) | copy-start | bytes 1540
  0.7 0.9 %copy-start = (bf16[1024,128]{1,0:T(8,128)(2,1)S(1)}, bf16[1024,128]{1,0:T(8,128)(2,1)}, u32[]{:S(2)}) copy-start(bf16[1024,128]{1,0:T(8,128)(2,1)} %key_ref.1) | copy-start | bytes 786436
  1.6 0.9 %copy-start.2 = (bf16[1024,128]{1,0:T(8,128)(2,1)S(1)}, bf16[1024,128]{1,0:T(8,128)(2,1)}, u32[]{:S(2)}) copy-start(bf16[1024,128]{1,0:T(8,128)(2,1)} %value_ref.1) | copy-start | bytes 786436
  2.6 1.0 %copy-start.4 = (f32[1024,128]{1,0:T(8,128)S(1)}, f32[1024,128]{1,0:T(8,128)}, u32[]{:S(2)}) copy-start(f32[1024,128]{1,0:T(8,128)} %refs_2_.1) | copy-start | bytes 1572868
  6.8 29.6 %copy-start.7 = (bf16[768,256]{1,0:T(8,128)(2,1)S(1)}, bf16[768,256]{1,0:T(8,128)(2,1)}, u32[]{:S(2)}) copy-start(bf16[768,256]{1,0:T(8,128)(2,1)} %constant.19.clone.back_tail_ref) | copy-start | bytes 1179652
  6.9 29.6 %copy-start.8 = (bf16[768,256]{1,0:T(8,128)(2,1)S(1)}, bf16[768,256]{1,0:T(8,128)(2,1)}, u32[]{:S(2)}) copy-start(bf16[768,256]{1,0:T(8,128)(2,1)} %constant.18.clone.tail_ref) | copy-start | bytes 1179652
  6.9 29.6 %copy-start.9 = (f32[64,256]{1,0:T(8,128)S(1)}, f32[64,256]{1,0:T(8,128)}, u32[]{:S(2)}) copy-start(f32[64,256]{1,0:T(8,128)} %constant.17.clone.twist_ref) | copy-start | bytes 196612
  6.9 29.6 %copy-start.10 = (bf16[128,192]{1,0:T(8,128)(2,1)S(1)}, bf16[128,192]{1,0:T(8,128)(2,1)}, u32[]{:S(2)}) copy-start(bf16[128,192]{1,0:T(8,128)(2,1)} %constant.16.clone.head_ref) | copy-start | bytes 147460
  6.9 29.6 %copy-start.11 = (bf16[64,384]{1,0:T(8,128)(2,1)S(1)}, bf16[64,384]{1,0:T(8,128)(2,1)}, u32[]{:S(2)}) copy-start(bf16[64,384]{1,0:T(8,128)(2,1)} %constant.20.clone.back_head_ref) | copy-start | bytes 147460
  39.2 17.9 %copy-start.1 = (bf16[1024,128]{1,0:T(8,128)(2,1)S(1)}, bf16[1024,128]{1,0:T(8,128)(2,1)}, u32[]{:S(2)}) copy-start(bf16[1024,128]{1,0:T(8,128)(2,1)} %key_ref.1) | copy-start | bytes 786436
  39.2 17.8 %copy-start.3 = (bf16[1024,128]{1,0:T(8,128)(2,1)S(1)}, bf16[1024,128]{1,0:T(8,128)(2,1)}, u32[]{:S(2)}) copy-start(bf16[1024,128]{1,0:T(8,128)(2,1)} %value_ref.1) | copy-start | bytes 786436
  39.3 17.8 %copy-start.5 = (bf16[1024,128]{1,0:T(8,128)(2,1)S(1)}, bf16[1024,128]{1,0:T(8,128)(2,1)}, u32[]{:S(2)}) copy-start(bf16[1024,128]{1,0:T(8,128)(2,1)} %query_ref.1) | copy-start | bytes 786436

commit v3 on v2

--- a/solution.py
+++ b/solution.py
@@ -78,7 +78,8 @@
 
 def pack_kernel(rows, own, share, which_ref, *refs):
     sources, bias_ref, out_ref, bias_out = refs[:3], refs[3], refs[4], refs[5]
-    held, turned, sems = refs[6:9], refs[9], refs[10]
+    held, turned, sems, bias_sem = refs[6:9], refs[9], refs[10], refs[11]
+    bias_copy = pltpu.make_async_copy(bias_ref, bias_out, bias_sem)
 
     def fetch(place, row):
         span = pl.ds(row * LANES, LANES)
@@ -87,7 +88,7 @@
     for row in range(rows):
         for place in range(3):
             fetch(place, row).start()
-    bias_out[...] = bias_ref[...]
+    bias_copy.start()
     for row in range(rows):
         span = pl.ds(row * LANES, LANES)
         fetch(0, row).wait()
@@ -102,6 +103,7 @@
         out_ref[peer, : own * rows] = turned[0, pl.ds(start, own * rows), :]
         taken = pl.ds(pl.multiple_of(start + first, rows), share * rows)
         out_ref[peer, own * rows :] = turned[1, taken, :]
+    bias_copy.wait()
 
 
 def conv_kernel(rows, own, share, moved_ref, head_ref, twist_ref, tail_ref, back_tail_ref, back_head_ref, out_ref):
@@ -147,7 +149,7 @@
 
 
 VMEM = pl.BlockSpec(memory_space=pltpu.VMEM)
-ANY = pl.BlockSpec(memory_space=pl.ANY)
+HBM = pl.BlockSpec(memory_space=pltpu.HBM)
 SMEM = pl.BlockSpec(memory_space=pltpu.SMEM)
 
 
@@ -177,11 +179,14 @@
     packed, bias = call(
         functools.partial(pack_kernel, rows, own, share),
         [((groups * blocks, (own + share) * rows, LANES), F32), ((1, chans), F32)],
-        [SMEM, ANY, ANY, ANY, VMEM], size // 4, size * 4,
+        [SMEM, HBM, HBM, HBM, HBM], size // 4, size * 4,
         [pltpu.VMEM((tokens, chans), BF16), pltpu.VMEM((tokens, chans), BF16), pltpu.VMEM((tokens, chans), F32),
-         pltpu.VMEM((2, chans * rows, LANES), F32), pltpu.SemaphoreType.DMA((3, rows))],
-    )(lax.axis_index("groups").reshape(1).astype(jnp.int32), key_proj, value_proj, long_filter,
-      skip_bias.reshape(1, chans))
+         pltpu.VMEM((2, chans * rows, LANES), F32), pltpu.SemaphoreType.DMA((3, rows)),
+         pltpu.SemaphoreType.DMA],
+    )(lax.axis_index("groups").reshape(1).astype(jnp.int32), *(
+        pltpu.with_memory_space_constraint(source, pltpu.HBM)
+        for source in (key_proj, value_proj, long_filter, skip_bias.reshape(1, chans))
+    ))
     moved = lax.all_to_all(packed, ("groups", "seq"), 0, 0, tiled=True)
     macs = 2 * 3 * own * seq_len * (2 * outer + 4 * LANES)
     local = call(

time: 58.3 us -> 54.1 us (0.928)
  local copies, waits for them, and re-layouts: 3.65 us -> 0.05 us
    unnamed x24 -> x16, local copies, waits for them, and re-layouts: 3.65 us -> 0.05 us
where the time goes in v3:
time: 54.1 us; the launch traced here: 53.9 us
  blocking collectives  47.3 us (87%)
  Pallas kernels  6.4 us (12%)
    all_to_all x1, blocking collectives, shards(): moved = lax.all_to_all(packed, ('groups', 'seq'), 0, 0, tiled=True)  29.5 us
    all_to_all x1, blocking collectives, shards(): lax.all_to_all(local.reshape(chans * rows, LANES), ('groups', 'seq'), 0,...  17.8 us
    pallas_call x1, Pallas kernels, shards(): call(functools.partial(conv_kernel, rows, own, share), [((groups, blocks,...  2.78 us
    pallas_call x1, Pallas kernels, shards(): call(functools.partial(pack_kernel, rows, own, share), [((groups * blocks...  2.7 us

profile of v3, /device:TPU:0, one launch (start us, length us, event | category | flops | bytes accessed | tf_op | source)
XLA Modules:
  0.0 53.9 jit_solution(4956749627663393273)
XLA Ops:
  0.0 2.7 %shard_map.100 = (f32[16,96,128]{2,1,0:T(8,128)S(1)}, f32[1,128]{1,0:T(1,128)S(1)}) custom-call(s32[1]{0:T(128)} %bitcast.which_ref, bf16[1024,128]{1,0:T(8,128)(2,1)} %key_ref.1, bf16[1024,128]{1,0:T(8,128)(2,1)} %value_ref.1, f32[1024,128]{1,0:T(8,128)} %refs_2_.1, f32[1,128]{1,0:T(1,128)} %bitcast.8), custom_call_target="tpu_custom_call" | custom-call | flops 131072 | bytes 2097152 | tf_op jit(solution)/shard_map/pallas_call | solution.py:179
  2.7 0.0 copy-start.3
  2.7 0.0 copy-start.4
  2.7 0.0 copy-start.5
  2.7 0.0 copy-start.6
  2.8 0.0 copy-start.7
  2.8 29.5 %all_to_all.16 = f32[16,96,128]{2,1,0:T(8,128)S(1)} all-to-all(f32[16,96,128]{2,1,0:T(8,128)S(1)} %get-tuple-element.7), channel_id=1, replica_groups=mesh['groups'=2,'seq'=8,'chan'=2] {'groups','seq'}, dimensions={0} | all-to-all | bytes 1572864 | tf_op jit(solution)/shard_map/all_to_all | solution.py:190
  32.3 0.0 copy-done.3
  32.3 0.0 copy-done.4
  32.3 0.0 copy-done.5
  32.3 0.0 copy-done.6
  32.3 0.0 copy-done.7
  32.3 2.8 %shard_map.101 = f32[2,8,8,8,128]{4,3,2,1,0:T(8,128)S(1)} custom-call(f32[2,8,96,128]{3,2,1,0:T(8,128)S(1)} %bitcast.6, bf16[128,192]{1,0:T(8,128)(2,1)S(1)} %copy-done.6, f32[64,256]{1,0:T(8,128)S(1)} %copy-done.5, bf16[768,256]{1,0:T(8,128)(2,1)S(1)} %copy-done.4, bf16[768,256]{1,0:T(8,128)(2,1)S(1)} %copy-done.3, bf16[64,384]{1,0:T(8,128)(2,1)S(1)} %copy-done.7), custom_call_target="tpu_custom_call" | custom-call | flops 1258291200 | bytes 1572864 | tf_op jit(solution)/shard_map/pallas_call | solution.py:192
  35.1 0.0 copy-start
  35.1 0.0 copy-start.1
  35.1 0.0 copy-start.2
  35.1 17.8 %all_to_all.17 = f32[16,64,128]{2,1,0:T(8,128)S(1)} all-to-all(f32[16,64,128]{2,1,0:T(8,128)S(1)} %bitcast.7), channel_id=1, replica_groups=mesh['groups'=2,'seq'=8,'chan'=2] {'groups','seq'}, dimensions={0} | all-to-all | bytes 1048576 | tf_op jit(solution)/shard_map/all_to_all | solution.py:196
  53.0 0.0 copy-done
  53.0 0.0 copy-done.1
  53.0 0.0 copy-done.2
  53.0 0.9 %shard_map.102 = bf16[1024,128]{1,0:T(8,128)(2,1)} custom-call(f32[1024,128]{1,0:T(8,128)S(1)} %bitcast.5, bf16[1024,128]{1,0:T(8,128)(2,1)S(1)} %copy-done.2, bf16[1024,128]{1,0:T(8,128)(2,1)S(1)} %copy-done, bf16[1024,128]{1,0:T(8,128)(2,1)S(1)} %copy-done.1, f32[1,128]{1,0:T(1,128)S(1)} %get-tuple-element.8.bias_ref), custom_call_target="tpu_custom_call" | custom-call | flops 524288 | bytes 1572864 | tf_op jit(solution)/shard_map/pallas_call | solution.py:197
Async XLA Ops:
  2.7 29.6 %copy-start.3 = (bf16[768,256]{1,0:T(8,128)(2,1)S(1)}, bf16[768,256]{1,0:T(8,128)(2,1)}, u32[]{:S(2)}) copy-start(bf16[768,256]{1,0:T(8,128)(2,1)} %constant.19.clone.back_tail_ref) | copy-start | bytes 1179652
  2.7 29.6 %copy-start.4 = (bf16[768,256]{1,0:T(8,128)(2,1)S(1)}, bf16[768,256]{1,0:T(8,128)(2,1)}, u32[]{:S(2)}) copy-start(bf16[768,256]{1,0:T(8,128)(2,1)} %constant.18.clone.tail_ref) | copy-start | bytes 1179652
  2.7 29.6 %copy-start.5 = (f32[64,256]{1,0:T(8,128)S(1)}, f32[64,256]{1,0:T(8,128)}, u32[]{:S(2)}) copy-start(f32[64,256]{1,0:T(8,128)} %constant.17.clone.twist_ref) | copy-start | bytes 196612
  2.7 29.6 %copy-start.6 = (bf16[128,192]{1,0:T(8,128)(2,1)S(1)}, bf16[128,192]{1,0:T(8,128)(2,1)}, u32[]{:S(2)}) copy-start(bf16[128,192]{1,0:T(8,128)(2,1)} %constant.16.clone.head_ref) | copy-start | bytes 147460
  2.8 29.6 %copy-start.7 = (bf16[64,384]{1,0:T(8,128)(2,1)S(1)}, bf16[64,384]{1,0:T(8,128)(2,1)}, u32[]{:S(2)}) copy-start(bf16[64,384]{1,0:T(8,128)(2,1)} %constant.20.clone.back_head_ref) | copy-start | bytes 147460
  35.1 17.9 %copy-start = (bf16[1024,128]{1,0:T(8,128)(2,1)S(1)}, bf16[1024,128]{1,0:T(8,128)(2,1)}, u32[]{:S(2)}) copy-start(bf16[1024,128]{1,0:T(8,128)(2,1)} %key_ref.1) | copy-start | bytes 786436
  35.1 17.8 %copy-start.1 = (bf16[1024,128]{1,0:T(8,128)(2,1)S(1)}, bf16[1024,128]{1,0:T(8,128)(2,1)}, u32[]{:S(2)}) copy-start(bf16[1024,128]{1,0:T(8,128)(2,1)} %value_ref.1) | copy-start | bytes 786436
  35.1 17.8 %copy-start.2 = (bf16[1024,128]{1,0:T(8,128)(2,1)S(1)}, bf16[1024,128]{1,0:T(8,128)(2,1)}, u32[]{:S(2)}) copy-start(bf16[1024,128]{1,0:T(8,128)(2,1)} %query_ref.1) | copy-start | bytes 786436

commit v4 on v3

--- a/solution.py
+++ b/solution.py
@@ -76,43 +76,62 @@
     return mat(by_lanes(jnp.concatenate(rows, axis=0)), tail)
 
 
-def pack_kernel(rows, own, share, which_ref, *refs):
-    sources, bias_ref, out_ref, bias_out = refs[:3], refs[3], refs[4], refs[5]
-    held, turned, sems, bias_sem = refs[6:9], refs[9], refs[10], refs[11]
+def partner(place, step, count):
+    return place ^ step if count & (count - 1) == 0 else (place + count - step) % count
+
+
+def receiver(place, step, count):
+    return place ^ step if count & (count - 1) == 0 else (place + step) % count
+
+
+def exchange(parts, axes):
+    count = len(parts)
+    return [parts[0]] + [
+        lax.ppermute(parts[step], axes, [(place, receiver(place, step, count)) for place in range(count)])
+        for step in range(1, count)
+    ]
+
+
+def pack_kernel(rows, own, share, count, where_ref, *refs):
+    sources, bias_ref = refs[:3], refs[3]
+    outs, bias_out = refs[4 : 4 + count], refs[4 + count]
+    held, turned, sems, bias_sem = refs[5 + count : 8 + count], refs[-3], refs[-2], refs[-1]
     bias_copy = pltpu.make_async_copy(bias_ref, bias_out, bias_sem)
-
-    def fetch(place, row):
-        span = pl.ds(row * LANES, LANES)
-        return pltpu.make_async_copy(sources[place].at[span], held[place].at[span], sems.at[place, row])
-
-    for row in range(rows):
-        for place in range(3):
-            fetch(place, row).start()
+    fetches = [pltpu.make_async_copy(sources[idx], held[idx], sems.at[idx]) for idx in range(3)]
+    for fetch in fetches:
+        fetch.start()
     bias_copy.start()
+    fetches[0].wait()
+    fetches[1].wait()
     for row in range(rows):
         span = pl.ds(row * LANES, LANES)
-        fetch(0, row).wait()
-        fetch(1, row).wait()
         driver = held[0][span, :].astype(F32) * held[1][span, :].astype(F32)
         turned[0, pl.ds(row, LANES, stride=rows), :] = driver.T
-        fetch(2, row).wait()
+    fetches[2].wait()
+    for row in range(rows):
+        span = pl.ds(row * LANES, LANES)
         turned[1, pl.ds(row, LANES, stride=rows), :] = held[2][span, :].T
-    first = which_ref[0] * (share * rows if share < own else 0)
-    for peer in range(out_ref.shape[0]):
-        start = peer * own * rows
-        out_ref[peer, : own * rows] = turned[0, pl.ds(start, own * rows), :]
+    first = where_ref[1] * (share * rows if share < own else 0)
+    for step in range(count):
+        start = pl.multiple_of(receiver(where_ref[0], step, count) * (own * rows), own * rows)
+        outs[step][: own * rows] = turned[0, pl.ds(start, own * rows), :]
         taken = pl.ds(pl.multiple_of(start + first, rows), share * rows)
-        out_ref[peer, own * rows :] = turned[1, taken, :]
+        outs[step][own * rows :] = turned[1, taken, :]
     bias_copy.wait()
 
 
-def conv_kernel(rows, own, share, moved_ref, head_ref, twist_ref, tail_ref, back_tail_ref, back_head_ref, out_ref):
-    groups, blocks = moved_ref.shape[:2]
+def conv_kernel(rows, own, share, groups, blocks, where_ref, *refs):
+    count = groups * blocks
+    arrived, outs = refs[:count], refs[count + 5 : 2 * count + 5]
+    head_ref, twist_ref, tail_ref, back_tail_ref, back_head_ref = refs[count : count + 5]
+    moved_ref, result_ref = refs[-2:]
+    for step in range(count):
+        moved_ref[partner(where_ref[0], step, count)] = arrived[step][...]
     outer = blocks * rows
     scale = 1.0 / (outer * LANES)
 
     def signal(group, place):
-        return moved_ref[group, :, place * rows : (place + 1) * rows].reshape(outer, LANES)
+        return moved_ref[pl.ds(group * blocks, blocks), place * rows : (place + 1) * rows].reshape(outer, LANES)
 
     signals = [signal(chan // share, own + chan % share) for chan in range(own)]
     signals += [signal(group, chan) for chan in range(own) for group in range(groups)]
@@ -136,10 +155,19 @@
     result = mat(back_head_ref[...], by_rows(mixed))
     for idx in range(len(prods)):
         chan, group = divmod(idx, groups)
-        out_ref[group, :, chan] = result[:, idx * LANES : (idx + 1) * LANES].reshape(blocks, rows, LANES)
-
-
-def gate_kernel(rows, conv_ref, query_ref, key_ref, value_ref, bias_ref, out_ref):
+        result_ref[pl.ds(group * blocks, blocks), chan * rows : (chan + 1) * rows] = result[
+            :, idx * LANES : (idx + 1) * LANES
+        ].reshape(blocks, rows, LANES)
+    for step in range(count):
+        outs[step][...] = result_ref[receiver(where_ref[0], step, count)]
+
+
+def gate_kernel(rows, count, where_ref, *refs):
+    arrived, (query_ref, key_ref, value_ref, bias_ref, out_ref, conv_ref) = refs[:count], refs[count:]
+    size = arrived[0].shape[0]
+    for step in range(count):
+        start = pl.multiple_of(partner(where_ref[0], step, count) * size, size)
+        conv_ref[pl.ds(start, size), :] = arrived[step][...]
     bias = bias_ref[...]
     for row in range(rows):
         span = pl.ds(row * LANES, LANES)
@@ -176,27 +204,31 @@
     size = tokens * chans * 4
 
     share = own // groups if own % groups == 0 else own
-    packed, bias = call(
-        functools.partial(pack_kernel, rows, own, share),
-        [((groups * blocks, (own + share) * rows, LANES), F32), ((1, chans), F32)],
+    count, axes = groups * blocks, ("groups", "seq")
+    where = jnp.stack([lax.axis_index(axes), lax.axis_index("groups")]).astype(jnp.int32)
+    *packed, bias = call(
+        functools.partial(pack_kernel, rows, own, share, count),
+        [(((own + share) * rows, LANES), F32)] * count + [((1, chans), F32)],
         [SMEM, HBM, HBM, HBM, HBM], size // 4, size * 4,
         [pltpu.VMEM((tokens, chans), BF16), pltpu.VMEM((tokens, chans), BF16), pltpu.VMEM((tokens, chans), F32),
-         pltpu.VMEM((2, chans * rows, LANES), F32), pltpu.SemaphoreType.DMA((3, rows)),
-         pltpu.SemaphoreType.DMA],
-    )(lax.axis_index("groups").reshape(1).astype(jnp.int32), *(
+         pltpu.VMEM((2, chans * rows, LANES), F32), pltpu.SemaphoreType.DMA((3,)), pltpu.SemaphoreType.DMA],
+    )(where, *(
         pltpu.with_memory_space_constraint(source, pltpu.HBM)
         for source in (key_proj, value_proj, long_filter, skip_bias.reshape(1, chans))
     ))
-    moved = lax.all_to_all(packed, ("groups", "seq"), 0, 0, tiled=True)
+    moved = exchange(packed, axes)
     macs = 2 * 3 * own * seq_len * (2 * outer + 4 * LANES)
     local = call(
-        functools.partial(conv_kernel, rows, own, share),
-        [((groups, blocks, own, rows, LANES), F32)], [VMEM] * 6, 5 * macs, 3 * size,
-    )(moved.reshape(groups, blocks, (own + share) * rows, LANES), head, twist, tail, back_tail, back_head)[0]
-    convolved = lax.all_to_all(local.reshape(chans * rows, LANES), ("groups", "seq"), 0, 0, tiled=True)
-    return call(functools.partial(gate_kernel, rows), [((tokens, chans), BF16)], [VMEM] * 5, size, 3 * size)(
-        convolved, query_proj, key_proj, value_proj, bias
-    )[0]
+        functools.partial(conv_kernel, rows, own, share, groups, blocks),
+        [((own * rows, LANES), F32)] * count, [SMEM] + [VMEM] * (count + 5), 5 * macs, 3 * size,
+        [pltpu.VMEM((count, (own + share) * rows, LANES), F32), pltpu.VMEM((count, own * rows, LANES), F32)],
+    )(where, *moved, head, twist, tail, back_tail, back_head)
+    convolved = exchange(local, axes)
+    return call(
+        functools.partial(gate_kernel, rows, count),
+        [((tokens, chans), BF16)], [SMEM] + [VMEM] * (count + 4), size, 3 * size,
+        [pltpu.VMEM((chans * rows, LANES), F32)],
+    )(where, *convolved, query_proj, key_proj, value_proj, bias)[0]
 
 
 def solution(mesh):

time: 54.1 us -> 72.8 us (1.35)
  starting transfers between devices: 0 us -> 55.7 us
  blocking collectives: 47.3 us -> 0 us
  waiting for transfers between devices: 0 us -> 9.62 us
    ppermute x0 -> x30, starting transfers between devices: none -> 55.7 us  [exchange(): lax.ppermute(parts[step], axes, [(place, receiver(place, step, count)) fo...]
    all_to_all x2 -> x0, blocking collectives: 47.3 us -> none  [the longest x1 29.5 us: shards(): moved = lax.all_to_all(packed, ('groups', 'seq'), 0, 0, tiled=True)]
    ppermute x0 -> x30, waiting for transfers between devices: none -> 9.62 us  [exchange(): lax.ppermute(parts[step], axes, [(place, receiver(place, step, count)) fo...]
  transfers between devices with their start and end apart: 0 -> 30, of which waited for: 0 -> 4; matrix products, arithmetic and copies ran while one was open for 0% -> 0% of each run, Pallas kernels for 0% -> 0%
where the time goes in v4:
time: 72.8 us; the launch traced here: 72.6 us
  starting transfers between devices  55.7 us (77%)
  waiting for transfers between devices  9.62 us (13%)
  Pallas kernels  7.05 us (10%)
    ppermute x30, starting transfers between devices, exchange(): lax.ppermute(parts[step], axes, [(place, receiver(place, step, count)) fo...  55.7 us
    ppermute x30, waiting for transfers between devices, exchange(): lax.ppermute(parts[step], axes, [(place, receiver(place, step, count)) fo...  9.62 us
    pallas_call x1, Pallas kernels, shards(): call(functools.partial(conv_kernel, rows, own, share, groups, blocks), [(...  3.46 us
    pallas_call x1, Pallas kernels, shards(): call(functools.partial(pack_kernel, rows, own, share, count), [(((own + s...  2.08 us
    pallas_call x1, Pallas kernels, shards(): call(functools.partial(gate_kernel, rows, count), [((tokens, chans), BF16...  1.5 us
  transfers between devices with their start and end apart: 30, of which 4 were waited for; matrix products, arithmetic and copies ran while one was open for 0% of the time, Pallas kernels for 0%

profile of v4, /device:TPU:0, one launch (start us, length us, event | category | flops | bytes accessed | tf_op | source)
XLA Modules:
  0.0 72.6 jit_solution(2777858684513209467)
XLA Ops:
  0.0 0.1 pad_add_fusion.where_ref
  0.1 0.0 copy-start.7
  0.1 2.1 %shard_map.100 = (f32[96,128]{1,0:T(8,128)S(1)}, f32[96,128]{1,0:T(8,128)S(1)}, f32[96,128]{1,0:T(8,128)S(1)}, f32[96,128]{1,0:T(8,128)S(1)}, f32[96,128]{1,0:T(...) custom-call(s32[2]{0:T(128)S(1)} %pad_add_fusion.where_ref, ...), custom_call_target="tpu_custom_call" | custom-call | flops 131072 | bytes 2097152 | tf_op jit(solution)/shard_map/pallas_call | solution.py:209
  2.2 3.0 %collective-permute-start = (f32[96,128]{1,0:T(8,128)S(1)}, f32[96,128]{1,0:T(8,128)S(1)}, u32[]{:S(2)}, u32[]{:S(2)}) collective-permute-start(f32[96,128]{1,0:T(8,128)S(1)} %get-tuple-element.39), channel_id=1, source_target_pairs={{0,2},{2,0},{4,6},{6,4},{8,10},{10,8},{12,14},{14,12},{16,18},{18,... | collective-permute-start | bytes 147464 | tf_op jit(solution)/shard_map/ppermute | solution.py:90
  5.2 1.6 %collective-permute-start.1 = (f32[96,128]{1,0:T(8,128)S(1)}, f32[96,128]{1,0:T(8,128)S(1)}, u32[]{:S(2)}, u32[]{:S(2)}) collective-permute-start(f32[96,128]{1,0:T(8,128)S(1)} %get-tuple-element.40), channel_id=1, source_target_pairs={{0,4},{2,6},{4,0},{6,2},{8,12},{10,14},{12,8},{14,10},{16,20},{18,... | collective-permute-start | bytes 147464 | tf_op jit(solution)/shard_map/ppermute | solution.py:90
  6.8 0.0 collective-permute-start.2
  6.8 3.0 %collective-permute-start.3 = (f32[96,128]{1,0:T(8,128)S(1)}, f32[96,128]{1,0:T(8,128)S(1)}, u32[]{:S(2)}, u32[]{:S(2)}) collective-permute-start(f32[96,128]{1,0:T(8,128)S(1)} %get-tuple-element.42), channel_id=1, source_target_pairs={{0,8},{2,10},{4,12},{6,14},{8,0},{10,2},{12,4},{14,6},{16,24},{18,... | collective-permute-start | bytes 147464 | tf_op jit(solution)/shard_map/ppermute | solution.py:90
  9.8 1.3 %collective-permute-start.4 = (f32[96,128]{1,0:T(8,128)S(1)}, f32[96,128]{1,0:T(8,128)S(1)}, u32[]{:S(2)}, u32[]{:S(2)}) collective-permute-start(f32[96,128]{1,0:T(8,128)S(1)} %get-tuple-element.43), channel_id=1, source_target_pairs={{0,10},{2,8},{4,14},{6,12},{8,2},{10,0},{12,6},{14,4},{16,26},{18,... | collective-permute-start | bytes 147464 | tf_op jit(solution)/shard_map/ppermute | solution.py:90
  11.1 0.0 collective-permute-done.refs_1_
  11.1 3.6 %collective-permute-start.5 = (f32[96,128]{1,0:T(8,128)S(1)}, f32[96,128]{1,0:T(8,128)S(1)}, u32[]{:S(2)}, u32[]{:S(2)}) collective-permute-start(f32[96,128]{1,0:T(8,128)S(1)} %get-tuple-element.44), channel_id=1, source_target_pairs={{0,12},{2,14},{4,8},{6,10},{8,4},{10,6},{12,0},{14,2},{16,28},{18,... | collective-permute-start | bytes 147464 | tf_op jit(solution)/shard_map/ppermute | solution.py:90
  14.7 0.0 collective-permute-done.1.refs_2_
  14.7 0.0 collective-permute-start.6
  14.7 0.0 collective-permute-done.2.refs_3_
  14.7 1.6 %collective-permute-start.7 = (f32[96,128]{1,0:T(8,128)S(1)}, f32[96,128]{1,0:T(8,128)S(1)}, u32[]{:S(2)}, u32[]{:S(2)}) collective-permute-start(f32[96,128]{1,0:T(8,128)S(1)} %get-tuple-element.46), channel_id=1, source_target_pairs={{0,16},{2,18},{4,20},{6,22},{8,24},{10,26},{12,28},{14,30},{16,0},... | collective-permute-start | bytes 147464 | tf_op jit(solution)/shard_map/ppermute | solution.py:90
  16.3 0.0 collective-permute-done.3.refs_4_
  16.3 1.5 %collective-permute-start.8 = (f32[96,128]{1,0:T(8,128)S(1)}, f32[96,128]{1,0:T(8,128)S(1)}, u32[]{:S(2)}, u32[]{:S(2)}) collective-permute-start(f32[96,128]{1,0:T(8,128)S(1)} %get-tuple-element.47), channel_id=1, source_target_pairs={{0,18},{2,16},{4,22},{6,20},{8,26},{10,24},{12,30},{14,28},{16,2},... | collective-permute-start | bytes 147464 | tf_op jit(solution)/shard_map/ppermute | solution.py:90
  17.8 0.0 collective-permute-done.4.refs_5_
  17.8 0.8 %collective-permute-start.9 = (f32[96,128]{1,0:T(8,128)S(1)}, f32[96,128]{1,0:T(8,128)S(1)}, u32[]{:S(2)}, u32[]{:S(2)}) collective-permute-start(f32[96,128]{1,0:T(8,128)S(1)} %get-tuple-element.48), channel_id=1, source_target_pairs={{0,20},{2,22},{4,16},{6,18},{8,28},{10,30},{12,24},{14,26},{16,4},... | collective-permute-start | bytes 147464 | tf_op jit(solution)/shard_map/ppermute | solution.py:90
  18.7 0.0 collective-permute-done.5.refs_6_
  18.7 3.3 %collective-permute-start.10 = (f32[96,128]{1,0:T(8,128)S(1)}, f32[96,128]{1,0:T(8,128)S(1)}, u32[]{:S(2)}, u32[]{:S(2)}) collective-permute-start(f32[96,128]{1,0:T(8,128)S(1)} %get-tuple-element.49), channel_id=1, source_target_pairs={{0,22},{2,20},{4,18},{6,16},{8,30},{10,28},{12,26},{14,24},{16,6},... | collective-permute-start | bytes 147464 | tf_op jit(solution)/shard_map/ppermute | solution.py:90
  22.0 0.0 collective-permute-done.6.refs_7_
  22.0 1.1 %collective-permute-start.11 = (f32[96,128]{1,0:T(8,128)S(1)}, f32[96,128]{1,0:T(8,128)S(1)}, u32[]{:S(2)}, u32[]{:S(2)}) collective-permute-start(f32[96,128]{1,0:T(8,128)S(1)} %get-tuple-element.50), channel_id=1, source_target_pairs={{0,24},{2,26},{4,28},{6,30},{8,16},{10,18},{12,20},{14,22},{16,8},... | collective-permute-start | bytes 147464 | tf_op jit(solution)/shard_map/ppermute | solution.py:90
  23.1 0.0 collective-permute-done.7.refs_8_
  23.1 2.7 %collective-permute-start.12 = (f32[96,128]{1,0:T(8,128)S(1)}, f32[96,128]{1,0:T(8,128)S(1)}, u32[]{:S(2)}, u32[]{:S(2)}) collective-permute-start(f32[96,128]{1,0:T(8,128)S(1)} %get-tuple-element.51), channel_id=1, source_target_pairs={{0,26},{2,24},{4,30},{6,28},{8,18},{10,16},{12,22},{14,20},{16,10}... | collective-permute-start | bytes 147464 | tf_op jit(solution)/shard_map/ppermute | solution.py:90
  25.8 0.0 collective-permute-done.8.refs_9_
  25.8 4.3 %collective-permute-start.13 = (f32[96,128]{1,0:T(8,128)S(1)}, f32[96,128]{1,0:T(8,128)S(1)}, u32[]{:S(2)}, u32[]{:S(2)}) collective-permute-start(f32[96,128]{1,0:T(8,128)S(1)} %get-tuple-element.52), channel_id=1, source_target_pairs={{0,28},{2,30},{4,24},{6,26},{8,20},{10,22},{12,16},{14,18},{16,12}... | collective-permute-start | bytes 147464 | tf_op jit(solution)/shard_map/ppermute | solution.py:90
  30.0 0.0 collective-permute-done.9.refs_10_
  30.0 1.4 %collective-permute-start.14 = (f32[96,128]{1,0:T(8,128)S(1)}, f32[96,128]{1,0:T(8,128)S(1)}, u32[]{:S(2)}, u32[]{:S(2)}) collective-permute-start(f32[96,128]{1,0:T(8,128)S(1)} %get-tuple-element.53), channel_id=1, source_target_pairs={{0,30},{2,28},{4,26},{6,24},{8,22},{10,20},{12,18},{14,16},{16,14}... | collective-permute-start | bytes 147464 | tf_op jit(solution)/shard_map/ppermute | solution.py:90
  31.5 0.0 collective-permute-done.10.refs_11_
  31.5 0.0 collective-permute-done.11.refs_12_
  31.5 0.0 collective-permute-done.12.refs_13_
  31.5 1.4 %collective-permute-done.13.refs_14_ = f32[96,128]{1,0:T(8,128)S(1)} collective-permute-done((f32[96,128]{1,0:T(8,128)S(1)}, f32[96,128]{1,0:T(8,128)S(1)}, u32[]{:S(2)}, u32[]{:S(2)}) %collective-permute-start.13) | collective-permute-done | bytes 49184 | tf_op jit(solution)/shard_map/ppermute | solution.py:90
  32.9 4.9 %collective-permute-done.14.refs_15_ = f32[96,128]{1,0:T(8,128)S(1)} collective-permute-done((f32[96,128]{1,0:T(8,128)S(1)}, f32[96,128]{1,0:T(8,128)S(1)}, u32[]{:S(2)}, u32[]{:S(2)}) %collective-permute-start.14) | collective-permute-done | bytes 49184 | tf_op jit(solution)/shard_map/ppermute | solution.py:90
  37.8 0.0 copy-start
  37.8 0.0 copy-start.1
  37.8 0.0 copy-start.2
  37.8 3.5 %shard_map.101 = (f32[64,128]{1,0:T(8,128)S(1)}, f32[64,128]{1,0:T(8,128)S(1)}, f32[64,128]{1,0:T(8,128)S(1)}, f32[64,128]{1,0:T(8,128)S(1)}, f32[64,128]{1,0:T(...) custom-call(s32[2]{0:T(128)S(1)} %pad_add_fusion.where_ref, ...), custom_call_target="tpu_custom_call" | custom-call | flops 1258291200 | bytes 1572864 | tf_op jit(solution)/shard_map/pallas_call | solution.py:221
  41.3 0.6 collective-permute-start.15
  41.8 0.0 collective-permute-start.16
  41.8 3.0 %collective-permute-start.17 = (f32[64,128]{1,0:T(8,128)S(1)}, f32[64,128]{1,0:T(8,128)S(1)}, u32[]{:S(2)}, u32[]{:S(2)}) collective-permute-start(f32[64,128]{1,0:T(8,128)S(1)} %get-tuple-element.57), channel_id=1, source_target_pairs={{0,6},{2,4},{4,2},{6,0},{8,14},{10,12},{12,10},{14,8},{16,22},{18,... | collective-permute-start | bytes 98312 | tf_op jit(solution)/shard_map/ppermute | solution.py:90
  44.8 0.0 collective-permute-start.18
  44.8 2.9 %collective-permute-start.19 = (f32[64,128]{1,0:T(8,128)S(1)}, f32[64,128]{1,0:T(8,128)S(1)}, u32[]{:S(2)}, u32[]{:S(2)}) collective-permute-start(f32[64,128]{1,0:T(8,128)S(1)} %get-tuple-element.59), channel_id=1, source_target_pairs={{0,10},{2,8},{4,14},{6,12},{8,2},{10,0},{12,6},{14,4},{16,26},{18,... | collective-permute-start | bytes 98312 | tf_op jit(solution)/shard_map/ppermute | solution.py:90
  47.7 0.0 collective-permute-done.15.refs_1_
  47.7 1.0 %collective-permute-start.20 = (f32[64,128]{1,0:T(8,128)S(1)}, f32[64,128]{1,0:T(8,128)S(1)}, u32[]{:S(2)}, u32[]{:S(2)}) collective-permute-start(f32[64,128]{1,0:T(8,128)S(1)} %get-tuple-element.60), channel_id=1, source_target_pairs={{0,12},{2,14},{4,8},{6,10},{8,4},{10,6},{12,0},{14,2},{16,28},{18,... | collective-permute-start | bytes 98312 | tf_op jit(solution)/shard_map/ppermute | solution.py:90
  48.7 0.0 collective-permute-done.16.refs_2_
  48.7 3.8 %collective-permute-start.21 = (f32[64,128]{1,0:T(8,128)S(1)}, f32[64,128]{1,0:T(8,128)S(1)}, u32[]{:S(2)}, u32[]{:S(2)}) collective-permute-start(f32[64,128]{1,0:T(8,128)S(1)} %get-tuple-element.61), channel_id=1, source_target_pairs={{0,14},{2,12},{4,10},{6,8},{8,6},{10,4},{12,2},{14,0},{16,30},{18,... | collective-permute-start | bytes 98312 | tf_op jit(solution)/shard_map/ppermute | solution.py:90
  52.5 0.0 collective-permute-done.17.refs_3_
  52.5 0.5 collective-permute-start.22
  53.0 0.0 collective-permute-done.18.refs_4_
  53.0 1.4 %collective-permute-start.23 = (f32[64,128]{1,0:T(8,128)S(1)}, f32[64,128]{1,0:T(8,128)S(1)}, u32[]{:S(2)}, u32[]{:S(2)}) collective-permute-start(f32[64,128]{1,0:T(8,128)S(1)} %get-tuple-element.63), channel_id=1, source_target_pairs={{0,18},{2,16},{4,22},{6,20},{8,26},{10,24},{12,30},{14,28},{16,2},... | collective-permute-start | bytes 98312 | tf_op jit(solution)/shard_map/ppermute | solution.py:90
  54.5 0.0 collective-permute-done.19.refs_5_
  54.5 0.0 collective-permute-start.24
  54.5 0.0 collective-permute-done.20.refs_6_
  54.5 3.9 %collective-permute-start.25 = (f32[64,128]{1,0:T(8,128)S(1)}, f32[64,128]{1,0:T(8,128)S(1)}, u32[]{:S(2)}, u32[]{:S(2)}) collective-permute-start(f32[64,128]{1,0:T(8,128)S(1)} %get-tuple-element.65), channel_id=1, source_target_pairs={{0,22},{2,20},{4,18},{6,16},{8,30},{10,28},{12,26},{14,24},{16,6},... | collective-permute-start | bytes 98312 | tf_op jit(solution)/shard_map/ppermute | solution.py:90
  58.3 0.0 collective-permute-done.21.refs_7_
  58.4 3.8 %collective-permute-start.27 = (f32[64,128]{1,0:T(8,128)S(1)}, f32[64,128]{1,0:T(8,128)S(1)}, u32[]{:S(2)}, u32[]{:S(2)}) collective-permute-start(f32[64,128]{1,0:T(8,128)S(1)} %get-tuple-element.67), channel_id=1, source_target_pairs={{0,26},{2,24},{4,30},{6,28},{8,18},{10,16},{12,22},{14,20},{16,10}... | collective-permute-start | bytes 98312 | tf_op jit(solution)/shard_map/ppermute | solution.py:90
  62.1 0.0 collective-permute-done.23.refs_9_
  62.1 1.5 %collective-permute-start.28 = (f32[64,128]{1,0:T(8,128)S(1)}, f32[64,128]{1,0:T(8,128)S(1)}, u32[]{:S(2)}, u32[]{:S(2)}) collective-permute-start(f32[64,128]{1,0:T(8,128)S(1)} %get-tuple-element.68), channel_id=1, source_target_pairs={{0,28},{2,30},{4,24},{6,26},{8,20},{10,22},{12,16},{14,18},{16,12}... | collective-permute-start | bytes 98312 | tf_op jit(solution)/shard_map/ppermute | solution.py:90
  63.6 0.0 collective-permute-done.24.refs_10_
  63.6 4.2 %collective-permute-start.29 = (f32[64,128]{1,0:T(8,128)S(1)}, f32[64,128]{1,0:T(8,128)S(1)}, u32[]{:S(2)}, u32[]{:S(2)}) collective-permute-start(f32[64,128]{1,0:T(8,128)S(1)} %get-tuple-element.69), channel_id=1, source_target_pairs={{0,30},{2,28},{4,26},{6,24},{8,22},{10,20},{12,18},{14,16},{16,14}... | collective-permute-start | bytes 98312 | tf_op jit(solution)/shard_map/ppermute | solution.py:90
  67.8 0.0 collective-permute-done.25.refs_11_
  67.8 0.9 %collective-permute-done.28.refs_14_ = f32[64,128]{1,0:T(8,128)S(1)} collective-permute-done((f32[64,128]{1,0:T(8,128)S(1)}, f32[64,128]{1,0:T(8,128)S(1)}, u32[]{:S(2)}, u32[]{:S(2)}) %collective-permute-start.28) | collective-permute-done | bytes 32800 | tf_op jit(solution)/shard_map/ppermute | solution.py:90
  68.7 2.4 %collective-permute-done.29.refs_15_ = f32[64,128]{1,0:T(8,128)S(1)} collective-permute-done((f32[64,128]{1,0:T(8,128)S(1)}, f32[64,128]{1,0:T(8,128)S(1)}, u32[]{:S(2)}, u32[]{:S(2)}) %collective-permute-start.29) | collective-permute-done | bytes 32800 | tf_op jit(solution)/shard_map/ppermute | solution.py:90
  71.1 1.5 %shard_map.102 = bf16[1024,128]{1,0:T(8,128)(2,1)} custom-call(s32[2]{0:T(128)S(1)} %pad_add_fusion.where_ref, f32[64,128]{1,0:T(8,128)S(1)} %get-tuple-element.54.refs_0_, f32[64,128]{1,0:T(8,128)S(1)} %collective-permute-done.15.refs_1_, f32[64,128]{1,0:T(8,128)S(1)} %collective-permute-done.16.refs_2_, f32[64,128]{1,0:T(8,128)S(1)} %collective-permute-done.17.refs_3_, ...), custom_call_target="tpu_custom_call" | custom-call | flops 524288 | bytes 1572864 | tf_op jit(solution)/shard_map/pallas_call | solution.py:227
  (16 shorter events, 0.0 us)
Async XLA Ops:
  0.1 37.7 %copy-start.3 = (bf16[768,256]{1,0:T(8,128)(2,1)S(1)}, bf16[768,256]{1,0:T(8,128)(2,1)}, u32[]{:S(2)}) copy-start(bf16[768,256]{1,0:T(8,128)(2,1)} %constant.25.clone.refs_19_) | copy-start | bytes 1179652
  0.1 37.7 %copy-start.4 = (bf16[768,256]{1,0:T(8,128)(2,1)S(1)}, bf16[768,256]{1,0:T(8,128)(2,1)}, u32[]{:S(2)}) copy-start(bf16[768,256]{1,0:T(8,128)(2,1)} %constant.24.clone.refs_18_) | copy-start | bytes 1179652
  0.1 37.7 %copy-start.5 = (f32[64,256]{1,0:T(8,128)S(1)}, f32[64,256]{1,0:T(8,128)}, u32[]{:S(2)}) copy-start(f32[64,256]{1,0:T(8,128)} %constant.23.clone.refs_17_) | copy-start | bytes 196612
  0.1 37.7 %copy-start.6 = (bf16[128,192]{1,0:T(8,128)(2,1)S(1)}, bf16[128,192]{1,0:T(8,128)(2,1)}, u32[]{:S(2)}) copy-start(bf16[128,192]{1,0:T(8,128)(2,1)} %constant.22.clone.refs_16_) | copy-start | bytes 147460
  0.1 37.7 %copy-start.7 = (bf16[64,384]{1,0:T(8,128)(2,1)S(1)}, bf16[64,384]{1,0:T(8,128)(2,1)}, u32[]{:S(2)}) copy-start(bf16[64,384]{1,0:T(8,128)(2,1)} %constant.26.clone.refs_20_) | copy-start | bytes 147460
  2.2 8.9 %collective-permute-start = (f32[96,128]{1,0:T(8,128)S(1)}, f32[96,128]{1,0:T(8,128)S(1)}, u32[]{:S(2)}, u32[]{:S(2)}) collective-permute-start(f32[96,128]{1,0:T(8,128)S(1)} %get-tuple-element.39), channel_id=1, source_target_pairs={{0,2},{2,0},{4,6},{6,4},{8,10},{10,8},{12,14},{14,12},{16,18},{18,... | collective-permute-start | bytes 147464 | tf_op jit(solution)/shard_map/ppermute | solution.py:90
  5.2 9.5 %collective-permute-start.1 = (f32[96,128]{1,0:T(8,128)S(1)}, f32[96,128]{1,0:T(8,128)S(1)}, u32[]{:S(2)}, u32[]{:S(2)}) collective-permute-start(f32[96,128]{1,0:T(8,128)S(1)} %get-tuple-element.40), channel_id=1, source_target_pairs={{0,4},{2,6},{4,0},{6,2},{8,12},{10,14},{12,8},{14,10},{16,20},{18,... | collective-permute-start | bytes 147464 | tf_op jit(solution)/shard_map/ppermute | solution.py:90
  6.8 7.9 %collective-permute-start.2 = (f32[96,128]{1,0:T(8,128)S(1)}, f32[96,128]{1,0:T(8,128)S(1)}, u32[]{:S(2)}, u32[]{:S(2)}) collective-permute-start(f32[96,128]{1,0:T(8,128)S(1)} %get-tuple-element.41), channel_id=1, source_target_pairs={{0,6},{2,4},{4,2},{6,0},{8,14},{10,12},{12,10},{14,8},{16,22},{18,... | collective-permute-start | bytes 147464 | tf_op jit(solution)/shard_map/ppermute | solution.py:90
  6.8 9.5 %collective-permute-start.3 = (f32[96,128]{1,0:T(8,128)S(1)}, f32[96,128]{1,0:T(8,128)S(1)}, u32[]{:S(2)}, u32[]{:S(2)}) collective-permute-start(f32[96,128]{1,0:T(8,128)S(1)} %get-tuple-element.42), channel_id=1, source_target_pairs={{0,8},{2,10},{4,12},{6,14},{8,0},{10,2},{12,4},{14,6},{16,24},{18,... | collective-permute-start | bytes 147464 | tf_op jit(solution)/shard_map/ppermute | solution.py:90
  9.8 8.1 %collective-permute-start.4 = (f32[96,128]{1,0:T(8,128)S(1)}, f32[96,128]{1,0:T(8,128)S(1)}, u32[]{:S(2)}, u32[]{:S(2)}) collective-permute-start(f32[96,128]{1,0:T(8,128)S(1)} %get-tuple-element.43), channel_id=1, source_target_pairs={{0,10},{2,8},{4,14},{6,12},{8,2},{10,0},{12,6},{14,4},{16,26},{18,... | collective-permute-start | bytes 147464 | tf_op jit(solution)/shard_map/ppermute | solution.py:90
  11.1 7.6 %collective-permute-start.5 = (f32[96,128]{1,0:T(8,128)S(1)}, f32[96,128]{1,0:T(8,128)S(1)}, u32[]{:S(2)}, u32[]{:S(2)}) collective-permute-start(f32[96,128]{1,0:T(8,128)S(1)} %get-tuple-element.44), channel_id=1, source_target_pairs={{0,12},{2,14},{4,8},{6,10},{8,4},{10,6},{12,0},{14,2},{16,28},{18,... | collective-permute-start | bytes 147464 | tf_op jit(solution)/shard_map/ppermute | solution.py:90
  14.7 7.3 %collective-permute-start.6 = (f32[96,128]{1,0:T(8,128)S(1)}, f32[96,128]{1,0:T(8,128)S(1)}, u32[]{:S(2)}, u32[]{:S(2)}) collective-permute-start(f32[96,128]{1,0:T(8,128)S(1)} %get-tuple-element.45), channel_id=1, source_target_pairs={{0,14},{2,12},{4,10},{6,8},{8,6},{10,4},{12,2},{14,0},{16,30},{18,... | collective-permute-start | bytes 147464 | tf_op jit(solution)/shard_map/ppermute | solution.py:90
  14.7 8.4 %collective-permute-start.7 = (f32[96,128]{1,0:T(8,128)S(1)}, f32[96,128]{1,0:T(8,128)S(1)}, u32[]{:S(2)}, u32[]{:S(2)}) collective-permute-start(f32[96,128]{1,0:T(8,128)S(1)} %get-tuple-element.46), channel_id=1, source_target_pairs={{0,16},{2,18},{4,20},{6,22},{8,24},{10,26},{12,28},{14,30},{16,0},... | collective-permute-start | bytes 147464 | tf_op jit(solution)/shard_map/ppermute | solution.py:90
  16.3 9.4 %collective-permute-start.8 = (f32[96,128]{1,0:T(8,128)S(1)}, f32[96,128]{1,0:T(8,128)S(1)}, u32[]{:S(2)}, u32[]{:S(2)}) collective-permute-start(f32[96,128]{1,0:T(8,128)S(1)} %get-tuple-element.47), channel_id=1, source_target_pairs={{0,18},{2,16},{4,22},{6,20},{8,26},{10,24},{12,30},{14,28},{16,2},... | collective-permute-start | bytes 147464 | tf_op jit(solution)/shard_map/ppermute | solution.py:90
  17.8 12.2 %collective-permute-start.9 = (f32[96,128]{1,0:T(8,128)S(1)}, f32[96,128]{1,0:T(8,128)S(1)}, u32[]{:S(2)}, u32[]{:S(2)}) collective-permute-start(f32[96,128]{1,0:T(8,128)S(1)} %get-tuple-element.48), channel_id=1, source_target_pairs={{0,20},{2,22},{4,16},{6,18},{8,28},{10,30},{12,24},{14,26},{16,4},... | collective-permute-start | bytes 147464 | tf_op jit(solution)/shard_map/ppermute | solution.py:90
  18.7 12.8 %collective-permute-start.10 = (f32[96,128]{1,0:T(8,128)S(1)}, f32[96,128]{1,0:T(8,128)S(1)}, u32[]{:S(2)}, u32[]{:S(2)}) collective-permute-start(f32[96,128]{1,0:T(8,128)S(1)} %get-tuple-element.49), channel_id=1, source_target_pairs={{0,22},{2,20},{4,18},{6,16},{8,30},{10,28},{12,26},{14,24},{16,6},... | collective-permute-start | bytes 147464 | tf_op jit(solution)/shard_map/ppermute | solution.py:90
  22.0 9.5 %collective-permute-start.11 = (f32[96,128]{1,0:T(8,128)S(1)}, f32[96,128]{1,0:T(8,128)S(1)}, u32[]{:S(2)}, u32[]{:S(2)}) collective-permute-start(f32[96,128]{1,0:T(8,128)S(1)} %get-tuple-element.50), channel_id=1, source_target_pairs={{0,24},{2,26},{4,28},{6,30},{8,16},{10,18},{12,20},{14,22},{16,8},... | collective-permute-start | bytes 147464 | tf_op jit(solution)/shard_map/ppermute | solution.py:90
  23.1 8.4 %collective-permute-start.12 = (f32[96,128]{1,0:T(8,128)S(1)}, f32[96,128]{1,0:T(8,128)S(1)}, u32[]{:S(2)}, u32[]{:S(2)}) collective-permute-start(f32[96,128]{1,0:T(8,128)S(1)} %get-tuple-element.51), channel_id=1, source_target_pairs={{0,26},{2,24},{4,30},{6,28},{8,18},{10,16},{12,22},{14,20},{16,10}... | collective-permute-start | bytes 147464 | tf_op jit(solution)/shard_map/ppermute | solution.py:90
  25.8 7.1 %collective-permute-start.13 = (f32[96,128]{1,0:T(8,128)S(1)}, f32[96,128]{1,0:T(8,128)S(1)}, u32[]{:S(2)}, u32[]{:S(2)}) collective-permute-start(f32[96,128]{1,0:T(8,128)S(1)} %get-tuple-element.52), channel_id=1, source_target_pairs={{0,28},{2,30},{4,24},{6,26},{8,20},{10,22},{12,16},{14,18},{16,12}... | collective-permute-start | bytes 147464 | tf_op jit(solution)/shard_map/ppermute | solution.py:90
  30.0 7.7 %collective-permute-start.14 = (f32[96,128]{1,0:T(8,128)S(1)}, f32[96,128]{1,0:T(8,128)S(1)}, u32[]{:S(2)}, u32[]{:S(2)}) collective-permute-start(f32[96,128]{1,0:T(8,128)S(1)} %get-tuple-element.53), channel_id=1, source_target_pairs={{0,30},{2,28},{4,26},{6,24},{8,22},{10,20},{12,18},{14,16},{16,14}... | collective-permute-start | bytes 147464 | tf_op jit(solution)/shard_map/ppermute | solution.py:90
  37.8 33.4 %copy-start = (bf16[1024,128]{1,0:T(8,128)(2,1)S(1)}, bf16[1024,128]{1,0:T(8,128)(2,1)}, u32[]{:S(2)}) copy-start(bf16[1024,128]{1,0:T(8,128)(2,1)} %refs_17_.2) | copy-start | bytes 786436
  37.8 33.3 %copy-start.1 = (bf16[1024,128]{1,0:T(8,128)(2,1)S(1)}, bf16[1024,128]{1,0:T(8,128)(2,1)}, u32[]{:S(2)}) copy-start(bf16[1024,128]{1,0:T(8,128)(2,1)} %refs_18_.2) | copy-start | bytes 786436
  37.8 33.3 %copy-start.2 = (bf16[1024,128]{1,0:T(8,128)(2,1)S(1)}, bf16[1024,128]{1,0:T(8,128)(2,1)}, u32[]{:S(2)}) copy-start(bf16[1024,128]{1,0:T(8,128)(2,1)} %refs_16_.2) | copy-start | bytes 786436
  41.3 6.4 %collective-permute-start.15 = (f32[64,128]{1,0:T(8,128)S(1)}, f32[64,128]{1,0:T(8,128)S(1)}, u32[]{:S(2)}, u32[]{:S(2)}) collective-permute-start(f32[64,128]{1,0:T(8,128)S(1)} %get-tuple-element.55), channel_id=1, source_target_pairs={{0,2},{2,0},{4,6},{6,4},{8,10},{10,8},{12,14},{14,12},{16,18},{18,... | collective-permute-start | bytes 98312 | tf_op jit(solution)/shard_map/ppermute | solution.py:90
  41.8 6.8 %collective-permute-start.16 = (f32[64,128]{1,0:T(8,128)S(1)}, f32[64,128]{1,0:T(8,128)S(1)}, u32[]{:S(2)}, u32[]{:S(2)}) collective-permute-start(f32[64,128]{1,0:T(8,128)S(1)} %get-tuple-element.56), channel_id=1, source_target_pairs={{0,4},{2,6},{4,0},{6,2},{8,12},{10,14},{12,8},{14,10},{16,20},{18,... | collective-permute-start | bytes 98312 | tf_op jit(solution)/shard_map/ppermute | solution.py:90
  41.8 10.6 %collective-permute-start.17 = (f32[64,128]{1,0:T(8,128)S(1)}, f32[64,128]{1,0:T(8,128)S(1)}, u32[]{:S(2)}, u32[]{:S(2)}) collective-permute-start(f32[64,128]{1,0:T(8,128)S(1)} %get-tuple-element.57), channel_id=1, source_target_pairs={{0,6},{2,4},{4,2},{6,0},{8,14},{10,12},{12,10},{14,8},{16,22},{18,... | collective-permute-start | bytes 98312 | tf_op jit(solution)/shard_map/ppermute | solution.py:90
  44.8 8.2 %collective-permute-start.18 = (f32[64,128]{1,0:T(8,128)S(1)}, f32[64,128]{1,0:T(8,128)S(1)}, u32[]{:S(2)}, u32[]{:S(2)}) collective-permute-start(f32[64,128]{1,0:T(8,128)S(1)} %get-tuple-element.58), channel_id=1, source_target_pairs={{0,8},{2,10},{4,12},{6,14},{8,0},{10,2},{12,4},{14,6},{16,24},{18,... | collective-permute-start | bytes 98312 | tf_op jit(solution)/shard_map/ppermute | solution.py:90
  44.8 9.6 %collective-permute-start.19 = (f32[64,128]{1,0:T(8,128)S(1)}, f32[64,128]{1,0:T(8,128)S(1)}, u32[]{:S(2)}, u32[]{:S(2)}) collective-permute-start(f32[64,128]{1,0:T(8,128)S(1)} %get-tuple-element.59), channel_id=1, source_target_pairs={{0,10},{2,8},{4,14},{6,12},{8,2},{10,0},{12,6},{14,4},{16,26},{18,... | collective-permute-start | bytes 98312 | tf_op jit(solution)/shard_map/ppermute | solution.py:90
  47.7 6.8 %collective-permute-start.20 = (f32[64,128]{1,0:T(8,128)S(1)}, f32[64,128]{1,0:T(8,128)S(1)}, u32[]{:S(2)}, u32[]{:S(2)}) collective-permute-start(f32[64,128]{1,0:T(8,128)S(1)} %get-tuple-element.60), channel_id=1, source_target_pairs={{0,12},{2,14},{4,8},{6,10},{8,4},{10,6},{12,0},{14,2},{16,28},{18,... | collective-permute-start | bytes 98312 | tf_op jit(solution)/shard_map/ppermute | solution.py:90
  48.7 9.7 %collective-permute-start.21 = (f32[64,128]{1,0:T(8,128)S(1)}, f32[64,128]{1,0:T(8,128)S(1)}, u32[]{:S(2)}, u32[]{:S(2)}) collective-permute-start(f32[64,128]{1,0:T(8,128)S(1)} %get-tuple-element.61), channel_id=1, source_target_pairs={{0,14},{2,12},{4,10},{6,8},{8,6},{10,4},{12,2},{14,0},{16,30},{18,... | collective-permute-start | bytes 98312 | tf_op jit(solution)/shard_map/ppermute | solution.py:90
  52.5 5.9 %collective-permute-start.22 = (f32[64,128]{1,0:T(8,128)S(1)}, f32[64,128]{1,0:T(8,128)S(1)}, u32[]{:S(2)}, u32[]{:S(2)}) collective-permute-start(f32[64,128]{1,0:T(8,128)S(1)} %get-tuple-element.62), channel_id=1, source_target_pairs={{0,16},{2,18},{4,20},{6,22},{8,24},{10,26},{12,28},{14,30},{16,0},... | collective-permute-start | bytes 98312 | tf_op jit(solution)/shard_map/ppermute | solution.py:90
  53.0 9.1 %collective-permute-start.23 = (f32[64,128]{1,0:T(8,128)S(1)}, f32[64,128]{1,0:T(8,128)S(1)}, u32[]{:S(2)}, u32[]{:S(2)}) collective-permute-start(f32[64,128]{1,0:T(8,128)S(1)} %get-tuple-element.63), channel_id=1, source_target_pairs={{0,18},{2,16},{4,22},{6,20},{8,26},{10,24},{12,30},{14,28},{16,2},... | collective-permute-start | bytes 98312 | tf_op jit(solution)/shard_map/ppermute | solution.py:90
  54.5 9.2 %collective-permute-start.24 = (f32[64,128]{1,0:T(8,128)S(1)}, f32[64,128]{1,0:T(8,128)S(1)}, u32[]{:S(2)}, u32[]{:S(2)}) collective-permute-start(f32[64,128]{1,0:T(8,128)S(1)} %get-tuple-element.64), channel_id=1, source_target_pairs={{0,20},{2,22},{4,16},{6,18},{8,28},{10,30},{12,24},{14,26},{16,4},... | collective-permute-start | bytes 98312 | tf_op jit(solution)/shard_map/ppermute | solution.py:90
  54.5 13.3 %collective-permute-start.25 = (f32[64,128]{1,0:T(8,128)S(1)}, f32[64,128]{1,0:T(8,128)S(1)}, u32[]{:S(2)}, u32[]{:S(2)}) collective-permute-start(f32[64,128]{1,0:T(8,128)S(1)} %get-tuple-element.65), channel_id=1, source_target_pairs={{0,22},{2,20},{4,18},{6,16},{8,30},{10,28},{12,26},{14,24},{16,6},... | collective-permute-start | bytes 98312 | tf_op jit(solution)/shard_map/ppermute | solution.py:90
  58.3 9.5 %collective-permute-start.26 = (f32[64,128]{1,0:T(8,128)S(1)}, f32[64,128]{1,0:T(8,128)S(1)}, u32[]{:S(2)}, u32[]{:S(2)}) collective-permute-start(f32[64,128]{1,0:T(8,128)S(1)} %get-tuple-element.66), channel_id=1, source_target_pairs={{0,24},{2,26},{4,28},{6,30},{8,16},{10,18},{12,20},{14,22},{16,8},... | collective-permute-start | bytes 98312 | tf_op jit(solution)/shard_map/ppermute | solution.py:90
  58.4 9.5 %collective-permute-start.27 = (f32[64,128]{1,0:T(8,128)S(1)}, f32[64,128]{1,0:T(8,128)S(1)}, u32[]{:S(2)}, u32[]{:S(2)}) collective-permute-start(f32[64,128]{1,0:T(8,128)S(1)} %get-tuple-element.67), channel_id=1, source_target_pairs={{0,26},{2,24},{4,30},{6,28},{8,18},{10,16},{12,22},{14,20},{16,10}... | collective-permute-start | bytes 98312 | tf_op jit(solution)/shard_map/ppermute | solution.py:90
  62.1 6.6 %collective-permute-start.28 = (f32[64,128]{1,0:T(8,128)S(1)}, f32[64,128]{1,0:T(8,128)S(1)}, u32[]{:S(2)}, u32[]{:S(2)}) collective-permute-start(f32[64,128]{1,0:T(8,128)S(1)} %get-tuple-element.68), channel_id=1, source_target_pairs={{0,28},{2,30},{4,24},{6,26},{8,20},{10,22},{12,16},{14,18},{16,12}... | collective-permute-start | bytes 98312 | tf_op jit(solution)/shard_map/ppermute | solution.py:90
  63.6 7.5 %collective-permute-start.29 = (f32[64,128]{1,0:T(8,128)S(1)}, f32[64,128]{1,0:T(8,128)S(1)}, u32[]{:S(2)}, u32[]{:S(2)}) collective-permute-start(f32[64,128]{1,0:T(8,128)S(1)} %get-tuple-element.69), channel_id=1, source_target_pairs={{0,30},{2,28},{4,26},{6,24},{8,22},{10,20},{12,18},{14,16},{16,14}... | collective-permute-start | bytes 98312 | tf_op jit(solution)/shard_map/ppermute | solution.py:90

commit v5 on v1

--- a/solution.py
+++ b/solution.py
@@ -76,33 +76,87 @@
     return mat(by_lanes(jnp.concatenate(rows, axis=0)), tail)
 
 
-def pack_kernel(rows, own, share, which_ref, key_ref, value_ref, filter_ref, out_ref, turned):
-    for row in range(rows):
-        span = pl.ds(row * LANES, LANES)
-        turned[0, pl.ds(row, LANES, stride=rows), :] = (
-            key_ref[span, :].astype(F32) * value_ref[span, :].astype(F32)
-        ).T
-        turned[1, pl.ds(row, LANES, stride=rows), :] = filter_ref[span, :].T
-    first = which_ref[0] * (share * rows if share < own else 0)
-    for peer in range(out_ref.shape[0]):
-        start = peer * own * rows
-        out_ref[peer, : own * rows] = turned[0, pl.ds(start, own * rows), :]
-        taken = pl.ds(pl.multiple_of(start + first, rows), share * rows)
-        out_ref[peer, own * rows :] = turned[1, taken, :]
-
-
-def conv_kernel(rows, own, share, moved_ref, head_ref, twist_ref, tail_ref, back_tail_ref, back_head_ref, out_ref):
-    groups, blocks = moved_ref.shape[:2]
+def pack_kernel(layout, with_driver, with_filter, where_ref, *refs):
+    rows, own, part, groups = layout
+    refs = list(refs)
+    sources = [refs.pop(0) for _ in range(2 * with_driver + with_filter)]
+    bias_ref = refs.pop(0) if with_driver else None
+    out_ref = refs.pop(0)
+    bias_out = refs.pop(0) if with_driver else None
+    held = [refs.pop(0) for _ in sources]
+    sems = refs.pop(0)
+    fetches = []
+    for idx, source in enumerate(sources):
+        if idx == 2 * with_driver:
+            first = where_ref[0] * (part * LANES if part < rows else 0)
+            source = source.at[pl.ds(pl.multiple_of(first, part * LANES), part * LANES)]
+        fetches.append(pltpu.make_async_copy(source, held[idx], sems.at[idx]))
+    if with_driver:
+        fetches.append(pltpu.make_async_copy(bias_ref, bias_out, sems.at[len(sources)]))
+    for fetch in fetches:
+        fetch.start()
+    base = 0
+    if with_driver:
+        base = own * rows
+        fetches[0].wait()
+        fetches[1].wait()
+        for row in range(rows):
+            span = pl.ds(row * LANES, LANES)
+            turned = (held[0][span, :].astype(F32) * held[1][span, :].astype(F32)).T
+            for peer in range(out_ref.shape[0]):
+                out_ref[peer, pl.ds(row, own, stride=rows), :] = turned[peer * own : (peer + 1) * own]
+    if with_filter:
+        fetches[2 * with_driver].wait()
+        for row in range(part):
+            turned = held[-1][pl.ds(row * LANES, LANES), :].T
+            for peer in range(out_ref.shape[0]):
+                out_ref[peer, pl.ds(base + row, own, stride=part), :] = turned[peer * own : (peer + 1) * own]
+    if with_driver:
+        fetches[-1].wait()
+
+
+def driver_signals(layout, moved_ref):
+    rows, own, part, groups = layout
+    blocks = moved_ref.shape[0] // groups
+    return [
+        moved_ref[pl.ds(group * blocks, blocks), chan * rows : (chan + 1) * rows].reshape(blocks * rows, LANES)
+        for chan in range(own)
+        for group in range(groups)
+    ]
+
+
+def filter_signals(layout, base, moved_ref):
+    rows, own, part, groups = layout
+    blocks = moved_ref.shape[0] // groups
+    signals = []
+    for chan in range(own):
+        start = base + chan * part
+        pieces = [
+            moved_ref[pl.ds(group * blocks, blocks), start : start + part]
+            for group in range(groups if part < rows else 1)
+        ]
+        signals.append(jnp.concatenate(pieces, axis=1).reshape(blocks * rows, LANES))
+    return signals
+
+
+def filter_kernel(layout, moved_ref, head_ref, twist_ref, tail_ref, out_ref):
+    signals = filter_signals(layout, 0, moved_ref)
+    out_ref[...] = forward(signals, head_ref[...], twist_ref[...], tail_ref[...])
+
+
+def conv_kernel(layout, joint, moved_ref, *refs):
+    rows, own, part, groups = layout
+    spec_ref = None if joint else refs[0]
+    head_ref, twist_ref, tail_ref, back_tail_ref, back_head_ref, out_ref = refs[-6:]
+    blocks = moved_ref.shape[0] // groups
     outer = blocks * rows
     scale = 1.0 / (outer * LANES)
-
-    def signal(group, place):
-        return moved_ref[group, :, place * rows : (place + 1) * rows].reshape(outer, LANES)
-
-    signals = [signal(chan // share, own + chan % share) for chan in range(own)]
-    signals += [signal(group, chan) for chan in range(own) for group in range(groups)]
+    signals = filter_signals(layout, own * rows, moved_ref) if joint else []
+    signals += driver_signals(layout, moved_ref)
     spec = forward(signals, head_ref[...], twist_ref[...], tail_ref[...])
     pieces = [spec[idx * outer : (idx + 1) * outer] for idx in range(len(signals))]
+    if not joint:
+        pieces = [spec_ref[pl.ds(chan * outer, outer), :] for chan in range(own)] + pieces
     prods = []
     for idx, mine in enumerate(pieces[own:]):
         other = pieces[idx // groups]
@@ -121,7 +175,9 @@
     result = mat(back_head_ref[...], by_rows(mixed))
     for idx in range(len(prods)):
         chan, group = divmod(idx, groups)
-        out_ref[group, :, chan] = result[:, idx * LANES : (idx + 1) * LANES].reshape(blocks, rows, LANES)
+        out_ref[pl.ds(group * blocks, blocks), chan * rows : (chan + 1) * rows] = result[
+            :, idx * LANES : (idx + 1) * LANES
+        ].reshape(blocks, rows, LANES)
 
 
 def gate_kernel(rows, conv_ref, query_ref, key_ref, value_ref, bias_ref, out_ref):
@@ -134,46 +190,81 @@
 
 
 VMEM = pl.BlockSpec(memory_space=pltpu.VMEM)
+HBM = pl.BlockSpec(memory_space=pltpu.HBM)
 SMEM = pl.BlockSpec(memory_space=pltpu.SMEM)
 
 
-def call(kernel, shape, dtype, specs, flops, moved, scratch=()):
+def call(kernel, outs, specs, flops, moved, scratch=()):
     return pl.pallas_call(
         kernel,
-        out_shape=jax.ShapeDtypeStruct(shape, dtype),
+        out_shape=[jax.ShapeDtypeStruct(*out) for out in outs],
         in_specs=specs,
-        out_specs=VMEM,
+        out_specs=[VMEM] * len(outs),
         scratch_shapes=scratch,
         compiler_params=pltpu.CompilerParams(vmem_limit_bytes=VMEM_LIMIT),
         cost_estimate=pl.CostEstimate(flops=flops, bytes_accessed=moved, transcendentals=0),
     )
 
 
-def shards(groups, blocks, query_proj, key_proj, value_proj, long_filter, skip_bias):
+def convolve(groups, blocks, joint, query_proj, key_proj, value_proj, long_filter, skip_bias):
     tokens, chans = key_proj.shape
     rows = tokens // LANES
-    own = chans // (groups * blocks)
+    count, axes = groups * blocks, ("groups", "seq")
+    own = chans // count
     outer = blocks * rows
     seq_len = blocks * tokens
-    tables = make_tables(seq_len)
-    head, twist, tail, back_tail, back_head = (jnp.asarray(table) for table in tables)
+    part = rows // groups
+    if rows % groups or own * part % 8:
+        part = rows
+    layout = (rows, own, part, groups)
+    head, twist, tail, back_tail, back_head = (jnp.asarray(table) for table in make_tables(seq_len))
     size = tokens * chans * 4
-
-    share = own // groups if own % groups == 0 else own
-    packed = call(
-        functools.partial(pack_kernel, rows, own, share),
-        (groups * blocks, (own + share) * rows, LANES), F32, [SMEM, VMEM, VMEM, VMEM], size // 4, size * 4,
-        [pltpu.VMEM((2, chans * rows, LANES), F32)],
-    )(lax.axis_index("groups").reshape(1).astype(jnp.int32), key_proj, value_proj, long_filter)
-    moved = lax.all_to_all(packed, ("groups", "seq"), 0, 0, tiled=True)
     macs = 2 * 3 * own * seq_len * (2 * outer + 4 * LANES)
+    where = lax.axis_index("groups").reshape(1).astype(jnp.int32)
+
+    def pack(with_driver, with_filter):
+        height = own * (rows * with_driver + part * with_filter)
+        sources = [key_proj, value_proj] * with_driver + [long_filter] * with_filter
+        heights = [tokens, tokens] * with_driver + [part * LANES] * with_filter
+        scratch = [pltpu.VMEM((tall, chans), source.dtype) for tall, source in zip(heights, sources)]
+        sources += [skip_bias.reshape(1, chans)] * with_driver
+        return call(
+            functools.partial(pack_kernel, layout, with_driver, with_filter),
+            [((count, height, LANES), F32)] + [((1, chans), F32)] * with_driver,
+            [SMEM] + [HBM] * len(sources), size // 4, size * 3,
+            scratch + [pltpu.SemaphoreType.DMA((len(sources),))],
+        )(where, *(pltpu.with_memory_space_constraint(source, pltpu.HBM) for source in sources))
+
+    def exchange(array):
+        return lax.all_to_all(array, axes, 0, 0, tiled=True)
+
+    spec = []
+    if joint:
+        packed, bias = pack(1, 1)
+    else:
+        moved_filter = exchange(pack(0, 1)[0])
+        packed, bias = pack(1, 0)
+        spec = call(
+            functools.partial(filter_kernel, layout), [((own * outer, 2 * LANES), F32)], [VMEM] * 4, macs, size
+        )(moved_filter, head, twist, tail)
     local = call(
-        functools.partial(conv_kernel, rows, own, share),
-        (groups, blocks, own, rows, LANES), F32, [VMEM] * 6, 5 * macs, 3 * size,
-    )(moved.reshape(groups, blocks, (own + share) * rows, LANES), head, twist, tail, back_tail, back_head)
-    convolved = lax.all_to_all(local.reshape(chans * rows, LANES), ("groups", "seq"), 0, 0, tiled=True)
-    return call(functools.partial(gate_kernel, rows), (tokens, chans), BF16, [VMEM] * 5, size, 3 * size)(
-        convolved, query_proj, key_proj, value_proj, skip_bias.reshape(1, chans)
+        functools.partial(conv_kernel, layout, joint),
+        [((count, own * rows, LANES), F32)], [VMEM] * (6 + len(spec)), 5 * macs, 3 * size,
+    )(exchange(packed), *spec, head, twist, tail, back_tail, back_head)[0]
+    convolved = exchange(local).reshape(chans * rows, LANES)
+    return call(functools.partial(gate_kernel, rows), [((tokens, chans), BF16)], [VMEM] * 5, size, 3 * size)(
+        convolved, query_proj, key_proj, value_proj, bias
+    )[0]
+
+
+def shards(groups, blocks, cores, *args):
+    if cores == 1:
+        return convolve(groups, blocks, True, *args)
+    return lax.cond(
+        lax.axis_index("chan") % 2 == 1,
+        functools.partial(convolve, groups, blocks, True),
+        functools.partial(convolve, groups, blocks, False),
+        *args,
     )
 
 
@@ -185,7 +276,7 @@
         P("seq", "chan"),
         P("chan"),
     )
-    body = functools.partial(shards, mesh.shape["groups"], mesh.shape["seq"])
+    body = functools.partial(shards, *(mesh.shape[axis] for axis in ("groups", "seq", "chan")))
     return jax.shard_map(
         body, mesh=mesh, in_specs=placed, out_specs=P(("groups", "seq"), "chan"), check_vma=False
     )

time: 55.5 us -> 59.6 us (1.074)
  blocking collectives: 47.3 us -> 16.1 us
  waiting for transfers between devices: 0 us -> 23.6 us
  starting transfers between devices: 0 us -> 12 us
  local copies, waits for them, and re-layouts: 3.64 us -> 0.74 us
  Pallas kernels: 4.07 us -> 6.64 us
    all_to_all x2 -> x1, blocking collectives: 47.3 us -> 16.1 us  [exchange(): return lax.all_to_all(array, axes, 0, 0, tiled=True)]
    all_to_all x0 -> x2, waiting for transfers between devices: none -> 23.6 us  [exchange(): return lax.all_to_all(array, axes, 0, 0, tiled=True)]
    all_to_all x0 -> x2, starting transfers between devices: none -> 12 us  [exchange(): return lax.all_to_all(array, axes, 0, 0, tiled=True)]
    unnamed x24 -> x2, local copies, waits for them, and re-layouts: 3.64 us -> 0.7 us
    pallas_call x3 -> x5, Pallas kernels: 4.07 us -> 6.64 us  [the longest x2 3.87 us: pack(): call(functools.partial(pack_kernel, layout, with_driver, with_filter), [(...]
  transfers between devices with their start and end apart: 0 -> 2, of which waited for: 0 -> 2; matrix products, arithmetic and copies ran while one was open for 0% -> 0% of each run, Pallas kernels for 0% -> 4%
where the time goes in v5:
time: 59.6 us; the launch traced here: 59.2 us
  waiting for transfers between devices  23.6 us (40%)
  blocking collectives  16.1 us (27%)
  starting transfers between devices  12 us (20%)
  Pallas kernels  6.64 us (11%)
  local copies, waits for them, and re-layouts  0.74 us (1%)
    all_to_all x2, waiting for transfers between devices, exchange(): return lax.all_to_all(array, axes, 0, 0, tiled=True)  23.6 us
    all_to_all x1, blocking collectives, exchange(): return lax.all_to_all(array, axes, 0, 0, tiled=True)  16.1 us
    all_to_all x2, starting transfers between devices, exchange(): return lax.all_to_all(array, axes, 0, 0, tiled=True)  12 us
    pallas_call x2, Pallas kernels, pack(): call(functools.partial(pack_kernel, layout, with_driver, with_filter), [(...  3.87 us
    pallas_call x1, Pallas kernels, convolve(): call(functools.partial(conv_kernel, layout, joint), [((count, own * rows,...  2.04 us
  transfers between devices with their start and end apart: 2, of which 2 were waited for; matrix products, arithmetic and copies ran while one was open for 0% of the time, Pallas kernels for 4%

profile of v5, /device:TPU:0, one launch (start us, length us, event | category | flops | bytes accessed | tf_op | source)
XLA Modules:
  0.0 59.2 jit_solution(6811281552979600608)
XLA Ops:
  0.0 58.5 %conditional.1 = (bf16[1024,128]{1,0:T(8,128)(2,1)S(1)}) conditional(s32[]{:T(128)} %convert_element_type.3, (f32[128]{0:T(128)}, bf16[1024,128]{1,0:T(8,128)(2,1)}, bf16[1024,128]{1,0:T(8,128)(2,1)}, f32[1024,128]{1,0:T(8,128)}, bf16[128,192]{1,0:T(8,128)(2,1)}, /*index=5*/f32[64,256]{1,0:T(8,128)}, bf16[768,256]{1,0:T(8,128)(2,1)}, ...), branch_computations={%region_0.1_spmd, %region_1.2_spmd} | conditional | flops 1510735872 | bytes 17170760 | solution.py:263
  0.0 1.8 %branch_0_fun.6 = f32[16,32,128]{2,1,0:T(8,128)} custom-call(s32[1]{0:T(128)} %bitcast.where_ref, f32[1024,128]{1,0:T(8,128)} %get-tuple-element.52.refs_0_), custom_call_target="tpu_custom_call" | custom-call | flops 131072 | bytes 1572864 | tf_op jit(solution)/shard_map/cond/branch_0_fun/pallas_call | solution.py:231
  1.8 8.3 %all-to-all-start.1 = ((f32[16,32,128]{2,1,0:T(8,128)}), f32[16,32,128]{2,1,0:T(8,128)S(1)}, u32[]{:S(2)}, u32[]{:S(2)}) async-start(f32[16,32,128]{2,1,0:T(8,128)} %branch_0_fun.6), calls=%async_computation.1 | async-start | bytes 524288 | tf_op jit(solution)/shard_map/cond/branch_0_fun/all_to_all | solution.py:239
  10.1 2.1 %branch_0_fun.5 = (f32[16,64,128]{2,1,0:T(8,128)}, f32[1,128]{1,0:T(1,128)S(1)}) custom-call(s32[1]{0:T(128)} %bitcast.where_ref, bf16[1024,128]{1,0:T(8,128)(2,1)} %get-tuple-element.48.refs_0_.key_ref, bf16[1024,128]{1,0:T(8,128)(2,1)} %get-tuple-element.49.refs_1_.value_ref, f32[1,128]{1,0:T(1,128)} %bitcast.8), custom_call_target="tpu_custom_call" | custom-call | flops 131072 | bytes 1572864 | tf_op jit(solution)/shard_map/cond/branch_0_fun/pallas_call | solution.py:231
  12.2 11.0 %all-to-all-done.1.moved_ref = f32[16,32,128]{2,1,0:T(8,128)S(1)} async-done(((f32[16,32,128]{2,1,0:T(8,128)}), f32[16,32,128]{2,1,0:T(8,128)S(1)}, u32[]{:S(2)}, u32[]{:S(2)}) %all-to-all-start.1) | async-done | bytes 262176 | tf_op jit(solution)/shard_map/cond/branch_0_fun/all_to_all | solution.py:239
  23.2 0.0 copy-start.6
  23.2 0.0 copy-start.9
  23.2 0.0 copy-start.11
  23.2 3.7 %all-to-all-start = ((f32[16,64,128]{2,1,0:T(8,128)}), f32[16,64,128]{2,1,0:T(8,128)S(1)}, u32[]{:S(2)}, u32[]{:S(2)}) async-start(f32[16,64,128]{2,1,0:T(8,128)} %get-tuple-element.51), calls=%async_computation | async-start | bytes 1048576 | tf_op jit(solution)/shard_map/cond/branch_0_fun/all_to_all | solution.py:239
  26.9 0.0 copy-done.6
  26.9 0.0 copy-done.9
  26.9 0.0 copy-done.11
  26.9 0.0 copy-start.13
  26.9 0.0 copy-start.15
  27.0 0.5 branch_0_fun.7.refs_0_
  27.5 12.6 %all-to-all-done.moved_ref = f32[16,64,128]{2,1,0:T(8,128)S(1)} async-done(((f32[16,64,128]{2,1,0:T(8,128)}), f32[16,64,128]{2,1,0:T(8,128)S(1)}, u32[]{:S(2)}, u32[]{:S(2)}) %all-to-all-start) | async-done | bytes 524320 | tf_op jit(solution)/shard_map/cond/branch_0_fun/all_to_all | solution.py:239
  40.1 0.0 copy-done.13
  40.1 0.0 copy-done.15
  40.1 2.0 %branch_0_fun.8 = f32[16,64,128]{2,1,0:T(8,128)S(1)} custom-call(f32[16,64,128]{2,1,0:T(8,128)S(1)} %all-to-all-done.moved_ref, f32[512,256]{1,0:T(8,128)S(1)} %branch_0_fun.7.refs_0_, bf16[128,192]{1,0:T(8,128)(2,1)S(1)} %copy-done.11, f32[64,256]{1,0:T(8,128)S(1)} %copy-done.9, bf16[768,256]{1,0:T(8,128)(2,1)S(1)} %copy-done.6, ...), custom_call_target="tpu_custom_call" | custom-call | flops 1258291200 | bytes 1572864 | tf_op jit(solution)/shard_map/cond/branch_0_fun/pallas_call | solution.py:250
  42.1 0.0 copy-start
  42.1 0.0 copy-start.2
  42.1 0.0 copy-start.4
  42.2 16.1 %all_to_all.20 = f32[16,64,128]{2,1,0:T(8,128)S(1)} all-to-all(f32[16,64,128]{2,1,0:T(8,128)S(1)} %branch_0_fun.8), channel_id=1, replica_groups=mesh['groups'=2,'seq'=8,'chan'=2] {'groups','seq'}, dimensions={0} | all-to-all | bytes 1048576 | tf_op jit(solution)/shard_map/cond/branch_0_fun/all_to_all | solution.py:239
  58.3 0.0 copy-done
  58.3 0.0 copy-done.2
  58.3 0.0 copy-done.4
  58.3 0.2 branch_0_fun.9
  58.5 0.0 copy-start.8
  58.5 0.7 %copy-done.8 = bf16[1024,128]{1,0:T(8,128)(2,1)} copy-done((bf16[1024,128]{1,0:T(8,128)(2,1)}, bf16[1024,128]{1,0:T(8,128)(2,1)S(1)}, u32[]{:S(2)}) %copy-start.8) | copy-done | bytes 262168
Async XLA Ops:
  1.8 21.4 %all-to-all-start.1 = ((f32[16,32,128]{2,1,0:T(8,128)}), f32[16,32,128]{2,1,0:T(8,128)S(1)}, u32[]{:S(2)}, u32[]{:S(2)}) async-start(f32[16,32,128]{2,1,0:T(8,128)} %branch_0_fun.6), calls=%async_computation.1 | async-start | bytes 524288 | tf_op jit(solution)/shard_map/cond/branch_0_fun/all_to_all | solution.py:239
  23.2 3.7 %copy-start.6 = (bf16[768,256]{1,0:T(8,128)(2,1)S(1)}, bf16[768,256]{1,0:T(8,128)(2,1)}, u32[]{:S(2)}) copy-start(bf16[768,256]{1,0:T(8,128)(2,1)} %get-tuple-element.55.tail_ref.refs_3_) | copy-start | bytes 1179652 | tf_op jit(solution)/shard_map/cond
  23.2 3.7 %copy-start.9 = (f32[64,256]{1,0:T(8,128)S(1)}, f32[64,256]{1,0:T(8,128)}, u32[]{:S(2)}) copy-start(f32[64,256]{1,0:T(8,128)} %get-tuple-element.54.twist_ref.refs_2_) | copy-start | bytes 196612 | tf_op jit(solution)/shard_map/cond
  23.2 3.7 %copy-start.11 = (bf16[128,192]{1,0:T(8,128)(2,1)S(1)}, bf16[128,192]{1,0:T(8,128)(2,1)}, u32[]{:S(2)}) copy-start(bf16[128,192]{1,0:T(8,128)(2,1)} %get-tuple-element.53.head_ref.refs_1_) | copy-start | bytes 147460 | tf_op jit(solution)/shard_map/cond
  23.2 16.9 %all-to-all-start = ((f32[16,64,128]{2,1,0:T(8,128)}), f32[16,64,128]{2,1,0:T(8,128)S(1)}, u32[]{:S(2)}, u32[]{:S(2)}) async-start(f32[16,64,128]{2,1,0:T(8,128)} %get-tuple-element.51), calls=%async_computation | async-start | bytes 1048576 | tf_op jit(solution)/shard_map/cond/branch_0_fun/all_to_all | solution.py:239
  26.9 13.1 %copy-start.13 = (bf16[768,256]{1,0:T(8,128)(2,1)S(1)}, bf16[768,256]{1,0:T(8,128)(2,1)}, u32[]{:S(2)}) copy-start(bf16[768,256]{1,0:T(8,128)(2,1)} %get-tuple-element.56.refs_4_) | copy-start | bytes 1179652 | tf_op jit(solution)/shard_map/cond
  26.9 13.1 %copy-start.15 = (bf16[64,384]{1,0:T(8,128)(2,1)S(1)}, bf16[64,384]{1,0:T(8,128)(2,1)}, u32[]{:S(2)}) copy-start(bf16[64,384]{1,0:T(8,128)(2,1)} %get-tuple-element.57.refs_5_) | copy-start | bytes 147460 | tf_op jit(solution)/shard_map/cond
  42.1 16.2 %copy-start = (bf16[1024,128]{1,0:T(8,128)(2,1)S(1)}, bf16[1024,128]{1,0:T(8,128)(2,1)}, u32[]{:S(2)}) copy-start(bf16[1024,128]{1,0:T(8,128)(2,1)} %get-tuple-element.48.refs_0_.key_ref) | copy-start | bytes 786436 | tf_op jit(solution)/shard_map/cond
  42.1 16.2 %copy-start.2 = (bf16[1024,128]{1,0:T(8,128)(2,1)S(1)}, bf16[1024,128]{1,0:T(8,128)(2,1)}, u32[]{:S(2)}) copy-start(bf16[1024,128]{1,0:T(8,128)(2,1)} %get-tuple-element.49.refs_1_.value_ref) | copy-start | bytes 786436 | tf_op jit(solution)/shard_map/cond
  42.1 16.2 %copy-start.4 = (bf16[1024,128]{1,0:T(8,128)(2,1)S(1)}, bf16[1024,128]{1,0:T(8,128)(2,1)}, u32[]{:S(2)}) copy-start(bf16[1024,128]{1,0:T(8,128)(2,1)} %get-tuple-element.58.query_ref) | copy-start | bytes 786436 | tf_op jit(solution)/shard_map/cond
  58.5 0.7 %copy-start.8 = (bf16[1024,128]{1,0:T(8,128)(2,1)}, bf16[1024,128]{1,0:T(8,128)(2,1)S(1)}, u32[]{:S(2)}) copy-start(bf16[1024,128]{1,0:T(8,128)(2,1)S(1)} %get-tuple-element.77) | copy-start | bytes 786436

commit v6 on v1

--- a/solution.py
+++ b/solution.py
@@ -76,31 +76,59 @@
     return mat(by_lanes(jnp.concatenate(rows, axis=0)), tail)
 
 
-def pack_kernel(rows, own, share, which_ref, key_ref, value_ref, filter_ref, out_ref, turned):
+def pack_kernel(layout, where_ref, key_ref, value_ref, filter_ref, bias_ref, out_ref, bias_out, key, value, taps, sems):
+    rows, own, part, groups = layout
+    first = where_ref[0] * (part * LANES if part < rows else 0)
+    taken = filter_ref.at[pl.ds(pl.multiple_of(first, part * LANES), part * LANES)]
+    pairs = ((key_ref, key), (value_ref, value), (taken, taps), (bias_ref, bias_out))
+    fetches = [pltpu.make_async_copy(*pair, sems.at[idx]) for idx, pair in enumerate(pairs)]
+    for fetch in fetches:
+        fetch.start()
+    fetches[0].wait()
+    fetches[1].wait()
     for row in range(rows):
         span = pl.ds(row * LANES, LANES)
-        turned[0, pl.ds(row, LANES, stride=rows), :] = (
-            key_ref[span, :].astype(F32) * value_ref[span, :].astype(F32)
-        ).T
-        turned[1, pl.ds(row, LANES, stride=rows), :] = filter_ref[span, :].T
-    first = which_ref[0] * (share * rows if share < own else 0)
-    for peer in range(out_ref.shape[0]):
-        start = peer * own * rows
-        out_ref[peer, : own * rows] = turned[0, pl.ds(start, own * rows), :]
-        taken = pl.ds(pl.multiple_of(start + first, rows), share * rows)
-        out_ref[peer, own * rows :] = turned[1, taken, :]
-
-
-def conv_kernel(rows, own, share, moved_ref, head_ref, twist_ref, tail_ref, back_tail_ref, back_head_ref, out_ref):
-    groups, blocks = moved_ref.shape[:2]
+        turned = (key[span, :].astype(F32) * value[span, :].astype(F32)).T
+        for peer in range(out_ref.shape[0]):
+            out_ref[peer, pl.ds(row, own, stride=rows), :] = turned[peer * own : (peer + 1) * own]
+    fetches[2].wait()
+    for row in range(part):
+        turned = taps[pl.ds(row * LANES, LANES), :].T
+        for peer in range(out_ref.shape[0]):
+            out_ref[peer, pl.ds(own * rows + row, own, stride=part), :] = turned[peer * own : (peer + 1) * own]
+    fetches[3].wait()
+
+
+def driver_signals(layout, moved_ref):
+    rows, own, part, groups = layout
+    blocks = moved_ref.shape[0] // groups
+    return [
+        moved_ref[pl.ds(group * blocks, blocks), chan * rows : (chan + 1) * rows].reshape(blocks * rows, LANES)
+        for chan in range(own)
+        for group in range(groups)
+    ]
+
+
+def filter_signals(layout, moved_ref):
+    rows, own, part, groups = layout
+    blocks = moved_ref.shape[0] // groups
+    signals = []
+    for chan in range(own):
+        start = own * rows + chan * part
+        pieces = [
+            moved_ref[pl.ds(group * blocks, blocks), start : start + part]
+            for group in range(groups if part < rows else 1)
+        ]
+        signals.append(jnp.concatenate(pieces, axis=1).reshape(blocks * rows, LANES))
+    return signals
+
+
+def conv_kernel(layout, moved_ref, head_ref, twist_ref, tail_ref, back_tail_ref, back_head_ref, out_ref):
+    rows, own, part, groups = layout
+    blocks = moved_ref.shape[0] // groups
     outer = blocks * rows
     scale = 1.0 / (outer * LANES)
-
-    def signal(group, place):
-        return moved_ref[group, :, place * rows : (place + 1) * rows].reshape(outer, LANES)
-
-    signals = [signal(chan // share, own + chan % share) for chan in range(own)]
-    signals += [signal(group, chan) for chan in range(own) for group in range(groups)]
+    signals = filter_signals(layout, moved_ref) + driver_signals(layout, moved_ref)
     spec = forward(signals, head_ref[...], twist_ref[...], tail_ref[...])
     pieces = [spec[idx * outer : (idx + 1) * outer] for idx in range(len(signals))]
     prods = []
@@ -121,7 +149,9 @@
     result = mat(back_head_ref[...], by_rows(mixed))
     for idx in range(len(prods)):
         chan, group = divmod(idx, groups)
-        out_ref[group, :, chan] = result[:, idx * LANES : (idx + 1) * LANES].reshape(blocks, rows, LANES)
+        out_ref[pl.ds(group * blocks, blocks), chan * rows : (chan + 1) * rows] = result[
+            :, idx * LANES : (idx + 1) * LANES
+        ].reshape(blocks, rows, LANES)
 
 
 def gate_kernel(rows, conv_ref, query_ref, key_ref, value_ref, bias_ref, out_ref):
@@ -134,15 +164,16 @@
 
 
 VMEM = pl.BlockSpec(memory_space=pltpu.VMEM)
+HBM = pl.BlockSpec(memory_space=pltpu.HBM)
 SMEM = pl.BlockSpec(memory_space=pltpu.SMEM)
 
 
-def call(kernel, shape, dtype, specs, flops, moved, scratch=()):
+def call(kernel, outs, specs, flops, moved, scratch=()):
     return pl.pallas_call(
         kernel,
-        out_shape=jax.ShapeDtypeStruct(shape, dtype),
+        out_shape=[jax.ShapeDtypeStruct(*out) for out in outs],
         in_specs=specs,
-        out_specs=VMEM,
+        out_specs=[VMEM] * len(outs),
         scratch_shapes=scratch,
         compiler_params=pltpu.CompilerParams(vmem_limit_bytes=VMEM_LIMIT),
         cost_estimate=pl.CostEstimate(flops=flops, bytes_accessed=moved, transcendentals=0),
@@ -152,29 +183,38 @@
 def shards(groups, blocks, query_proj, key_proj, value_proj, long_filter, skip_bias):
     tokens, chans = key_proj.shape
     rows = tokens // LANES
-    own = chans // (groups * blocks)
+    count, axes = groups * blocks, ("groups", "seq")
+    own = chans // count
     outer = blocks * rows
     seq_len = blocks * tokens
-    tables = make_tables(seq_len)
-    head, twist, tail, back_tail, back_head = (jnp.asarray(table) for table in tables)
+    part = rows // groups
+    if rows % groups or own * part % 8:
+        part = rows
+    layout = (rows, own, part, groups)
+    head, twist, tail, back_tail, back_head = (jnp.asarray(table) for table in make_tables(seq_len))
     size = tokens * chans * 4
-
-    share = own // groups if own % groups == 0 else own
-    packed = call(
-        functools.partial(pack_kernel, rows, own, share),
-        (groups * blocks, (own + share) * rows, LANES), F32, [SMEM, VMEM, VMEM, VMEM], size // 4, size * 4,
-        [pltpu.VMEM((2, chans * rows, LANES), F32)],
-    )(lax.axis_index("groups").reshape(1).astype(jnp.int32), key_proj, value_proj, long_filter)
-    moved = lax.all_to_all(packed, ("groups", "seq"), 0, 0, tiled=True)
     macs = 2 * 3 * own * seq_len * (2 * outer + 4 * LANES)
+    where = lax.axis_index("groups").reshape(1).astype(jnp.int32)
+
+    def exchange(array):
+        return lax.all_to_all(array, axes, 0, 0, tiled=True)
+
+    sources = (key_proj, value_proj, long_filter, skip_bias.reshape(1, chans))
+    packed, bias = call(
+        functools.partial(pack_kernel, layout),
+        [((count, own * (rows + part), LANES), F32), ((1, chans), F32)],
+        [SMEM] + [HBM] * 4, size // 4, size * 3,
+        [pltpu.VMEM((tokens, chans), BF16), pltpu.VMEM((tokens, chans), BF16), pltpu.VMEM((part * LANES, chans), F32),
+         pltpu.SemaphoreType.DMA((4,))],
+    )(where, *(pltpu.with_memory_space_constraint(source, pltpu.HBM) for source in sources))
     local = call(
-        functools.partial(conv_kernel, rows, own, share),
-        (groups, blocks, own, rows, LANES), F32, [VMEM] * 6, 5 * macs, 3 * size,
-    )(moved.reshape(groups, blocks, (own + share) * rows, LANES), head, twist, tail, back_tail, back_head)
-    convolved = lax.all_to_all(local.reshape(chans * rows, LANES), ("groups", "seq"), 0, 0, tiled=True)
-    return call(functools.partial(gate_kernel, rows), (tokens, chans), BF16, [VMEM] * 5, size, 3 * size)(
-        convolved, query_proj, key_proj, value_proj, skip_bias.reshape(1, chans)
-    )
+        functools.partial(conv_kernel, layout),
+        [((count, own * rows, LANES), F32)], [VMEM] * 6, 5 * macs, 3 * size,
+    )(exchange(packed), head, twist, tail, back_tail, back_head)[0]
+    convolved = exchange(local).reshape(chans * rows, LANES)
+    return call(functools.partial(gate_kernel, rows), [((tokens, chans), BF16)], [VMEM] * 5, size, 3 * size)(
+        convolved, query_proj, key_proj, value_proj, bias
+    )[0]
 
 
 def solution(mesh):

time: 55.5 us -> 52.8 us (0.951)
  local copies, waits for them, and re-layouts: 3.64 us -> 0.05 us
  Pallas kernels: 4.07 us -> 5.11 us
    unnamed x24 -> x16, local copies, waits for them, and re-layouts: 3.64 us -> 0.05 us
    pallas_call x3, Pallas kernels: 4.07 us -> 5.11 us  [the longest x1 2.78 us: shards(): call(functools.partial(conv_kernel, layout), [((count, own * rows, LANES)...]
where the time goes in v6:
time: 52.8 us; the launch traced here: 52.6 us
  blocking collectives  47.3 us (90%)
  Pallas kernels  5.11 us (10%)
    all_to_all x2, blocking collectives, exchange(): return lax.all_to_all(array, axes, 0, 0, tiled=True)  47.3 us
    pallas_call x1, Pallas kernels, shards(): call(functools.partial(conv_kernel, layout), [((count, own * rows, LANES)...  2.78 us
    pallas_call x1, Pallas kernels, shards(): call(functools.partial(pack_kernel, layout), [((count, own * (rows + part...  1.4 us

profile of v6, /device:TPU:0, one launch (start us, length us, event | category | flops | bytes accessed | tf_op | source)
XLA Modules:
  0.0 52.6 jit_solution(7594207831656994043)
XLA Ops:
  0.0 1.4 %shard_map.100 = (f32[16,96,128]{2,1,0:T(8,128)S(1)}, f32[1,128]{1,0:T(1,128)S(1)}) custom-call(s32[1]{0:T(128)} %bitcast.where_ref, bf16[1024,128]{1,0:T(8,128)(2,1)} %key_ref.3, bf16[1024,128]{1,0:T(8,128)(2,1)} %value_ref.3, f32[1024,128]{1,0:T(8,128)} %filter_ref.1, f32[1,128]{1,0:T(1,128)} %bitcast.4), custom_call_target="tpu_custom_call" | custom-call | flops 131072 | bytes 1572864 | tf_op jit(solution)/shard_map/pallas_call | solution.py:203
  1.4 0.0 copy-start.3
  1.4 0.0 copy-start.4
  1.4 0.0 copy-start.5
  1.5 0.0 copy-start.6
  1.5 0.0 copy-start.7
  1.5 29.5 %all_to_all.10.moved_ref = f32[16,96,128]{2,1,0:T(8,128)S(1)} all-to-all(f32[16,96,128]{2,1,0:T(8,128)S(1)} %get-tuple-element.7), channel_id=1, replica_groups=mesh['groups'=2,'seq'=8,'chan'=2] {'groups','seq'}, dimensions={0} | all-to-all | bytes 1572864 | tf_op jit(solution)/shard_map/all_to_all | solution.py:200
  31.0 0.0 copy-done.3
  31.0 0.0 copy-done.4
  31.0 0.0 copy-done.5
  31.0 0.0 copy-done.6
  31.0 0.0 copy-done.7
  31.0 2.8 %shard_map.101 = f32[16,64,128]{2,1,0:T(8,128)S(1)} custom-call(f32[16,96,128]{2,1,0:T(8,128)S(1)} %all_to_all.10.moved_ref, bf16[128,192]{1,0:T(8,128)(2,1)S(1)} %copy-done.6, f32[64,256]{1,0:T(8,128)S(1)} %copy-done.5, bf16[768,256]{1,0:T(8,128)(2,1)S(1)} %copy-done.4, bf16[768,256]{1,0:T(8,128)(2,1)S(1)} %copy-done.3, bf16[64,384]{1,0:T(8,128)(2,1)S(1)} %copy-done.7), custom_call_target="tpu_custom_call" | custom-call | flops 1258291200 | bytes 1572864 | tf_op jit(solution)/shard_map/pallas_call | solution.py:210
  33.8 0.0 copy-start
  33.8 0.0 copy-start.1
  33.8 0.0 copy-start.2
  33.8 17.8 %all_to_all.11 = f32[16,64,128]{2,1,0:T(8,128)S(1)} all-to-all(f32[16,64,128]{2,1,0:T(8,128)S(1)} %shard_map.101), channel_id=1, replica_groups=mesh['groups'=2,'seq'=8,'chan'=2] {'groups','seq'}, dimensions={0} | all-to-all | bytes 1048576 | tf_op jit(solution)/shard_map/all_to_all | solution.py:200
  51.7 0.0 copy-done
  51.7 0.0 copy-done.1
  51.7 0.0 copy-done.2
  51.7 0.9 %shard_map.102 = bf16[1024,128]{1,0:T(8,128)(2,1)} custom-call(f32[1024,128]{1,0:T(8,128)S(1)} %bitcast.3, bf16[1024,128]{1,0:T(8,128)(2,1)S(1)} %copy-done.2, bf16[1024,128]{1,0:T(8,128)(2,1)S(1)} %copy-done, bf16[1024,128]{1,0:T(8,128)(2,1)S(1)} %copy-done.1, f32[1,128]{1,0:T(1,128)S(1)} %get-tuple-element.8.bias_ref), custom_call_target="tpu_custom_call" | custom-call | flops 524288 | bytes 1572864 | tf_op jit(solution)/shard_map/pallas_call | solution.py:215
Async XLA Ops:
  1.4 29.6 %copy-start.3 = (bf16[768,256]{1,0:T(8,128)(2,1)S(1)}, bf16[768,256]{1,0:T(8,128)(2,1)}, u32[]{:S(2)}) copy-start(bf16[768,256]{1,0:T(8,128)(2,1)} %constant.19.clone.back_tail_ref) | copy-start | bytes 1179652
  1.4 29.6 %copy-start.4 = (bf16[768,256]{1,0:T(8,128)(2,1)S(1)}, bf16[768,256]{1,0:T(8,128)(2,1)}, u32[]{:S(2)}) copy-start(bf16[768,256]{1,0:T(8,128)(2,1)} %constant.18.clone.tail_ref) | copy-start | bytes 1179652
  1.4 29.6 %copy-start.5 = (f32[64,256]{1,0:T(8,128)S(1)}, f32[64,256]{1,0:T(8,128)}, u32[]{:S(2)}) copy-start(f32[64,256]{1,0:T(8,128)} %constant.17.clone.twist_ref) | copy-start | bytes 196612
  1.5 29.6 %copy-start.6 = (bf16[128,192]{1,0:T(8,128)(2,1)S(1)}, bf16[128,192]{1,0:T(8,128)(2,1)}, u32[]{:S(2)}) copy-start(bf16[128,192]{1,0:T(8,128)(2,1)} %constant.16.clone.head_ref) | copy-start | bytes 147460
  1.5 29.6 %copy-start.7 = (bf16[64,384]{1,0:T(8,128)(2,1)S(1)}, bf16[64,384]{1,0:T(8,128)(2,1)}, u32[]{:S(2)}) copy-start(bf16[64,384]{1,0:T(8,128)(2,1)} %constant.20.clone.back_head_ref) | copy-start | bytes 147460
  33.8 17.9 %copy-start = (bf16[1024,128]{1,0:T(8,128)(2,1)S(1)}, bf16[1024,128]{1,0:T(8,128)(2,1)}, u32[]{:S(2)}) copy-start(bf16[1024,128]{1,0:T(8,128)(2,1)} %key_ref.3) | copy-start | bytes 786436
  33.8 17.8 %copy-start.1 = (bf16[1024,128]{1,0:T(8,128)(2,1)S(1)}, bf16[1024,128]{1,0:T(8,128)(2,1)}, u32[]{:S(2)}) copy-start(bf16[1024,128]{1,0:T(8,128)(2,1)} %value_ref.3) | copy-start | bytes 786436
  33.8 17.8 %copy-start.2 = (bf16[1024,128]{1,0:T(8,128)(2,1)S(1)}, bf16[1024,128]{1,0:T(8,128)(2,1)}, u32[]{:S(2)}) copy-start(bf16[1024,128]{1,0:T(8,128)(2,1)} %query_ref.1) | copy-start | bytes 786436

commit v7 on v6

--- a/solution.py
+++ b/solution.py
@@ -40,7 +40,7 @@
     high, low = split_np(block(tail.conj()))
     back_tail_tab = np.concatenate([high, high, low], axis=0)
     high, low = split_np(np.concatenate([head.real, head.imag], axis=1))
-    back_head_tab = np.concatenate([high, high, low], axis=1)
+    back_head_tab = np.block([[high, high], [low, np.zeros_like(low)]])
     twist_tab = np.concatenate([twist.real, twist.imag], axis=1).astype(np.float32)
     return head_tab, twist_tab, tail_tab, back_tail_tab, back_head_tab
 
@@ -64,7 +64,7 @@
     return jnp.dot(left, right, preferred_element_type=F32)
 
 
-def forward(signals, head, twist, tail):
+def head_stage(signals, head, twist):
     outer = signals[0].shape[0]
     mixed = mat(head, by_rows(jnp.concatenate(signals, axis=1)))
     cos, sin = twist[:, :LANES], twist[:, LANES:]
@@ -73,7 +73,30 @@
         real = mixed[:outer, idx * LANES : (idx + 1) * LANES]
         imag = mixed[outer:, idx * LANES : (idx + 1) * LANES]
         rows.append(jnp.concatenate([real * cos - imag * sin, real * sin + imag * cos], axis=1))
-    return mat(by_lanes(jnp.concatenate(rows, axis=0)), tail)
+    return jnp.concatenate(rows, axis=0)
+
+
+def product_stage(spec, outer, groups):
+    pieces = [spec[idx * outer : (idx + 1) * outer] for idx in range(spec.shape[0] // outer)]
+    own = len(pieces) // (groups + 1)
+    prods = []
+    for idx, mine in enumerate(pieces[own:]):
+        other = pieces[idx // groups]
+        f_re, f_im = other[:, :LANES], other[:, LANES:]
+        d_re, d_im = mine[:, :LANES], mine[:, LANES:]
+        prods.append(jnp.concatenate([d_re * f_re - d_im * f_im, d_re * f_im + d_im * f_re], axis=1))
+    return jnp.concatenate(prods, axis=0)
+
+
+def back_stage(back, cos, sin):
+    outer = cos.shape[0]
+    reals, imags = [], []
+    for idx in range(back.shape[0] // outer):
+        mine = back[idx * outer : (idx + 1) * outer]
+        real, imag = mine[:, :LANES], mine[:, LANES:]
+        reals.append(real * cos + imag * sin)
+        imags.append(imag * cos - real * sin)
+    return jnp.concatenate([jnp.concatenate(reals, axis=1), jnp.concatenate(imags, axis=1)], axis=0)
 
 
 def pack_kernel(layout, where_ref, key_ref, value_ref, filter_ref, bias_ref, out_ref, bias_out, key, value, taps, sems):
@@ -99,21 +122,21 @@
     fetches[3].wait()
 
 
-def driver_signals(layout, moved_ref):
+def driver_signals(layout, moved_ref, chans):
     rows, own, part, groups = layout
     blocks = moved_ref.shape[0] // groups
     return [
         moved_ref[pl.ds(group * blocks, blocks), chan * rows : (chan + 1) * rows].reshape(blocks * rows, LANES)
-        for chan in range(own)
+        for chan in chans
         for group in range(groups)
     ]
 
 
-def filter_signals(layout, moved_ref):
+def filter_signals(layout, moved_ref, chans):
     rows, own, part, groups = layout
     blocks = moved_ref.shape[0] // groups
     signals = []
-    for chan in range(own):
+    for chan in chans:
         start = own * rows + chan * part
         pieces = [
             moved_ref[pl.ds(group * blocks, blocks), start : start + part]
@@ -123,35 +146,34 @@
     return signals
 
 
-def conv_kernel(layout, moved_ref, head_ref, twist_ref, tail_ref, back_tail_ref, back_head_ref, out_ref):
+def conv_kernel(layout, pieces, moved_ref, head_ref, twist_ref, tail_ref, back_tail_ref, back_head_ref, out_ref):
     rows, own, part, groups = layout
     blocks = moved_ref.shape[0] // groups
     outer = blocks * rows
     scale = 1.0 / (outer * LANES)
-    signals = filter_signals(layout, moved_ref) + driver_signals(layout, moved_ref)
-    spec = forward(signals, head_ref[...], twist_ref[...], tail_ref[...])
-    pieces = [spec[idx * outer : (idx + 1) * outer] for idx in range(len(signals))]
-    prods = []
-    for idx, mine in enumerate(pieces[own:]):
-        other = pieces[idx // groups]
-        f_re, f_im = other[:, :LANES], other[:, LANES:]
-        d_re, d_im = mine[:, :LANES], mine[:, LANES:]
-        prods.append(jnp.concatenate([d_re * f_re - d_im * f_im, d_re * f_im + d_im * f_re], axis=1))
-    back = mat(by_lanes(jnp.concatenate(prods, axis=0)), back_tail_ref[...])
     cos, sin = twist_ref[:, :LANES] * scale, twist_ref[:, LANES:] * scale
-    reals, imags = [], []
-    for idx in range(len(prods)):
-        mine = back[idx * outer : (idx + 1) * outer]
-        real, imag = mine[:, :LANES], mine[:, LANES:]
-        reals.append(real * cos + imag * sin)
-        imags.append(imag * cos - real * sin)
-    mixed = jnp.concatenate([jnp.concatenate(reals, axis=1), jnp.concatenate(imags, axis=1)], axis=0)
-    result = mat(back_head_ref[...], by_rows(mixed))
-    for idx in range(len(prods)):
-        chan, group = divmod(idx, groups)
-        out_ref[pl.ds(group * blocks, blocks), chan * rows : (chan + 1) * rows] = result[
-            :, idx * LANES : (idx + 1) * LANES
-        ].reshape(blocks, rows, LANES)
+    sets = [range(piece * own // pieces, (piece + 1) * own // pieces) for piece in range(pieces)]
+    mixed = [
+        head_stage(
+            filter_signals(layout, moved_ref, chans) + driver_signals(layout, moved_ref, chans),
+            head_ref[...],
+            twist_ref[...],
+        )
+        for chans in sets
+    ]
+    specs = [mat(by_lanes(values), tail_ref[...]) for values in mixed]
+    prods = [product_stage(spec, outer, groups) for spec in specs]
+    backs = [mat(by_lanes(values), back_tail_ref[...]) for values in prods]
+    turned = [back_stage(back, cos, sin) for back in backs]
+    results = [mat(back_head_ref[...], jnp.concatenate(halves(values), axis=0)) for values in turned]
+    for chans, result in zip(sets, results):
+        result = result[:outer] + result[outer:]
+        for idx in range(len(chans) * groups):
+            chan, group = divmod(idx, groups)
+            start = (chans[0] + chan) * rows
+            out_ref[pl.ds(group * blocks, blocks), start : start + rows] = result[
+                :, idx * LANES : (idx + 1) * LANES
+            ].reshape(blocks, rows, LANES)
 
 
 def gate_kernel(rows, conv_ref, query_ref, key_ref, value_ref, bias_ref, out_ref):
@@ -208,7 +230,7 @@
          pltpu.SemaphoreType.DMA((4,))],
     )(where, *(pltpu.with_memory_space_constraint(source, pltpu.HBM) for source in sources))
     local = call(
-        functools.partial(conv_kernel, layout),
+        functools.partial(conv_kernel, layout, min(own, 2)),
         [((count, own * rows, LANES), F32)], [VMEM] * 6, 5 * macs, 3 * size,
     )(exchange(packed), head, twist, tail, back_tail, back_head)[0]
     convolved = exchange(local).reshape(chans * rows, LANES)

time: 52.8 us -> 51.9 us (0.983)
  Pallas kernels: 5.11 us -> 4.15 us
    pallas_call x1, Pallas kernels: 2.78 us -> 1.83 us  [shards(): call(functools.partial(conv_kernel, layout, min(own, 2)), [((count, own *...]
where the time goes in v7:
time: 51.9 us; the launch traced here: 51.6 us
  blocking collectives  47.3 us (91%)
  Pallas kernels  4.15 us (8%)
    all_to_all x2, blocking collectives, exchange(): return lax.all_to_all(array, axes, 0, 0, tiled=True)  47.3 us
    pallas_call x1, Pallas kernels, shards(): call(functools.partial(conv_kernel, layout, min(own, 2)), [((count, own *...  1.83 us
    pallas_call x1, Pallas kernels, shards(): call(functools.partial(pack_kernel, layout), [((count, own * (rows + part...  1.4 us

profile of v7, /device:TPU:0, one launch (start us, length us, event | category | flops | bytes accessed | tf_op | source)
XLA Modules:
  0.0 51.6 jit_solution(2891899790237257983)
XLA Ops:
  0.0 1.4 %shard_map.100 = (f32[16,96,128]{2,1,0:T(8,128)S(1)}, f32[1,128]{1,0:T(1,128)S(1)}) custom-call(s32[1]{0:T(128)} %bitcast.where_ref, bf16[1024,128]{1,0:T(8,128)(2,1)} %key_ref.3, bf16[1024,128]{1,0:T(8,128)(2,1)} %value_ref.3, f32[1024,128]{1,0:T(8,128)} %filter_ref.1, f32[1,128]{1,0:T(1,128)} %bitcast.4), custom_call_target="tpu_custom_call" | custom-call | flops 131072 | bytes 1572864 | tf_op jit(solution)/shard_map/pallas_call | solution.py:225
  1.4 0.0 copy-start.3
  1.4 0.0 copy-start.4
  1.4 0.0 copy-start.5
  1.5 0.0 copy-start.6
  1.5 0.0 copy-start.7
  1.5 29.5 %all_to_all.10.moved_ref = f32[16,96,128]{2,1,0:T(8,128)S(1)} all-to-all(f32[16,96,128]{2,1,0:T(8,128)S(1)} %get-tuple-element.7), channel_id=1, replica_groups=mesh['groups'=2,'seq'=8,'chan'=2] {'groups','seq'}, dimensions={0} | all-to-all | bytes 1572864 | tf_op jit(solution)/shard_map/all_to_all | solution.py:222
  31.0 0.0 copy-done.3
  31.0 0.0 copy-done.4
  31.0 0.0 copy-done.5
  31.0 0.0 copy-done.6
  31.0 0.0 copy-done.7
  31.0 1.8 %shard_map.101 = f32[16,64,128]{2,1,0:T(8,128)S(1)} custom-call(f32[16,96,128]{2,1,0:T(8,128)S(1)} %all_to_all.10.moved_ref, bf16[128,192]{1,0:T(8,128)(2,1)S(1)} %copy-done.7, f32[64,256]{1,0:T(8,128)S(1)} %copy-done.6, bf16[768,256]{1,0:T(8,128)(2,1)S(1)} %copy-done.4, bf16[768,256]{1,0:T(8,128)(2,1)S(1)} %copy-done.3, bf16[128,256]{1,0:T(8,128)(2,1)S(1)} %copy-done.5), custom_call_target="tpu_custom_call" | custom-call | flops 1258291200 | bytes 1572864 | tf_op jit(solution)/shard_map/pallas_call | solution.py:232
  32.9 0.0 copy-start
  32.9 0.0 copy-start.1
  32.9 0.0 copy-start.2
  32.9 17.8 %all_to_all.11 = f32[16,64,128]{2,1,0:T(8,128)S(1)} all-to-all(f32[16,64,128]{2,1,0:T(8,128)S(1)} %shard_map.101), channel_id=1, replica_groups=mesh['groups'=2,'seq'=8,'chan'=2] {'groups','seq'}, dimensions={0} | all-to-all | bytes 1048576 | tf_op jit(solution)/shard_map/all_to_all | solution.py:222
  50.7 0.0 copy-done
  50.7 0.0 copy-done.1
  50.7 0.0 copy-done.2
  50.7 0.9 %shard_map.102 = bf16[1024,128]{1,0:T(8,128)(2,1)} custom-call(f32[1024,128]{1,0:T(8,128)S(1)} %bitcast.3, bf16[1024,128]{1,0:T(8,128)(2,1)S(1)} %copy-done.2, bf16[1024,128]{1,0:T(8,128)(2,1)S(1)} %copy-done, bf16[1024,128]{1,0:T(8,128)(2,1)S(1)} %copy-done.1, f32[1,128]{1,0:T(1,128)S(1)} %get-tuple-element.8.bias_ref), custom_call_target="tpu_custom_call" | custom-call | flops 524288 | bytes 1572864 | tf_op jit(solution)/shard_map/pallas_call | solution.py:237
Async XLA Ops:
  1.4 29.6 %copy-start.3 = (bf16[768,256]{1,0:T(8,128)(2,1)S(1)}, bf16[768,256]{1,0:T(8,128)(2,1)}, u32[]{:S(2)}) copy-start(bf16[768,256]{1,0:T(8,128)(2,1)} %constant.19.clone.back_tail_ref) | copy-start | bytes 1179652
  1.4 29.6 %copy-start.4 = (bf16[768,256]{1,0:T(8,128)(2,1)S(1)}, bf16[768,256]{1,0:T(8,128)(2,1)}, u32[]{:S(2)}) copy-start(bf16[768,256]{1,0:T(8,128)(2,1)} %constant.18.clone.tail_ref) | copy-start | bytes 1179652
  1.4 29.6 %copy-start.5 = (bf16[128,256]{1,0:T(8,128)(2,1)S(1)}, bf16[128,256]{1,0:T(8,128)(2,1)}, u32[]{:S(2)}) copy-start(bf16[128,256]{1,0:T(8,128)(2,1)} %constant.20.clone.back_head_ref) | copy-start | bytes 196612
  1.5 29.6 %copy-start.6 = (f32[64,256]{1,0:T(8,128)S(1)}, f32[64,256]{1,0:T(8,128)}, u32[]{:S(2)}) copy-start(f32[64,256]{1,0:T(8,128)} %constant.17.clone.twist_ref) | copy-start | bytes 196612
  1.5 29.6 %copy-start.7 = (bf16[128,192]{1,0:T(8,128)(2,1)S(1)}, bf16[128,192]{1,0:T(8,128)(2,1)}, u32[]{:S(2)}) copy-start(bf16[128,192]{1,0:T(8,128)(2,1)} %constant.16.clone.head_ref) | copy-start | bytes 147460
  32.9 17.9 %copy-start = (bf16[1024,128]{1,0:T(8,128)(2,1)S(1)}, bf16[1024,128]{1,0:T(8,128)(2,1)}, u32[]{:S(2)}) copy-start(bf16[1024,128]{1,0:T(8,128)(2,1)} %key_ref.3) | copy-start | bytes 786436
  32.9 17.8 %copy-start.1 = (bf16[1024,128]{1,0:T(8,128)(2,1)S(1)}, bf16[1024,128]{1,0:T(8,128)(2,1)}, u32[]{:S(2)}) copy-start(bf16[1024,128]{1,0:T(8,128)(2,1)} %value_ref.3) | copy-start | bytes 786436
  32.9 17.8 %copy-start.2 = (bf16[1024,128]{1,0:T(8,128)(2,1)S(1)}, bf16[1024,128]{1,0:T(8,128)(2,1)}, u32[]{:S(2)}) copy-start(bf16[1024,128]{1,0:T(8,128)(2,1)} %query_ref.1) | copy-start | bytes 786436

commit v8 on v7

--- a/solution.py
+++ b/solution.py
@@ -122,40 +122,45 @@
     fetches[3].wait()
 
 
-def driver_signals(layout, moved_ref, chans):
-    rows, own, part, groups = layout
+def arrived(layout, staged, moved_ref, group, start, height):
+    rows, own, part, groups = layout
+    if staged:
+        start += group * own * (rows + part)
+        return moved_ref[:, start : start + height]
     blocks = moved_ref.shape[0] // groups
-    return [
-        moved_ref[pl.ds(group * blocks, blocks), chan * rows : (chan + 1) * rows].reshape(blocks * rows, LANES)
-        for chan in chans
-        for group in range(groups)
+    return moved_ref[pl.ds(group * blocks, blocks), start : start + height]
+
+
+def driver_signals(layout, staged, moved_ref, chans):
+    rows, own, part, groups = layout
+    parts = [
+        arrived(layout, staged, moved_ref, group, chan * rows, rows) for chan in chans for group in range(groups)
     ]
-
-
-def filter_signals(layout, moved_ref, chans):
-    rows, own, part, groups = layout
-    blocks = moved_ref.shape[0] // groups
+    return [values.reshape(values.shape[0] * rows, LANES) for values in parts]
+
+
+def filter_signals(layout, staged, moved_ref, chans):
+    rows, own, part, groups = layout
     signals = []
     for chan in chans:
-        start = own * rows + chan * part
         pieces = [
-            moved_ref[pl.ds(group * blocks, blocks), start : start + part]
+            arrived(layout, staged, moved_ref, group, own * rows + chan * part, part)
             for group in range(groups if part < rows else 1)
         ]
-        signals.append(jnp.concatenate(pieces, axis=1).reshape(blocks * rows, LANES))
+        signals.append(jnp.concatenate(pieces, axis=1).reshape(pieces[0].shape[0] * rows, LANES))
     return signals
 
 
-def conv_kernel(layout, pieces, moved_ref, head_ref, twist_ref, tail_ref, back_tail_ref, back_head_ref, out_ref):
-    rows, own, part, groups = layout
-    blocks = moved_ref.shape[0] // groups
+def conv_kernel(layout, staged, pieces, moved_ref, head_ref, twist_ref, tail_ref, back_tail_ref, back_head_ref, out_ref):
+    rows, own, part, groups = layout
+    blocks = out_ref.shape[0] // groups
     outer = blocks * rows
     scale = 1.0 / (outer * LANES)
     cos, sin = twist_ref[:, :LANES] * scale, twist_ref[:, LANES:] * scale
     sets = [range(piece * own // pieces, (piece + 1) * own // pieces) for piece in range(pieces)]
     mixed = [
         head_stage(
-            filter_signals(layout, moved_ref, chans) + driver_signals(layout, moved_ref, chans),
+            filter_signals(layout, staged, moved_ref, chans) + driver_signals(layout, staged, moved_ref, chans),
             head_ref[...],
             twist_ref[...],
         )
@@ -202,7 +207,7 @@
     )
 
 
-def shards(groups, blocks, query_proj, key_proj, value_proj, long_filter, skip_bias):
+def convolve(groups, blocks, staged, query_proj, key_proj, value_proj, long_filter, skip_bias):
     tokens, chans = key_proj.shape
     rows = tokens // LANES
     count, axes = groups * blocks, ("groups", "seq")
@@ -229,14 +234,36 @@
         [pltpu.VMEM((tokens, chans), BF16), pltpu.VMEM((tokens, chans), BF16), pltpu.VMEM((part * LANES, chans), F32),
          pltpu.SemaphoreType.DMA((4,))],
     )(where, *(pltpu.with_memory_space_constraint(source, pltpu.HBM) for source in sources))
+    if staged:
+        mine = lax.axis_index("groups")
+        height = own * (rows + part)
+        by_group = packed.reshape(2, blocks, height, LANES)
+        first = mine == 0
+        kept = jnp.where(first, by_group[0], by_group[1])
+        other = lax.ppermute(jnp.where(first, by_group[1], by_group[0]), "groups", [(0, 1), (1, 0)])
+        pair = jnp.concatenate([jnp.where(first, kept, other), jnp.where(first, other, kept)], axis=1)
+        moved = lax.all_to_all(pair, "seq", 0, 0, tiled=True)
+    else:
+        moved = exchange(packed)
     local = call(
-        functools.partial(conv_kernel, layout, min(own, 2)),
+        functools.partial(conv_kernel, layout, staged, min(own, 2)),
         [((count, own * rows, LANES), F32)], [VMEM] * 6, 5 * macs, 3 * size,
-    )(exchange(packed), head, twist, tail, back_tail, back_head)[0]
+    )(moved, head, twist, tail, back_tail, back_head)[0]
     convolved = exchange(local).reshape(chans * rows, LANES)
     return call(functools.partial(gate_kernel, rows), [((tokens, chans), BF16)], [VMEM] * 5, size, 3 * size)(
         convolved, query_proj, key_proj, value_proj, bias
     )[0]
+
+
+def shards(groups, blocks, cores, *args):
+    if cores == 1 or groups != 2:
+        return convolve(groups, blocks, False, *args)
+    return lax.cond(
+        lax.axis_index("chan") % 2 == 1,
+        functools.partial(convolve, groups, blocks, False),
+        functools.partial(convolve, groups, blocks, True),
+        *args,
+    )
 
 
 def solution(mesh):
@@ -247,7 +274,7 @@
         P("seq", "chan"),
         P("chan"),
     )
-    body = functools.partial(shards, mesh.shape["groups"], mesh.shape["seq"])
+    body = functools.partial(shards, *(mesh.shape[axis] for axis in ("groups", "seq", "chan")))
     return jax.shard_map(
         body, mesh=mesh, in_specs=placed, out_specs=P(("groups", "seq"), "chan"), check_vma=False
     )

time: 51.9 us -> 48.6 us (0.936)
  blocking collectives: 47.3 us -> 35.1 us
  waiting for transfers between devices: 0 us -> 5.76 us
  starting transfers between devices: 0 us -> 3 us
  Pallas kernels: 4.15 us -> 3.4 us
  local copies, waits for them, and re-layouts: 0.05 us -> 0.75 us
    all_to_all x2 -> x1, blocking collectives: 47.3 us -> 15.7 us  [exchange(): return lax.all_to_all(array, axes, 0, 0, tiled=True)]
    all_to_all x0 -> x1, blocking collectives: none -> 19.4 us  [convolve(): moved = lax.all_to_all(pair, 'seq', 0, 0, tiled=True)]
    ppermute x0 -> x1, waiting for transfers between devices: none -> 5.76 us  [convolve(): lax.ppermute(jnp.where(first, by_group[1], by_group[0]), 'groups', [(0, 1...]
    ppermute x0 -> x1, starting transfers between devices: none -> 3 us  [convolve(): lax.ppermute(jnp.where(first, by_group[1], by_group[0]), 'groups', [(0, 1...]
    pallas_call x3, Pallas kernels: 4.15 us -> 3.4 us  [the longest x1 1.79 us: convolve(): call(functools.partial(conv_kernel, layout, staged, min(own, 2)), [((coun...]
    unnamed x16 -> x2, local copies, waits for them, and re-layouts: 0.05 us -> 0.7 us
  transfers between devices with their start and end apart: 0 -> 1, of which waited for: 0 -> 1; matrix products, arithmetic and copies ran while one was open for 0% -> 0% of each run, Pallas kernels for 0% -> 0%
where the time goes in v8:
time: 48.6 us; the launch traced here: 48.3 us
  blocking collectives  35.1 us (72%)
  waiting for transfers between devices  5.76 us (12%)
  Pallas kernels  3.4 us (7%)
  starting transfers between devices  3 us (6%)
  local copies, waits for them, and re-layouts  0.75 us (2%)
    all_to_all x1, blocking collectives, convolve(): moved = lax.all_to_all(pair, 'seq', 0, 0, tiled=True)  19.4 us
    all_to_all x1, blocking collectives, exchange(): return lax.all_to_all(array, axes, 0, 0, tiled=True)  15.7 us
    ppermute x1, waiting for transfers between devices, convolve(): lax.ppermute(jnp.where(first, by_group[1], by_group[0]), 'groups', [(0, 1...  5.76 us
    ppermute x1, starting transfers between devices, convolve(): lax.ppermute(jnp.where(first, by_group[1], by_group[0]), 'groups', [(0, 1...  3 us
    pallas_call x1, Pallas kernels, convolve(): call(functools.partial(conv_kernel, layout, staged, min(own, 2)), [((coun...  1.79 us
    pallas_call x1, Pallas kernels, convolve(): call(functools.partial(pack_kernel, layout), [((count, own * (rows + part...  1.4 us
  transfers between devices with their start and end apart: 1, of which 1 were waited for; matrix products, arithmetic and copies ran while one was open for 0% of the time, Pallas kernels for 0%

profile of v8, /device:TPU:0, one launch (start us, length us, event | category | flops | bytes accessed | tf_op | source)
XLA Modules:
  0.0 48.3 jit_solution(16420021696393736839)
XLA Ops:
  0.0 47.6 %conditional.1 = (bf16[1024,128]{1,0:T(8,128)(2,1)S(1)}) conditional(s32[]{:T(128)} %convert_element_type.3, (f32[128]{0:T(128)}, bf16[1024,128]{1,0:T(8,128)(2,1)}, bf16[1024,128]{1,0:T(8,128)(2,1)}, f32[1024,128]{1,0:T(8,128)}, bf16[128,192]{1,0:T(8,128)(2,1)}, /*index=5*/f32[64,256]{1,0:T(8,128)}, bf16[768,256]{1,0:T(8,128)(2,1)}, ...), branch_computations={%region_0.1_spmd, %region_1.2_spmd} | conditional | flops 1259536384 | bytes 20644156 | solution.py:261
  0.0 1.4 %branch_0_fun.3 = (f32[16,96,128]{2,1,0:T(8,128)S(1)}, f32[1,128]{1,0:T(1,128)S(1)}) custom-call(s32[1]{0:T(128)} %bitcast.where_ref, bf16[1024,128]{1,0:T(8,128)(2,1)} %get-tuple-element.48.key_ref, bf16[1024,128]{1,0:T(8,128)(2,1)} %get-tuple-element.49.value_ref, f32[1024,128]{1,0:T(8,128)} %get-tuple-element.50.filter_ref, f32[1,128]{1,0:T(1,128)} %bitcast.8), custom_call_target="tpu_custom_call" | custom-call | flops 131072 | bytes 1572864 | tf_op jit(solution)/shard_map/cond/branch_0_fun/pallas_call | solution.py:230
  1.5 3.0 %collective-permute-start = (f32[8,96,128]{2,1,0:T(8,128)S(1)}, f32[8,96,128]{2,1,0:T(8,128)S(1)}, u32[]{:S(2)}, u32[]{:S(2)}) collective-permute-start(f32[8,96,128]{2,1,0:T(8,128)S(1)} %slice_select_fusion), channel_id=1, source_target_pairs={{0,16},{16,0},{1,17},{17,1},{2,18},{18,2},{3,19},{19,3},{4,20},{20... | collective-permute-start | bytes 1179656 | tf_op jit(solution)/shard_map/cond/branch_0_fun/ppermute | solution.py:243
  4.5 5.8 %collective-permute-done = f32[8,96,128]{2,1,0:T(8,128)S(1)} collective-permute-done((f32[8,96,128]{2,1,0:T(8,128)S(1)}, f32[8,96,128]{2,1,0:T(8,128)S(1)}, u32[]{:S(2)}, u32[]{:S(2)}) %collective-permute-start) | collective-permute-done | bytes 393248 | tf_op jit(solution)/shard_map/cond/branch_0_fun/ppermute | solution.py:243
  10.2 0.1 broadcast_select_fusion.1
  10.3 0.1 pad_maximum_fusion
  10.4 0.0 copy-start.7
  10.4 0.0 copy-start.9
  10.4 0.0 copy-start.11
  10.4 0.0 copy-start.13
  10.4 0.0 copy-start.15
  10.4 19.4 %all_to_all.16.moved_ref = f32[8,192,128]{2,1,0:T(8,128)S(1)} all-to-all(f32[8,192,128]{2,1,0:T(8,128)S(1)} %pad_maximum_fusion), channel_id=1, replica_groups=mesh['groups'=2,'seq'=8,'chan'=2] {'seq'}, dimensions={0} | all-to-all | bytes 1572864 | tf_op jit(solution)/shard_map/cond/branch_0_fun/all_to_all | solution.py:245
  29.9 0.0 copy-done.7
  29.9 0.0 copy-done.9
  29.9 0.0 copy-done.11
  29.9 0.0 copy-done.13
  29.9 0.0 copy-done.15
  29.9 1.8 %branch_0_fun.4 = f32[16,64,128]{2,1,0:T(8,128)S(1)} custom-call(f32[8,192,128]{2,1,0:T(8,128)S(1)} %all_to_all.16.moved_ref, bf16[128,192]{1,0:T(8,128)(2,1)S(1)} %copy-done.15, f32[64,256]{1,0:T(8,128)S(1)} %copy-done.13, bf16[768,256]{1,0:T(8,128)(2,1)S(1)} %copy-done.9, bf16[768,256]{1,0:T(8,128)(2,1)S(1)} %copy-done.7, bf16[128,256]{1,0:T(8,128)(2,1)S(1)} %copy-done.11), custom_call_target="tpu_custom_call" | custom-call | flops 1258291200 | bytes 1572864 | tf_op jit(solution)/shard_map/cond/branch_0_fun/pallas_call | solution.py:248
  31.7 0.0 copy-start
  31.7 0.0 copy-start.2
  31.7 0.0 copy-start.4
  31.7 15.7 %all_to_all.17 = f32[16,64,128]{2,1,0:T(8,128)S(1)} all-to-all(f32[16,64,128]{2,1,0:T(8,128)S(1)} %branch_0_fun.4), channel_id=1, replica_groups=mesh['groups'=2,'seq'=8,'chan'=2] {'groups','seq'}, dimensions={0} | all-to-all | bytes 1048576 | tf_op jit(solution)/shard_map/cond/branch_0_fun/all_to_all | solution.py:227
  47.4 0.0 copy-done
  47.4 0.0 copy-done.2
  47.4 0.0 copy-done.4
  47.4 0.2 branch_0_fun.5
  47.6 0.0 copy-start.6
  47.7 0.7 %copy-done.6 = bf16[1024,128]{1,0:T(8,128)(2,1)} copy-done((bf16[1024,128]{1,0:T(8,128)(2,1)}, bf16[1024,128]{1,0:T(8,128)(2,1)S(1)}, u32[]{:S(2)}) %copy-start.6) | copy-done | bytes 262168
  (1 shorter events, 0.0 us)
Async XLA Ops:
  1.5 8.8 %collective-permute-start = (f32[8,96,128]{2,1,0:T(8,128)S(1)}, f32[8,96,128]{2,1,0:T(8,128)S(1)}, u32[]{:S(2)}, u32[]{:S(2)}) collective-permute-start(f32[8,96,128]{2,1,0:T(8,128)S(1)} %slice_select_fusion), channel_id=1, source_target_pairs={{0,16},{16,0},{1,17},{17,1},{2,18},{18,2},{3,19},{19,3},{4,20},{20... | collective-permute-start | bytes 1179656 | tf_op jit(solution)/shard_map/cond/branch_0_fun/ppermute | solution.py:243
  10.4 19.5 %copy-start.7 = (bf16[768,256]{1,0:T(8,128)(2,1)S(1)}, bf16[768,256]{1,0:T(8,128)(2,1)}, u32[]{:S(2)}) copy-start(bf16[768,256]{1,0:T(8,128)(2,1)} %get-tuple-element.56.back_tail_ref) | copy-start | bytes 1179652 | tf_op jit(solution)/shard_map/cond
  10.4 19.5 %copy-start.9 = (bf16[768,256]{1,0:T(8,128)(2,1)S(1)}, bf16[768,256]{1,0:T(8,128)(2,1)}, u32[]{:S(2)}) copy-start(bf16[768,256]{1,0:T(8,128)(2,1)} %get-tuple-element.55.tail_ref) | copy-start | bytes 1179652 | tf_op jit(solution)/shard_map/cond
  10.4 19.5 %copy-start.11 = (bf16[128,256]{1,0:T(8,128)(2,1)S(1)}, bf16[128,256]{1,0:T(8,128)(2,1)}, u32[]{:S(2)}) copy-start(bf16[128,256]{1,0:T(8,128)(2,1)} %get-tuple-element.57.back_head_ref) | copy-start | bytes 196612 | tf_op jit(solution)/shard_map/cond
  10.4 19.5 %copy-start.13 = (f32[64,256]{1,0:T(8,128)S(1)}, f32[64,256]{1,0:T(8,128)}, u32[]{:S(2)}) copy-start(f32[64,256]{1,0:T(8,128)} %get-tuple-element.54.twist_ref) | copy-start | bytes 196612 | tf_op jit(solution)/shard_map/cond
  10.4 19.5 %copy-start.15 = (bf16[128,192]{1,0:T(8,128)(2,1)S(1)}, bf16[128,192]{1,0:T(8,128)(2,1)}, u32[]{:S(2)}) copy-start(bf16[128,192]{1,0:T(8,128)(2,1)} %get-tuple-element.53.head_ref) | copy-start | bytes 147460 | tf_op jit(solution)/shard_map/cond
  31.7 15.7 %copy-start = (bf16[1024,128]{1,0:T(8,128)(2,1)S(1)}, bf16[1024,128]{1,0:T(8,128)(2,1)}, u32[]{:S(2)}) copy-start(bf16[1024,128]{1,0:T(8,128)(2,1)} %get-tuple-element.48.key_ref) | copy-start | bytes 786436 | tf_op jit(solution)/shard_map/cond
  31.7 15.7 %copy-start.2 = (bf16[1024,128]{1,0:T(8,128)(2,1)S(1)}, bf16[1024,128]{1,0:T(8,128)(2,1)}, u32[]{:S(2)}) copy-start(bf16[1024,128]{1,0:T(8,128)(2,1)} %get-tuple-element.49.value_ref) | copy-start | bytes 786436 | tf_op jit(solution)/shard_map/cond
  31.7 15.7 %copy-start.4 = (bf16[1024,128]{1,0:T(8,128)(2,1)S(1)}, bf16[1024,128]{1,0:T(8,128)(2,1)}, u32[]{:S(2)}) copy-start(bf16[1024,128]{1,0:T(8,128)(2,1)} %get-tuple-element.58.query_ref) | copy-start | bytes 786436 | tf_op jit(solution)/shard_map/cond
  47.6 0.7 %copy-start.6 = (bf16[1024,128]{1,0:T(8,128)(2,1)}, bf16[1024,128]{1,0:T(8,128)(2,1)S(1)}, u32[]{:S(2)}) copy-start(bf16[1024,128]{1,0:T(8,128)(2,1)S(1)} %get-tuple-element.79) | copy-start | bytes 786436

commit v9 on v8

--- a/solution.py
+++ b/solution.py
@@ -99,8 +99,12 @@
     return jnp.concatenate([jnp.concatenate(reals, axis=1), jnp.concatenate(imags, axis=1)], axis=0)
 
 
-def pack_kernel(layout, where_ref, key_ref, value_ref, filter_ref, bias_ref, out_ref, bias_out, key, value, taps, sems):
-    rows, own, part, groups = layout
+def pack_kernel(layout, staged, where_ref, key_ref, value_ref, filter_ref, bias_ref, *refs):
+    rows, own, part, groups = layout
+    refs = list(refs)
+    out_ref = refs.pop(0)
+    filter_out = refs.pop(0) if staged else None
+    bias_out, key, value, taps, turned_ref, sems = refs
     first = where_ref[0] * (part * LANES if part < rows else 0)
     taken = filter_ref.at[pl.ds(pl.multiple_of(first, part * LANES), part * LANES)]
     pairs = ((key_ref, key), (value_ref, value), (taken, taps), (bias_ref, bias_out))
@@ -117,15 +121,21 @@
     fetches[2].wait()
     for row in range(part):
         turned = taps[pl.ds(row * LANES, LANES), :].T
-        for peer in range(out_ref.shape[0]):
-            out_ref[peer, pl.ds(own * rows + row, own, stride=part), :] = turned[peer * own : (peer + 1) * own]
+        if staged:
+            turned_ref[row] = turned
+            for peer in range(filter_out.shape[0]):
+                start = pl.multiple_of((where_ref[0] * filter_out.shape[0] + peer) * own, own)
+                filter_out[peer, pl.ds(row, own, stride=part), :] = turned_ref[row, pl.ds(start, own), :]
+        else:
+            for peer in range(out_ref.shape[0]):
+                out_ref[peer, pl.ds(own * rows + row, own, stride=part), :] = turned[peer * own : (peer + 1) * own]
     fetches[3].wait()
 
 
 def arrived(layout, staged, moved_ref, group, start, height):
     rows, own, part, groups = layout
     if staged:
-        start += group * own * (rows + part)
+        start += group * own * rows
         return moved_ref[:, start : start + height]
     blocks = moved_ref.shape[0] // groups
     return moved_ref[pl.ds(group * blocks, blocks), start : start + height]
@@ -141,10 +151,11 @@
 
 def filter_signals(layout, staged, moved_ref, chans):
     rows, own, part, groups = layout
+    first = own * rows * (groups if staged else 1)
     signals = []
     for chan in chans:
         pieces = [
-            arrived(layout, staged, moved_ref, group, own * rows + chan * part, part)
+            arrived(layout, staged, moved_ref, group, first + chan * part, part)
             for group in range(groups if part < rows else 1)
         ]
         signals.append(jnp.concatenate(pieces, axis=1).reshape(pieces[0].shape[0] * rows, LANES))
@@ -215,7 +226,7 @@
     outer = blocks * rows
     seq_len = blocks * tokens
     part = rows // groups
-    if rows % groups or own * part % 8:
+    if staged or rows % groups or own * part % 8:
         part = rows
     layout = (rows, own, part, groups)
     head, twist, tail, back_tail, back_head = (jnp.asarray(table) for table in make_tables(seq_len))
@@ -227,21 +238,24 @@
         return lax.all_to_all(array, axes, 0, 0, tiled=True)
 
     sources = (key_proj, value_proj, long_filter, skip_bias.reshape(1, chans))
-    packed, bias = call(
-        functools.partial(pack_kernel, layout),
-        [((count, own * (rows + part), LANES), F32), ((1, chans), F32)],
+    if staged:
+        outs = [((count, own * rows, LANES), F32), ((blocks, own * rows, LANES), F32)]
+    else:
+        outs = [((count, own * (rows + part), LANES), F32)]
+    packed, *filter_blocks, bias = call(
+        functools.partial(pack_kernel, layout, staged), outs + [((1, chans), F32)],
         [SMEM] + [HBM] * 4, size // 4, size * 3,
         [pltpu.VMEM((tokens, chans), BF16), pltpu.VMEM((tokens, chans), BF16), pltpu.VMEM((part * LANES, chans), F32),
-         pltpu.SemaphoreType.DMA((4,))],
+         pltpu.VMEM((part, chans, LANES), F32), pltpu.SemaphoreType.DMA((4,))],
     )(where, *(pltpu.with_memory_space_constraint(source, pltpu.HBM) for source in sources))
     if staged:
         mine = lax.axis_index("groups")
-        height = own * (rows + part)
-        by_group = packed.reshape(2, blocks, height, LANES)
+        by_group = packed.reshape(2, blocks, own * rows, LANES)
         first = mine == 0
         kept = jnp.where(first, by_group[0], by_group[1])
         other = lax.ppermute(jnp.where(first, by_group[1], by_group[0]), "groups", [(0, 1), (1, 0)])
-        pair = jnp.concatenate([jnp.where(first, kept, other), jnp.where(first, other, kept)], axis=1)
+        pair = [jnp.where(first, kept, other), jnp.where(first, other, kept)]
+        pair = jnp.concatenate(pair + filter_blocks, axis=1)
         moved = lax.all_to_all(pair, "seq", 0, 0, tiled=True)
     else:
         moved = exchange(packed)

time: 48.6 us -> 49.6 us (1.021)
  blocking collectives: 35.1 us -> 37.5 us
  waiting for transfers between devices: 5.76 us -> 4.35 us
    ppermute x1, waiting for transfers between devices: 5.76 us -> 4.35 us  [convolve(): lax.ppermute(jnp.where(first, by_group[1], by_group[0]), 'groups', [(0, 1...]
    all_to_all x1, blocking collectives: 15.7 us -> 16.9 us  [exchange(): return lax.all_to_all(array, axes, 0, 0, tiled=True)]
    all_to_all x1, blocking collectives: 19.4 us -> 20.6 us  [convolve(): moved = lax.all_to_all(pair, 'seq', 0, 0, tiled=True)]
where the time goes in v9:
time: 49.6 us; the launch traced here: 49.4 us
  blocking collectives  37.5 us (76%)
  waiting for transfers between devices  4.35 us (9%)
  Pallas kernels  3.51 us (7%)
  starting transfers between devices  3.01 us (6%)
  local copies, waits for them, and re-layouts  0.75 us (2%)
    all_to_all x1, blocking collectives, convolve(): moved = lax.all_to_all(pair, 'seq', 0, 0, tiled=True)  20.6 us
    all_to_all x1, blocking collectives, exchange(): return lax.all_to_all(array, axes, 0, 0, tiled=True)  16.9 us
    ppermute x1, waiting for transfers between devices, convolve(): lax.ppermute(jnp.where(first, by_group[1], by_group[0]), 'groups', [(0, 1...  4.35 us
    ppermute x1, starting transfers between devices, convolve(): lax.ppermute(jnp.where(first, by_group[1], by_group[0]), 'groups', [(0, 1...  3.01 us
    pallas_call x1, Pallas kernels, convolve(): call(functools.partial(conv_kernel, layout, staged, min(own, 2)), [((coun...  1.8 us
    pallas_call x1, Pallas kernels, convolve(): call(functools.partial(pack_kernel, layout, staged), outs + [((1, chans),...  1.51 us
  transfers between devices with their start and end apart: 1, of which 1 were waited for; matrix products, arithmetic and copies ran while one was open for 0% of the time, Pallas kernels for 0%

profile of v9, /device:TPU:0, one launch (start us, length us, event | category | flops | bytes accessed | tf_op | source)
XLA Modules:
  0.0 49.4 jit_solution(536264168411274257)
XLA Ops:
  0.0 48.7 %conditional.1 = (bf16[1024,128]{1,0:T(8,128)(2,1)S(1)}) conditional(s32[]{:T(128)} %convert_element_type.3, (f32[128]{0:T(128)}, bf16[1024,128]{1,0:T(8,128)(2,1)}, bf16[1024,128]{1,0:T(8,128)(2,1)}, f32[1024,128]{1,0:T(8,128)}, bf16[128,192]{1,0:T(8,128)(2,1)}, /*index=5*/f32[64,256]{1,0:T(8,128)}, bf16[768,256]{1,0:T(8,128)(2,1)}, ...), branch_computations={%region_0.1_spmd, %region_1.2_spmd} | conditional | flops 1259601920 | bytes 19071292 | solution.py:275
  0.0 1.5 %branch_0_fun.3 = (f32[16,64,128]{2,1,0:T(8,128)S(1)}, f32[8,64,128]{2,1,0:T(8,128)S(1)}, f32[1,128]{1,0:T(1,128)S(1)}) custom-call(s32[1]{0:T(128)} %bitcast.where_ref, bf16[1024,128]{1,0:T(8,128)(2,1)} %get-tuple-element.48.key_ref, bf16[1024,128]{1,0:T(8,128)(2,1)} %get-tuple-element.49.value_ref, f32[1024,128]{1,0:T(8,128)} %get-tuple-element.50.filter_ref, ...), custom_call_target="tpu_custom_call" | custom-call | flops 131072 | bytes 1572864 | tf_op jit(solution)/shard_map/cond/branch_0_fun/pallas_call | solution.py:245
  1.6 3.0 %collective-permute-start = (f32[8,64,128]{2,1,0:T(8,128)S(1)}, f32[8,64,128]{2,1,0:T(8,128)S(1)}, u32[]{:S(2)}, u32[]{:S(2)}) collective-permute-start(f32[8,64,128]{2,1,0:T(8,128)S(1)} %slice_select_fusion), channel_id=1, source_target_pairs={{0,16},{16,0},{1,17},{17,1},{2,18},{18,2},{3,19},{19,3},{4,20},{20... | collective-permute-start | bytes 786440 | tf_op jit(solution)/shard_map/cond/branch_0_fun/ppermute | solution.py:256
  4.6 4.4 %collective-permute-done = f32[8,64,128]{2,1,0:T(8,128)S(1)} collective-permute-done((f32[8,64,128]{2,1,0:T(8,128)S(1)}, f32[8,64,128]{2,1,0:T(8,128)S(1)}, u32[]{:S(2)}, u32[]{:S(2)}) %collective-permute-start) | collective-permute-done | bytes 262176 | tf_op jit(solution)/shard_map/cond/branch_0_fun/ppermute | solution.py:256
  9.0 0.1 pad_maximum_fusion
  9.0 0.0 copy-start.7
  9.0 0.0 copy-start.9
  9.1 0.0 copy-start.11
  9.1 0.0 copy-start.13
  9.1 0.0 copy-start.15
  9.1 20.6 %all_to_all.16.moved_ref = f32[8,192,128]{2,1,0:T(8,128)S(1)} all-to-all(f32[8,192,128]{2,1,0:T(8,128)S(1)} %pad_maximum_fusion), channel_id=1, replica_groups=mesh['groups'=2,'seq'=8,'chan'=2] {'seq'}, dimensions={0} | all-to-all | bytes 1572864 | tf_op jit(solution)/shard_map/cond/branch_0_fun/all_to_all | solution.py:259
  29.7 0.0 copy-done.7
  29.7 0.0 copy-done.9
  29.7 0.0 copy-done.11
  29.7 0.0 copy-done.13
  29.7 0.0 copy-done.15
  29.8 1.8 %branch_0_fun.4 = f32[16,64,128]{2,1,0:T(8,128)S(1)} custom-call(f32[8,192,128]{2,1,0:T(8,128)S(1)} %all_to_all.16.moved_ref, bf16[128,192]{1,0:T(8,128)(2,1)S(1)} %copy-done.15, f32[64,256]{1,0:T(8,128)S(1)} %copy-done.13, bf16[768,256]{1,0:T(8,128)(2,1)S(1)} %copy-done.9, bf16[768,256]{1,0:T(8,128)(2,1)S(1)} %copy-done.7, bf16[128,256]{1,0:T(8,128)(2,1)S(1)} %copy-done.11), custom_call_target="tpu_custom_call" | custom-call | flops 1258291200 | bytes 1572864 | tf_op jit(solution)/shard_map/cond/branch_0_fun/pallas_call | solution.py:262
  31.6 0.0 copy-start
  31.6 0.0 copy-start.2
  31.6 0.0 copy-start.4
  31.6 16.9 %all_to_all.17 = f32[16,64,128]{2,1,0:T(8,128)S(1)} all-to-all(f32[16,64,128]{2,1,0:T(8,128)S(1)} %branch_0_fun.4), channel_id=1, replica_groups=mesh['groups'=2,'seq'=8,'chan'=2] {'groups','seq'}, dimensions={0} | all-to-all | bytes 1048576 | tf_op jit(solution)/shard_map/cond/branch_0_fun/all_to_all | solution.py:238
  48.5 0.0 copy-done
  48.5 0.0 copy-done.2
  48.5 0.0 copy-done.4
  48.5 0.2 branch_0_fun.5
  48.7 0.0 copy-start.6
  48.7 0.7 %copy-done.6 = bf16[1024,128]{1,0:T(8,128)(2,1)} copy-done((bf16[1024,128]{1,0:T(8,128)(2,1)}, bf16[1024,128]{1,0:T(8,128)(2,1)S(1)}, u32[]{:S(2)}) %copy-start.6) | copy-done | bytes 262168
  (2 shorter events, 0.1 us)
Async XLA Ops:
  1.6 7.4 %collective-permute-start = (f32[8,64,128]{2,1,0:T(8,128)S(1)}, f32[8,64,128]{2,1,0:T(8,128)S(1)}, u32[]{:S(2)}, u32[]{:S(2)}) collective-permute-start(f32[8,64,128]{2,1,0:T(8,128)S(1)} %slice_select_fusion), channel_id=1, source_target_pairs={{0,16},{16,0},{1,17},{17,1},{2,18},{18,2},{3,19},{19,3},{4,20},{20... | collective-permute-start | bytes 786440 | tf_op jit(solution)/shard_map/cond/branch_0_fun/ppermute | solution.py:256
  9.0 20.7 %copy-start.7 = (bf16[768,256]{1,0:T(8,128)(2,1)S(1)}, bf16[768,256]{1,0:T(8,128)(2,1)}, u32[]{:S(2)}) copy-start(bf16[768,256]{1,0:T(8,128)(2,1)} %get-tuple-element.57.back_tail_ref) | copy-start | bytes 1179652 | tf_op jit(solution)/shard_map/cond
  9.0 20.7 %copy-start.9 = (bf16[768,256]{1,0:T(8,128)(2,1)S(1)}, bf16[768,256]{1,0:T(8,128)(2,1)}, u32[]{:S(2)}) copy-start(bf16[768,256]{1,0:T(8,128)(2,1)} %get-tuple-element.56.tail_ref) | copy-start | bytes 1179652 | tf_op jit(solution)/shard_map/cond
  9.1 20.7 %copy-start.11 = (bf16[128,256]{1,0:T(8,128)(2,1)S(1)}, bf16[128,256]{1,0:T(8,128)(2,1)}, u32[]{:S(2)}) copy-start(bf16[128,256]{1,0:T(8,128)(2,1)} %get-tuple-element.58.back_head_ref) | copy-start | bytes 196612 | tf_op jit(solution)/shard_map/cond
  9.1 20.7 %copy-start.13 = (f32[64,256]{1,0:T(8,128)S(1)}, f32[64,256]{1,0:T(8,128)}, u32[]{:S(2)}) copy-start(f32[64,256]{1,0:T(8,128)} %get-tuple-element.55.twist_ref) | copy-start | bytes 196612 | tf_op jit(solution)/shard_map/cond
  9.1 20.7 %copy-start.15 = (bf16[128,192]{1,0:T(8,128)(2,1)S(1)}, bf16[128,192]{1,0:T(8,128)(2,1)}, u32[]{:S(2)}) copy-start(bf16[128,192]{1,0:T(8,128)(2,1)} %get-tuple-element.54.head_ref) | copy-start | bytes 147460 | tf_op jit(solution)/shard_map/cond
  31.6 16.9 %copy-start = (bf16[1024,128]{1,0:T(8,128)(2,1)S(1)}, bf16[1024,128]{1,0:T(8,128)(2,1)}, u32[]{:S(2)}) copy-start(bf16[1024,128]{1,0:T(8,128)(2,1)} %get-tuple-element.48.key_ref) | copy-start | bytes 786436 | tf_op jit(solution)/shard_map/cond
  31.6 16.9 %copy-start.2 = (bf16[1024,128]{1,0:T(8,128)(2,1)S(1)}, bf16[1024,128]{1,0:T(8,128)(2,1)}, u32[]{:S(2)}) copy-start(bf16[1024,128]{1,0:T(8,128)(2,1)} %get-tuple-element.49.value_ref) | copy-start | bytes 786436 | tf_op jit(solution)/shard_map/cond
  31.6 16.9 %copy-start.4 = (bf16[1024,128]{1,0:T(8,128)(2,1)S(1)}, bf16[1024,128]{1,0:T(8,128)(2,1)}, u32[]{:S(2)}) copy-start(bf16[1024,128]{1,0:T(8,128)(2,1)} %get-tuple-element.59.query_ref) | copy-start | bytes 786436 | tf_op jit(solution)/shard_map/cond
  48.7 0.7 %copy-start.6 = (bf16[1024,128]{1,0:T(8,128)(2,1)}, bf16[1024,128]{1,0:T(8,128)(2,1)S(1)}, u32[]{:S(2)}) copy-start(bf16[1024,128]{1,0:T(8,128)(2,1)S(1)} %get-tuple-element.80) | copy-start | bytes 786436

commit v10 on v8

--- a/solution.py
+++ b/solution.py
@@ -99,8 +99,28 @@
     return jnp.concatenate([jnp.concatenate(reals, axis=1), jnp.concatenate(imags, axis=1)], axis=0)
 
 
-def pack_kernel(layout, where_ref, key_ref, value_ref, filter_ref, bias_ref, out_ref, bias_out, key, value, taps, sems):
-    rows, own, part, groups = layout
+def place_of(halved, groups, blocks, peer):
+    group, block = divmod(peer, blocks)
+    side, inner = divmod(block, blocks // 2)
+    return side * (groups * blocks // 2) + group * (blocks // 2) + inner if halved else peer
+
+
+def chans_of(halved, groups, blocks, peer):
+    group, block = divmod(peer, blocks)
+    side, inner = divmod(block, blocks // 2)
+    return (group * (blocks // 2) + inner) * 2 + side if halved else peer
+
+
+def pack_kernel(layout, halved_in, halved_out, where_ref, key_ref, value_ref, filter_ref, bias_ref, out_ref, bias_out, key, value, taps, sems):
+    rows, own, part, groups = layout
+    count = out_ref.shape[0]
+    homes = [
+        (
+            place_of(halved_in, groups, count // groups, peer),
+            chans_of(halved_out, groups, count // groups, peer) * own,
+        )
+        for peer in range(count)
+    ]
     first = where_ref[0] * (part * LANES if part < rows else 0)
     taken = filter_ref.at[pl.ds(pl.multiple_of(first, part * LANES), part * LANES)]
     pairs = ((key_ref, key), (value_ref, value), (taken, taps), (bias_ref, bias_out))
@@ -112,46 +132,48 @@
     for row in range(rows):
         span = pl.ds(row * LANES, LANES)
         turned = (key[span, :].astype(F32) * value[span, :].astype(F32)).T
-        for peer in range(out_ref.shape[0]):
-            out_ref[peer, pl.ds(row, own, stride=rows), :] = turned[peer * own : (peer + 1) * own]
+        for place, chan in homes:
+            out_ref[place, pl.ds(row, own, stride=rows), :] = turned[chan : chan + own]
     fetches[2].wait()
     for row in range(part):
         turned = taps[pl.ds(row * LANES, LANES), :].T
-        for peer in range(out_ref.shape[0]):
-            out_ref[peer, pl.ds(own * rows + row, own, stride=part), :] = turned[peer * own : (peer + 1) * own]
+        for place, chan in homes:
+            out_ref[place, pl.ds(own * rows + row, own, stride=part), :] = turned[chan : chan + own]
     fetches[3].wait()
 
 
-def arrived(layout, staged, moved_ref, group, start, height):
-    rows, own, part, groups = layout
-    if staged:
-        start += group * own * (rows + part)
-        return moved_ref[:, start : start + height]
-    blocks = moved_ref.shape[0] // groups
-    return moved_ref[pl.ds(group * blocks, blocks), start : start + height]
-
-
-def driver_signals(layout, staged, moved_ref, chans):
+def arrived(layout, halved, moved_ref, group, start, height):
+    rows, own, part, groups = layout
+    span = pl.ds(group * (moved_ref.shape[0] // groups), moved_ref.shape[0] // groups)
+    if not halved:
+        return moved_ref[span, start : start + height]
+    second = start + own * (rows + part)
+    return jnp.concatenate(
+        [moved_ref[span, start : start + height], moved_ref[span, second : second + height]], axis=0
+    )
+
+
+def driver_signals(layout, halved, moved_ref, chans):
     rows, own, part, groups = layout
     parts = [
-        arrived(layout, staged, moved_ref, group, chan * rows, rows) for chan in chans for group in range(groups)
+        arrived(layout, halved, moved_ref, group, chan * rows, rows) for chan in chans for group in range(groups)
     ]
     return [values.reshape(values.shape[0] * rows, LANES) for values in parts]
 
 
-def filter_signals(layout, staged, moved_ref, chans):
+def filter_signals(layout, halved, moved_ref, chans):
     rows, own, part, groups = layout
     signals = []
     for chan in chans:
         pieces = [
-            arrived(layout, staged, moved_ref, group, own * rows + chan * part, part)
+            arrived(layout, halved, moved_ref, group, own * rows + chan * part, part)
             for group in range(groups if part < rows else 1)
         ]
         signals.append(jnp.concatenate(pieces, axis=1).reshape(pieces[0].shape[0] * rows, LANES))
     return signals
 
 
-def conv_kernel(layout, staged, pieces, moved_ref, head_ref, twist_ref, tail_ref, back_tail_ref, back_head_ref, out_ref):
+def conv_kernel(layout, halved, halved_out, pieces, moved_ref, head_ref, twist_ref, tail_ref, back_tail_ref, back_head_ref, out_ref):
     rows, own, part, groups = layout
     blocks = out_ref.shape[0] // groups
     outer = blocks * rows
@@ -160,7 +182,7 @@
     sets = [range(piece * own // pieces, (piece + 1) * own // pieces) for piece in range(pieces)]
     mixed = [
         head_stage(
-            filter_signals(layout, staged, moved_ref, chans) + driver_signals(layout, staged, moved_ref, chans),
+            filter_signals(layout, halved, moved_ref, chans) + driver_signals(layout, halved, moved_ref, chans),
             head_ref[...],
             twist_ref[...],
         )
@@ -176,9 +198,14 @@
         for idx in range(len(chans) * groups):
             chan, group = divmod(idx, groups)
             start = (chans[0] + chan) * rows
-            out_ref[pl.ds(group * blocks, blocks), start : start + rows] = result[
-                :, idx * LANES : (idx + 1) * LANES
-            ].reshape(blocks, rows, LANES)
+            values = result[:, idx * LANES : (idx + 1) * LANES].reshape(blocks, rows, LANES)
+            if halved_out:
+                inner = blocks // 2
+                for side in range(2):
+                    place = side * groups * inner + group * inner
+                    out_ref[place : place + inner, start : start + rows] = values[side * inner : (side + 1) * inner]
+            else:
+                out_ref[group * blocks : (group + 1) * blocks, start : start + rows] = values
 
 
 def gate_kernel(rows, conv_ref, query_ref, key_ref, value_ref, bias_ref, out_ref):
@@ -207,7 +234,7 @@
     )
 
 
-def convolve(groups, blocks, staged, query_proj, key_proj, value_proj, long_filter, skip_bias):
+def convolve(groups, blocks, halved_in, halved_out, query_proj, key_proj, value_proj, long_filter, skip_bias):
     tokens, chans = key_proj.shape
     rows = tokens // LANES
     count, axes = groups * blocks, ("groups", "seq")
@@ -223,45 +250,48 @@
     macs = 2 * 3 * own * seq_len * (2 * outer + 4 * LANES)
     where = lax.axis_index("groups").reshape(1).astype(jnp.int32)
 
-    def exchange(array):
-        return lax.all_to_all(array, axes, 0, 0, tiled=True)
+    def exchange(array, halved):
+        if not halved:
+            return lax.all_to_all(array, axes, 0, 0, tiled=True)
+        inner = blocks // 2
+        low = lax.axis_index("seq") < inner
+        by_side = array.reshape(2, count // 2, array.shape[1], LANES)
+        kept = jnp.where(low, by_side[0], by_side[1])
+        swap = [(block, (block + inner) % blocks) for block in range(blocks)]
+        other = lax.ppermute(jnp.where(low, by_side[1], by_side[0]), "seq", swap)
+        pair = jnp.concatenate([jnp.where(low, kept, other), jnp.where(low, other, kept)], axis=1)
+        sides = [
+            [group * blocks + side * inner + block for group in range(groups) for block in range(inner)]
+            for side in range(2)
+        ]
+        return lax.all_to_all(pair, axes, 0, 0, axis_index_groups=sides, tiled=True)
 
     sources = (key_proj, value_proj, long_filter, skip_bias.reshape(1, chans))
     packed, bias = call(
-        functools.partial(pack_kernel, layout),
+        functools.partial(pack_kernel, layout, halved_in, halved_out),
         [((count, own * (rows + part), LANES), F32), ((1, chans), F32)],
         [SMEM] + [HBM] * 4, size // 4, size * 3,
         [pltpu.VMEM((tokens, chans), BF16), pltpu.VMEM((tokens, chans), BF16), pltpu.VMEM((part * LANES, chans), F32),
          pltpu.SemaphoreType.DMA((4,))],
     )(where, *(pltpu.with_memory_space_constraint(source, pltpu.HBM) for source in sources))
-    if staged:
-        mine = lax.axis_index("groups")
-        height = own * (rows + part)
-        by_group = packed.reshape(2, blocks, height, LANES)
-        first = mine == 0
-        kept = jnp.where(first, by_group[0], by_group[1])
-        other = lax.ppermute(jnp.where(first, by_group[1], by_group[0]), "groups", [(0, 1), (1, 0)])
-        pair = jnp.concatenate([jnp.where(first, kept, other), jnp.where(first, other, kept)], axis=1)
-        moved = lax.all_to_all(pair, "seq", 0, 0, tiled=True)
-    else:
-        moved = exchange(packed)
+    moved = exchange(packed, halved_in)
     local = call(
-        functools.partial(conv_kernel, layout, staged, min(own, 2)),
+        functools.partial(conv_kernel, layout, halved_in, halved_out, min(own, 2)),
         [((count, own * rows, LANES), F32)], [VMEM] * 6, 5 * macs, 3 * size,
     )(moved, head, twist, tail, back_tail, back_head)[0]
-    convolved = exchange(local).reshape(chans * rows, LANES)
+    convolved = exchange(local, halved_out).reshape(chans * rows, LANES)
     return call(functools.partial(gate_kernel, rows), [((tokens, chans), BF16)], [VMEM] * 5, size, 3 * size)(
         convolved, query_proj, key_proj, value_proj, bias
     )[0]
 
 
 def shards(groups, blocks, cores, *args):
-    if cores == 1 or groups != 2:
-        return convolve(groups, blocks, False, *args)
+    if cores == 1 or blocks % 2:
+        return convolve(groups, blocks, False, False, *args)
     return lax.cond(
         lax.axis_index("chan") % 2 == 1,
-        functools.partial(convolve, groups, blocks, False),
-        functools.partial(convolve, groups, blocks, True),
+        functools.partial(convolve, groups, blocks, False, False),
+        functools.partial(convolve, groups, blocks, True, False),
         *args,
     )
 

time: 48.6 us -> 60.6 us (1.25)
  waiting for transfers between devices: 5.76 us -> 16.8 us
  starting transfers between devices: 3 us -> 4.1 us
    ppermute x1, waiting for transfers between devices: 5.76 us -> 16.8 us  [exchange(): other = lax.ppermute(jnp.where(low, by_side[1], by_side[0]), 'seq', swap)]
    ppermute x1, starting transfers between devices: 3 us -> 4.1 us  [exchange(): other = lax.ppermute(jnp.where(low, by_side[1], by_side[0]), 'seq', swap)]
    all_to_all x1, blocking collectives: 19.4 us -> 18.4 us  [exchange(): return lax.all_to_all(pair, axes, 0, 0, axis_index_groups=sides, tiled=True)]
    all_to_all x1, blocking collectives: 15.7 us -> 16.6 us  [exchange(): return lax.all_to_all(array, axes, 0, 0, tiled=True)]
where the time goes in v10:
time: 60.6 us; the launch traced here: 60.4 us
  blocking collectives  35 us (58%)
  waiting for transfers between devices  16.8 us (28%)
  starting transfers between devices  4.1 us (7%)
  Pallas kernels  3.4 us (6%)
  local copies, waits for them, and re-layouts  0.75 us (1%)
    all_to_all x1, blocking collectives, exchange(): return lax.all_to_all(pair, axes, 0, 0, axis_index_groups=sides, tiled=True)  18.4 us
    ppermute x1, waiting for transfers between devices, exchange(): other = lax.ppermute(jnp.where(low, by_side[1], by_side[0]), 'seq', swap)  16.8 us
    all_to_all x1, blocking collectives, exchange(): return lax.all_to_all(array, axes, 0, 0, tiled=True)  16.6 us
    ppermute x1, starting transfers between devices, exchange(): other = lax.ppermute(jnp.where(low, by_side[1], by_side[0]), 'seq', swap)  4.1 us
    pallas_call x1, Pallas kernels, convolve(): call(functools.partial(conv_kernel, layout, halved_in, halved_out, min(ow...  1.79 us
    pallas_call x1, Pallas kernels, convolve(): call(functools.partial(pack_kernel, layout, halved_in, halved_out), [((co...  1.4 us
  transfers between devices with their start and end apart: 1, of which 1 were waited for; matrix products, arithmetic and copies ran while one was open for 0% of the time, Pallas kernels for 0%

profile of v10, /device:TPU:0, one launch (start us, length us, event | category | flops | bytes accessed | tf_op | source)
XLA Modules:
  0.0 60.4 jit_solution(12585010190036195639)
XLA Ops:
  0.0 59.7 %conditional.1 = (bf16[1024,128]{1,0:T(8,128)(2,1)S(1)}) conditional(s32[]{:T(128)} %convert_element_type.3, (f32[128]{0:T(128)}, bf16[1024,128]{1,0:T(8,128)(2,1)}, bf16[1024,128]{1,0:T(8,128)(2,1)}, f32[1024,128]{1,0:T(8,128)}, bf16[128,192]{1,0:T(8,128)(2,1)}, /*index=5*/f32[64,256]{1,0:T(8,128)}, bf16[768,256]{1,0:T(8,128)(2,1)}, ...), branch_computations={%region_0.1_spmd, %region_1.2_spmd} | conditional | flops 1259536384 | bytes 20644188 | solution.py:291
  0.0 1.4 %branch_0_fun.3 = (f32[16,96,128]{2,1,0:T(8,128)S(1)}, f32[1,128]{1,0:T(1,128)S(1)}) custom-call(s32[1]{0:T(128)} %bitcast.where_ref, bf16[1024,128]{1,0:T(8,128)(2,1)} %get-tuple-element.48.key_ref, bf16[1024,128]{1,0:T(8,128)(2,1)} %get-tuple-element.49.value_ref, f32[1024,128]{1,0:T(8,128)} %get-tuple-element.50.filter_ref, f32[1,128]{1,0:T(1,128)} %bitcast.8), custom_call_target="tpu_custom_call" | custom-call | flops 131072 | bytes 1572864 | tf_op jit(solution)/shard_map/cond/branch_0_fun/pallas_call | solution.py:270
  1.5 4.1 %collective-permute-start = (f32[8,96,128]{2,1,0:T(8,128)S(1)}, f32[8,96,128]{2,1,0:T(8,128)S(1)}, u32[]{:S(2)}, u32[]{:S(2)}) collective-permute-start(f32[8,96,128]{2,1,0:T(8,128)S(1)} %slice_select_fusion), channel_id=1, source_target_pairs={{0,8},{2,10},{4,12},{6,14},{8,0},{10,2},{12,4},{14,6},{1,9},{3,11}... | collective-permute-start | bytes 1179656 | tf_op jit(solution)/shard_map/cond/branch_0_fun/ppermute | solution.py:261
  5.6 16.8 %collective-permute-done = f32[8,96,128]{2,1,0:T(8,128)S(1)} collective-permute-done((f32[8,96,128]{2,1,0:T(8,128)S(1)}, f32[8,96,128]{2,1,0:T(8,128)S(1)}, u32[]{:S(2)}, u32[]{:S(2)}) %collective-permute-start) | collective-permute-done | bytes 393248 | tf_op jit(solution)/shard_map/cond/branch_0_fun/ppermute | solution.py:261
  22.3 0.1 broadcast_select_fusion.1
  22.4 0.1 pad_maximum_fusion
  22.5 0.0 copy-start.7
  22.5 0.0 copy-start.9
  22.5 0.0 copy-start.11
  22.5 0.0 copy-start.13
  22.5 0.0 copy-start.15
  22.6 18.4 %all_to_all.16.moved_ref = f32[8,192,128]{2,1,0:T(8,128)S(1)} all-to-all(f32[8,192,128]{2,1,0:T(8,128)S(1)} %pad_maximum_fusion), channel_id=1, replica_groups={{0,2,4,6,16,18,20,22},{8,10,12,14,24,26,28,30},{1,3,5,7,17,19,21,23},{9..., dimensions={0} | all-to-all | bytes 1572864 | tf_op jit(solution)/shard_map/cond/branch_0_fun/all_to_all | solution.py:267
  41.0 0.0 copy-done.7
  41.0 0.0 copy-done.9
  41.0 0.0 copy-done.11
  41.0 0.0 copy-done.13
  41.0 0.0 copy-done.15
  41.0 1.8 %branch_0_fun.4 = f32[16,64,128]{2,1,0:T(8,128)S(1)} custom-call(f32[8,192,128]{2,1,0:T(8,128)S(1)} %all_to_all.16.moved_ref, bf16[128,192]{1,0:T(8,128)(2,1)S(1)} %copy-done.15, f32[64,256]{1,0:T(8,128)S(1)} %copy-done.13, bf16[768,256]{1,0:T(8,128)(2,1)S(1)} %copy-done.9, bf16[768,256]{1,0:T(8,128)(2,1)S(1)} %copy-done.7, bf16[128,256]{1,0:T(8,128)(2,1)S(1)} %copy-done.11), custom_call_target="tpu_custom_call" | custom-call | flops 1258291200 | bytes 1572864 | tf_op jit(solution)/shard_map/cond/branch_0_fun/pallas_call | solution.py:278
  42.8 0.0 copy-start
  42.8 0.0 copy-start.2
  42.8 0.0 copy-start.4
  42.8 16.6 %all_to_all.17 = f32[16,64,128]{2,1,0:T(8,128)S(1)} all-to-all(f32[16,64,128]{2,1,0:T(8,128)S(1)} %branch_0_fun.4), channel_id=1, replica_groups=mesh['groups'=2,'seq'=8,'chan'=2] {'groups','seq'}, dimensions={0} | all-to-all | bytes 1048576 | tf_op jit(solution)/shard_map/cond/branch_0_fun/all_to_all | solution.py:255
  59.4 0.0 copy-done
  59.5 0.0 copy-done.2
  59.5 0.0 copy-done.4
  59.5 0.2 branch_0_fun.5
  59.7 0.0 copy-start.6
  59.7 0.7 %copy-done.6 = bf16[1024,128]{1,0:T(8,128)(2,1)} copy-done((bf16[1024,128]{1,0:T(8,128)(2,1)}, bf16[1024,128]{1,0:T(8,128)(2,1)S(1)}, u32[]{:S(2)}) %copy-start.6) | copy-done | bytes 262168
  (1 shorter events, 0.0 us)
Async XLA Ops:
  1.5 20.9 %collective-permute-start = (f32[8,96,128]{2,1,0:T(8,128)S(1)}, f32[8,96,128]{2,1,0:T(8,128)S(1)}, u32[]{:S(2)}, u32[]{:S(2)}) collective-permute-start(f32[8,96,128]{2,1,0:T(8,128)S(1)} %slice_select_fusion), channel_id=1, source_target_pairs={{0,8},{2,10},{4,12},{6,14},{8,0},{10,2},{12,4},{14,6},{1,9},{3,11}... | collective-permute-start | bytes 1179656 | tf_op jit(solution)/shard_map/cond/branch_0_fun/ppermute | solution.py:261
  22.5 18.5 %copy-start.7 = (bf16[768,256]{1,0:T(8,128)(2,1)S(1)}, bf16[768,256]{1,0:T(8,128)(2,1)}, u32[]{:S(2)}) copy-start(bf16[768,256]{1,0:T(8,128)(2,1)} %get-tuple-element.56.back_tail_ref) | copy-start | bytes 1179652 | tf_op jit(solution)/shard_map/cond
  22.5 18.5 %copy-start.9 = (bf16[768,256]{1,0:T(8,128)(2,1)S(1)}, bf16[768,256]{1,0:T(8,128)(2,1)}, u32[]{:S(2)}) copy-start(bf16[768,256]{1,0:T(8,128)(2,1)} %get-tuple-element.55.tail_ref) | copy-start | bytes 1179652 | tf_op jit(solution)/shard_map/cond
  22.5 18.5 %copy-start.11 = (bf16[128,256]{1,0:T(8,128)(2,1)S(1)}, bf16[128,256]{1,0:T(8,128)(2,1)}, u32[]{:S(2)}) copy-start(bf16[128,256]{1,0:T(8,128)(2,1)} %get-tuple-element.57.back_head_ref) | copy-start | bytes 196612 | tf_op jit(solution)/shard_map/cond
  22.5 18.4 %copy-start.13 = (f32[64,256]{1,0:T(8,128)S(1)}, f32[64,256]{1,0:T(8,128)}, u32[]{:S(2)}) copy-start(f32[64,256]{1,0:T(8,128)} %get-tuple-element.54.twist_ref) | copy-start | bytes 196612 | tf_op jit(solution)/shard_map/cond
  22.5 18.4 %copy-start.15 = (bf16[128,192]{1,0:T(8,128)(2,1)S(1)}, bf16[128,192]{1,0:T(8,128)(2,1)}, u32[]{:S(2)}) copy-start(bf16[128,192]{1,0:T(8,128)(2,1)} %get-tuple-element.53.head_ref) | copy-start | bytes 147460 | tf_op jit(solution)/shard_map/cond
  42.8 16.7 %copy-start = (bf16[1024,128]{1,0:T(8,128)(2,1)S(1)}, bf16[1024,128]{1,0:T(8,128)(2,1)}, u32[]{:S(2)}) copy-start(bf16[1024,128]{1,0:T(8,128)(2,1)} %get-tuple-element.48.key_ref) | copy-start | bytes 786436 | tf_op jit(solution)/shard_map/cond
  42.8 16.6 %copy-start.2 = (bf16[1024,128]{1,0:T(8,128)(2,1)S(1)}, bf16[1024,128]{1,0:T(8,128)(2,1)}, u32[]{:S(2)}) copy-start(bf16[1024,128]{1,0:T(8,128)(2,1)} %get-tuple-element.49.value_ref) | copy-start | bytes 786436 | tf_op jit(solution)/shard_map/cond
  42.8 16.6 %copy-start.4 = (bf16[1024,128]{1,0:T(8,128)(2,1)S(1)}, bf16[1024,128]{1,0:T(8,128)(2,1)}, u32[]{:S(2)}) copy-start(bf16[1024,128]{1,0:T(8,128)(2,1)} %get-tuple-element.58.query_ref) | copy-start | bytes 786436 | tf_op jit(solution)/shard_map/cond
  59.7 0.7 %copy-start.6 = (bf16[1024,128]{1,0:T(8,128)(2,1)}, bf16[1024,128]{1,0:T(8,128)(2,1)S(1)}, u32[]{:S(2)}) copy-start(bf16[1024,128]{1,0:T(8,128)(2,1)S(1)} %get-tuple-element.79) | copy-start | bytes 786436

commit v11 on v10

--- a/solution.py
+++ b/solution.py
@@ -102,25 +102,13 @@
 def place_of(halved, groups, blocks, peer):
     group, block = divmod(peer, blocks)
     side, inner = divmod(block, blocks // 2)
-    return side * (groups * blocks // 2) + group * (blocks // 2) + inner if halved else peer
-
-
-def chans_of(halved, groups, blocks, peer):
-    group, block = divmod(peer, blocks)
-    side, inner = divmod(block, blocks // 2)
     return (group * (blocks // 2) + inner) * 2 + side if halved else peer
 
 
-def pack_kernel(layout, halved_in, halved_out, where_ref, key_ref, value_ref, filter_ref, bias_ref, out_ref, bias_out, key, value, taps, sems):
+def pack_kernel(layout, halved, where_ref, key_ref, value_ref, filter_ref, bias_ref, out_ref, bias_out, key, value, taps, sems):
     rows, own, part, groups = layout
     count = out_ref.shape[0]
-    homes = [
-        (
-            place_of(halved_in, groups, count // groups, peer),
-            chans_of(halved_out, groups, count // groups, peer) * own,
-        )
-        for peer in range(count)
-    ]
+    homes = [(place_of(halved, groups, count // groups, peer), peer * own) for peer in range(count)]
     first = where_ref[0] * (part * LANES if part < rows else 0)
     taken = filter_ref.at[pl.ds(pl.multiple_of(first, part * LANES), part * LANES)]
     pairs = ((key_ref, key), (value_ref, value), (taken, taps), (bias_ref, bias_out))
@@ -173,7 +161,7 @@
     return signals
 
 
-def conv_kernel(layout, halved, halved_out, pieces, moved_ref, head_ref, twist_ref, tail_ref, back_tail_ref, back_head_ref, out_ref):
+def conv_kernel(layout, halved, pieces, moved_ref, head_ref, twist_ref, tail_ref, back_tail_ref, back_head_ref, out_ref):
     rows, own, part, groups = layout
     blocks = out_ref.shape[0] // groups
     outer = blocks * rows
@@ -199,13 +187,7 @@
             chan, group = divmod(idx, groups)
             start = (chans[0] + chan) * rows
             values = result[:, idx * LANES : (idx + 1) * LANES].reshape(blocks, rows, LANES)
-            if halved_out:
-                inner = blocks // 2
-                for side in range(2):
-                    place = side * groups * inner + group * inner
-                    out_ref[place : place + inner, start : start + rows] = values[side * inner : (side + 1) * inner]
-            else:
-                out_ref[group * blocks : (group + 1) * blocks, start : start + rows] = values
+            out_ref[group * blocks : (group + 1) * blocks, start : start + rows] = values
 
 
 def gate_kernel(rows, conv_ref, query_ref, key_ref, value_ref, bias_ref, out_ref):
@@ -234,7 +216,7 @@
     )
 
 
-def convolve(groups, blocks, halved_in, halved_out, query_proj, key_proj, value_proj, long_filter, skip_bias):
+def convolve(groups, blocks, halved, query_proj, key_proj, value_proj, long_filter, skip_bias):
     tokens, chans = key_proj.shape
     rows = tokens // LANES
     count, axes = groups * blocks, ("groups", "seq")
@@ -250,36 +232,39 @@
     macs = 2 * 3 * own * seq_len * (2 * outer + 4 * LANES)
     where = lax.axis_index("groups").reshape(1).astype(jnp.int32)
 
-    def exchange(array, halved):
-        if not halved:
-            return lax.all_to_all(array, axes, 0, 0, tiled=True)
-        inner = blocks // 2
-        low = lax.axis_index("seq") < inner
-        by_side = array.reshape(2, count // 2, array.shape[1], LANES)
-        kept = jnp.where(low, by_side[0], by_side[1])
-        swap = [(block, (block + inner) % blocks) for block in range(blocks)]
-        other = lax.ppermute(jnp.where(low, by_side[1], by_side[0]), "seq", swap)
-        pair = jnp.concatenate([jnp.where(low, kept, other), jnp.where(low, other, kept)], axis=1)
+    def exchange(array):
+        return lax.all_to_all(array, axes, 0, 0, tiled=True)
+
+    def exchange_halved(array):
+        inner, height = blocks // 2, array.shape[1]
         sides = [
             [group * blocks + side * inner + block for group in range(groups) for block in range(inner)]
             for side in range(2)
         ]
-        return lax.all_to_all(pair, axes, 0, 0, axis_index_groups=sides, tiled=True)
+        inside = lax.all_to_all(
+            array.reshape(count // 2, 2 * height, LANES), axes, 0, 0, axis_index_groups=sides, tiled=True
+        )
+        low = lax.axis_index("seq") < inner
+        to_low, to_high = inside[:, :height], inside[:, height:]
+        kept = jnp.where(low, to_low, to_high)
+        swap = [(block, (block + inner) % blocks) for block in range(blocks)]
+        other = lax.ppermute(jnp.where(low, to_high, to_low), "seq", swap)
+        return jnp.concatenate([jnp.where(low, kept, other), jnp.where(low, other, kept)], axis=1)
 
     sources = (key_proj, value_proj, long_filter, skip_bias.reshape(1, chans))
     packed, bias = call(
-        functools.partial(pack_kernel, layout, halved_in, halved_out),
+        functools.partial(pack_kernel, layout, halved),
         [((count, own * (rows + part), LANES), F32), ((1, chans), F32)],
         [SMEM] + [HBM] * 4, size // 4, size * 3,
         [pltpu.VMEM((tokens, chans), BF16), pltpu.VMEM((tokens, chans), BF16), pltpu.VMEM((part * LANES, chans), F32),
          pltpu.SemaphoreType.DMA((4,))],
     )(where, *(pltpu.with_memory_space_constraint(source, pltpu.HBM) for source in sources))
-    moved = exchange(packed, halved_in)
+    moved = (exchange_halved if halved else exchange)(packed)
     local = call(
-        functools.partial(conv_kernel, layout, halved_in, halved_out, min(own, 2)),
+        functools.partial(conv_kernel, layout, halved, min(own, 2)),
         [((count, own * rows, LANES), F32)], [VMEM] * 6, 5 * macs, 3 * size,
     )(moved, head, twist, tail, back_tail, back_head)[0]
-    convolved = exchange(local, halved_out).reshape(chans * rows, LANES)
+    convolved = exchange(local).reshape(chans * rows, LANES)
     return call(functools.partial(gate_kernel, rows), [((tokens, chans), BF16)], [VMEM] * 5, size, 3 * size)(
         convolved, query_proj, key_proj, value_proj, bias
     )[0]
@@ -287,11 +272,11 @@
 
 def shards(groups, blocks, cores, *args):
     if cores == 1 or blocks % 2:
-        return convolve(groups, blocks, False, False, *args)
+        return convolve(groups, blocks, False, *args)
     return lax.cond(
         lax.axis_index("chan") % 2 == 1,
-        functools.partial(convolve, groups, blocks, False, False),
-        functools.partial(convolve, groups, blocks, True, False),
+        functools.partial(convolve, groups, blocks, False),
+        functools.partial(convolve, groups, blocks, True),
         *args,
     )
 

time: 60.6 us -> 60.9 us (level)
  blocking collectives: 35 us -> 14.7 us
  waiting for transfers between devices: 16.8 us -> 31.9 us
  starting transfers between devices: 4.1 us -> 7.65 us
  local copies, waits for them, and re-layouts: 0.75 us -> 1.74 us
  Pallas kernels: 3.4 us -> 4.3 us
    all_to_all x1 -> x0, blocking collectives: 18.4 us -> none  [exchange(): return lax.all_to_all(pair, axes, 0, 0, axis_index_groups=sides, tiled=True)]
    all_to_all x0 -> x1, waiting for transfers between devices: none -> 15.1 us  [exchange_halved(): lax.all_to_all(array.reshape(count // 2, 2 * height, LANES), axes, 0, 0,...]
    all_to_all x0 -> x1, starting transfers between devices: none -> 6.2 us  [exchange_halved(): lax.all_to_all(array.reshape(count // 2, 2 * height, LANES), axes, 0, 0,...]
    ppermute x1, starting transfers between devices: 4.1 us -> 1.46 us  [exchange_halved(): other = lax.ppermute(jnp.where(low, to_high, to_low), 'seq', swap)]
    all_to_all x1, blocking collectives: 16.6 us -> 14.7 us  [exchange(): return lax.all_to_all(array, axes, 0, 0, tiled=True)]
    cond x16, local copies, waits for them, and re-layouts: 0.05 us -> 1.04 us
    pallas_call x2, Pallas kernels: 3.2 us -> 4.1 us  [the longest x1 2.28 us: convolve(): call(functools.partial(pack_kernel, layout, halved), [((count, own * (row...]
  transfers between devices with their start and end apart: 1 -> 2, of which waited for: 1 -> 2; matrix products, arithmetic and copies ran while one was open for 0% -> 0% of each run, Pallas kernels for 0% -> 0%
where the time goes in v11:
time: 60.9 us; the launch traced here: 60.6 us
  waiting for transfers between devices  31.9 us (52%)
  blocking collectives  14.7 us (24%)
  starting transfers between devices  7.65 us (13%)
  Pallas kernels  4.3 us (7%)
  local copies, waits for them, and re-layouts  1.74 us (3%)
    ppermute x1, waiting for transfers between devices, exchange_halved(): other = lax.ppermute(jnp.where(low, to_high, to_low), 'seq', swap)  16.8 us
    all_to_all x1, waiting for transfers between devices, exchange_halved(): lax.all_to_all(array.reshape(count // 2, 2 * height, LANES), axes, 0, 0,...  15.1 us
    all_to_all x1, blocking collectives, exchange(): return lax.all_to_all(array, axes, 0, 0, tiled=True)  14.7 us
    all_to_all x1, starting transfers between devices, exchange_halved(): lax.all_to_all(array.reshape(count // 2, 2 * height, LANES), axes, 0, 0,...  6.2 us
    pallas_call x1, Pallas kernels, convolve(): call(functools.partial(pack_kernel, layout, halved), [((count, own * (row...  2.28 us
    pallas_call x1, Pallas kernels, convolve(): call(functools.partial(conv_kernel, layout, halved, min(own, 2)), [((coun...  1.81 us
    ppermute x1, starting transfers between devices, exchange_halved(): other = lax.ppermute(jnp.where(low, to_high, to_low), 'seq', swap)  1.46 us
  transfers between devices with their start and end apart: 2, of which 2 were waited for; matrix products, arithmetic and copies ran while one was open for 0% of the time, Pallas kernels for 0%

profile of v11, /device:TPU:0, one launch (start us, length us, event | category | flops | bytes accessed | tf_op | source)
XLA Modules:
  0.0 60.6 jit_solution(2068275597657077894)
XLA Ops:
  0.0 59.9 %conditional.1 = (bf16[1024,128]{1,0:T(8,128)(2,1)S(1)}) conditional(s32[]{:T(128)} %convert_element_type.3, (f32[128]{0:T(128)}, bf16[1024,128]{1,0:T(8,128)(2,1)}, bf16[1024,128]{1,0:T(8,128)(2,1)}, f32[1024,128]{1,0:T(8,128)}, bf16[128,192]{1,0:T(8,128)(2,1)}, /*index=5*/f32[64,256]{1,0:T(8,128)}, bf16[768,256]{1,0:T(8,128)(2,1)}, ...), branch_computations={%region_0.1_spmd, %region_1.2_spmd} | conditional | flops 1259536384 | bytes 21430652 | solution.py:276
  0.0 2.3 %branch_0_fun.3 = (f32[16,96,128]{2,1,0:T(8,128)}, f32[1,128]{1,0:T(1,128)S(1)}) custom-call(s32[1]{0:T(128)} %bitcast.where_ref, bf16[1024,128]{1,0:T(8,128)(2,1)} %get-tuple-element.48.key_ref, bf16[1024,128]{1,0:T(8,128)(2,1)} %get-tuple-element.49.value_ref, f32[1024,128]{1,0:T(8,128)} %get-tuple-element.50.filter_ref, f32[1,128]{1,0:T(1,128)} %bitcast.9), custom_call_target="tpu_custom_call" | custom-call | flops 131072 | bytes 1572864 | tf_op jit(solution)/shard_map/cond/branch_0_fun/pallas_call | solution.py:255
  2.3 6.2 %all-to-all-start.2 = ((f32[8,192,128]{2,1,0:T(8,128)}), f32[8,192,128]{2,1,0:T(8,128)S(1)}, u32[]{:S(2)}, u32[]{:S(2)}) async-start(f32[8,192,128]{2,1,0:T(8,128)} %bitcast.2), calls=%async_computation.2 | async-start | bytes 1572864 | tf_op jit(solution)/shard_map/cond/branch_0_fun/all_to_all | solution.py:244
  8.5 15.1 %all-to-all-done.2 = f32[8,192,128]{2,1,0:T(8,128)S(1)} async-done(((f32[8,192,128]{2,1,0:T(8,128)}), f32[8,192,128]{2,1,0:T(8,128)S(1)}, u32[]{:S(2)}, u32[]{:S(2)}) %all-to-all-start.2) | async-done | bytes 786464 | tf_op jit(solution)/shard_map/cond/branch_0_fun/all_to_all | solution.py:244
  23.7 1.5 %collective-permute-start = (f32[8,96,128]{2,1,0:T(8,128)S(1)}, f32[8,96,128]{2,1,0:T(8,128)S(1)}, u32[]{:S(2)}, u32[]{:S(2)}) collective-permute-start(f32[8,96,128]{2,1,0:T(8,128)S(1)} %slice_select_fusion), channel_id=1, source_target_pairs={{0,8},{2,10},{4,12},{6,14},{8,0},{10,2},{12,4},{14,6},{1,9},{3,11}... | collective-permute-start | bytes 1179656 | tf_op jit(solution)/shard_map/cond/branch_0_fun/ppermute | solution.py:251
  25.1 16.8 %collective-permute-done = f32[8,96,128]{2,1,0:T(8,128)S(1)} collective-permute-done((f32[8,96,128]{2,1,0:T(8,128)S(1)}, f32[8,96,128]{2,1,0:T(8,128)S(1)}, u32[]{:S(2)}, u32[]{:S(2)}) %collective-permute-start) | collective-permute-done | bytes 393248 | tf_op jit(solution)/shard_map/cond/branch_0_fun/ppermute | solution.py:251
  41.9 0.1 broadcast_select_fusion.1
  42.0 0.0 copy-start.7
  42.0 0.0 copy-start.9
  42.0 0.0 copy-start.11
  42.0 0.0 copy-start.13
  42.0 0.0 copy-start.15
  42.0 0.1 pad_maximum_fusion.moved_ref
  42.1 0.9 %copy-done.7 = bf16[768,256]{1,0:T(8,128)(2,1)S(1)} copy-done((bf16[768,256]{1,0:T(8,128)(2,1)S(1)}, bf16[768,256]{1,0:T(8,128)(2,1)}, u32[]{:S(2)}) %copy-start.7) | copy-done | bytes 393240 | tf_op jit(solution)/shard_map/cond
  43.0 0.1 copy-done.9
  43.1 0.0 copy-done.11
  43.1 0.0 copy-done.13
  43.1 0.0 copy-done.15
  43.1 1.8 %branch_0_fun.4 = f32[16,64,128]{2,1,0:T(8,128)S(1)} custom-call(f32[8,192,128]{2,1,0:T(8,128)S(1)} %pad_maximum_fusion.moved_ref, bf16[128,192]{1,0:T(8,128)(2,1)S(1)} %copy-done.15, f32[64,256]{1,0:T(8,128)S(1)} %copy-done.13, bf16[768,256]{1,0:T(8,128)(2,1)S(1)} %copy-done.9, bf16[768,256]{1,0:T(8,128)(2,1)S(1)} %copy-done.7, bf16[128,256]{1,0:T(8,128)(2,1)S(1)} %copy-done.11), custom_call_target="tpu_custom_call" | custom-call | flops 1258291200 | bytes 1572864 | tf_op jit(solution)/shard_map/cond/branch_0_fun/pallas_call | solution.py:263
  44.9 0.0 copy-start
  44.9 0.0 copy-start.2
  44.9 0.0 copy-start.4
  44.9 14.7 %all_to_all.16 = f32[16,64,128]{2,1,0:T(8,128)S(1)} all-to-all(f32[16,64,128]{2,1,0:T(8,128)S(1)} %branch_0_fun.4), channel_id=1, replica_groups=mesh['groups'=2,'seq'=8,'chan'=2] {'groups','seq'}, dimensions={0} | all-to-all | bytes 1048576 | tf_op jit(solution)/shard_map/cond/branch_0_fun/all_to_all | solution.py:236
  59.7 0.0 copy-done
  59.7 0.0 copy-done.2
  59.7 0.0 copy-done.4
  59.7 0.2 branch_0_fun.5
  59.9 0.0 copy-start.6
  59.9 0.7 %copy-done.6 = bf16[1024,128]{1,0:T(8,128)(2,1)} copy-done((bf16[1024,128]{1,0:T(8,128)(2,1)}, bf16[1024,128]{1,0:T(8,128)(2,1)S(1)}, u32[]{:S(2)}) %copy-start.6) | copy-done | bytes 262168
  (1 shorter events, 0.0 us)
Async XLA Ops:
  2.3 21.3 %all-to-all-start.2 = ((f32[8,192,128]{2,1,0:T(8,128)}), f32[8,192,128]{2,1,0:T(8,128)S(1)}, u32[]{:S(2)}, u32[]{:S(2)}) async-start(f32[8,192,128]{2,1,0:T(8,128)} %bitcast.2), calls=%async_computation.2 | async-start | bytes 1572864 | tf_op jit(solution)/shard_map/cond/branch_0_fun/all_to_all | solution.py:244
  23.7 18.2 %collective-permute-start = (f32[8,96,128]{2,1,0:T(8,128)S(1)}, f32[8,96,128]{2,1,0:T(8,128)S(1)}, u32[]{:S(2)}, u32[]{:S(2)}) collective-permute-start(f32[8,96,128]{2,1,0:T(8,128)S(1)} %slice_select_fusion), channel_id=1, source_target_pairs={{0,8},{2,10},{4,12},{6,14},{8,0},{10,2},{12,4},{14,6},{1,9},{3,11}... | collective-permute-start | bytes 1179656 | tf_op jit(solution)/shard_map/cond/branch_0_fun/ppermute | solution.py:251
  42.0 1.0 %copy-start.7 = (bf16[768,256]{1,0:T(8,128)(2,1)S(1)}, bf16[768,256]{1,0:T(8,128)(2,1)}, u32[]{:S(2)}) copy-start(bf16[768,256]{1,0:T(8,128)(2,1)} %get-tuple-element.56.back_tail_ref) | copy-start | bytes 1179652 | tf_op jit(solution)/shard_map/cond
  42.0 1.1 %copy-start.9 = (bf16[768,256]{1,0:T(8,128)(2,1)S(1)}, bf16[768,256]{1,0:T(8,128)(2,1)}, u32[]{:S(2)}) copy-start(bf16[768,256]{1,0:T(8,128)(2,1)} %get-tuple-element.55.tail_ref) | copy-start | bytes 1179652 | tf_op jit(solution)/shard_map/cond
  42.0 1.1 %copy-start.11 = (bf16[128,256]{1,0:T(8,128)(2,1)S(1)}, bf16[128,256]{1,0:T(8,128)(2,1)}, u32[]{:S(2)}) copy-start(bf16[128,256]{1,0:T(8,128)(2,1)} %get-tuple-element.57.back_head_ref) | copy-start | bytes 196612 | tf_op jit(solution)/shard_map/cond
  42.0 1.1 %copy-start.13 = (f32[64,256]{1,0:T(8,128)S(1)}, f32[64,256]{1,0:T(8,128)}, u32[]{:S(2)}) copy-start(f32[64,256]{1,0:T(8,128)} %get-tuple-element.54.twist_ref) | copy-start | bytes 196612 | tf_op jit(solution)/shard_map/cond
  42.0 1.1 %copy-start.15 = (bf16[128,192]{1,0:T(8,128)(2,1)S(1)}, bf16[128,192]{1,0:T(8,128)(2,1)}, u32[]{:S(2)}) copy-start(bf16[128,192]{1,0:T(8,128)(2,1)} %get-tuple-element.53.head_ref) | copy-start | bytes 147460 | tf_op jit(solution)/shard_map/cond
  44.9 14.8 %copy-start = (bf16[1024,128]{1,0:T(8,128)(2,1)S(1)}, bf16[1024,128]{1,0:T(8,128)(2,1)}, u32[]{:S(2)}) copy-start(bf16[1024,128]{1,0:T(8,128)(2,1)} %get-tuple-element.48.key_ref) | copy-start | bytes 786436 | tf_op jit(solution)/shard_map/cond
  44.9 14.8 %copy-start.2 = (bf16[1024,128]{1,0:T(8,128)(2,1)S(1)}, bf16[1024,128]{1,0:T(8,128)(2,1)}, u32[]{:S(2)}) copy-start(bf16[1024,128]{1,0:T(8,128)(2,1)} %get-tuple-element.49.value_ref) | copy-start | bytes 786436 | tf_op jit(solution)/shard_map/cond
  44.9 14.8 %copy-start.4 = (bf16[1024,128]{1,0:T(8,128)(2,1)S(1)}, bf16[1024,128]{1,0:T(8,128)(2,1)}, u32[]{:S(2)}) copy-start(bf16[1024,128]{1,0:T(8,128)(2,1)} %get-tuple-element.58.query_ref) | copy-start | bytes 786436 | tf_op jit(solution)/shard_map/cond
  59.9 0.7 %copy-start.6 = (bf16[1024,128]{1,0:T(8,128)(2,1)}, bf16[1024,128]{1,0:T(8,128)(2,1)S(1)}, u32[]{:S(2)}) copy-start(bf16[1024,128]{1,0:T(8,128)(2,1)S(1)} %get-tuple-element.80) | copy-start | bytes 786436

commit v12 on v8

--- a/solution.py
+++ b/solution.py
@@ -181,13 +181,25 @@
             ].reshape(blocks, rows, LANES)
 
 
-def gate_kernel(rows, conv_ref, query_ref, key_ref, value_ref, bias_ref, out_ref):
+def gate_kernel(rows, conv_ref, query_ref, key_ref, value_ref, bias_ref, out_ref, gated, sems):
     bias = bias_ref[...]
+    half = rows * LANES // 2
+    stores = [
+        pltpu.make_async_copy(gated.at[pl.ds(idx * half, half)], out_ref.at[pl.ds(idx * half, half)], sems.at[idx])
+        for idx in range(2)
+    ]
     for row in range(rows):
         span = pl.ds(row * LANES, LANES)
         driver = key_ref[span, :].astype(F32) * value_ref[span, :].astype(F32)
         convolved = conv_ref[pl.ds(row, LANES, stride=rows), :].T
-        out_ref[span, :] = (query_ref[span, :].astype(F32) * (convolved + bias * driver)).astype(BF16)
+        gated[span, :] = (query_ref[span, :].astype(F32) * (convolved + bias * driver)).astype(BF16)
+        if (row + 1) * LANES == half:
+            stores[0].start()
+    if rows % 2:
+        stores[0].start()
+    stores[1].start()
+    for store in stores:
+        store.wait()
 
 
 VMEM = pl.BlockSpec(memory_space=pltpu.VMEM)
@@ -246,20 +258,26 @@
     else:
         moved = exchange(packed)
     local = call(
-        functools.partial(conv_kernel, layout, staged, min(own, 2)),
+        functools.partial(conv_kernel, layout, staged, min(own, 4)),
         [((count, own * rows, LANES), F32)], [VMEM] * 6, 5 * macs, 3 * size,
     )(moved, head, twist, tail, back_tail, back_head)[0]
     convolved = exchange(local).reshape(chans * rows, LANES)
-    return call(functools.partial(gate_kernel, rows), [((tokens, chans), BF16)], [VMEM] * 5, size, 3 * size)(
-        convolved, query_proj, key_proj, value_proj, bias
-    )[0]
+    return pl.pallas_call(
+        functools.partial(gate_kernel, rows),
+        out_shape=pltpu.HBM((tokens, chans), BF16),
+        in_specs=[VMEM] * 5,
+        out_specs=HBM,
+        scratch_shapes=[pltpu.VMEM((tokens, chans), BF16), pltpu.SemaphoreType.DMA((2,))],
+        compiler_params=pltpu.CompilerParams(vmem_limit_bytes=VMEM_LIMIT),
+        cost_estimate=pl.CostEstimate(flops=size, bytes_accessed=3 * size, transcendentals=0),
+    )(convolved, query_proj, key_proj, value_proj, bias)
 
 
 def shards(groups, blocks, cores, *args):
     if cores == 1 or groups != 2:
         return convolve(groups, blocks, False, *args)
     return lax.cond(
-        lax.axis_index("chan") % 2 == 1,
+        lax.axis_index("chan") % 2 == 0,
         functools.partial(convolve, groups, blocks, False),
         functools.partial(convolve, groups, blocks, True),
         *args,

time: 48.6 us -> 53 us (1.091)
  blocking collectives: 35.1 us -> 48.6 us
  waiting for transfers between devices: 5.76 us -> 0 us
  starting transfers between devices: 3 us -> 0 us
  local copies, waits for them, and re-layouts: 0.75 us -> 0.05 us
  Pallas kernels: 3.4 us -> 4.06 us
    all_to_all x1 -> x2, blocking collectives: 15.7 us -> 48.6 us  [exchange(): return lax.all_to_all(array, axes, 0, 0, tiled=True)]
    all_to_all x1 -> x0, blocking collectives: 19.4 us -> none  [convolve(): moved = lax.all_to_all(pair, 'seq', 0, 0, tiled=True)]
    ppermute x1 -> x0, waiting for transfers between devices: 5.76 us -> none  [convolve(): lax.ppermute(jnp.where(first, by_group[1], by_group[0]), 'groups', [(0, 1...]
    ppermute x1 -> x0, starting transfers between devices: 3 us -> none  [convolve(): lax.ppermute(jnp.where(first, by_group[1], by_group[0]), 'groups', [(0, 1...]
    unnamed x2 -> x0, local copies, waits for them, and re-layouts: 0.7 us -> none
    pallas_call x2, Pallas kernels: 1.99 us -> 2.65 us  [the longest x1 1.77 us: convolve(): call(functools.partial(conv_kernel, layout, staged, min(own, 4)), [((coun...]
  transfers between devices with their start and end apart: 1 -> 0, of which waited for: 1 -> 0; matrix products, arithmetic and copies ran while one was open for 0% -> 0% of each run, Pallas kernels for 0% -> 0%
where the time goes in v12:
time: 53 us; the launch traced here: 52.8 us
  blocking collectives  48.6 us (92%)
  Pallas kernels  4.06 us (8%)
    all_to_all x2, blocking collectives, exchange(): return lax.all_to_all(array, axes, 0, 0, tiled=True)  48.6 us
    pallas_call x1, Pallas kernels, convolve(): call(functools.partial(conv_kernel, layout, staged, min(own, 4)), [((coun...  1.77 us
    pallas_call x1, Pallas kernels, convolve(): call(functools.partial(pack_kernel, layout), [((count, own * (rows + part...  1.4 us

profile of v12, /device:TPU:0, one launch (start us, length us, event | category | flops | bytes accessed | tf_op | source)
XLA Modules:
  0.0 52.8 jit_solution(18140780001075051613)
XLA Ops:
  0.0 52.8 %conditional.1 = (bf16[1024,128]{1,0:T(8,128)(2,1)}) conditional(s32[]{:T(128)} %convert_element_type.3, (f32[128]{0:T(128)}, bf16[1024,128]{1,0:T(8,128)(2,1)}, bf16[1024,128]{1,0:T(8,128)(2,1)}, f32[1024,128]{1,0:T(8,128)}, bf16[128,192]{1,0:T(8,128)(2,1)}, /*index=5*/f32[64,256]{1,0:T(8,128)}, bf16[768,256]{1,0:T(8,128)(2,1)}, ...), branch_computations={%region_0.1_spmd, %region_1.2_spmd} | conditional | flops 1259536384 | bytes 20644156 | solution.py:279
  0.0 1.4 %branch_1_fun.3 = (f32[16,96,128]{2,1,0:T(8,128)S(1)}, f32[1,128]{1,0:T(1,128)S(1)}) custom-call(s32[1]{0:T(128)} %bitcast.3.where_ref, bf16[1024,128]{1,0:T(8,128)(2,1)} %get-tuple-element.60.key_ref, bf16[1024,128]{1,0:T(8,128)(2,1)} %get-tuple-element.61.value_ref, f32[1024,128]{1,0:T(8,128)} %get-tuple-element.62.filter_ref, f32[1,128]{1,0:T(1,128)} %bitcast.9), custom_call_target="tpu_custom_call" | custom-call | flops 131072 | bytes 1572864 | tf_op jit(solution)/shard_map/cond/branch_1_fun/pallas_call | solution.py:242
  1.4 0.0 copy-start.7
  1.4 0.0 copy-start.9
  1.4 0.0 copy-start.11
  1.5 0.0 copy-start.13
  1.5 0.0 copy-start.15
  1.5 28.2 %all_to_all.18.moved_ref = f32[16,96,128]{2,1,0:T(8,128)S(1)} all-to-all(f32[16,96,128]{2,1,0:T(8,128)S(1)} %get-tuple-element.64), channel_id=1, replica_groups=mesh['groups'=2,'seq'=8,'chan'=2] {'groups','seq'}, dimensions={0} | all-to-all | bytes 1572864 | tf_op jit(solution)/shard_map/cond/branch_1_fun/all_to_all | solution.py:239
  29.7 0.0 copy-done.7
  29.7 0.0 copy-done.9
  29.7 0.0 copy-done.11
  29.7 0.0 copy-done.13
  29.7 0.0 copy-done.15
  29.7 1.8 %branch_1_fun.4 = f32[16,64,128]{2,1,0:T(8,128)S(1)} custom-call(f32[16,96,128]{2,1,0:T(8,128)S(1)} %all_to_all.18.moved_ref, bf16[128,192]{1,0:T(8,128)(2,1)S(1)} %copy-done.15, f32[64,256]{1,0:T(8,128)S(1)} %copy-done.13, bf16[768,256]{1,0:T(8,128)(2,1)S(1)} %copy-done.9, bf16[768,256]{1,0:T(8,128)(2,1)S(1)} %copy-done.7, bf16[128,256]{1,0:T(8,128)(2,1)S(1)} %copy-done.11), custom_call_target="tpu_custom_call" | custom-call | flops 1258291200 | bytes 1572864 | tf_op jit(solution)/shard_map/cond/branch_1_fun/pallas_call | solution.py:260
  31.5 0.0 copy-start.1
  31.5 0.0 copy-start.3
  31.5 0.0 copy-start.5
  31.6 20.3 %all_to_all.19 = f32[16,64,128]{2,1,0:T(8,128)S(1)} all-to-all(f32[16,64,128]{2,1,0:T(8,128)S(1)} %branch_1_fun.4), channel_id=1, replica_groups=mesh['groups'=2,'seq'=8,'chan'=2] {'groups','seq'}, dimensions={0} | all-to-all | bytes 1048576 | tf_op jit(solution)/shard_map/cond/branch_1_fun/all_to_all | solution.py:239
  51.9 0.0 copy-done.1
  51.9 0.0 copy-done.3
  51.9 0.0 copy-done.5
  51.9 0.9 %branch_1_fun.5 = bf16[1024,128]{1,0:T(8,128)(2,1)} custom-call(f32[1024,128]{1,0:T(8,128)S(1)} %bitcast.7, bf16[1024,128]{1,0:T(8,128)(2,1)S(1)} %copy-done.5, bf16[1024,128]{1,0:T(8,128)(2,1)S(1)} %copy-done.1, bf16[1024,128]{1,0:T(8,128)(2,1)S(1)} %copy-done.3, f32[1,128]{1,0:T(1,128)S(1)} %get-tuple-element.71.bias_ref), custom_call_target="tpu_custom_call" | custom-call | flops 524288 | bytes 1572864 | tf_op jit(solution)/shard_map/cond/branch_1_fun/pallas_call | solution.py:265
Async XLA Ops:
  1.4 28.3 %copy-start.7 = (bf16[768,256]{1,0:T(8,128)(2,1)S(1)}, bf16[768,256]{1,0:T(8,128)(2,1)}, u32[]{:S(2)}) copy-start(bf16[768,256]{1,0:T(8,128)(2,1)} %get-tuple-element.68.back_tail_ref) | copy-start | bytes 1179652 | tf_op jit(solution)/shard_map/cond
  1.4 28.3 %copy-start.9 = (bf16[768,256]{1,0:T(8,128)(2,1)S(1)}, bf16[768,256]{1,0:T(8,128)(2,1)}, u32[]{:S(2)}) copy-start(bf16[768,256]{1,0:T(8,128)(2,1)} %get-tuple-element.67.tail_ref) | copy-start | bytes 1179652 | tf_op jit(solution)/shard_map/cond
  1.4 28.3 %copy-start.11 = (bf16[128,256]{1,0:T(8,128)(2,1)S(1)}, bf16[128,256]{1,0:T(8,128)(2,1)}, u32[]{:S(2)}) copy-start(bf16[128,256]{1,0:T(8,128)(2,1)} %get-tuple-element.69.back_head_ref) | copy-start | bytes 196612 | tf_op jit(solution)/shard_map/cond
  1.5 28.3 %copy-start.13 = (f32[64,256]{1,0:T(8,128)S(1)}, f32[64,256]{1,0:T(8,128)}, u32[]{:S(2)}) copy-start(f32[64,256]{1,0:T(8,128)} %get-tuple-element.66.twist_ref) | copy-start | bytes 196612 | tf_op jit(solution)/shard_map/cond
  1.5 28.3 %copy-start.15 = (bf16[128,192]{1,0:T(8,128)(2,1)S(1)}, bf16[128,192]{1,0:T(8,128)(2,1)}, u32[]{:S(2)}) copy-start(bf16[128,192]{1,0:T(8,128)(2,1)} %get-tuple-element.65.head_ref) | copy-start | bytes 147460 | tf_op jit(solution)/shard_map/cond
  31.5 20.4 %copy-start.1 = (bf16[1024,128]{1,0:T(8,128)(2,1)S(1)}, bf16[1024,128]{1,0:T(8,128)(2,1)}, u32[]{:S(2)}) copy-start(bf16[1024,128]{1,0:T(8,128)(2,1)} %get-tuple-element.60.key_ref) | copy-start | bytes 786436 | tf_op jit(solution)/shard_map/cond
  31.5 20.4 %copy-start.3 = (bf16[1024,128]{1,0:T(8,128)(2,1)S(1)}, bf16[1024,128]{1,0:T(8,128)(2,1)}, u32[]{:S(2)}) copy-start(bf16[1024,128]{1,0:T(8,128)(2,1)} %get-tuple-element.61.value_ref) | copy-start | bytes 786436 | tf_op jit(solution)/shard_map/cond
  31.5 20.4 %copy-start.5 = (bf16[1024,128]{1,0:T(8,128)(2,1)S(1)}, bf16[1024,128]{1,0:T(8,128)(2,1)}, u32[]{:S(2)}) copy-start(bf16[1024,128]{1,0:T(8,128)(2,1)} %get-tuple-element.70.query_ref) | copy-start | bytes 786436 | tf_op jit(solution)/shard_map/cond

commit v13 on v12

--- a/solution.py
+++ b/solution.py
@@ -103,23 +103,27 @@
     rows, own, part, groups = layout
     first = where_ref[0] * (part * LANES if part < rows else 0)
     taken = filter_ref.at[pl.ds(pl.multiple_of(first, part * LANES), part * LANES)]
-    pairs = ((key_ref, key), (value_ref, value), (taken, taps), (bias_ref, bias_out))
+    cuts = 2 if rows % 2 == 0 else 1
+    spans = [pl.ds(cut * rows // cuts * LANES, rows // cuts * LANES) for cut in range(cuts)]
+    pairs = [(source.at[span], held.at[span]) for span in spans for source, held in ((key_ref, key), (value_ref, value))]
+    pairs += [(taken, taps), (bias_ref, bias_out)]
     fetches = [pltpu.make_async_copy(*pair, sems.at[idx]) for idx, pair in enumerate(pairs)]
     for fetch in fetches:
         fetch.start()
-    fetches[0].wait()
-    fetches[1].wait()
     for row in range(rows):
+        if row % (rows // cuts) == 0:
+            for fetch in fetches[row // (rows // cuts) * 2 :][:2]:
+                fetch.wait()
         span = pl.ds(row * LANES, LANES)
         turned = (key[span, :].astype(F32) * value[span, :].astype(F32)).T
         for peer in range(out_ref.shape[0]):
             out_ref[peer, pl.ds(row, own, stride=rows), :] = turned[peer * own : (peer + 1) * own]
-    fetches[2].wait()
+    fetches[-2].wait()
     for row in range(part):
         turned = taps[pl.ds(row * LANES, LANES), :].T
         for peer in range(out_ref.shape[0]):
             out_ref[peer, pl.ds(own * rows + row, own, stride=part), :] = turned[peer * own : (peer + 1) * own]
-    fetches[3].wait()
+    fetches[-1].wait()
 
 
 def arrived(layout, staged, moved_ref, group, start, height):
@@ -244,7 +248,7 @@
         [((count, own * (rows + part), LANES), F32), ((1, chans), F32)],
         [SMEM] + [HBM] * 4, size // 4, size * 3,
         [pltpu.VMEM((tokens, chans), BF16), pltpu.VMEM((tokens, chans), BF16), pltpu.VMEM((part * LANES, chans), F32),
-         pltpu.SemaphoreType.DMA((4,))],
+         pltpu.SemaphoreType.DMA((6,))],
     )(where, *(pltpu.with_memory_space_constraint(source, pltpu.HBM) for source in sources))
     if staged:
         mine = lax.axis_index("groups")
@@ -277,7 +281,7 @@
     if cores == 1 or groups != 2:
         return convolve(groups, blocks, False, *args)
     return lax.cond(
-        lax.axis_index("chan") % 2 == 0,
+        lax.axis_index("chan") % 2 == 1,
         functools.partial(convolve, groups, blocks, False),
         functools.partial(convolve, groups, blocks, True),
         *args,

time: 53 us -> 48.5 us (0.915)
  blocking collectives: 48.6 us -> 35.1 us
  waiting for transfers between devices: 0 us -> 5.76 us
  starting transfers between devices: 0 us -> 3 us
    all_to_all x2 -> x1, blocking collectives: 48.6 us -> 15.7 us  [exchange(): return lax.all_to_all(array, axes, 0, 0, tiled=True)]
    all_to_all x0 -> x1, blocking collectives: none -> 19.4 us  [convolve(): moved = lax.all_to_all(pair, 'seq', 0, 0, tiled=True)]
    ppermute x0 -> x1, waiting for transfers between devices: none -> 5.76 us  [convolve(): lax.ppermute(jnp.where(first, by_group[1], by_group[0]), 'groups', [(0, 1...]
    ppermute x0 -> x1, starting transfers between devices: none -> 3 us  [convolve(): lax.ppermute(jnp.where(first, by_group[1], by_group[0]), 'groups', [(0, 1...]
  transfers between devices with their start and end apart: 0 -> 1, of which waited for: 0 -> 1; matrix products, arithmetic and copies ran while one was open for 0% -> 0% of each run, Pallas kernels for 0% -> 0%
where the time goes in v13:
time: 48.5 us; the launch traced here: 48.3 us
  blocking collectives  35.1 us (72%)
  waiting for transfers between devices  5.76 us (12%)
  Pallas kernels  4.09 us (8%)
  starting transfers between devices  3 us (6%)
    all_to_all x1, blocking collectives, convolve(): moved = lax.all_to_all(pair, 'seq', 0, 0, tiled=True)  19.4 us
    all_to_all x1, blocking collectives, exchange(): return lax.all_to_all(array, axes, 0, 0, tiled=True)  15.7 us
    ppermute x1, waiting for transfers between devices, convolve(): lax.ppermute(jnp.where(first, by_group[1], by_group[0]), 'groups', [(0, 1...  5.76 us
    ppermute x1, starting transfers between devices, convolve(): lax.ppermute(jnp.where(first, by_group[1], by_group[0]), 'groups', [(0, 1...  3 us
    pallas_call x1, Pallas kernels, convolve(): call(functools.partial(conv_kernel, layout, staged, min(own, 4)), [((coun...  1.77 us
    pallas_call x1, Pallas kernels, convolve(): call(functools.partial(pack_kernel, layout), [((count, own * (rows + part...  1.43 us
  transfers between devices with their start and end apart: 1, of which 1 were waited for; matrix products, arithmetic and copies ran while one was open for 0% of the time, Pallas kernels for 0%

profile of v13, /device:TPU:0, one launch (start us, length us, event | category | flops | bytes accessed | tf_op | source)
XLA Modules:
  0.0 48.3 jit_solution(5979426745798405203)
XLA Ops:
  0.0 48.3 %conditional.1 = (bf16[1024,128]{1,0:T(8,128)(2,1)}) conditional(s32[]{:T(128)} %convert_element_type.3, (f32[128]{0:T(128)}, bf16[1024,128]{1,0:T(8,128)(2,1)}, bf16[1024,128]{1,0:T(8,128)(2,1)}, f32[1024,128]{1,0:T(8,128)}, bf16[128,192]{1,0:T(8,128)(2,1)}, /*index=5*/f32[64,256]{1,0:T(8,128)}, bf16[768,256]{1,0:T(8,128)(2,1)}, ...), branch_computations={%region_0.1_spmd, %region_1.2_spmd} | conditional | flops 1259536384 | bytes 20644156 | solution.py:283
  0.0 1.4 %branch_0_fun.3 = (f32[16,96,128]{2,1,0:T(8,128)S(1)}, f32[1,128]{1,0:T(1,128)S(1)}) custom-call(s32[1]{0:T(128)} %bitcast.where_ref, bf16[1024,128]{1,0:T(8,128)(2,1)} %get-tuple-element.48.key_ref, bf16[1024,128]{1,0:T(8,128)(2,1)} %get-tuple-element.49.value_ref, f32[1024,128]{1,0:T(8,128)} %get-tuple-element.50.filter_ref, f32[1,128]{1,0:T(1,128)} %bitcast.8), custom_call_target="tpu_custom_call" | custom-call | flops 131072 | bytes 1572864 | tf_op jit(solution)/shard_map/cond/branch_0_fun/pallas_call | solution.py:246
  1.5 3.0 %collective-permute-start = (f32[8,96,128]{2,1,0:T(8,128)S(1)}, f32[8,96,128]{2,1,0:T(8,128)S(1)}, u32[]{:S(2)}, u32[]{:S(2)}) collective-permute-start(f32[8,96,128]{2,1,0:T(8,128)S(1)} %slice_select_fusion), channel_id=1, source_target_pairs={{0,16},{16,0},{1,17},{17,1},{2,18},{18,2},{3,19},{19,3},{4,20},{20... | collective-permute-start | bytes 1179656 | tf_op jit(solution)/shard_map/cond/branch_0_fun/ppermute | solution.py:259
  4.5 5.8 %collective-permute-done = f32[8,96,128]{2,1,0:T(8,128)S(1)} collective-permute-done((f32[8,96,128]{2,1,0:T(8,128)S(1)}, f32[8,96,128]{2,1,0:T(8,128)S(1)}, u32[]{:S(2)}, u32[]{:S(2)}) %collective-permute-start) | collective-permute-done | bytes 393248 | tf_op jit(solution)/shard_map/cond/branch_0_fun/ppermute | solution.py:259
  10.3 0.1 broadcast_select_fusion.1
  10.3 0.1 pad_maximum_fusion
  10.4 0.0 copy-start.6
  10.4 0.0 copy-start.8
  10.4 0.0 copy-start.10
  10.4 0.0 copy-start.12
  10.5 0.0 copy-start.14
  10.5 19.4 %all_to_all.16.moved_ref = f32[8,192,128]{2,1,0:T(8,128)S(1)} all-to-all(f32[8,192,128]{2,1,0:T(8,128)S(1)} %pad_maximum_fusion), channel_id=1, replica_groups=mesh['groups'=2,'seq'=8,'chan'=2] {'seq'}, dimensions={0} | all-to-all | bytes 1572864 | tf_op jit(solution)/shard_map/cond/branch_0_fun/all_to_all | solution.py:261
  29.9 0.0 copy-done.6
  29.9 0.0 copy-done.8
  29.9 0.0 copy-done.10
  29.9 0.0 copy-done.12
  29.9 0.0 copy-done.14
  29.9 1.8 %branch_0_fun.4 = f32[16,64,128]{2,1,0:T(8,128)S(1)} custom-call(f32[8,192,128]{2,1,0:T(8,128)S(1)} %all_to_all.16.moved_ref, bf16[128,192]{1,0:T(8,128)(2,1)S(1)} %copy-done.14, f32[64,256]{1,0:T(8,128)S(1)} %copy-done.12, bf16[768,256]{1,0:T(8,128)(2,1)S(1)} %copy-done.8, bf16[768,256]{1,0:T(8,128)(2,1)S(1)} %copy-done.6, bf16[128,256]{1,0:T(8,128)(2,1)S(1)} %copy-done.10), custom_call_target="tpu_custom_call" | custom-call | flops 1258291200 | bytes 1572864 | tf_op jit(solution)/shard_map/cond/branch_0_fun/pallas_call | solution.py:264
  31.7 0.0 copy-start
  31.7 0.0 copy-start.2
  31.7 0.0 copy-start.4
  31.7 15.7 %all_to_all.17 = f32[16,64,128]{2,1,0:T(8,128)S(1)} all-to-all(f32[16,64,128]{2,1,0:T(8,128)S(1)} %branch_0_fun.4), channel_id=1, replica_groups=mesh['groups'=2,'seq'=8,'chan'=2] {'groups','seq'}, dimensions={0} | all-to-all | bytes 1048576 | tf_op jit(solution)/shard_map/cond/branch_0_fun/all_to_all | solution.py:243
  47.4 0.0 copy-done
  47.4 0.0 copy-done.2
  47.4 0.0 copy-done.4
  47.4 0.9 %branch_0_fun.5 = bf16[1024,128]{1,0:T(8,128)(2,1)} custom-call(f32[1024,128]{1,0:T(8,128)S(1)} %bitcast.6, bf16[1024,128]{1,0:T(8,128)(2,1)S(1)} %copy-done.4, bf16[1024,128]{1,0:T(8,128)(2,1)S(1)} %copy-done, bf16[1024,128]{1,0:T(8,128)(2,1)S(1)} %copy-done.2, f32[1,128]{1,0:T(1,128)S(1)} %get-tuple-element.59.bias_ref), custom_call_target="tpu_custom_call" | custom-call | flops 524288 | bytes 1572864 | tf_op jit(solution)/shard_map/cond/branch_0_fun/pallas_call | solution.py:269
  (1 shorter events, 0.0 us)
Async XLA Ops:
  1.5 8.8 %collective-permute-start = (f32[8,96,128]{2,1,0:T(8,128)S(1)}, f32[8,96,128]{2,1,0:T(8,128)S(1)}, u32[]{:S(2)}, u32[]{:S(2)}) collective-permute-start(f32[8,96,128]{2,1,0:T(8,128)S(1)} %slice_select_fusion), channel_id=1, source_target_pairs={{0,16},{16,0},{1,17},{17,1},{2,18},{18,2},{3,19},{19,3},{4,20},{20... | collective-permute-start | bytes 1179656 | tf_op jit(solution)/shard_map/cond/branch_0_fun/ppermute | solution.py:259
  10.4 19.5 %copy-start.6 = (bf16[768,256]{1,0:T(8,128)(2,1)S(1)}, bf16[768,256]{1,0:T(8,128)(2,1)}, u32[]{:S(2)}) copy-start(bf16[768,256]{1,0:T(8,128)(2,1)} %get-tuple-element.56.back_tail_ref) | copy-start | bytes 1179652 | tf_op jit(solution)/shard_map/cond
  10.4 19.5 %copy-start.8 = (bf16[768,256]{1,0:T(8,128)(2,1)S(1)}, bf16[768,256]{1,0:T(8,128)(2,1)}, u32[]{:S(2)}) copy-start(bf16[768,256]{1,0:T(8,128)(2,1)} %get-tuple-element.55.tail_ref) | copy-start | bytes 1179652 | tf_op jit(solution)/shard_map/cond
  10.4 19.5 %copy-start.10 = (bf16[128,256]{1,0:T(8,128)(2,1)S(1)}, bf16[128,256]{1,0:T(8,128)(2,1)}, u32[]{:S(2)}) copy-start(bf16[128,256]{1,0:T(8,128)(2,1)} %get-tuple-element.57.back_head_ref) | copy-start | bytes 196612 | tf_op jit(solution)/shard_map/cond
  10.4 19.5 %copy-start.12 = (f32[64,256]{1,0:T(8,128)S(1)}, f32[64,256]{1,0:T(8,128)}, u32[]{:S(2)}) copy-start(f32[64,256]{1,0:T(8,128)} %get-tuple-element.54.twist_ref) | copy-start | bytes 196612 | tf_op jit(solution)/shard_map/cond
  10.5 19.5 %copy-start.14 = (bf16[128,192]{1,0:T(8,128)(2,1)S(1)}, bf16[128,192]{1,0:T(8,128)(2,1)}, u32[]{:S(2)}) copy-start(bf16[128,192]{1,0:T(8,128)(2,1)} %get-tuple-element.53.head_ref) | copy-start | bytes 147460 | tf_op jit(solution)/shard_map/cond
  31.7 15.7 %copy-start = (bf16[1024,128]{1,0:T(8,128)(2,1)S(1)}, bf16[1024,128]{1,0:T(8,128)(2,1)}, u32[]{:S(2)}) copy-start(bf16[1024,128]{1,0:T(8,128)(2,1)} %get-tuple-element.48.key_ref) | copy-start | bytes 786436 | tf_op jit(solution)/shard_map/cond
  31.7 15.7 %copy-start.2 = (bf16[1024,128]{1,0:T(8,128)(2,1)S(1)}, bf16[1024,128]{1,0:T(8,128)(2,1)}, u32[]{:S(2)}) copy-start(bf16[1024,128]{1,0:T(8,128)(2,1)} %get-tuple-element.49.value_ref) | copy-start | bytes 786436 | tf_op jit(solution)/shard_map/cond
  31.7 15.7 %copy-start.4 = (bf16[1024,128]{1,0:T(8,128)(2,1)S(1)}, bf16[1024,128]{1,0:T(8,128)(2,1)}, u32[]{:S(2)}) copy-start(bf16[1024,128]{1,0:T(8,128)(2,1)} %get-tuple-element.58.query_ref) | copy-start | bytes 786436 | tf_op jit(solution)/shard_map/cond

commit v14 on v13

--- a/solution.py
+++ b/solution.py
@@ -99,8 +99,17 @@
     return jnp.concatenate([jnp.concatenate(reals, axis=1), jnp.concatenate(imags, axis=1)], axis=0)
 
 
-def pack_kernel(layout, where_ref, key_ref, value_ref, filter_ref, bias_ref, out_ref, bias_out, key, value, taps, sems):
-    rows, own, part, groups = layout
+def pack_kernel(layout, staged, where_ref, key_ref, value_ref, filter_ref, bias_ref, out_ref, bias_out, key, value, taps, sems):
+    rows, own, part, groups = layout
+    count = out_ref.shape[0]
+    blocks = count // groups
+    homes = [(peer, peer * own) for peer in range(count)]
+    if staged:
+        near = where_ref[0] * 2 + where_ref[1]
+        homes = [
+            (((peer // blocks * 2 + peer % 2) ^ near) * (blocks // 2) + peer % blocks // 2, peer * own)
+            for peer in range(count)
+        ]
     first = where_ref[0] * (part * LANES if part < rows else 0)
     taken = filter_ref.at[pl.ds(pl.multiple_of(first, part * LANES), part * LANES)]
     cuts = 2 if rows % 2 == 0 else 1
@@ -116,21 +125,22 @@
                 fetch.wait()
         span = pl.ds(row * LANES, LANES)
         turned = (key[span, :].astype(F32) * value[span, :].astype(F32)).T
-        for peer in range(out_ref.shape[0]):
-            out_ref[peer, pl.ds(row, own, stride=rows), :] = turned[peer * own : (peer + 1) * own]
+        for place, chan in homes:
+            out_ref[place, pl.ds(row, own, stride=rows), :] = turned[chan : chan + own]
     fetches[-2].wait()
     for row in range(part):
         turned = taps[pl.ds(row * LANES, LANES), :].T
-        for peer in range(out_ref.shape[0]):
-            out_ref[peer, pl.ds(own * rows + row, own, stride=part), :] = turned[peer * own : (peer + 1) * own]
+        for place, chan in homes:
+            out_ref[place, pl.ds(own * rows + row, own, stride=part), :] = turned[chan : chan + own]
     fetches[-1].wait()
 
 
 def arrived(layout, staged, moved_ref, group, start, height):
     rows, own, part, groups = layout
     if staged:
-        start += group * own * (rows + part)
-        return moved_ref[:, start : start + height]
+        pair = [moved_ref[group * 2 + near, :, start : start + height] for near in range(2)]
+        values = jnp.stack(pair, axis=1)
+        return values.reshape(values.shape[0] * 2, height, LANES)
     blocks = moved_ref.shape[0] // groups
     return moved_ref[pl.ds(group * blocks, blocks), start : start + height]
 
@@ -155,8 +165,16 @@
     return signals
 
 
-def conv_kernel(layout, staged, pieces, moved_ref, head_ref, twist_ref, tail_ref, back_tail_ref, back_head_ref, out_ref):
-    rows, own, part, groups = layout
+def conv_kernel(
+    layout, staged, pieces, where_ref, moved_ref, head_ref, twist_ref, tail_ref, back_tail_ref, back_head_ref, out_ref, *held
+):
+    rows, own, part, groups = layout
+    if staged:
+        near = where_ref[0] * 2 + where_ref[1]
+        height = own * (rows + part)
+        for place in range(2 * groups):
+            held[0][near ^ place] = moved_ref[:, place * height : (place + 1) * height]
+        moved_ref = held[0]
     blocks = out_ref.shape[0] // groups
     outer = blocks * rows
     scale = 1.0 / (outer * LANES)
@@ -237,34 +255,40 @@
     head, twist, tail, back_tail, back_head = (jnp.asarray(table) for table in make_tables(seq_len))
     size = tokens * chans * 4
     macs = 2 * 3 * own * seq_len * (2 * outer + 4 * LANES)
-    where = lax.axis_index("groups").reshape(1).astype(jnp.int32)
+    where = jnp.stack([lax.axis_index("groups"), lax.axis_index("seq") % 2]).astype(jnp.int32)
 
     def exchange(array):
         return lax.all_to_all(array, axes, 0, 0, tiled=True)
 
     sources = (key_proj, value_proj, long_filter, skip_bias.reshape(1, chans))
     packed, bias = call(
-        functools.partial(pack_kernel, layout),
+        functools.partial(pack_kernel, layout, staged),
         [((count, own * (rows + part), LANES), F32), ((1, chans), F32)],
         [SMEM] + [HBM] * 4, size // 4, size * 3,
         [pltpu.VMEM((tokens, chans), BF16), pltpu.VMEM((tokens, chans), BF16), pltpu.VMEM((part * LANES, chans), F32),
          pltpu.SemaphoreType.DMA((6,))],
     )(where, *(pltpu.with_memory_space_constraint(source, pltpu.HBM) for source in sources))
     if staged:
-        mine = lax.axis_index("groups")
-        height = own * (rows + part)
-        by_group = packed.reshape(2, blocks, height, LANES)
-        first = mine == 0
-        kept = jnp.where(first, by_group[0], by_group[1])
-        other = lax.ppermute(jnp.where(first, by_group[1], by_group[0]), "groups", [(0, 1), (1, 0)])
-        pair = jnp.concatenate([jnp.where(first, kept, other), jnp.where(first, other, kept)], axis=1)
-        moved = lax.all_to_all(pair, "seq", 0, 0, tiled=True)
+        far, height = blocks // 2, own * (rows + part)
+        by_near = packed.reshape(4, far, height, LANES)
+        places = [(group, block) for group in range(groups) for block in range(blocks)]
+        held = [by_near[0]]
+        for near in range(1, 4):
+            pairs = [
+                (group * blocks + block, (group ^ near // 2) * blocks + (block ^ near % 2)) for group, block in places
+            ]
+            held.append(lax.ppermute(by_near[near], axes, pairs))
+        columns = [[2 * block + near for block in range(far)] for near in range(2)]
+        moved = lax.all_to_all(
+            jnp.concatenate(held, axis=1), "seq", 0, 0, axis_index_groups=columns, tiled=True
+        )
     else:
         moved = exchange(packed)
     local = call(
         functools.partial(conv_kernel, layout, staged, min(own, 4)),
-        [((count, own * rows, LANES), F32)], [VMEM] * 6, 5 * macs, 3 * size,
-    )(moved, head, twist, tail, back_tail, back_head)[0]
+        [((count, own * rows, LANES), F32)], [SMEM] + [VMEM] * 6, 5 * macs, 3 * size,
+        [pltpu.VMEM((2 * groups, blocks // 2, own * (rows + part), LANES), F32)] * staged,
+    )(where, moved, head, twist, tail, back_tail, back_head)[0]
     convolved = exchange(local).reshape(chans * rows, LANES)
     return pl.pallas_call(
         functools.partial(gate_kernel, rows),
@@ -278,7 +302,7 @@
 
 
 def shards(groups, blocks, cores, *args):
-    if cores == 1 or groups != 2:
+    if cores == 1 or groups != 2 or blocks % 2:
         return convolve(groups, blocks, False, *args)
     return lax.cond(
         lax.axis_index("chan") % 2 == 1,

time: 48.5 us -> 55.5 us (1.14)
  blocking collectives: 35.1 us -> 38.6 us
  starting transfers between devices: 3 us -> 4.6 us
  Pallas kernels: 4.09 us -> 5.27 us
  waiting for transfers between devices: 5.76 us -> 6.49 us
    all_to_all x1, blocking collectives: 15.7 us -> 20.2 us  [exchange(): return lax.all_to_all(array, axes, 0, 0, tiled=True)]
    ppermute x1 -> x3, starting transfers between devices: 3 us -> 4.6 us  [convolve(): held.append(lax.ppermute(by_near[near], axes, pairs))]
    all_to_all x1, blocking collectives: 19.4 us -> 18.4 us  [convolve(): lax.all_to_all(jnp.concatenate(held, axis=1), 'seq', 0, 0, axis_index_gro...]
    ppermute x1 -> x3, waiting for transfers between devices: 5.76 us -> 6.49 us  [convolve(): held.append(lax.ppermute(by_near[near], axes, pairs))]
    pallas_call x1, Pallas kernels: 1.77 us -> 2.37 us  [convolve(): call(functools.partial(conv_kernel, layout, staged, min(own, 4)), [((coun...]
    pallas_call x1, Pallas kernels: 1.43 us -> 2.02 us  [convolve(): call(functools.partial(pack_kernel, layout, staged), [((count, own * (row...]
  transfers between devices with their start and end apart: 1 -> 3, of which waited for: 1 -> 2; matrix products, arithmetic and copies ran while one was open for 0% -> 0% of each run, Pallas kernels for 0% -> 0%
where the time goes in v14:
time: 55.5 us; the launch traced here: 55.3 us
  blocking collectives  38.6 us (70%)
  waiting for transfers between devices  6.49 us (12%)
  Pallas kernels  5.27 us (9%)
  starting transfers between devices  4.6 us (8%)
    all_to_all x1, blocking collectives, exchange(): return lax.all_to_all(array, axes, 0, 0, tiled=True)  20.2 us
    all_to_all x1, blocking collectives, convolve(): lax.all_to_all(jnp.concatenate(held, axis=1), 'seq', 0, 0, axis_index_gro...  18.4 us
    ppermute x3, waiting for transfers between devices, convolve(): held.append(lax.ppermute(by_near[near], axes, pairs))  6.49 us
    ppermute x3, starting transfers between devices, convolve(): held.append(lax.ppermute(by_near[near], axes, pairs))  4.6 us
    pallas_call x1, Pallas kernels, convolve(): call(functools.partial(conv_kernel, layout, staged, min(own, 4)), [((coun...  2.37 us
    pallas_call x1, Pallas kernels, convolve(): call(functools.partial(pack_kernel, layout, staged), [((count, own * (row...  2.02 us
  transfers between devices with their start and end apart: 3, of which 2 were waited for; matrix products, arithmetic and copies ran while one was open for 0% of the time, Pallas kernels for 0%

profile of v14, /device:TPU:0, one launch (start us, length us, event | category | flops | bytes accessed | tf_op | source)
XLA Modules:
  0.0 55.3 jit_solution(12800006799467300124)
XLA Ops:
  0.0 55.3 %conditional.1 = (bf16[1024,128]{1,0:T(8,128)(2,1)}) conditional(s32[]{:T(128)} %convert_element_type.3, (f32[128]{0:T(128)}, bf16[1024,128]{1,0:T(8,128)(2,1)}, bf16[1024,128]{1,0:T(8,128)(2,1)}, f32[1024,128]{1,0:T(8,128)}, bf16[128,192]{1,0:T(8,128)(2,1)}, /*index=5*/f32[64,256]{1,0:T(8,128)}, bf16[768,256]{1,0:T(8,128)(2,1)}, ...), branch_computations={%region_0.1_spmd, %region_1.2_spmd} | conditional | flops 1259536384 | bytes 19857948 | solution.py:307
  0.0 0.1 pad_add_fusion.where_ref
  0.1 2.0 %branch_0_fun.3 = (f32[16,96,128]{2,1,0:T(8,128)S(1)}, f32[1,128]{1,0:T(1,128)S(1)}) custom-call(s32[2]{0:T(128)S(1)} %pad_add_fusion.where_ref, bf16[1024,128]{1,0:T(8,128)(2,1)} %get-tuple-element.48.key_ref, bf16[1024,128]{1,0:T(8,128)(2,1)} %get-tuple-element.49.value_ref, f32[1024,128]{1,0:T(8,128)} %get-tuple-element.50.filter_ref, f32[1,128]{1,0:T(1,128)} %bitcast.10), custom_call_target="tpu_custom_call" | custom-call | flops 131072 | bytes 1572864 | tf_op jit(solution)/shard_map/cond/branch_0_fun/pallas_call | solution.py:264
  2.1 0.1 fusion
  2.2 4.0 %collective-permute-start.2 = (f32[4,96,128]{2,1,0:T(8,128)S(1)}, f32[4,96,128]{2,1,0:T(8,128)S(1)}, u32[]{:S(2)}, u32[]{:S(2)}) collective-permute-start(f32[4,96,128]{2,1,0:T(8,128)S(1)} %get-tuple-element.74), channel_id=1, source_target_pairs={{0,18},{2,16},{4,22},{6,20},{8,26},{10,24},{12,30},{14,28},{16,2},... | collective-permute-start | bytes 589832 | tf_op jit(solution)/shard_map/cond/branch_0_fun/ppermute | solution.py:280
  6.1 0.5 collective-permute-start.1
  6.7 0.1 collective-permute-start
  6.8 3.0 %collective-permute-done.2 = f32[4,96,128]{2,1,0:T(8,128)S(1)} collective-permute-done((f32[4,96,128]{2,1,0:T(8,128)S(1)}, f32[4,96,128]{2,1,0:T(8,128)S(1)}, u32[]{:S(2)}, u32[]{:S(2)}) %collective-permute-start.2) | collective-permute-done | bytes 196640 | tf_op jit(solution)/shard_map/cond/branch_0_fun/ppermute | solution.py:280
  9.8 3.5 %collective-permute-done.1 = f32[4,96,128]{2,1,0:T(8,128)S(1)} collective-permute-done((f32[4,96,128]{2,1,0:T(8,128)S(1)}, f32[4,96,128]{2,1,0:T(8,128)S(1)}, u32[]{:S(2)}, u32[]{:S(2)}) %collective-permute-start.1) | collective-permute-done | bytes 196640 | tf_op jit(solution)/shard_map/cond/branch_0_fun/ppermute | solution.py:280
  13.3 0.0 collective-permute-done
  13.3 0.1 pad_maximum_fusion
  13.3 0.0 copy-start.6
  13.3 0.0 copy-start.8
  13.3 0.0 copy-start.10
  13.4 0.0 copy-start.12
  13.4 0.0 copy-start.14
  13.4 18.4 %all_to_all.16.moved_ref = f32[4,384,128]{2,1,0:T(8,128)S(1)} all-to-all(f32[4,384,128]{2,1,0:T(8,128)S(1)} %pad_maximum_fusion), channel_id=1, replica_groups={{0,4,8,12},{2,6,10,14},{1,5,9,13},{3,7,11,15},{16,20,24,28},{18,22,26,3..., dimensions={0} | all-to-all | bytes 1572864 | tf_op jit(solution)/shard_map/cond/branch_0_fun/all_to_all | solution.py:282
  31.7 0.0 copy-done.6
  31.7 0.0 copy-done.8
  31.7 0.0 copy-done.10
  31.8 0.0 copy-done.12
  31.8 0.0 copy-done.14
  31.8 2.4 %branch_0_fun.4 = f32[16,64,128]{2,1,0:T(8,128)S(1)} custom-call(s32[2]{0:T(128)S(1)} %pad_add_fusion.where_ref, f32[4,384,128]{2,1,0:T(8,128)S(1)} %all_to_all.16.moved_ref, bf16[128,192]{1,0:T(8,128)(2,1)S(1)} %copy-done.14, f32[64,256]{1,0:T(8,128)S(1)} %copy-done.12, bf16[768,256]{1,0:T(8,128)(2,1)S(1)} %copy-done.8, bf16[768,256]{1,0:T(8,128)(2,1)S(1)} %copy-done.6, ...), custom_call_target="tpu_custom_call" | custom-call | flops 1258291200 | bytes 1572864 | tf_op jit(solution)/shard_map/cond/branch_0_fun/pallas_call | solution.py:287
  34.1 0.0 copy-start
  34.2 0.0 copy-start.2
  34.2 0.0 copy-start.4
  34.2 20.2 %all_to_all.17 = f32[16,64,128]{2,1,0:T(8,128)S(1)} all-to-all(f32[16,64,128]{2,1,0:T(8,128)S(1)} %branch_0_fun.4), channel_id=1, replica_groups=mesh['groups'=2,'seq'=8,'chan'=2] {'groups','seq'}, dimensions={0} | all-to-all | bytes 1048576 | tf_op jit(solution)/shard_map/cond/branch_0_fun/all_to_all | solution.py:261
  54.4 0.0 copy-done
  54.4 0.0 copy-done.2
  54.4 0.0 copy-done.4
  54.4 0.9 %branch_0_fun.5 = bf16[1024,128]{1,0:T(8,128)(2,1)} custom-call(f32[1024,128]{1,0:T(8,128)S(1)} %bitcast.8, bf16[1024,128]{1,0:T(8,128)(2,1)S(1)} %copy-done.4, bf16[1024,128]{1,0:T(8,128)(2,1)S(1)} %copy-done, bf16[1024,128]{1,0:T(8,128)(2,1)S(1)} %copy-done.2, f32[1,128]{1,0:T(1,128)S(1)} %get-tuple-element.59.bias_ref), custom_call_target="tpu_custom_call" | custom-call | flops 524288 | bytes 1572864 | tf_op jit(solution)/shard_map/cond/branch_0_fun/pallas_call | solution.py:293
Async XLA Ops:
  2.2 7.6 %collective-permute-start.2 = (f32[4,96,128]{2,1,0:T(8,128)S(1)}, f32[4,96,128]{2,1,0:T(8,128)S(1)}, u32[]{:S(2)}, u32[]{:S(2)}) collective-permute-start(f32[4,96,128]{2,1,0:T(8,128)S(1)} %get-tuple-element.74), channel_id=1, source_target_pairs={{0,18},{2,16},{4,22},{6,20},{8,26},{10,24},{12,30},{14,28},{16,2},... | collective-permute-start | bytes 589832 | tf_op jit(solution)/shard_map/cond/branch_0_fun/ppermute | solution.py:280
  6.1 7.1 %collective-permute-start.1 = (f32[4,96,128]{2,1,0:T(8,128)S(1)}, f32[4,96,128]{2,1,0:T(8,128)S(1)}, u32[]{:S(2)}, u32[]{:S(2)}) collective-permute-start(f32[4,96,128]{2,1,0:T(8,128)S(1)} %get-tuple-element.75), channel_id=1, source_target_pairs={{0,16},{2,18},{4,20},{6,22},{8,24},{10,26},{12,28},{14,30},{16,0},... | collective-permute-start | bytes 589832 | tf_op jit(solution)/shard_map/cond/branch_0_fun/ppermute | solution.py:280
  6.7 6.6 %collective-permute-start = (f32[4,96,128]{2,1,0:T(8,128)S(1)}, f32[4,96,128]{2,1,0:T(8,128)S(1)}, u32[]{:S(2)}, u32[]{:S(2)}) collective-permute-start(f32[4,96,128]{2,1,0:T(8,128)S(1)} %get-tuple-element.76), channel_id=1, source_target_pairs={{0,2},{2,0},{4,6},{6,4},{8,10},{10,8},{12,14},{14,12},{16,18},{18,... | collective-permute-start | bytes 589832 | tf_op jit(solution)/shard_map/cond/branch_0_fun/ppermute | solution.py:280
  13.3 18.4 %copy-start.6 = (bf16[768,256]{1,0:T(8,128)(2,1)S(1)}, bf16[768,256]{1,0:T(8,128)(2,1)}, u32[]{:S(2)}) copy-start(bf16[768,256]{1,0:T(8,128)(2,1)} %get-tuple-element.56.back_tail_ref) | copy-start | bytes 1179652 | tf_op jit(solution)/shard_map/cond
  13.3 18.4 %copy-start.8 = (bf16[768,256]{1,0:T(8,128)(2,1)S(1)}, bf16[768,256]{1,0:T(8,128)(2,1)}, u32[]{:S(2)}) copy-start(bf16[768,256]{1,0:T(8,128)(2,1)} %get-tuple-element.55.tail_ref) | copy-start | bytes 1179652 | tf_op jit(solution)/shard_map/cond
  13.3 18.4 %copy-start.10 = (bf16[128,256]{1,0:T(8,128)(2,1)S(1)}, bf16[128,256]{1,0:T(8,128)(2,1)}, u32[]{:S(2)}) copy-start(bf16[128,256]{1,0:T(8,128)(2,1)} %get-tuple-element.57.back_head_ref) | copy-start | bytes 196612 | tf_op jit(solution)/shard_map/cond
  13.4 18.4 %copy-start.12 = (f32[64,256]{1,0:T(8,128)S(1)}, f32[64,256]{1,0:T(8,128)}, u32[]{:S(2)}) copy-start(f32[64,256]{1,0:T(8,128)} %get-tuple-element.54.twist_ref) | copy-start | bytes 196612 | tf_op jit(solution)/shard_map/cond
  13.4 18.4 %copy-start.14 = (bf16[128,192]{1,0:T(8,128)(2,1)S(1)}, bf16[128,192]{1,0:T(8,128)(2,1)}, u32[]{:S(2)}) copy-start(bf16[128,192]{1,0:T(8,128)(2,1)} %get-tuple-element.53.head_ref) | copy-start | bytes 147460 | tf_op jit(solution)/shard_map/cond
  34.1 20.3 %copy-start = (bf16[1024,128]{1,0:T(8,128)(2,1)S(1)}, bf16[1024,128]{1,0:T(8,128)(2,1)}, u32[]{:S(2)}) copy-start(bf16[1024,128]{1,0:T(8,128)(2,1)} %get-tuple-element.48.key_ref) | copy-start | bytes 786436 | tf_op jit(solution)/shard_map/cond
  34.2 20.3 %copy-start.2 = (bf16[1024,128]{1,0:T(8,128)(2,1)S(1)}, bf16[1024,128]{1,0:T(8,128)(2,1)}, u32[]{:S(2)}) copy-start(bf16[1024,128]{1,0:T(8,128)(2,1)} %get-tuple-element.49.value_ref) | copy-start | bytes 786436 | tf_op jit(solution)/shard_map/cond
  34.2 20.3 %copy-start.4 = (bf16[1024,128]{1,0:T(8,128)(2,1)S(1)}, bf16[1024,128]{1,0:T(8,128)(2,1)}, u32[]{:S(2)}) copy-start(bf16[1024,128]{1,0:T(8,128)(2,1)} %get-tuple-element.58.query_ref) | copy-start | bytes 786436 | tf_op jit(solution)/shard_map/cond

commit v15 on v13

--- a/solution.py
+++ b/solution.py
@@ -251,13 +251,9 @@
          pltpu.SemaphoreType.DMA((6,))],
     )(where, *(pltpu.with_memory_space_constraint(source, pltpu.HBM) for source in sources))
     if staged:
-        mine = lax.axis_index("groups")
-        height = own * (rows + part)
-        by_group = packed.reshape(2, blocks, height, LANES)
-        first = mine == 0
-        kept = jnp.where(first, by_group[0], by_group[1])
-        other = lax.ppermute(jnp.where(first, by_group[1], by_group[0]), "groups", [(0, 1), (1, 0)])
-        pair = jnp.concatenate([jnp.where(first, kept, other), jnp.where(first, other, kept)], axis=1)
+        by_group = packed.reshape(groups, blocks, own * (rows + part), LANES)
+        by_group = lax.all_to_all(by_group, "groups", 0, 0, tiled=True)
+        pair = jnp.concatenate([by_group[group] for group in range(groups)], axis=1)
         moved = lax.all_to_all(pair, "seq", 0, 0, tiled=True)
     else:
         moved = exchange(packed)
@@ -278,10 +274,10 @@
 
 
 def shards(groups, blocks, cores, *args):
-    if cores == 1 or groups != 2:
+    if cores == 1 or groups == 1:
         return convolve(groups, blocks, False, *args)
     return lax.cond(
-        lax.axis_index("chan") % 2 == 1,
+        lax.axis_index("chan") % 2 == 0,
         functools.partial(convolve, groups, blocks, False),
         functools.partial(convolve, groups, blocks, True),
         *args,

time: 48.5 us -> 52.3 us (1.078); the launches traced: 48.3 us -> 51.3 us
  blocking collectives: 35.1 us -> 47.1 us
  waiting for transfers between devices: 5.76 us -> 0 us
  starting transfers between devices: 3 us -> 0 us
    all_to_all x1 -> x2, blocking collectives: 15.7 us -> 47.1 us  [exchange(): return lax.all_to_all(array, axes, 0, 0, tiled=True)]
    all_to_all x1 -> x0, blocking collectives: 19.4 us -> none  [convolve(): moved = lax.all_to_all(pair, 'seq', 0, 0, tiled=True)]
    ppermute x1 -> x0, waiting for transfers between devices: 5.76 us -> none  [convolve(): lax.ppermute(jnp.where(first, by_group[1], by_group[0]), 'groups', [(0, 1...]
    ppermute x1 -> x0, starting transfers between devices: 3 us -> none  [convolve(): lax.ppermute(jnp.where(first, by_group[1], by_group[0]), 'groups', [(0, 1...]
  transfers between devices with their start and end apart: 1 -> 0, of which waited for: 1 -> 0; matrix products, arithmetic and copies ran while one was open for 0% -> 0% of each run, Pallas kernels for 0% -> 0%
where the time goes in v15:
time: 52.3 us; the launch traced here: 51.3 us
  blocking collectives  47.1 us (90%)
  Pallas kernels  4.09 us (8%)
    all_to_all x2, blocking collectives, exchange(): return lax.all_to_all(array, axes, 0, 0, tiled=True)  47.1 us
    pallas_call x1, Pallas kernels, convolve(): call(functools.partial(conv_kernel, layout, staged, min(own, 4)), [((coun...  1.77 us
    pallas_call x1, Pallas kernels, convolve(): call(functools.partial(pack_kernel, layout), [((count, own * (rows + part...  1.43 us

profile of v15, /device:TPU:0, one launch (start us, length us, event | category | flops | bytes accessed | tf_op | source)
XLA Modules:
  0.0 51.3 jit_solution(1085687961167632206)
XLA Ops:
  0.0 51.3 %conditional.1 = (bf16[1024,128]{1,0:T(8,128)(2,1)}) conditional(s32[]{:T(128)} %convert_element_type.3, (f32[128]{0:T(128)}, bf16[1024,128]{1,0:T(8,128)(2,1)}, bf16[1024,128]{1,0:T(8,128)(2,1)}, f32[1024,128]{1,0:T(8,128)}, bf16[128,192]{1,0:T(8,128)(2,1)}, /*index=5*/f32[64,256]{1,0:T(8,128)}, bf16[768,256]{1,0:T(8,128)(2,1)}, ...), branch_computations={%region_0.1_spmd, %region_1.2_spmd} | conditional | flops 1259143168 | bytes 19071240 | solution.py:279
  0.0 1.4 %branch_1_fun.3 = (f32[16,96,128]{2,1,0:T(8,128)S(1)}, f32[1,128]{1,0:T(1,128)S(1)}) custom-call(s32[1]{0:T(128)} %bitcast.6.where_ref, bf16[1024,128]{1,0:T(8,128)(2,1)} %get-tuple-element.60.key_ref, bf16[1024,128]{1,0:T(8,128)(2,1)} %get-tuple-element.61.value_ref, f32[1024,128]{1,0:T(8,128)} %get-tuple-element.62.filter_ref, f32[1,128]{1,0:T(1,128)} %bitcast.15), custom_call_target="tpu_custom_call" | custom-call | flops 131072 | bytes 1572864 | tf_op jit(solution)/shard_map/cond/branch_1_fun/pallas_call | solution.py:246
  1.4 0.0 copy-start.7
  1.5 0.0 copy-start.9
  1.5 0.0 copy-start.11
  1.5 0.0 copy-start.13
  1.5 0.0 copy-start.15
  1.5 27.1 %all_to_all.23.moved_ref = f32[16,96,128]{2,1,0:T(8,128)S(1)} all-to-all(f32[16,96,128]{2,1,0:T(8,128)S(1)} %get-tuple-element.64), channel_id=1, replica_groups=mesh['groups'=2,'seq'=8,'chan'=2] {'groups','seq'}, dimensions={0} | all-to-all | bytes 1572864 | tf_op jit(solution)/shard_map/cond/branch_1_fun/all_to_all | solution.py:243
  28.6 0.0 copy-done.7
  28.6 0.0 copy-done.9
  28.6 0.0 copy-done.11
  28.6 0.0 copy-done.13
  28.6 0.0 copy-done.15
  28.6 1.8 %branch_1_fun.4 = f32[16,64,128]{2,1,0:T(8,128)S(1)} custom-call(f32[16,96,128]{2,1,0:T(8,128)S(1)} %all_to_all.23.moved_ref, bf16[128,192]{1,0:T(8,128)(2,1)S(1)} %copy-done.15, f32[64,256]{1,0:T(8,128)S(1)} %copy-done.13, bf16[768,256]{1,0:T(8,128)(2,1)S(1)} %copy-done.9, bf16[768,256]{1,0:T(8,128)(2,1)S(1)} %copy-done.7, bf16[128,256]{1,0:T(8,128)(2,1)S(1)} %copy-done.11), custom_call_target="tpu_custom_call" | custom-call | flops 1258291200 | bytes 1572864 | tf_op jit(solution)/shard_map/cond/branch_1_fun/pallas_call | solution.py:260
  30.4 0.0 copy-start.1
  30.4 0.0 copy-start.3
  30.4 0.0 copy-start.5
  30.5 19.9 %all_to_all.24 = f32[16,64,128]{2,1,0:T(8,128)S(1)} all-to-all(f32[16,64,128]{2,1,0:T(8,128)S(1)} %branch_1_fun.4), channel_id=1, replica_groups=mesh['groups'=2,'seq'=8,'chan'=2] {'groups','seq'}, dimensions={0} | all-to-all | bytes 1048576 | tf_op jit(solution)/shard_map/cond/branch_1_fun/all_to_all | solution.py:243
  50.4 0.0 copy-done.1
  50.4 0.0 copy-done.3
  50.4 0.0 copy-done.5
  50.4 0.9 %branch_1_fun.5 = bf16[1024,128]{1,0:T(8,128)(2,1)} custom-call(f32[1024,128]{1,0:T(8,128)S(1)} %bitcast.12, bf16[1024,128]{1,0:T(8,128)(2,1)S(1)} %copy-done.5, bf16[1024,128]{1,0:T(8,128)(2,1)S(1)} %copy-done.1, bf16[1024,128]{1,0:T(8,128)(2,1)S(1)} %copy-done.3, f32[1,128]{1,0:T(1,128)S(1)} %get-tuple-element.71.bias_ref), custom_call_target="tpu_custom_call" | custom-call | flops 524288 | bytes 1572864 | tf_op jit(solution)/shard_map/cond/branch_1_fun/pallas_call | solution.py:265
Async XLA Ops:
  1.4 27.2 %copy-start.7 = (bf16[768,256]{1,0:T(8,128)(2,1)S(1)}, bf16[768,256]{1,0:T(8,128)(2,1)}, u32[]{:S(2)}) copy-start(bf16[768,256]{1,0:T(8,128)(2,1)} %get-tuple-element.68.back_tail_ref) | copy-start | bytes 1179652 | tf_op jit(solution)/shard_map/cond
  1.5 27.2 %copy-start.9 = (bf16[768,256]{1,0:T(8,128)(2,1)S(1)}, bf16[768,256]{1,0:T(8,128)(2,1)}, u32[]{:S(2)}) copy-start(bf16[768,256]{1,0:T(8,128)(2,1)} %get-tuple-element.67.tail_ref) | copy-start | bytes 1179652 | tf_op jit(solution)/shard_map/cond
  1.5 27.2 %copy-start.11 = (bf16[128,256]{1,0:T(8,128)(2,1)S(1)}, bf16[128,256]{1,0:T(8,128)(2,1)}, u32[]{:S(2)}) copy-start(bf16[128,256]{1,0:T(8,128)(2,1)} %get-tuple-element.69.back_head_ref) | copy-start | bytes 196612 | tf_op jit(solution)/shard_map/cond
  1.5 27.1 %copy-start.13 = (f32[64,256]{1,0:T(8,128)S(1)}, f32[64,256]{1,0:T(8,128)}, u32[]{:S(2)}) copy-start(f32[64,256]{1,0:T(8,128)} %get-tuple-element.66.twist_ref) | copy-start | bytes 196612 | tf_op jit(solution)/shard_map/cond
  1.5 27.1 %copy-start.15 = (bf16[128,192]{1,0:T(8,128)(2,1)S(1)}, bf16[128,192]{1,0:T(8,128)(2,1)}, u32[]{:S(2)}) copy-start(bf16[128,192]{1,0:T(8,128)(2,1)} %get-tuple-element.65.head_ref) | copy-start | bytes 147460 | tf_op jit(solution)/shard_map/cond
  30.4 20.0 %copy-start.1 = (bf16[1024,128]{1,0:T(8,128)(2,1)S(1)}, bf16[1024,128]{1,0:T(8,128)(2,1)}, u32[]{:S(2)}) copy-start(bf16[1024,128]{1,0:T(8,128)(2,1)} %get-tuple-element.60.key_ref) | copy-start | bytes 786436 | tf_op jit(solution)/shard_map/cond
  30.4 20.0 %copy-start.3 = (bf16[1024,128]{1,0:T(8,128)(2,1)S(1)}, bf16[1024,128]{1,0:T(8,128)(2,1)}, u32[]{:S(2)}) copy-start(bf16[1024,128]{1,0:T(8,128)(2,1)} %get-tuple-element.61.value_ref) | copy-start | bytes 786436 | tf_op jit(solution)/shard_map/cond
  30.4 20.0 %copy-start.5 = (bf16[1024,128]{1,0:T(8,128)(2,1)S(1)}, bf16[1024,128]{1,0:T(8,128)(2,1)}, u32[]{:S(2)}) copy-start(bf16[1024,128]{1,0:T(8,128)(2,1)} %get-tuple-element.70.query_ref) | copy-start | bytes 786436 | tf_op jit(solution)/shard_map/cond

commit v16 on v13

--- a/solution.py
+++ b/solution.py
@@ -36,9 +36,9 @@
     high, low = split_np(fwd_head)
     head_tab = np.concatenate([high, high, low], axis=1)
     high, low = split_np(block(tail))
-    tail_tab = np.concatenate([high, high, low], axis=0)
+    tail_tab = np.concatenate([high, low], axis=0)
     high, low = split_np(block(tail.conj()))
-    back_tail_tab = np.concatenate([high, high, low], axis=0)
+    back_tail_tab = np.concatenate([high, low], axis=0)
     high, low = split_np(np.concatenate([head.real, head.imag], axis=1))
     back_head_tab = np.block([[high, high], [low, np.zeros_like(low)]])
     twist_tab = np.concatenate([twist.real, twist.imag], axis=1).astype(np.float32)
@@ -55,13 +55,14 @@
     return jnp.concatenate([high, low, high], axis=0)
 
 
-def by_lanes(values):
-    high, low = halves(values)
-    return jnp.concatenate([high, low, high], axis=1)
-
-
 def mat(left, right):
     return jnp.dot(left, right, preferred_element_type=F32)
+
+
+def mat_split(values, table):
+    high, low = halves(values)
+    depth = values.shape[1]
+    return mat(high, table[:depth]) + (mat(low, table[:depth]) + mat(high, table[depth:]))
 
 
 def head_stage(signals, head, twist):
@@ -170,9 +171,9 @@
         )
         for chans in sets
     ]
-    specs = [mat(by_lanes(values), tail_ref[...]) for values in mixed]
+    specs = [mat_split(values, tail_ref[...]) for values in mixed]
     prods = [product_stage(spec, outer, groups) for spec in specs]
-    backs = [mat(by_lanes(values), back_tail_ref[...]) for values in prods]
+    backs = [mat_split(values, back_tail_ref[...]) for values in prods]
     turned = [back_stage(back, cos, sin) for back in backs]
     results = [mat(back_head_ref[...], jnp.concatenate(halves(values), axis=0)) for values in turned]
     for chans, result in zip(sets, results):
@@ -256,7 +257,9 @@
         by_group = packed.reshape(2, blocks, height, LANES)
         first = mine == 0
         kept = jnp.where(first, by_group[0], by_group[1])
-        other = lax.ppermute(jnp.where(first, by_group[1], by_group[0]), "groups", [(0, 1), (1, 0)])
+        sent = jnp.where(first, by_group[1], by_group[0])
+        cut = blocks // 2
+        other = jnp.concatenate([lax.ppermute(piece, "groups", [(0, 1), (1, 0)]) for piece in (sent[:cut], sent[cut:])])
         pair = jnp.concatenate([jnp.where(first, kept, other), jnp.where(first, other, kept)], axis=1)
         moved = lax.all_to_all(pair, "seq", 0, 0, tiled=True)
     else:

time: 48.5 us -> 48.6 us (level)
    ppermute x1 -> x2, waiting for transfers between devices: 5.76 us -> 5.66 us  [convolve(): lax.ppermute(piece, 'groups', [(0, 1), (1, 0)])]
    ppermute x1 -> x2, starting transfers between devices: 3 us -> 3.08 us  [convolve(): lax.ppermute(piece, 'groups', [(0, 1), (1, 0)])]
  transfers between devices with their start and end apart: 1 -> 2, of which waited for: 1 -> 2; matrix products, arithmetic and copies ran while one was open for 0% -> 0% of each run, Pallas kernels for 0% -> 0%
where the time goes in v16:
time: 48.6 us; the launch traced here: 48.4 us
  blocking collectives  35.1 us (72%)
  waiting for transfers between devices  5.66 us (12%)
  Pallas kernels  4.09 us (8%)
  starting transfers between devices  3.08 us (6%)
    all_to_all x1, blocking collectives, convolve(): moved = lax.all_to_all(pair, 'seq', 0, 0, tiled=True)  19.4 us
    all_to_all x1, blocking collectives, exchange(): return lax.all_to_all(array, axes, 0, 0, tiled=True)  15.7 us
    ppermute x2, waiting for transfers between devices, convolve(): lax.ppermute(piece, 'groups', [(0, 1), (1, 0)])  5.66 us
    ppermute x2, starting transfers between devices, convolve(): lax.ppermute(piece, 'groups', [(0, 1), (1, 0)])  3.08 us
    pallas_call x1, Pallas kernels, convolve(): call(functools.partial(conv_kernel, layout, staged, min(own, 4)), [((coun...  1.77 us
    pallas_call x1, Pallas kernels, convolve(): call(functools.partial(pack_kernel, layout), [((count, own * (rows + part...  1.43 us
  transfers between devices with their start and end apart: 2, of which 2 were waited for; matrix products, arithmetic and copies ran while one was open for 0% of the time, Pallas kernels for 0%

profile of v16, /device:TPU:0, one launch (start us, length us, event | category | flops | bytes accessed | tf_op | source)
XLA Modules:
  0.0 48.4 jit_solution(5324230912548308376)
XLA Ops:
  0.0 48.4 %conditional.1 = (bf16[1024,128]{1,0:T(8,128)(2,1)}) conditional(s32[]{:T(128)} %convert_element_type.3, (f32[128]{0:T(128)}, bf16[1024,128]{1,0:T(8,128)(2,1)}, bf16[1024,128]{1,0:T(8,128)(2,1)}, f32[1024,128]{1,0:T(8,128)}, bf16[128,192]{1,0:T(8,128)(2,1)}, /*index=5*/f32[64,256]{1,0:T(8,128)}, bf16[512,256]{1,0:T(8,128)(2,1)}, ...), branch_computations={%region_0.1_spmd, %region_1.2_spmd} | conditional | flops 1259536384 | bytes 21168484 | solution.py:286
  0.0 1.4 %branch_0_fun.3 = (f32[16,96,128]{2,1,0:T(8,128)S(1)}, f32[1,128]{1,0:T(1,128)S(1)}) custom-call(s32[1]{0:T(128)} %bitcast.where_ref, bf16[1024,128]{1,0:T(8,128)(2,1)} %get-tuple-element.48.key_ref, bf16[1024,128]{1,0:T(8,128)(2,1)} %get-tuple-element.49.value_ref, f32[1024,128]{1,0:T(8,128)} %get-tuple-element.50.filter_ref, f32[1,128]{1,0:T(1,128)} %bitcast.8), custom_call_target="tpu_custom_call" | custom-call | flops 131072 | bytes 1572864 | tf_op jit(solution)/shard_map/cond/branch_0_fun/pallas_call | solution.py:247
  1.5 3.0 %collective-permute-start = (f32[4,96,128]{2,1,0:T(8,128)S(1)}, f32[4,96,128]{2,1,0:T(8,128)S(1)}, u32[]{:S(2)}, u32[]{:S(2)}) collective-permute-start(f32[4,96,128]{2,1,0:T(8,128)S(1)} %get-tuple-element.76), channel_id=1, source_target_pairs={{0,16},{16,0},{1,17},{17,1},{2,18},{18,2},{3,19},{19,3},{4,20},{20... | collective-permute-start | bytes 589832 | tf_op jit(solution)/shard_map/cond/branch_0_fun/ppermute | solution.py:262
  4.5 0.1 collective-permute-start.1
  4.6 3.6 %collective-permute-done = f32[4,96,128]{2,1,0:T(8,128)S(1)} collective-permute-done((f32[4,96,128]{2,1,0:T(8,128)S(1)}, f32[4,96,128]{2,1,0:T(8,128)S(1)}, u32[]{:S(2)}, u32[]{:S(2)}) %collective-permute-start) | collective-permute-done | bytes 196640 | tf_op jit(solution)/shard_map/cond/branch_0_fun/ppermute | solution.py:262
  8.2 2.1 %collective-permute-done.1 = f32[4,96,128]{2,1,0:T(8,128)S(1)} collective-permute-done((f32[4,96,128]{2,1,0:T(8,128)S(1)}, f32[4,96,128]{2,1,0:T(8,128)S(1)}, u32[]{:S(2)}, u32[]{:S(2)}) %collective-permute-start.1) | collective-permute-done | bytes 196640 | tf_op jit(solution)/shard_map/cond/branch_0_fun/ppermute | solution.py:262
  10.3 0.1 broadcast_select_fusion.1
  10.4 0.1 pad_maximum_fusion
  10.5 0.0 copy-start.6
  10.5 0.0 copy-start.8
  10.5 0.0 copy-start.10
  10.5 0.0 copy-start.12
  10.5 0.0 copy-start.14
  10.5 19.4 %all_to_all.16.moved_ref = f32[8,192,128]{2,1,0:T(8,128)S(1)} all-to-all(f32[8,192,128]{2,1,0:T(8,128)S(1)} %pad_maximum_fusion), channel_id=1, replica_groups=mesh['groups'=2,'seq'=8,'chan'=2] {'seq'}, dimensions={0} | all-to-all | bytes 1572864 | tf_op jit(solution)/shard_map/cond/branch_0_fun/all_to_all | solution.py:264
  30.0 0.0 copy-done.6
  30.0 0.0 copy-done.8
  30.0 0.0 copy-done.10
  30.0 0.0 copy-done.12
  30.0 0.0 copy-done.14
  30.0 1.8 %branch_0_fun.4 = f32[16,64,128]{2,1,0:T(8,128)S(1)} custom-call(f32[8,192,128]{2,1,0:T(8,128)S(1)} %all_to_all.16.moved_ref, bf16[128,192]{1,0:T(8,128)(2,1)S(1)} %copy-done.14, f32[64,256]{1,0:T(8,128)S(1)} %copy-done.12, bf16[512,256]{1,0:T(8,128)(2,1)S(1)} %copy-done.8, bf16[512,256]{1,0:T(8,128)(2,1)S(1)} %copy-done.6, bf16[128,256]{1,0:T(8,128)(2,1)S(1)} %copy-done.10), custom_call_target="tpu_custom_call" | custom-call | flops 1258291200 | bytes 1572864 | tf_op jit(solution)/shard_map/cond/branch_0_fun/pallas_call | solution.py:267
  31.8 0.0 copy-start
  31.8 0.0 copy-start.2
  31.8 0.0 copy-start.4
  31.8 15.7 %all_to_all.17 = f32[16,64,128]{2,1,0:T(8,128)S(1)} all-to-all(f32[16,64,128]{2,1,0:T(8,128)S(1)} %branch_0_fun.4), channel_id=1, replica_groups=mesh['groups'=2,'seq'=8,'chan'=2] {'groups','seq'}, dimensions={0} | all-to-all | bytes 1048576 | tf_op jit(solution)/shard_map/cond/branch_0_fun/all_to_all | solution.py:244
  47.5 0.0 copy-done
  47.5 0.0 copy-done.2
  47.5 0.0 copy-done.4
  47.5 0.9 %branch_0_fun.5 = bf16[1024,128]{1,0:T(8,128)(2,1)} custom-call(f32[1024,128]{1,0:T(8,128)S(1)} %bitcast.6, bf16[1024,128]{1,0:T(8,128)(2,1)S(1)} %copy-done.4, bf16[1024,128]{1,0:T(8,128)(2,1)S(1)} %copy-done, bf16[1024,128]{1,0:T(8,128)(2,1)S(1)} %copy-done.2, f32[1,128]{1,0:T(1,128)S(1)} %get-tuple-element.59.bias_ref), custom_call_target="tpu_custom_call" | custom-call | flops 524288 | bytes 1572864 | tf_op jit(solution)/shard_map/cond/branch_0_fun/pallas_call | solution.py:272
  (4 shorter events, 0.1 us)
Async XLA Ops:
  1.5 6.7 %collective-permute-start = (f32[4,96,128]{2,1,0:T(8,128)S(1)}, f32[4,96,128]{2,1,0:T(8,128)S(1)}, u32[]{:S(2)}, u32[]{:S(2)}) collective-permute-start(f32[4,96,128]{2,1,0:T(8,128)S(1)} %get-tuple-element.76), channel_id=1, source_target_pairs={{0,16},{16,0},{1,17},{17,1},{2,18},{18,2},{3,19},{19,3},{4,20},{20... | collective-permute-start | bytes 589832 | tf_op jit(solution)/shard_map/cond/branch_0_fun/ppermute | solution.py:262
  4.5 5.8 %collective-permute-start.1 = (f32[4,96,128]{2,1,0:T(8,128)S(1)}, f32[4,96,128]{2,1,0:T(8,128)S(1)}, u32[]{:S(2)}, u32[]{:S(2)}) collective-permute-start(f32[4,96,128]{2,1,0:T(8,128)S(1)} %get-tuple-element.75), channel_id=1, source_target_pairs={{0,16},{16,0},{1,17},{17,1},{2,18},{18,2},{3,19},{19,3},{4,20},{20... | collective-permute-start | bytes 589832 | tf_op jit(solution)/shard_map/cond/branch_0_fun/ppermute | solution.py:262
  10.5 19.5 %copy-start.6 = (bf16[512,256]{1,0:T(8,128)(2,1)S(1)}, bf16[512,256]{1,0:T(8,128)(2,1)}, u32[]{:S(2)}) copy-start(bf16[512,256]{1,0:T(8,128)(2,1)} %get-tuple-element.56.back_tail_ref) | copy-start | bytes 786436 | tf_op jit(solution)/shard_map/cond
  10.5 19.5 %copy-start.8 = (bf16[512,256]{1,0:T(8,128)(2,1)S(1)}, bf16[512,256]{1,0:T(8,128)(2,1)}, u32[]{:S(2)}) copy-start(bf16[512,256]{1,0:T(8,128)(2,1)} %get-tuple-element.55.tail_ref) | copy-start | bytes 786436 | tf_op jit(solution)/shard_map/cond
  10.5 19.5 %copy-start.10 = (bf16[128,256]{1,0:T(8,128)(2,1)S(1)}, bf16[128,256]{1,0:T(8,128)(2,1)}, u32[]{:S(2)}) copy-start(bf16[128,256]{1,0:T(8,128)(2,1)} %get-tuple-element.57.back_head_ref) | copy-start | bytes 196612 | tf_op jit(solution)/shard_map/cond
  10.5 19.5 %copy-start.12 = (f32[64,256]{1,0:T(8,128)S(1)}, f32[64,256]{1,0:T(8,128)}, u32[]{:S(2)}) copy-start(f32[64,256]{1,0:T(8,128)} %get-tuple-element.54.twist_ref) | copy-start | bytes 196612 | tf_op jit(solution)/shard_map/cond
  10.5 19.5 %copy-start.14 = (bf16[128,192]{1,0:T(8,128)(2,1)S(1)}, bf16[128,192]{1,0:T(8,128)(2,1)}, u32[]{:S(2)}) copy-start(bf16[128,192]{1,0:T(8,128)(2,1)} %get-tuple-element.53.head_ref) | copy-start | bytes 147460 | tf_op jit(solution)/shard_map/cond
  31.8 15.7 %copy-start = (bf16[1024,128]{1,0:T(8,128)(2,1)S(1)}, bf16[1024,128]{1,0:T(8,128)(2,1)}, u32[]{:S(2)}) copy-start(bf16[1024,128]{1,0:T(8,128)(2,1)} %get-tuple-element.48.key_ref) | copy-start | bytes 786436 | tf_op jit(solution)/shard_map/cond
  31.8 15.7 %copy-start.2 = (bf16[1024,128]{1,0:T(8,128)(2,1)S(1)}, bf16[1024,128]{1,0:T(8,128)(2,1)}, u32[]{:S(2)}) copy-start(bf16[1024,128]{1,0:T(8,128)(2,1)} %get-tuple-element.49.value_ref) | copy-start | bytes 786436 | tf_op jit(solution)/shard_map/cond
  31.8 15.7 %copy-start.4 = (bf16[1024,128]{1,0:T(8,128)(2,1)S(1)}, bf16[1024,128]{1,0:T(8,128)(2,1)}, u32[]{:S(2)}) copy-start(bf16[1024,128]{1,0:T(8,128)(2,1)} %get-tuple-element.58.query_ref) | copy-start | bytes 786436 | tf_op jit(solution)/shard_map/cond

commit v17 on v13

--- a/solution.py
+++ b/solution.py
@@ -97,6 +97,14 @@
         reals.append(real * cos + imag * sin)
         imags.append(imag * cos - real * sin)
     return jnp.concatenate([jnp.concatenate(reals, axis=1), jnp.concatenate(imags, axis=1)], axis=0)
+
+
+def turn_exact(values):
+    size = values.shape[1]
+    rows = lax.broadcasted_iota(jnp.int32, (size, 2 * size), 0)
+    unit = (lax.broadcasted_iota(jnp.int32, (size, 2 * size), 1) % size == rows).astype(BF16)
+    parts = jnp.concatenate(halves(values), axis=1)
+    return lax.dot_general(unit, parts, (((1,), (1,)), ((), ())), preferred_element_type=F32)
 
 
 def pack_kernel(layout, where_ref, key_ref, value_ref, filter_ref, bias_ref, out_ref, bias_out, key, value, taps, sems):
@@ -115,7 +123,7 @@
             for fetch in fetches[row // (rows // cuts) * 2 :][:2]:
                 fetch.wait()
         span = pl.ds(row * LANES, LANES)
-        turned = (key[span, :].astype(F32) * value[span, :].astype(F32)).T
+        turned = turn_exact(key[span, :].astype(F32) * value[span, :].astype(F32))
         for peer in range(out_ref.shape[0]):
             out_ref[peer, pl.ds(row, own, stride=rows), :] = turned[peer * own : (peer + 1) * own]
     fetches[-2].wait()

time: 48.5 us -> 48.7 us (level)
  no operation moved by 1% of the time
where the time goes in v17:
time: 48.7 us; the launch traced here: 48.5 us
  blocking collectives  35.1 us (72%)
  waiting for transfers between devices  5.76 us (12%)
  Pallas kernels  4.29 us (9%)
  starting transfers between devices  3 us (6%)
    all_to_all x1, blocking collectives, convolve(): moved = lax.all_to_all(pair, 'seq', 0, 0, tiled=True)  19.4 us
    all_to_all x1, blocking collectives, exchange(): return lax.all_to_all(array, axes, 0, 0, tiled=True)  15.7 us
    ppermute x1, waiting for transfers between devices, convolve(): lax.ppermute(jnp.where(first, by_group[1], by_group[0]), 'groups', [(0, 1...  5.76 us
    ppermute x1, starting transfers between devices, convolve(): lax.ppermute(jnp.where(first, by_group[1], by_group[0]), 'groups', [(0, 1...  3 us
    pallas_call x1, Pallas kernels, convolve(): call(functools.partial(conv_kernel, layout, staged, min(own, 4)), [((coun...  1.77 us
    pallas_call x1, Pallas kernels, convolve(): call(functools.partial(pack_kernel, layout), [((count, own * (rows + part...  1.64 us
  transfers between devices with their start and end apart: 1, of which 1 were waited for; matrix products, arithmetic and copies ran while one was open for 0% of the time, Pallas kernels for 0%

profile of v17, /device:TPU:0, one launch (start us, length us, event | category | flops | bytes accessed | tf_op | source)
XLA Modules:
  0.0 48.5 jit_solution(10930785958610914238)
XLA Ops:
  0.0 48.5 %conditional.1 = (bf16[1024,128]{1,0:T(8,128)(2,1)}) conditional(s32[]{:T(128)} %convert_element_type.3, (f32[128]{0:T(128)}, bf16[1024,128]{1,0:T(8,128)(2,1)}, bf16[1024,128]{1,0:T(8,128)(2,1)}, f32[1024,128]{1,0:T(8,128)}, bf16[128,192]{1,0:T(8,128)(2,1)}, /*index=5*/f32[64,256]{1,0:T(8,128)}, bf16[768,256]{1,0:T(8,128)(2,1)}, ...), branch_computations={%region_0.1_spmd, %region_1.2_spmd} | conditional | flops 1259536384 | bytes 20644156 | solution.py:291
  0.0 1.6 %branch_0_fun.3 = (f32[16,96,128]{2,1,0:T(8,128)S(1)}, f32[1,128]{1,0:T(1,128)S(1)}) custom-call(s32[1]{0:T(128)} %bitcast.where_ref, bf16[1024,128]{1,0:T(8,128)(2,1)} %get-tuple-element.48.key_ref, bf16[1024,128]{1,0:T(8,128)(2,1)} %get-tuple-element.49.value_ref, f32[1024,128]{1,0:T(8,128)} %get-tuple-element.50.filter_ref, f32[1,128]{1,0:T(1,128)} %bitcast.8), custom_call_target="tpu_custom_call" | custom-call | flops 131072 | bytes 1572864 | tf_op jit(solution)/shard_map/cond/branch_0_fun/pallas_call | solution.py:254
  1.7 3.0 %collective-permute-start = (f32[8,96,128]{2,1,0:T(8,128)S(1)}, f32[8,96,128]{2,1,0:T(8,128)S(1)}, u32[]{:S(2)}, u32[]{:S(2)}) collective-permute-start(f32[8,96,128]{2,1,0:T(8,128)S(1)} %slice_select_fusion), channel_id=1, source_target_pairs={{0,16},{16,0},{1,17},{17,1},{2,18},{18,2},{3,19},{19,3},{4,20},{20... | collective-permute-start | bytes 1179656 | tf_op jit(solution)/shard_map/cond/branch_0_fun/ppermute | solution.py:267
  4.7 5.8 %collective-permute-done = f32[8,96,128]{2,1,0:T(8,128)S(1)} collective-permute-done((f32[8,96,128]{2,1,0:T(8,128)S(1)}, f32[8,96,128]{2,1,0:T(8,128)S(1)}, u32[]{:S(2)}, u32[]{:S(2)}) %collective-permute-start) | collective-permute-done | bytes 393248 | tf_op jit(solution)/shard_map/cond/branch_0_fun/ppermute | solution.py:267
  10.5 0.1 broadcast_select_fusion.1
  10.6 0.1 pad_maximum_fusion
  10.6 0.0 copy-start.6
  10.6 0.0 copy-start.8
  10.6 0.0 copy-start.10
  10.6 0.0 copy-start.12
  10.7 0.0 copy-start.14
  10.7 19.4 %all_to_all.16.moved_ref = f32[8,192,128]{2,1,0:T(8,128)S(1)} all-to-all(f32[8,192,128]{2,1,0:T(8,128)S(1)} %pad_maximum_fusion), channel_id=1, replica_groups=mesh['groups'=2,'seq'=8,'chan'=2] {'seq'}, dimensions={0} | all-to-all | bytes 1572864 | tf_op jit(solution)/shard_map/cond/branch_0_fun/all_to_all | solution.py:269
  30.1 0.0 copy-done.6
  30.1 0.0 copy-done.8
  30.1 0.0 copy-done.10
  30.1 0.0 copy-done.12
  30.1 0.0 copy-done.14
  30.1 1.8 %branch_0_fun.4 = f32[16,64,128]{2,1,0:T(8,128)S(1)} custom-call(f32[8,192,128]{2,1,0:T(8,128)S(1)} %all_to_all.16.moved_ref, bf16[128,192]{1,0:T(8,128)(2,1)S(1)} %copy-done.14, f32[64,256]{1,0:T(8,128)S(1)} %copy-done.12, bf16[768,256]{1,0:T(8,128)(2,1)S(1)} %copy-done.8, bf16[768,256]{1,0:T(8,128)(2,1)S(1)} %copy-done.6, bf16[128,256]{1,0:T(8,128)(2,1)S(1)} %copy-done.10), custom_call_target="tpu_custom_call" | custom-call | flops 1258291200 | bytes 1572864 | tf_op jit(solution)/shard_map/cond/branch_0_fun/pallas_call | solution.py:272
  31.9 0.0 copy-start
  31.9 0.0 copy-start.2
  31.9 0.0 copy-start.4
  32.0 15.7 %all_to_all.17 = f32[16,64,128]{2,1,0:T(8,128)S(1)} all-to-all(f32[16,64,128]{2,1,0:T(8,128)S(1)} %branch_0_fun.4), channel_id=1, replica_groups=mesh['groups'=2,'seq'=8,'chan'=2] {'groups','seq'}, dimensions={0} | all-to-all | bytes 1048576 | tf_op jit(solution)/shard_map/cond/branch_0_fun/all_to_all | solution.py:251
  47.6 0.0 copy-done
  47.6 0.0 copy-done.2
  47.6 0.0 copy-done.4
  47.6 0.9 %branch_0_fun.5 = bf16[1024,128]{1,0:T(8,128)(2,1)} custom-call(f32[1024,128]{1,0:T(8,128)S(1)} %bitcast.6, bf16[1024,128]{1,0:T(8,128)(2,1)S(1)} %copy-done.4, bf16[1024,128]{1,0:T(8,128)(2,1)S(1)} %copy-done, bf16[1024,128]{1,0:T(8,128)(2,1)S(1)} %copy-done.2, f32[1,128]{1,0:T(1,128)S(1)} %get-tuple-element.59.bias_ref), custom_call_target="tpu_custom_call" | custom-call | flops 524288 | bytes 1572864 | tf_op jit(solution)/shard_map/cond/branch_0_fun/pallas_call | solution.py:277
  (1 shorter events, 0.0 us)
Async XLA Ops:
  1.7 8.8 %collective-permute-start = (f32[8,96,128]{2,1,0:T(8,128)S(1)}, f32[8,96,128]{2,1,0:T(8,128)S(1)}, u32[]{:S(2)}, u32[]{:S(2)}) collective-permute-start(f32[8,96,128]{2,1,0:T(8,128)S(1)} %slice_select_fusion), channel_id=1, source_target_pairs={{0,16},{16,0},{1,17},{17,1},{2,18},{18,2},{3,19},{19,3},{4,20},{20... | collective-permute-start | bytes 1179656 | tf_op jit(solution)/shard_map/cond/branch_0_fun/ppermute | solution.py:267
  10.6 19.5 %copy-start.6 = (bf16[768,256]{1,0:T(8,128)(2,1)S(1)}, bf16[768,256]{1,0:T(8,128)(2,1)}, u32[]{:S(2)}) copy-start(bf16[768,256]{1,0:T(8,128)(2,1)} %get-tuple-element.56.back_tail_ref) | copy-start | bytes 1179652 | tf_op jit(solution)/shard_map/cond
  10.6 19.5 %copy-start.8 = (bf16[768,256]{1,0:T(8,128)(2,1)S(1)}, bf16[768,256]{1,0:T(8,128)(2,1)}, u32[]{:S(2)}) copy-start(bf16[768,256]{1,0:T(8,128)(2,1)} %get-tuple-element.55.tail_ref) | copy-start | bytes 1179652 | tf_op jit(solution)/shard_map/cond
  10.6 19.5 %copy-start.10 = (bf16[128,256]{1,0:T(8,128)(2,1)S(1)}, bf16[128,256]{1,0:T(8,128)(2,1)}, u32[]{:S(2)}) copy-start(bf16[128,256]{1,0:T(8,128)(2,1)} %get-tuple-element.57.back_head_ref) | copy-start | bytes 196612 | tf_op jit(solution)/shard_map/cond
  10.6 19.5 %copy-start.12 = (f32[64,256]{1,0:T(8,128)S(1)}, f32[64,256]{1,0:T(8,128)}, u32[]{:S(2)}) copy-start(f32[64,256]{1,0:T(8,128)} %get-tuple-element.54.twist_ref) | copy-start | bytes 196612 | tf_op jit(solution)/shard_map/cond
  10.7 19.5 %copy-start.14 = (bf16[128,192]{1,0:T(8,128)(2,1)S(1)}, bf16[128,192]{1,0:T(8,128)(2,1)}, u32[]{:S(2)}) copy-start(bf16[128,192]{1,0:T(8,128)(2,1)} %get-tuple-element.53.head_ref) | copy-start | bytes 147460 | tf_op jit(solution)/shard_map/cond
  31.9 15.7 %copy-start = (bf16[1024,128]{1,0:T(8,128)(2,1)S(1)}, bf16[1024,128]{1,0:T(8,128)(2,1)}, u32[]{:S(2)}) copy-start(bf16[1024,128]{1,0:T(8,128)(2,1)} %get-tuple-element.48.key_ref) | copy-start | bytes 786436 | tf_op jit(solution)/shard_map/cond
  31.9 15.7 %copy-start.2 = (bf16[1024,128]{1,0:T(8,128)(2,1)S(1)}, bf16[1024,128]{1,0:T(8,128)(2,1)}, u32[]{:S(2)}) copy-start(bf16[1024,128]{1,0:T(8,128)(2,1)} %get-tuple-element.49.value_ref) | copy-start | bytes 786436 | tf_op jit(solution)/shard_map/cond
  31.9 15.7 %copy-start.4 = (bf16[1024,128]{1,0:T(8,128)(2,1)S(1)}, bf16[1024,128]{1,0:T(8,128)(2,1)}, u32[]{:S(2)}) copy-start(bf16[1024,128]{1,0:T(8,128)(2,1)} %get-tuple-element.58.query_ref) | copy-start | bytes 786436 | tf_op jit(solution)/shard_map/cond

commit v18 on v15

--- a/solution.py
+++ b/solution.py
@@ -277,7 +277,7 @@
     if cores == 1 or groups == 1:
         return convolve(groups, blocks, False, *args)
     return lax.cond(
-        lax.axis_index("chan") % 2 == 0,
+        lax.axis_index("chan") % 2 == 1,
         functools.partial(convolve, groups, blocks, False),
         functools.partial(convolve, groups, blocks, True),
         *args,

time: 52.3 us -> 58.7 us (1.12); the launches traced: 51.3 us -> 58.4 us
  blocking collectives: 47.1 us -> 54 us
    all_to_all x0 -> x2, blocking collectives: none -> 39.1 us  [the longest x1 24.7 us: convolve(): moved = lax.all_to_all(pair, 'seq', 0, 0, tiled=True)]
    all_to_all x2 -> x1, blocking collectives: 47.1 us -> 14.9 us  [exchange(): return lax.all_to_all(array, axes, 0, 0, tiled=True)]
where the time goes in v18:
time: 58.7 us; the launch traced here: 58.4 us
  blocking collectives  54 us (92%)
  Pallas kernels  4.09 us (7%)
    all_to_all x1, blocking collectives, convolve(): moved = lax.all_to_all(pair, 'seq', 0, 0, tiled=True)  24.7 us
    all_to_all x1, blocking collectives, exchange(): return lax.all_to_all(array, axes, 0, 0, tiled=True)  14.9 us
    all_to_all x1, blocking collectives, convolve(): by_group = lax.all_to_all(by_group, 'groups', 0, 0, tiled=True)  14.4 us
    pallas_call x1, Pallas kernels, convolve(): call(functools.partial(conv_kernel, layout, staged, min(own, 4)), [((coun...  1.77 us
    pallas_call x1, Pallas kernels, convolve(): call(functools.partial(pack_kernel, layout), [((count, own * (rows + part...  1.43 us

profile of v18, /device:TPU:0, one launch (start us, length us, event | category | flops | bytes accessed | tf_op | source)
XLA Modules:
  0.0 58.4 jit_solution(13791651979403973717)
XLA Ops:
  0.0 58.4 %conditional.1 = (bf16[1024,128]{1,0:T(8,128)(2,1)}) conditional(s32[]{:T(128)} %convert_element_type.3, (f32[128]{0:T(128)}, bf16[1024,128]{1,0:T(8,128)(2,1)}, bf16[1024,128]{1,0:T(8,128)(2,1)}, f32[1024,128]{1,0:T(8,128)}, bf16[128,192]{1,0:T(8,128)(2,1)}, /*index=5*/f32[64,256]{1,0:T(8,128)}, bf16[768,256]{1,0:T(8,128)(2,1)}, ...), branch_computations={%region_0.1_spmd, %region_1.2_spmd} | conditional | flops 1259143168 | bytes 19071240 | solution.py:279
  0.0 1.4 %branch_0_fun.3 = (f32[16,96,128]{2,1,0:T(8,128)S(1)}, f32[1,128]{1,0:T(1,128)S(1)}) custom-call(s32[1]{0:T(128)} %bitcast.where_ref, bf16[1024,128]{1,0:T(8,128)(2,1)} %get-tuple-element.48.key_ref, bf16[1024,128]{1,0:T(8,128)(2,1)} %get-tuple-element.49.value_ref, f32[1024,128]{1,0:T(8,128)} %get-tuple-element.50.filter_ref, f32[1,128]{1,0:T(1,128)} %bitcast.14), custom_call_target="tpu_custom_call" | custom-call | flops 131072 | bytes 1572864 | tf_op jit(solution)/shard_map/cond/branch_0_fun/pallas_call | solution.py:246
  1.4 14.4 %all_to_all.20 = f32[2,8,96,128]{3,2,1,0:T(8,128)S(1)} all-to-all(f32[2,8,96,128]{3,2,1,0:T(8,128)S(1)} %bitcast.13), channel_id=1, replica_groups=mesh['groups'=2,'seq'=8,'chan'=2] {'groups'}, dimensions={0} | all-to-all | bytes 1572864 | tf_op jit(solution)/shard_map/cond/branch_0_fun/all_to_all | solution.py:255
  15.8 0.1 slice_bitcast_fusion.1
  15.9 0.1 pad_maximum_fusion
  15.9 0.0 copy-start.6
  15.9 0.0 copy-start.8
  15.9 0.0 copy-start.10
  16.0 0.0 copy-start.12
  16.0 0.0 copy-start.14
  16.0 24.7 %all_to_all.21.moved_ref = f32[8,192,128]{2,1,0:T(8,128)S(1)} all-to-all(f32[8,192,128]{2,1,0:T(8,128)S(1)} %pad_maximum_fusion), channel_id=1, replica_groups=mesh['groups'=2,'seq'=8,'chan'=2] {'seq'}, dimensions={0} | all-to-all | bytes 1572864 | tf_op jit(solution)/shard_map/cond/branch_0_fun/all_to_all | solution.py:257
  40.7 0.0 copy-done.6
  40.7 0.0 copy-done.8
  40.7 0.0 copy-done.10
  40.7 0.0 copy-done.12
  40.7 0.0 copy-done.14
  40.8 1.8 %branch_0_fun.4 = f32[16,64,128]{2,1,0:T(8,128)S(1)} custom-call(f32[8,192,128]{2,1,0:T(8,128)S(1)} %all_to_all.21.moved_ref, bf16[128,192]{1,0:T(8,128)(2,1)S(1)} %copy-done.14, f32[64,256]{1,0:T(8,128)S(1)} %copy-done.12, bf16[768,256]{1,0:T(8,128)(2,1)S(1)} %copy-done.8, bf16[768,256]{1,0:T(8,128)(2,1)S(1)} %copy-done.6, bf16[128,256]{1,0:T(8,128)(2,1)S(1)} %copy-done.10), custom_call_target="tpu_custom_call" | custom-call | flops 1258291200 | bytes 1572864 | tf_op jit(solution)/shard_map/cond/branch_0_fun/pallas_call | solution.py:260
  42.5 0.0 copy-start
  42.5 0.0 copy-start.2
  42.6 0.0 copy-start.4
  42.6 14.9 %all_to_all.22 = f32[16,64,128]{2,1,0:T(8,128)S(1)} all-to-all(f32[16,64,128]{2,1,0:T(8,128)S(1)} %branch_0_fun.4), channel_id=1, replica_groups=mesh['groups'=2,'seq'=8,'chan'=2] {'groups','seq'}, dimensions={0} | all-to-all | bytes 1048576 | tf_op jit(solution)/shard_map/cond/branch_0_fun/all_to_all | solution.py:243
  57.5 0.0 copy-done
  57.5 0.0 copy-done.2
  57.5 0.0 copy-done.4
  57.5 0.9 %branch_0_fun.5 = bf16[1024,128]{1,0:T(8,128)(2,1)} custom-call(f32[1024,128]{1,0:T(8,128)S(1)} %bitcast.11, bf16[1024,128]{1,0:T(8,128)(2,1)S(1)} %copy-done.4, bf16[1024,128]{1,0:T(8,128)(2,1)S(1)} %copy-done, bf16[1024,128]{1,0:T(8,128)(2,1)S(1)} %copy-done.2, f32[1,128]{1,0:T(1,128)S(1)} %get-tuple-element.59.bias_ref), custom_call_target="tpu_custom_call" | custom-call | flops 524288 | bytes 1572864 | tf_op jit(solution)/shard_map/cond/branch_0_fun/pallas_call | solution.py:265
Async XLA Ops:
  15.9 24.8 %copy-start.6 = (bf16[768,256]{1,0:T(8,128)(2,1)S(1)}, bf16[768,256]{1,0:T(8,128)(2,1)}, u32[]{:S(2)}) copy-start(bf16[768,256]{1,0:T(8,128)(2,1)} %get-tuple-element.56.back_tail_ref) | copy-start | bytes 1179652 | tf_op jit(solution)/shard_map/cond
  15.9 24.8 %copy-start.8 = (bf16[768,256]{1,0:T(8,128)(2,1)S(1)}, bf16[768,256]{1,0:T(8,128)(2,1)}, u32[]{:S(2)}) copy-start(bf16[768,256]{1,0:T(8,128)(2,1)} %get-tuple-element.55.tail_ref) | copy-start | bytes 1179652 | tf_op jit(solution)/shard_map/cond
  15.9 24.8 %copy-start.10 = (bf16[128,256]{1,0:T(8,128)(2,1)S(1)}, bf16[128,256]{1,0:T(8,128)(2,1)}, u32[]{:S(2)}) copy-start(bf16[128,256]{1,0:T(8,128)(2,1)} %get-tuple-element.57.back_head_ref) | copy-start | bytes 196612 | tf_op jit(solution)/shard_map/cond
  16.0 24.8 %copy-start.12 = (f32[64,256]{1,0:T(8,128)S(1)}, f32[64,256]{1,0:T(8,128)}, u32[]{:S(2)}) copy-start(f32[64,256]{1,0:T(8,128)} %get-tuple-element.54.twist_ref) | copy-start | bytes 196612 | tf_op jit(solution)/shard_map/cond
  16.0 24.8 %copy-start.14 = (bf16[128,192]{1,0:T(8,128)(2,1)S(1)}, bf16[128,192]{1,0:T(8,128)(2,1)}, u32[]{:S(2)}) copy-start(bf16[128,192]{1,0:T(8,128)(2,1)} %get-tuple-element.53.head_ref) | copy-start | bytes 147460 | tf_op jit(solution)/shard_map/cond
  42.5 15.0 %copy-start = (bf16[1024,128]{1,0:T(8,128)(2,1)S(1)}, bf16[1024,128]{1,0:T(8,128)(2,1)}, u32[]{:S(2)}) copy-start(bf16[1024,128]{1,0:T(8,128)(2,1)} %get-tuple-element.48.key_ref) | copy-start | bytes 786436 | tf_op jit(solution)/shard_map/cond
  42.5 15.0 %copy-start.2 = (bf16[1024,128]{1,0:T(8,128)(2,1)S(1)}, bf16[1024,128]{1,0:T(8,128)(2,1)}, u32[]{:S(2)}) copy-start(bf16[1024,128]{1,0:T(8,128)(2,1)} %get-tuple-element.49.value_ref) | copy-start | bytes 786436 | tf_op jit(solution)/shard_map/cond
  42.6 15.0 %copy-start.4 = (bf16[1024,128]{1,0:T(8,128)(2,1)S(1)}, bf16[1024,128]{1,0:T(8,128)(2,1)}, u32[]{:S(2)}) copy-start(bf16[1024,128]{1,0:T(8,128)(2,1)} %get-tuple-element.58.query_ref) | copy-start | bytes 786436 | tf_op jit(solution)/shard_map/cond

commit v19 on v13

--- a/solution.py
+++ b/solution.py
@@ -155,7 +155,9 @@
     return signals
 
 
-def conv_kernel(layout, staged, pieces, moved_ref, head_ref, twist_ref, tail_ref, back_tail_ref, back_head_ref, out_ref):
+def conv_kernel(
+    layout, staged, pieces, moved_ref, head_ref, twist_ref, tail_ref, back_tail_ref, back_head_ref, result_ref, out_ref, sem
+):
     rows, own, part, groups = layout
     blocks = out_ref.shape[0] // groups
     outer = blocks * rows
@@ -183,6 +185,9 @@
             out_ref[pl.ds(group * blocks, blocks), start : start + rows] = result[
                 :, idx * LANES : (idx + 1) * LANES
             ].reshape(blocks, rows, LANES)
+    store = pltpu.make_async_copy(out_ref, result_ref, sem)
+    store.start()
+    store.wait()
 
 
 def gate_kernel(rows, conv_ref, query_ref, key_ref, value_ref, bias_ref, out_ref, gated, sems):
@@ -261,10 +266,15 @@
         moved = lax.all_to_all(pair, "seq", 0, 0, tiled=True)
     else:
         moved = exchange(packed)
-    local = call(
+    local = pl.pallas_call(
         functools.partial(conv_kernel, layout, staged, min(own, 4)),
-        [((count, own * rows, LANES), F32)], [VMEM] * 6, 5 * macs, 3 * size,
-    )(moved, head, twist, tail, back_tail, back_head)[0]
+        out_shape=pltpu.HBM((count, own * rows, LANES), F32),
+        in_specs=[VMEM] * 6,
+        out_specs=HBM,
+        scratch_shapes=[pltpu.VMEM((count, own * rows, LANES), F32), pltpu.SemaphoreType.DMA],
+        compiler_params=pltpu.CompilerParams(vmem_limit_bytes=VMEM_LIMIT),
+        cost_estimate=pl.CostEstimate(flops=5 * macs, bytes_accessed=3 * size, transcendentals=0),
+    )(moved, head, twist, tail, back_tail, back_head)
     convolved = exchange(local).reshape(chans * rows, LANES)
     return pl.pallas_call(
         functools.partial(gate_kernel, rows),

time: 48.5 us -> 49.7 us (1.025)
  Pallas kernels: 4.09 us -> 4.91 us
    pallas_call x1, Pallas kernels: 1.77 us -> 2.6 us  [convolve(): pl.pallas_call(functools.partial(conv_kernel, layout, staged, min(own, 4)...]
where the time goes in v19:
time: 49.7 us; the launch traced here: 49.4 us
  blocking collectives  35.3 us (71%)
  waiting for transfers between devices  5.76 us (12%)
  Pallas kernels  4.91 us (10%)
  starting transfers between devices  3 us (6%)
    all_to_all x1, blocking collectives, convolve(): moved = lax.all_to_all(pair, 'seq', 0, 0, tiled=True)  19.4 us
    all_to_all x1, blocking collectives, exchange(): return lax.all_to_all(array, axes, 0, 0, tiled=True)  15.9 us
    ppermute x1, waiting for transfers between devices, convolve(): lax.ppermute(jnp.where(first, by_group[1], by_group[0]), 'groups', [(0, 1...  5.76 us
    ppermute x1, starting transfers between devices, convolve(): lax.ppermute(jnp.where(first, by_group[1], by_group[0]), 'groups', [(0, 1...  3 us
    pallas_call x1, Pallas kernels, convolve(): pl.pallas_call(functools.partial(conv_kernel, layout, staged, min(own, 4)...  2.6 us
    pallas_call x1, Pallas kernels, convolve(): call(functools.partial(pack_kernel, layout), [((count, own * (rows + part...  1.43 us
  transfers between devices with their start and end apart: 1, of which 1 were waited for; matrix products, arithmetic and copies ran while one was open for 0% of the time, Pallas kernels for 0%

profile of v19, /device:TPU:0, one launch (start us, length us, event | category | flops | bytes accessed | tf_op | source)
XLA Modules:
  0.0 49.4 jit_solution(2735510542748746907)
XLA Ops:
  0.0 49.4 %conditional.1 = (bf16[1024,128]{1,0:T(8,128)(2,1)}) conditional(s32[]{:T(128)} %convert_element_type.3, (f32[128]{0:T(128)}, bf16[1024,128]{1,0:T(8,128)(2,1)}, bf16[1024,128]{1,0:T(8,128)(2,1)}, f32[1024,128]{1,0:T(8,128)}, bf16[128,192]{1,0:T(8,128)(2,1)}, /*index=5*/f32[64,256]{1,0:T(8,128)}, bf16[768,256]{1,0:T(8,128)(2,1)}, ...), branch_computations={%region_0.1_spmd, %region_1.2_spmd} | conditional | flops 1259536384 | bytes 20644156 | solution.py:293
  0.0 1.4 %branch_0_fun.3 = (f32[16,96,128]{2,1,0:T(8,128)S(1)}, f32[1,128]{1,0:T(1,128)S(1)}) custom-call(s32[1]{0:T(128)} %bitcast.where_ref, bf16[1024,128]{1,0:T(8,128)(2,1)} %get-tuple-element.48.key_ref, bf16[1024,128]{1,0:T(8,128)(2,1)} %get-tuple-element.49.value_ref, f32[1024,128]{1,0:T(8,128)} %get-tuple-element.50.filter_ref, f32[1,128]{1,0:T(1,128)} %bitcast.8), custom_call_target="tpu_custom_call" | custom-call | flops 131072 | bytes 1572864 | tf_op jit(solution)/shard_map/cond/branch_0_fun/pallas_call | solution.py:251
  1.5 3.0 %collective-permute-start = (f32[8,96,128]{2,1,0:T(8,128)S(1)}, f32[8,96,128]{2,1,0:T(8,128)S(1)}, u32[]{:S(2)}, u32[]{:S(2)}) collective-permute-start(f32[8,96,128]{2,1,0:T(8,128)S(1)} %slice_select_fusion), channel_id=1, source_target_pairs={{0,16},{16,0},{1,17},{17,1},{2,18},{18,2},{3,19},{19,3},{4,20},{20... | collective-permute-start | bytes 1179656 | tf_op jit(solution)/shard_map/cond/branch_0_fun/ppermute | solution.py:264
  4.5 5.8 %collective-permute-done = f32[8,96,128]{2,1,0:T(8,128)S(1)} collective-permute-done((f32[8,96,128]{2,1,0:T(8,128)S(1)}, f32[8,96,128]{2,1,0:T(8,128)S(1)}, u32[]{:S(2)}, u32[]{:S(2)}) %collective-permute-start) | collective-permute-done | bytes 393248 | tf_op jit(solution)/shard_map/cond/branch_0_fun/ppermute | solution.py:264
  10.3 0.1 broadcast_select_fusion.1
  10.3 0.1 pad_maximum_fusion
  10.4 0.0 copy-start.6
  10.4 0.0 copy-start.8
  10.4 0.0 copy-start.10
  10.4 0.0 copy-start.12
  10.5 0.0 copy-start.14
  10.5 19.4 %all_to_all.16.moved_ref = f32[8,192,128]{2,1,0:T(8,128)S(1)} all-to-all(f32[8,192,128]{2,1,0:T(8,128)S(1)} %pad_maximum_fusion), channel_id=1, replica_groups=mesh['groups'=2,'seq'=8,'chan'=2] {'seq'}, dimensions={0} | all-to-all | bytes 1572864 | tf_op jit(solution)/shard_map/cond/branch_0_fun/all_to_all | solution.py:266
  29.9 0.0 copy-done.6
  29.9 0.0 copy-done.8
  29.9 0.0 copy-done.10
  29.9 0.0 copy-done.12
  29.9 0.0 copy-done.14
  29.9 2.6 %branch_0_fun.4 = f32[16,64,128]{2,1,0:T(8,128)} custom-call(f32[8,192,128]{2,1,0:T(8,128)S(1)} %all_to_all.16.moved_ref, bf16[128,192]{1,0:T(8,128)(2,1)S(1)} %copy-done.14, f32[64,256]{1,0:T(8,128)S(1)} %copy-done.12, bf16[768,256]{1,0:T(8,128)(2,1)S(1)} %copy-done.8, bf16[768,256]{1,0:T(8,128)(2,1)S(1)} %copy-done.6, bf16[128,256]{1,0:T(8,128)(2,1)S(1)} %copy-done.10), custom_call_target="tpu_custom_call" | custom-call | flops 1258291200 | bytes 1572864 | tf_op jit(solution)/shard_map/cond/branch_0_fun/pallas_call | solution.py:269
  32.5 0.0 copy-start
  32.6 0.0 copy-start.2
  32.6 0.0 copy-start.4
  32.6 15.9 %all_to_all.17 = f32[16,64,128]{2,1,0:T(8,128)S(1)} all-to-all(f32[16,64,128]{2,1,0:T(8,128)} %branch_0_fun.4), channel_id=1, replica_groups=mesh['groups'=2,'seq'=8,'chan'=2] {'groups','seq'}, dimensions={0} | all-to-all | bytes 1048576 | tf_op jit(solution)/shard_map/cond/branch_0_fun/all_to_all | solution.py:248
  48.5 0.0 copy-done
  48.5 0.0 copy-done.2
  48.5 0.0 copy-done.4
  48.5 0.9 %branch_0_fun.5 = bf16[1024,128]{1,0:T(8,128)(2,1)} custom-call(f32[1024,128]{1,0:T(8,128)S(1)} %bitcast.6, bf16[1024,128]{1,0:T(8,128)(2,1)S(1)} %copy-done.4, bf16[1024,128]{1,0:T(8,128)(2,1)S(1)} %copy-done, bf16[1024,128]{1,0:T(8,128)(2,1)S(1)} %copy-done.2, f32[1,128]{1,0:T(1,128)S(1)} %get-tuple-element.59.bias_ref), custom_call_target="tpu_custom_call" | custom-call | flops 524288 | bytes 1572864 | tf_op jit(solution)/shard_map/cond/branch_0_fun/pallas_call | solution.py:279
  (1 shorter events, 0.0 us)
Async XLA Ops:
  1.5 8.8 %collective-permute-start = (f32[8,96,128]{2,1,0:T(8,128)S(1)}, f32[8,96,128]{2,1,0:T(8,128)S(1)}, u32[]{:S(2)}, u32[]{:S(2)}) collective-permute-start(f32[8,96,128]{2,1,0:T(8,128)S(1)} %slice_select_fusion), channel_id=1, source_target_pairs={{0,16},{16,0},{1,17},{17,1},{2,18},{18,2},{3,19},{19,3},{4,20},{20... | collective-permute-start | bytes 1179656 | tf_op jit(solution)/shard_map/cond/branch_0_fun/ppermute | solution.py:264
  10.4 19.5 %copy-start.6 = (bf16[768,256]{1,0:T(8,128)(2,1)S(1)}, bf16[768,256]{1,0:T(8,128)(2,1)}, u32[]{:S(2)}) copy-start(bf16[768,256]{1,0:T(8,128)(2,1)} %get-tuple-element.56.back_tail_ref) | copy-start | bytes 1179652 | tf_op jit(solution)/shard_map/cond
  10.4 19.5 %copy-start.8 = (bf16[768,256]{1,0:T(8,128)(2,1)S(1)}, bf16[768,256]{1,0:T(8,128)(2,1)}, u32[]{:S(2)}) copy-start(bf16[768,256]{1,0:T(8,128)(2,1)} %get-tuple-element.55.tail_ref) | copy-start | bytes 1179652 | tf_op jit(solution)/shard_map/cond
  10.4 19.5 %copy-start.10 = (bf16[128,256]{1,0:T(8,128)(2,1)S(1)}, bf16[128,256]{1,0:T(8,128)(2,1)}, u32[]{:S(2)}) copy-start(bf16[128,256]{1,0:T(8,128)(2,1)} %get-tuple-element.57.back_head_ref) | copy-start | bytes 196612 | tf_op jit(solution)/shard_map/cond
  10.4 19.5 %copy-start.12 = (f32[64,256]{1,0:T(8,128)S(1)}, f32[64,256]{1,0:T(8,128)}, u32[]{:S(2)}) copy-start(f32[64,256]{1,0:T(8,128)} %get-tuple-element.54.twist_ref) | copy-start | bytes 196612 | tf_op jit(solution)/shard_map/cond
  10.5 19.5 %copy-start.14 = (bf16[128,192]{1,0:T(8,128)(2,1)S(1)}, bf16[128,192]{1,0:T(8,128)(2,1)}, u32[]{:S(2)}) copy-start(bf16[128,192]{1,0:T(8,128)(2,1)} %get-tuple-element.53.head_ref) | copy-start | bytes 147460 | tf_op jit(solution)/shard_map/cond
  32.5 15.9 %copy-start = (bf16[1024,128]{1,0:T(8,128)(2,1)S(1)}, bf16[1024,128]{1,0:T(8,128)(2,1)}, u32[]{:S(2)}) copy-start(bf16[1024,128]{1,0:T(8,128)(2,1)} %get-tuple-element.48.key_ref) | copy-start | bytes 786436 | tf_op jit(solution)/shard_map/cond
  32.6 15.9 %copy-start.2 = (bf16[1024,128]{1,0:T(8,128)(2,1)S(1)}, bf16[1024,128]{1,0:T(8,128)(2,1)}, u32[]{:S(2)}) copy-start(bf16[1024,128]{1,0:T(8,128)(2,1)} %get-tuple-element.49.value_ref) | copy-start | bytes 786436 | tf_op jit(solution)/shard_map/cond
  32.6 15.9 %copy-start.4 = (bf16[1024,128]{1,0:T(8,128)(2,1)S(1)}, bf16[1024,128]{1,0:T(8,128)(2,1)}, u32[]{:S(2)}) copy-start(bf16[1024,128]{1,0:T(8,128)(2,1)} %get-tuple-element.58.query_ref) | copy-start | bytes 786436 | tf_op jit(solution)/shard_map/cond

commit v20 on v18

--- a/solution.py
+++ b/solution.py
@@ -99,8 +99,14 @@
     return jnp.concatenate([jnp.concatenate(reals, axis=1), jnp.concatenate(imags, axis=1)], axis=0)
 
 
-def pack_kernel(layout, where_ref, key_ref, value_ref, filter_ref, bias_ref, out_ref, bias_out, key, value, taps, sems):
-    rows, own, part, groups = layout
+def pack_kernel(layout, staged, where_ref, key_ref, value_ref, filter_ref, bias_ref, out_ref, bias_out, key, value, taps, sems):
+    rows, own, part, groups = layout
+    count = out_ref.shape[0]
+    blocks = count // groups
+    homes = [
+        ((peer // blocks ^ where_ref[0]) * blocks + peer % blocks if staged else peer, peer * own)
+        for peer in range(count)
+    ]
     first = where_ref[0] * (part * LANES if part < rows else 0)
     taken = filter_ref.at[pl.ds(pl.multiple_of(first, part * LANES), part * LANES)]
     cuts = 2 if rows % 2 == 0 else 1
@@ -116,13 +122,13 @@
                 fetch.wait()
         span = pl.ds(row * LANES, LANES)
         turned = (key[span, :].astype(F32) * value[span, :].astype(F32)).T
-        for peer in range(out_ref.shape[0]):
-            out_ref[peer, pl.ds(row, own, stride=rows), :] = turned[peer * own : (peer + 1) * own]
+        for place, chan in homes:
+            out_ref[place, pl.ds(row, own, stride=rows), :] = turned[chan : chan + own]
     fetches[-2].wait()
     for row in range(part):
         turned = taps[pl.ds(row * LANES, LANES), :].T
-        for peer in range(out_ref.shape[0]):
-            out_ref[peer, pl.ds(own * rows + row, own, stride=part), :] = turned[peer * own : (peer + 1) * own]
+        for place, chan in homes:
+            out_ref[place, pl.ds(own * rows + row, own, stride=part), :] = turned[chan : chan + own]
     fetches[-1].wait()
 
 
@@ -143,7 +149,7 @@
     return [values.reshape(values.shape[0] * rows, LANES) for values in parts]
 
 
-def filter_signals(layout, staged, moved_ref, chans):
+def filter_signals(layout, staged, mine, moved_ref, chans):
     rows, own, part, groups = layout
     signals = []
     for chan in chans:
@@ -151,12 +157,17 @@
             arrived(layout, staged, moved_ref, group, own * rows + chan * part, part)
             for group in range(groups if part < rows else 1)
         ]
+        if staged and len(pieces) == 2:
+            pieces = [jnp.where(mine == 0, pieces[0], pieces[1]), jnp.where(mine == 0, pieces[1], pieces[0])]
         signals.append(jnp.concatenate(pieces, axis=1).reshape(pieces[0].shape[0] * rows, LANES))
     return signals
 
 
-def conv_kernel(layout, staged, pieces, moved_ref, head_ref, twist_ref, tail_ref, back_tail_ref, back_head_ref, out_ref):
-    rows, own, part, groups = layout
+def conv_kernel(
+    layout, staged, pieces, where_ref, moved_ref, head_ref, twist_ref, tail_ref, back_tail_ref, back_head_ref, out_ref
+):
+    rows, own, part, groups = layout
+    mine = where_ref[0]
     blocks = out_ref.shape[0] // groups
     outer = blocks * rows
     scale = 1.0 / (outer * LANES)
@@ -164,7 +175,7 @@
     sets = [range(piece * own // pieces, (piece + 1) * own // pieces) for piece in range(pieces)]
     mixed = [
         head_stage(
-            filter_signals(layout, staged, moved_ref, chans) + driver_signals(layout, staged, moved_ref, chans),
+            filter_signals(layout, staged, mine, moved_ref, chans) + driver_signals(layout, staged, moved_ref, chans),
             head_ref[...],
             twist_ref[...],
         )
@@ -180,6 +191,7 @@
         for idx in range(len(chans) * groups):
             chan, group = divmod(idx, groups)
             start = (chans[0] + chan) * rows
+            group = group ^ mine if staged else group
             out_ref[pl.ds(group * blocks, blocks), start : start + rows] = result[
                 :, idx * LANES : (idx + 1) * LANES
             ].reshape(blocks, rows, LANES)
@@ -244,23 +256,22 @@
 
     sources = (key_proj, value_proj, long_filter, skip_bias.reshape(1, chans))
     packed, bias = call(
-        functools.partial(pack_kernel, layout),
+        functools.partial(pack_kernel, layout, staged),
         [((count, own * (rows + part), LANES), F32), ((1, chans), F32)],
         [SMEM] + [HBM] * 4, size // 4, size * 3,
         [pltpu.VMEM((tokens, chans), BF16), pltpu.VMEM((tokens, chans), BF16), pltpu.VMEM((part * LANES, chans), F32),
          pltpu.SemaphoreType.DMA((6,))],
     )(where, *(pltpu.with_memory_space_constraint(source, pltpu.HBM) for source in sources))
     if staged:
-        by_group = packed.reshape(groups, blocks, own * (rows + part), LANES)
-        by_group = lax.all_to_all(by_group, "groups", 0, 0, tiled=True)
-        pair = jnp.concatenate([by_group[group] for group in range(groups)], axis=1)
+        kept, sent = packed[:blocks], packed[blocks:]
+        pair = jnp.concatenate([kept, lax.ppermute(sent, "groups", [(0, 1), (1, 0)])], axis=1)
         moved = lax.all_to_all(pair, "seq", 0, 0, tiled=True)
     else:
         moved = exchange(packed)
     local = call(
         functools.partial(conv_kernel, layout, staged, min(own, 4)),
-        [((count, own * rows, LANES), F32)], [VMEM] * 6, 5 * macs, 3 * size,
-    )(moved, head, twist, tail, back_tail, back_head)[0]
+        [((count, own * rows, LANES), F32)], [SMEM] + [VMEM] * 6, 5 * macs, 3 * size,
+    )(where, moved, head, twist, tail, back_tail, back_head)[0]
     convolved = exchange(local).reshape(chans * rows, LANES)
     return pl.pallas_call(
         functools.partial(gate_kernel, rows),
@@ -274,7 +285,7 @@
 
 
 def shards(groups, blocks, cores, *args):
-    if cores == 1 or groups == 1:
+    if cores == 1 or groups != 2:
         return convolve(groups, blocks, False, *args)
     return lax.cond(
         lax.axis_index("chan") % 2 == 1,

time: 58.7 us -> 48.6 us (0.83)
  blocking collectives: 54 us -> 35.2 us
  waiting for transfers between devices: 0 us -> 5.76 us
  starting transfers between devices: 0 us -> 3 us
    all_to_all x1 -> x0, blocking collectives: 14.4 us -> none  [convolve(): by_group = lax.all_to_all(by_group, 'groups', 0, 0, tiled=True)]
    ppermute x0 -> x1, waiting for transfers between devices: none -> 5.76 us  [convolve(): lax.ppermute(sent, 'groups', [(0, 1), (1, 0)])]
    all_to_all x1, blocking collectives: 24.7 us -> 19.4 us  [convolve(): moved = lax.all_to_all(pair, 'seq', 0, 0, tiled=True)]
    ppermute x0 -> x1, starting transfers between devices: none -> 3 us  [convolve(): lax.ppermute(sent, 'groups', [(0, 1), (1, 0)])]
    all_to_all x1, blocking collectives: 14.9 us -> 15.7 us  [exchange(): return lax.all_to_all(array, axes, 0, 0, tiled=True)]
  transfers between devices with their start and end apart: 0 -> 1, of which waited for: 0 -> 1; matrix products, arithmetic and copies ran while one was open for 0% -> 0% of each run, Pallas kernels for 0% -> 0%
where the time goes in v20:
time: 48.6 us; the launch traced here: 48.4 us
  blocking collectives  35.2 us (72%)
  waiting for transfers between devices  5.76 us (12%)
  Pallas kernels  4.15 us (9%)
  starting transfers between devices  3 us (6%)
    all_to_all x1, blocking collectives, convolve(): moved = lax.all_to_all(pair, 'seq', 0, 0, tiled=True)  19.4 us
    all_to_all x1, blocking collectives, exchange(): return lax.all_to_all(array, axes, 0, 0, tiled=True)  15.7 us
    ppermute x1, waiting for transfers between devices, convolve(): lax.ppermute(sent, 'groups', [(0, 1), (1, 0)])  5.76 us
    ppermute x1, starting transfers between devices, convolve(): lax.ppermute(sent, 'groups', [(0, 1), (1, 0)])  3 us
    pallas_call x1, Pallas kernels, convolve(): call(functools.partial(conv_kernel, layout, staged, min(own, 4)), [((coun...  1.79 us
    pallas_call x1, Pallas kernels, convolve(): call(functools.partial(pack_kernel, layout, staged), [((count, own * (row...  1.48 us
  transfers between devices with their start and end apart: 1, of which 1 were waited for; matrix products, arithmetic and copies ran while one was open for 0% of the time, Pallas kernels for 0%

profile of v20, /device:TPU:0, one launch (start us, length us, event | category | flops | bytes accessed | tf_op | source)
XLA Modules:
  0.0 48.4 jit_solution(15483668946933106262)
XLA Ops:
  0.0 48.4 %conditional.1 = (bf16[1024,128]{1,0:T(8,128)(2,1)}) conditional(s32[]{:T(128)} %convert_element_type.3, (f32[128]{0:T(128)}, bf16[1024,128]{1,0:T(8,128)(2,1)}, bf16[1024,128]{1,0:T(8,128)(2,1)}, f32[1024,128]{1,0:T(8,128)}, bf16[128,192]{1,0:T(8,128)(2,1)}, /*index=5*/f32[64,256]{1,0:T(8,128)}, bf16[768,256]{1,0:T(8,128)(2,1)}, ...), branch_computations={%region_0.1_spmd, %region_1.2_spmd} | conditional | flops 1259143168 | bytes 19071280 | solution.py:290
  0.0 1.5 %branch_0_fun.3 = (f32[16,96,128]{2,1,0:T(8,128)S(1)}, f32[1,128]{1,0:T(1,128)S(1)}) custom-call(s32[1]{0:T(128)} %bitcast.where_ref, bf16[1024,128]{1,0:T(8,128)(2,1)} %get-tuple-element.48.key_ref, bf16[1024,128]{1,0:T(8,128)(2,1)} %get-tuple-element.49.value_ref, f32[1024,128]{1,0:T(8,128)} %get-tuple-element.50.filter_ref, f32[1,128]{1,0:T(1,128)} %bitcast.8), custom_call_target="tpu_custom_call" | custom-call | flops 131072 | bytes 1572864 | tf_op jit(solution)/shard_map/cond/branch_0_fun/pallas_call | solution.py:258
  1.5 0.1 fusion
  1.6 3.0 %collective-permute-start = (f32[8,96,128]{2,1,0:T(8,128)S(1)}, f32[8,96,128]{2,1,0:T(8,128)S(1)}, u32[]{:S(2)}, u32[]{:S(2)}) collective-permute-start(f32[8,96,128]{2,1,0:T(8,128)S(1)} %get-tuple-element.74), channel_id=1, source_target_pairs={{0,16},{16,0},{1,17},{17,1},{2,18},{18,2},{3,19},{19,3},{4,20},{20... | collective-permute-start | bytes 1179656 | tf_op jit(solution)/shard_map/cond/branch_0_fun/ppermute | solution.py:267
  4.6 5.8 %collective-permute-done = f32[8,96,128]{2,1,0:T(8,128)S(1)} collective-permute-done((f32[8,96,128]{2,1,0:T(8,128)S(1)}, f32[8,96,128]{2,1,0:T(8,128)S(1)}, u32[]{:S(2)}, u32[]{:S(2)}) %collective-permute-start) | collective-permute-done | bytes 393248 | tf_op jit(solution)/shard_map/cond/branch_0_fun/ppermute | solution.py:267
  10.3 0.1 pad_maximum_fusion
  10.4 0.0 copy-start.6
  10.4 0.0 copy-start.8
  10.4 0.0 copy-start.10
  10.4 0.0 copy-start.12
  10.4 0.0 copy-start.14
  10.4 19.4 %all_to_all.16.moved_ref = f32[8,192,128]{2,1,0:T(8,128)S(1)} all-to-all(f32[8,192,128]{2,1,0:T(8,128)S(1)} %pad_maximum_fusion), channel_id=1, replica_groups=mesh['groups'=2,'seq'=8,'chan'=2] {'seq'}, dimensions={0} | all-to-all | bytes 1572864 | tf_op jit(solution)/shard_map/cond/branch_0_fun/all_to_all | solution.py:268
  29.9 0.0 copy-done.6
  29.9 0.0 copy-done.8
  29.9 0.0 copy-done.10
  29.9 0.0 copy-done.12
  29.9 0.0 copy-done.14
  29.9 1.8 %branch_0_fun.4 = f32[16,64,128]{2,1,0:T(8,128)S(1)} custom-call(s32[1]{0:T(128)} %bitcast.where_ref, f32[8,192,128]{2,1,0:T(8,128)S(1)} %all_to_all.16.moved_ref, bf16[128,192]{1,0:T(8,128)(2,1)S(1)} %copy-done.14, f32[64,256]{1,0:T(8,128)S(1)} %copy-done.12, bf16[768,256]{1,0:T(8,128)(2,1)S(1)} %copy-done.8, bf16[768,256]{1,0:T(8,128)(2,1)S(1)} %copy-done.6, ...), custom_call_target="tpu_custom_call" | custom-call | flops 1258291200 | bytes 1572864 | tf_op jit(solution)/shard_map/cond/branch_0_fun/pallas_call | solution.py:271
  31.7 0.0 copy-start
  31.7 0.0 copy-start.2
  31.7 0.0 copy-start.4
  31.7 15.7 %all_to_all.17 = f32[16,64,128]{2,1,0:T(8,128)S(1)} all-to-all(f32[16,64,128]{2,1,0:T(8,128)S(1)} %branch_0_fun.4), channel_id=1, replica_groups=mesh['groups'=2,'seq'=8,'chan'=2] {'groups','seq'}, dimensions={0} | all-to-all | bytes 1048576 | tf_op jit(solution)/shard_map/cond/branch_0_fun/all_to_all | solution.py:255
  47.5 0.0 copy-done
  47.5 0.0 copy-done.2
  47.5 0.0 copy-done.4
  47.5 0.9 %branch_0_fun.5 = bf16[1024,128]{1,0:T(8,128)(2,1)} custom-call(f32[1024,128]{1,0:T(8,128)S(1)} %bitcast.6, bf16[1024,128]{1,0:T(8,128)(2,1)S(1)} %copy-done.4, bf16[1024,128]{1,0:T(8,128)(2,1)S(1)} %copy-done, bf16[1024,128]{1,0:T(8,128)(2,1)S(1)} %copy-done.2, f32[1,128]{1,0:T(1,128)S(1)} %get-tuple-element.59.bias_ref), custom_call_target="tpu_custom_call" | custom-call | flops 524288 | bytes 1572864 | tf_op jit(solution)/shard_map/cond/branch_0_fun/pallas_call | solution.py:276
Async XLA Ops:
  1.6 8.8 %collective-permute-start = (f32[8,96,128]{2,1,0:T(8,128)S(1)}, f32[8,96,128]{2,1,0:T(8,128)S(1)}, u32[]{:S(2)}, u32[]{:S(2)}) collective-permute-start(f32[8,96,128]{2,1,0:T(8,128)S(1)} %get-tuple-element.74), channel_id=1, source_target_pairs={{0,16},{16,0},{1,17},{17,1},{2,18},{18,2},{3,19},{19,3},{4,20},{20... | collective-permute-start | bytes 1179656 | tf_op jit(solution)/shard_map/cond/branch_0_fun/ppermute | solution.py:267
  10.4 19.5 %copy-start.6 = (bf16[768,256]{1,0:T(8,128)(2,1)S(1)}, bf16[768,256]{1,0:T(8,128)(2,1)}, u32[]{:S(2)}) copy-start(bf16[768,256]{1,0:T(8,128)(2,1)} %get-tuple-element.56.back_tail_ref) | copy-start | bytes 1179652 | tf_op jit(solution)/shard_map/cond
  10.4 19.5 %copy-start.8 = (bf16[768,256]{1,0:T(8,128)(2,1)S(1)}, bf16[768,256]{1,0:T(8,128)(2,1)}, u32[]{:S(2)}) copy-start(bf16[768,256]{1,0:T(8,128)(2,1)} %get-tuple-element.55.tail_ref) | copy-start | bytes 1179652 | tf_op jit(solution)/shard_map/cond
  10.4 19.5 %copy-start.10 = (bf16[128,256]{1,0:T(8,128)(2,1)S(1)}, bf16[128,256]{1,0:T(8,128)(2,1)}, u32[]{:S(2)}) copy-start(bf16[128,256]{1,0:T(8,128)(2,1)} %get-tuple-element.57.back_head_ref) | copy-start | bytes 196612 | tf_op jit(solution)/shard_map/cond
  10.4 19.5 %copy-start.12 = (f32[64,256]{1,0:T(8,128)S(1)}, f32[64,256]{1,0:T(8,128)}, u32[]{:S(2)}) copy-start(f32[64,256]{1,0:T(8,128)} %get-tuple-element.54.twist_ref) | copy-start | bytes 196612 | tf_op jit(solution)/shard_map/cond
  10.4 19.5 %copy-start.14 = (bf16[128,192]{1,0:T(8,128)(2,1)S(1)}, bf16[128,192]{1,0:T(8,128)(2,1)}, u32[]{:S(2)}) copy-start(bf16[128,192]{1,0:T(8,128)(2,1)} %get-tuple-element.53.head_ref) | copy-start | bytes 147460 | tf_op jit(solution)/shard_map/cond
  31.7 15.8 %copy-start = (bf16[1024,128]{1,0:T(8,128)(2,1)S(1)}, bf16[1024,128]{1,0:T(8,128)(2,1)}, u32[]{:S(2)}) copy-start(bf16[1024,128]{1,0:T(8,128)(2,1)} %get-tuple-element.48.key_ref) | copy-start | bytes 786436 | tf_op jit(solution)/shard_map/cond
  31.7 15.8 %copy-start.2 = (bf16[1024,128]{1,0:T(8,128)(2,1)S(1)}, bf16[1024,128]{1,0:T(8,128)(2,1)}, u32[]{:S(2)}) copy-start(bf16[1024,128]{1,0:T(8,128)(2,1)} %get-tuple-element.49.value_ref) | copy-start | bytes 786436 | tf_op jit(solution)/shard_map/cond
  31.7 15.8 %copy-start.4 = (bf16[1024,128]{1,0:T(8,128)(2,1)S(1)}, bf16[1024,128]{1,0:T(8,128)(2,1)}, u32[]{:S(2)}) copy-start(bf16[1024,128]{1,0:T(8,128)(2,1)} %get-tuple-element.58.query_ref) | copy-start | bytes 786436 | tf_op jit(solution)/shard_map/cond

commit v21 on v20

--- a/solution.py
+++ b/solution.py
@@ -114,8 +114,8 @@
     pairs = [(source.at[span], held.at[span]) for span in spans for source, held in ((key_ref, key), (value_ref, value))]
     pairs += [(taken, taps), (bias_ref, bias_out)]
     fetches = [pltpu.make_async_copy(*pair, sems.at[idx]) for idx, pair in enumerate(pairs)]
-    for fetch in fetches:
-        fetch.start()
+    for idx, fetch in enumerate(fetches):
+        fetch.start(priority=idx % 2)
     for row in range(rows):
         if row % (rows // cuts) == 0:
             for fetch in fetches[row // (rows // cuts) * 2 :][:2]:
@@ -199,21 +199,20 @@
 
 def gate_kernel(rows, conv_ref, query_ref, key_ref, value_ref, bias_ref, out_ref, gated, sems):
     bias = bias_ref[...]
-    half = rows * LANES // 2
+    cuts = 4 if rows % 4 == 0 else 1
+    size = rows // cuts * LANES
     stores = [
-        pltpu.make_async_copy(gated.at[pl.ds(idx * half, half)], out_ref.at[pl.ds(idx * half, half)], sems.at[idx])
-        for idx in range(2)
+        pltpu.make_async_copy(gated.at[pl.ds(cut * size, size)], out_ref.at[pl.ds(cut * size, size)], sems.at[cut])
+        for cut in range(cuts)
     ]
     for row in range(rows):
         span = pl.ds(row * LANES, LANES)
         driver = key_ref[span, :].astype(F32) * value_ref[span, :].astype(F32)
         convolved = conv_ref[pl.ds(row, LANES, stride=rows), :].T
         gated[span, :] = (query_ref[span, :].astype(F32) * (convolved + bias * driver)).astype(BF16)
-        if (row + 1) * LANES == half:
-            stores[0].start()
-    if rows % 2:
-        stores[0].start()
-    stores[1].start()
+        if (row + 1) * LANES % size == 0:
+            cut = row * LANES // size
+            stores[cut].start(priority=cut % 2)
     for store in stores:
         store.wait()
 
@@ -278,7 +277,7 @@
         out_shape=pltpu.HBM((tokens, chans), BF16),
         in_specs=[VMEM] * 5,
         out_specs=HBM,
-        scratch_shapes=[pltpu.VMEM((tokens, chans), BF16), pltpu.SemaphoreType.DMA((2,))],
+        scratch_shapes=[pltpu.VMEM((tokens, chans), BF16), pltpu.SemaphoreType.DMA((4,))],
         compiler_params=pltpu.CompilerParams(vmem_limit_bytes=VMEM_LIMIT),
         cost_estimate=pl.CostEstimate(flops=size, bytes_accessed=3 * size, transcendentals=0),
     )(convolved, query_proj, key_proj, value_proj, bias)

time: 48.6 us -> 48.7 us (level)
  no operation moved by 1% of the time
where the time goes in v21:
time: 48.7 us; the launch traced here: 48.5 us
  blocking collectives  35.2 us (72%)
  waiting for transfers between devices  5.76 us (12%)
  Pallas kernels  4.28 us (9%)
  starting transfers between devices  3 us (6%)
    all_to_all x1, blocking collectives, convolve(): moved = lax.all_to_all(pair, 'seq', 0, 0, tiled=True)  19.4 us
    all_to_all x1, blocking collectives, exchange(): return lax.all_to_all(array, axes, 0, 0, tiled=True)  15.7 us
    ppermute x1, waiting for transfers between devices, convolve(): lax.ppermute(sent, 'groups', [(0, 1), (1, 0)])  5.76 us
    ppermute x1, starting transfers between devices, convolve(): lax.ppermute(sent, 'groups', [(0, 1), (1, 0)])  3 us
    pallas_call x1, Pallas kernels, convolve(): call(functools.partial(conv_kernel, layout, staged, min(own, 4)), [((coun...  1.79 us
    pallas_call x1, Pallas kernels, convolve(): call(functools.partial(pack_kernel, layout, staged), [((count, own * (row...  1.62 us
  transfers between devices with their start and end apart: 1, of which 1 were waited for; matrix products, arithmetic and copies ran while one was open for 0% of the time, Pallas kernels for 0%

profile of v21, /device:TPU:0, one launch (start us, length us, event | category | flops | bytes accessed | tf_op | source)
XLA Modules:
  0.0 48.5 jit_solution(15835305399508524152)
XLA Ops:
  0.0 48.5 %conditional.1 = (bf16[1024,128]{1,0:T(8,128)(2,1)}) conditional(s32[]{:T(128)} %convert_element_type.3, (f32[128]{0:T(128)}, bf16[1024,128]{1,0:T(8,128)(2,1)}, bf16[1024,128]{1,0:T(8,128)(2,1)}, f32[1024,128]{1,0:T(8,128)}, bf16[128,192]{1,0:T(8,128)(2,1)}, /*index=5*/f32[64,256]{1,0:T(8,128)}, bf16[768,256]{1,0:T(8,128)(2,1)}, ...), branch_computations={%region_0.1_spmd, %region_1.2_spmd} | conditional | flops 1259143168 | bytes 19071280 | solution.py:289
  0.0 1.6 %branch_0_fun.3 = (f32[16,96,128]{2,1,0:T(8,128)S(1)}, f32[1,128]{1,0:T(1,128)S(1)}) custom-call(s32[1]{0:T(128)} %bitcast.where_ref, bf16[1024,128]{1,0:T(8,128)(2,1)} %get-tuple-element.48.key_ref, bf16[1024,128]{1,0:T(8,128)(2,1)} %get-tuple-element.49.value_ref, f32[1024,128]{1,0:T(8,128)} %get-tuple-element.50.filter_ref, f32[1,128]{1,0:T(1,128)} %bitcast.8), custom_call_target="tpu_custom_call" | custom-call | flops 131072 | bytes 1572864 | tf_op jit(solution)/shard_map/cond/branch_0_fun/pallas_call | solution.py:257
  1.6 0.1 fusion
  1.7 3.0 %collective-permute-start = (f32[8,96,128]{2,1,0:T(8,128)S(1)}, f32[8,96,128]{2,1,0:T(8,128)S(1)}, u32[]{:S(2)}, u32[]{:S(2)}) collective-permute-start(f32[8,96,128]{2,1,0:T(8,128)S(1)} %get-tuple-element.74), channel_id=1, source_target_pairs={{0,16},{16,0},{1,17},{17,1},{2,18},{18,2},{3,19},{19,3},{4,20},{20... | collective-permute-start | bytes 1179656 | tf_op jit(solution)/shard_map/cond/branch_0_fun/ppermute | solution.py:266
  4.7 5.8 %collective-permute-done = f32[8,96,128]{2,1,0:T(8,128)S(1)} collective-permute-done((f32[8,96,128]{2,1,0:T(8,128)S(1)}, f32[8,96,128]{2,1,0:T(8,128)S(1)}, u32[]{:S(2)}, u32[]{:S(2)}) %collective-permute-start) | collective-permute-done | bytes 393248 | tf_op jit(solution)/shard_map/cond/branch_0_fun/ppermute | solution.py:266
  10.5 0.1 pad_maximum_fusion
  10.5 0.0 copy-start.6
  10.5 0.0 copy-start.8
  10.5 0.0 copy-start.10
  10.5 0.0 copy-start.12
  10.6 0.0 copy-start.14
  10.6 19.4 %all_to_all.16.moved_ref = f32[8,192,128]{2,1,0:T(8,128)S(1)} all-to-all(f32[8,192,128]{2,1,0:T(8,128)S(1)} %pad_maximum_fusion), channel_id=1, replica_groups=mesh['groups'=2,'seq'=8,'chan'=2] {'seq'}, dimensions={0} | all-to-all | bytes 1572864 | tf_op jit(solution)/shard_map/cond/branch_0_fun/all_to_all | solution.py:267
  30.0 0.0 copy-done.6
  30.0 0.0 copy-done.8
  30.0 0.0 copy-done.10
  30.0 0.0 copy-done.12
  30.0 0.0 copy-done.14
  30.0 1.8 %branch_0_fun.4 = f32[16,64,128]{2,1,0:T(8,128)S(1)} custom-call(s32[1]{0:T(128)} %bitcast.where_ref, f32[8,192,128]{2,1,0:T(8,128)S(1)} %all_to_all.16.moved_ref, bf16[128,192]{1,0:T(8,128)(2,1)S(1)} %copy-done.14, f32[64,256]{1,0:T(8,128)S(1)} %copy-done.12, bf16[768,256]{1,0:T(8,128)(2,1)S(1)} %copy-done.8, bf16[768,256]{1,0:T(8,128)(2,1)S(1)} %copy-done.6, ...), custom_call_target="tpu_custom_call" | custom-call | flops 1258291200 | bytes 1572864 | tf_op jit(solution)/shard_map/cond/branch_0_fun/pallas_call | solution.py:270
  31.8 0.0 copy-start
  31.8 0.0 copy-start.2
  31.9 0.0 copy-start.4
  31.9 15.7 %all_to_all.17 = f32[16,64,128]{2,1,0:T(8,128)S(1)} all-to-all(f32[16,64,128]{2,1,0:T(8,128)S(1)} %branch_0_fun.4), channel_id=1, replica_groups=mesh['groups'=2,'seq'=8,'chan'=2] {'groups','seq'}, dimensions={0} | all-to-all | bytes 1048576 | tf_op jit(solution)/shard_map/cond/branch_0_fun/all_to_all | solution.py:254
  47.6 0.0 copy-done
  47.6 0.0 copy-done.2
  47.6 0.0 copy-done.4
  47.6 0.9 %branch_0_fun.5 = bf16[1024,128]{1,0:T(8,128)(2,1)} custom-call(f32[1024,128]{1,0:T(8,128)S(1)} %bitcast.6, bf16[1024,128]{1,0:T(8,128)(2,1)S(1)} %copy-done.4, bf16[1024,128]{1,0:T(8,128)(2,1)S(1)} %copy-done, bf16[1024,128]{1,0:T(8,128)(2,1)S(1)} %copy-done.2, f32[1,128]{1,0:T(1,128)S(1)} %get-tuple-element.59.bias_ref), custom_call_target="tpu_custom_call" | custom-call | flops 524288 | bytes 1572864 | tf_op jit(solution)/shard_map/cond/branch_0_fun/pallas_call | solution.py:275
Async XLA Ops:
  1.7 8.8 %collective-permute-start = (f32[8,96,128]{2,1,0:T(8,128)S(1)}, f32[8,96,128]{2,1,0:T(8,128)S(1)}, u32[]{:S(2)}, u32[]{:S(2)}) collective-permute-start(f32[8,96,128]{2,1,0:T(8,128)S(1)} %get-tuple-element.74), channel_id=1, source_target_pairs={{0,16},{16,0},{1,17},{17,1},{2,18},{18,2},{3,19},{19,3},{4,20},{20... | collective-permute-start | bytes 1179656 | tf_op jit(solution)/shard_map/cond/branch_0_fun/ppermute | solution.py:266
  10.5 19.5 %copy-start.6 = (bf16[768,256]{1,0:T(8,128)(2,1)S(1)}, bf16[768,256]{1,0:T(8,128)(2,1)}, u32[]{:S(2)}) copy-start(bf16[768,256]{1,0:T(8,128)(2,1)} %get-tuple-element.56.back_tail_ref) | copy-start | bytes 1179652 | tf_op jit(solution)/shard_map/cond
  10.5 19.5 %copy-start.8 = (bf16[768,256]{1,0:T(8,128)(2,1)S(1)}, bf16[768,256]{1,0:T(8,128)(2,1)}, u32[]{:S(2)}) copy-start(bf16[768,256]{1,0:T(8,128)(2,1)} %get-tuple-element.55.tail_ref) | copy-start | bytes 1179652 | tf_op jit(solution)/shard_map/cond
  10.5 19.5 %copy-start.10 = (bf16[128,256]{1,0:T(8,128)(2,1)S(1)}, bf16[128,256]{1,0:T(8,128)(2,1)}, u32[]{:S(2)}) copy-start(bf16[128,256]{1,0:T(8,128)(2,1)} %get-tuple-element.57.back_head_ref) | copy-start | bytes 196612 | tf_op jit(solution)/shard_map/cond
  10.5 19.5 %copy-start.12 = (f32[64,256]{1,0:T(8,128)S(1)}, f32[64,256]{1,0:T(8,128)}, u32[]{:S(2)}) copy-start(f32[64,256]{1,0:T(8,128)} %get-tuple-element.54.twist_ref) | copy-start | bytes 196612 | tf_op jit(solution)/shard_map/cond
  10.6 19.5 %copy-start.14 = (bf16[128,192]{1,0:T(8,128)(2,1)S(1)}, bf16[128,192]{1,0:T(8,128)(2,1)}, u32[]{:S(2)}) copy-start(bf16[128,192]{1,0:T(8,128)(2,1)} %get-tuple-element.53.head_ref) | copy-start | bytes 147460 | tf_op jit(solution)/shard_map/cond
  31.8 15.8 %copy-start = (bf16[1024,128]{1,0:T(8,128)(2,1)S(1)}, bf16[1024,128]{1,0:T(8,128)(2,1)}, u32[]{:S(2)}) copy-start(bf16[1024,128]{1,0:T(8,128)(2,1)} %get-tuple-element.48.key_ref) | copy-start | bytes 786436 | tf_op jit(solution)/shard_map/cond
  31.8 15.8 %copy-start.2 = (bf16[1024,128]{1,0:T(8,128)(2,1)S(1)}, bf16[1024,128]{1,0:T(8,128)(2,1)}, u32[]{:S(2)}) copy-start(bf16[1024,128]{1,0:T(8,128)(2,1)} %get-tuple-element.49.value_ref) | copy-start | bytes 786436 | tf_op jit(solution)/shard_map/cond
  31.9 15.7 %copy-start.4 = (bf16[1024,128]{1,0:T(8,128)(2,1)S(1)}, bf16[1024,128]{1,0:T(8,128)(2,1)}, u32[]{:S(2)}) copy-start(bf16[1024,128]{1,0:T(8,128)(2,1)} %get-tuple-element.58.query_ref) | copy-start | bytes 786436 | tf_op jit(solution)/shard_map/cond

commit v22 on v20

--- a/solution.py
+++ b/solution.py
@@ -109,17 +109,13 @@
     ]
     first = where_ref[0] * (part * LANES if part < rows else 0)
     taken = filter_ref.at[pl.ds(pl.multiple_of(first, part * LANES), part * LANES)]
-    cuts = 2 if rows % 2 == 0 else 1
-    spans = [pl.ds(cut * rows // cuts * LANES, rows // cuts * LANES) for cut in range(cuts)]
-    pairs = [(source.at[span], held.at[span]) for span in spans for source, held in ((key_ref, key), (value_ref, value))]
-    pairs += [(taken, taps), (bias_ref, bias_out)]
+    pairs = ((key_ref, key), (value_ref, value), (taken, taps), (bias_ref, bias_out))
     fetches = [pltpu.make_async_copy(*pair, sems.at[idx]) for idx, pair in enumerate(pairs)]
     for fetch in fetches:
         fetch.start()
+    fetches[0].wait()
+    fetches[1].wait()
     for row in range(rows):
-        if row % (rows // cuts) == 0:
-            for fetch in fetches[row // (rows // cuts) * 2 :][:2]:
-                fetch.wait()
         span = pl.ds(row * LANES, LANES)
         turned = (key[span, :].astype(F32) * value[span, :].astype(F32)).T
         for place, chan in homes:
@@ -260,7 +256,7 @@
         [((count, own * (rows + part), LANES), F32), ((1, chans), F32)],
         [SMEM] + [HBM] * 4, size // 4, size * 3,
         [pltpu.VMEM((tokens, chans), BF16), pltpu.VMEM((tokens, chans), BF16), pltpu.VMEM((part * LANES, chans), F32),
-         pltpu.SemaphoreType.DMA((6,))],
+         pltpu.SemaphoreType.DMA((4,))],
     )(where, *(pltpu.with_memory_space_constraint(source, pltpu.HBM) for source in sources))
     if staged:
         kept, sent = packed[:blocks], packed[blocks:]
@@ -269,7 +265,7 @@
     else:
         moved = exchange(packed)
     local = call(
-        functools.partial(conv_kernel, layout, staged, min(own, 4)),
+        functools.partial(conv_kernel, layout, staged, own),
         [((count, own * rows, LANES), F32)], [SMEM] + [VMEM] * 6, 5 * macs, 3 * size,
     )(where, moved, head, twist, tail, back_tail, back_head)[0]
     convolved = exchange(local).reshape(chans * rows, LANES)

time: 48.6 us -> 48.6 us (level)
  no operation moved by 1% of the time
where the time goes in v22:
time: 48.6 us; the launch traced here: 48.3 us
  blocking collectives  35.2 us (72%)
  waiting for transfers between devices  5.76 us (12%)
  Pallas kernels  4.15 us (9%)
  starting transfers between devices  3 us (6%)
    all_to_all x1, blocking collectives, convolve(): moved = lax.all_to_all(pair, 'seq', 0, 0, tiled=True)  19.4 us
    all_to_all x1, blocking collectives, exchange(): return lax.all_to_all(array, axes, 0, 0, tiled=True)  15.7 us
    ppermute x1, waiting for transfers between devices, convolve(): lax.ppermute(sent, 'groups', [(0, 1), (1, 0)])  5.76 us
    ppermute x1, starting transfers between devices, convolve(): lax.ppermute(sent, 'groups', [(0, 1), (1, 0)])  3 us
    pallas_call x1, Pallas kernels, convolve(): call(functools.partial(conv_kernel, layout, staged, own), [((count, own *...  1.82 us
    pallas_call x1, Pallas kernels, convolve(): call(functools.partial(pack_kernel, layout, staged), [((count, own * (row...  1.45 us
  transfers between devices with their start and end apart: 1, of which 1 were waited for; matrix products, arithmetic and copies ran while one was open for 0% of the time, Pallas kernels for 0%

profile of v22, /device:TPU:0, one launch (start us, length us, event | category | flops | bytes accessed | tf_op | source)
XLA Modules:
  0.0 48.3 jit_solution(2615503742850521925)
XLA Ops:
  0.0 48.3 %conditional.1 = (bf16[1024,128]{1,0:T(8,128)(2,1)}) conditional(s32[]{:T(128)} %convert_element_type.3, (f32[128]{0:T(128)}, bf16[1024,128]{1,0:T(8,128)(2,1)}, bf16[1024,128]{1,0:T(8,128)(2,1)}, f32[1024,128]{1,0:T(8,128)}, bf16[128,192]{1,0:T(8,128)(2,1)}, /*index=5*/f32[64,256]{1,0:T(8,128)}, bf16[768,256]{1,0:T(8,128)(2,1)}, ...), branch_computations={%region_0.1_spmd, %region_1.2_spmd} | conditional | flops 1259143168 | bytes 19071280 | solution.py:286
  0.0 1.4 %branch_0_fun.3 = (f32[16,96,128]{2,1,0:T(8,128)S(1)}, f32[1,128]{1,0:T(1,128)S(1)}) custom-call(s32[1]{0:T(128)} %bitcast.where_ref, bf16[1024,128]{1,0:T(8,128)(2,1)} %get-tuple-element.48.key_ref, bf16[1024,128]{1,0:T(8,128)(2,1)} %get-tuple-element.49.value_ref, f32[1024,128]{1,0:T(8,128)} %get-tuple-element.50.filter_ref, f32[1,128]{1,0:T(1,128)} %bitcast.8), custom_call_target="tpu_custom_call" | custom-call | flops 131072 | bytes 1572864 | tf_op jit(solution)/shard_map/cond/branch_0_fun/pallas_call | solution.py:254
  1.5 0.1 fusion
  1.5 3.0 %collective-permute-start = (f32[8,96,128]{2,1,0:T(8,128)S(1)}, f32[8,96,128]{2,1,0:T(8,128)S(1)}, u32[]{:S(2)}, u32[]{:S(2)}) collective-permute-start(f32[8,96,128]{2,1,0:T(8,128)S(1)} %get-tuple-element.74), channel_id=1, source_target_pairs={{0,16},{16,0},{1,17},{17,1},{2,18},{18,2},{3,19},{19,3},{4,20},{20... | collective-permute-start | bytes 1179656 | tf_op jit(solution)/shard_map/cond/branch_0_fun/ppermute | solution.py:263
  4.5 5.8 %collective-permute-done = f32[8,96,128]{2,1,0:T(8,128)S(1)} collective-permute-done((f32[8,96,128]{2,1,0:T(8,128)S(1)}, f32[8,96,128]{2,1,0:T(8,128)S(1)}, u32[]{:S(2)}, u32[]{:S(2)}) %collective-permute-start) | collective-permute-done | bytes 393248 | tf_op jit(solution)/shard_map/cond/branch_0_fun/ppermute | solution.py:263
  10.3 0.1 pad_maximum_fusion
  10.3 0.0 copy-start.6
  10.3 0.0 copy-start.8
  10.4 0.0 copy-start.10
  10.4 0.0 copy-start.12
  10.4 0.0 copy-start.14
  10.4 19.4 %all_to_all.16.moved_ref = f32[8,192,128]{2,1,0:T(8,128)S(1)} all-to-all(f32[8,192,128]{2,1,0:T(8,128)S(1)} %pad_maximum_fusion), channel_id=1, replica_groups=mesh['groups'=2,'seq'=8,'chan'=2] {'seq'}, dimensions={0} | all-to-all | bytes 1572864 | tf_op jit(solution)/shard_map/cond/branch_0_fun/all_to_all | solution.py:264
  29.8 0.0 copy-done.6
  29.8 0.0 copy-done.8
  29.8 0.0 copy-done.10
  29.8 0.0 copy-done.12
  29.9 0.0 copy-done.14
  29.9 1.8 %branch_0_fun.4 = f32[16,64,128]{2,1,0:T(8,128)S(1)} custom-call(s32[1]{0:T(128)} %bitcast.where_ref, f32[8,192,128]{2,1,0:T(8,128)S(1)} %all_to_all.16.moved_ref, bf16[128,192]{1,0:T(8,128)(2,1)S(1)} %copy-done.14, f32[64,256]{1,0:T(8,128)S(1)} %copy-done.12, bf16[768,256]{1,0:T(8,128)(2,1)S(1)} %copy-done.8, bf16[768,256]{1,0:T(8,128)(2,1)S(1)} %copy-done.6, ...), custom_call_target="tpu_custom_call" | custom-call | flops 1258291200 | bytes 1572864 | tf_op jit(solution)/shard_map/cond/branch_0_fun/pallas_call | solution.py:267
  31.7 0.0 copy-start
  31.7 0.0 copy-start.2
  31.7 0.0 copy-start.4
  31.7 15.7 %all_to_all.17 = f32[16,64,128]{2,1,0:T(8,128)S(1)} all-to-all(f32[16,64,128]{2,1,0:T(8,128)S(1)} %branch_0_fun.4), channel_id=1, replica_groups=mesh['groups'=2,'seq'=8,'chan'=2] {'groups','seq'}, dimensions={0} | all-to-all | bytes 1048576 | tf_op jit(solution)/shard_map/cond/branch_0_fun/all_to_all | solution.py:251
  47.4 0.0 copy-done
  47.4 0.0 copy-done.2
  47.5 0.0 copy-done.4
  47.5 0.9 %branch_0_fun.5 = bf16[1024,128]{1,0:T(8,128)(2,1)} custom-call(f32[1024,128]{1,0:T(8,128)S(1)} %bitcast.6, bf16[1024,128]{1,0:T(8,128)(2,1)S(1)} %copy-done.4, bf16[1024,128]{1,0:T(8,128)(2,1)S(1)} %copy-done, bf16[1024,128]{1,0:T(8,128)(2,1)S(1)} %copy-done.2, f32[1,128]{1,0:T(1,128)S(1)} %get-tuple-element.59.bias_ref), custom_call_target="tpu_custom_call" | custom-call | flops 524288 | bytes 1572864 | tf_op jit(solution)/shard_map/cond/branch_0_fun/pallas_call | solution.py:272
Async XLA Ops:
  1.5 8.8 %collective-permute-start = (f32[8,96,128]{2,1,0:T(8,128)S(1)}, f32[8,96,128]{2,1,0:T(8,128)S(1)}, u32[]{:S(2)}, u32[]{:S(2)}) collective-permute-start(f32[8,96,128]{2,1,0:T(8,128)S(1)} %get-tuple-element.74), channel_id=1, source_target_pairs={{0,16},{16,0},{1,17},{17,1},{2,18},{18,2},{3,19},{19,3},{4,20},{20... | collective-permute-start | bytes 1179656 | tf_op jit(solution)/shard_map/cond/branch_0_fun/ppermute | solution.py:263
  10.3 19.5 %copy-start.6 = (bf16[768,256]{1,0:T(8,128)(2,1)S(1)}, bf16[768,256]{1,0:T(8,128)(2,1)}, u32[]{:S(2)}) copy-start(bf16[768,256]{1,0:T(8,128)(2,1)} %get-tuple-element.56.back_tail_ref) | copy-start | bytes 1179652 | tf_op jit(solution)/shard_map/cond
  10.3 19.5 %copy-start.8 = (bf16[768,256]{1,0:T(8,128)(2,1)S(1)}, bf16[768,256]{1,0:T(8,128)(2,1)}, u32[]{:S(2)}) copy-start(bf16[768,256]{1,0:T(8,128)(2,1)} %get-tuple-element.55.tail_ref) | copy-start | bytes 1179652 | tf_op jit(solution)/shard_map/cond
  10.4 19.5 %copy-start.10 = (bf16[128,256]{1,0:T(8,128)(2,1)S(1)}, bf16[128,256]{1,0:T(8,128)(2,1)}, u32[]{:S(2)}) copy-start(bf16[128,256]{1,0:T(8,128)(2,1)} %get-tuple-element.57.back_head_ref) | copy-start | bytes 196612 | tf_op jit(solution)/shard_map/cond
  10.4 19.5 %copy-start.12 = (f32[64,256]{1,0:T(8,128)S(1)}, f32[64,256]{1,0:T(8,128)}, u32[]{:S(2)}) copy-start(f32[64,256]{1,0:T(8,128)} %get-tuple-element.54.twist_ref) | copy-start | bytes 196612 | tf_op jit(solution)/shard_map/cond
  10.4 19.5 %copy-start.14 = (bf16[128,192]{1,0:T(8,128)(2,1)S(1)}, bf16[128,192]{1,0:T(8,128)(2,1)}, u32[]{:S(2)}) copy-start(bf16[128,192]{1,0:T(8,128)(2,1)} %get-tuple-element.53.head_ref) | copy-start | bytes 147460 | tf_op jit(solution)/shard_map/cond
  31.7 15.8 %copy-start = (bf16[1024,128]{1,0:T(8,128)(2,1)S(1)}, bf16[1024,128]{1,0:T(8,128)(2,1)}, u32[]{:S(2)}) copy-start(bf16[1024,128]{1,0:T(8,128)(2,1)} %get-tuple-element.48.key_ref) | copy-start | bytes 786436 | tf_op jit(solution)/shard_map/cond
  31.7 15.8 %copy-start.2 = (bf16[1024,128]{1,0:T(8,128)(2,1)S(1)}, bf16[1024,128]{1,0:T(8,128)(2,1)}, u32[]{:S(2)}) copy-start(bf16[1024,128]{1,0:T(8,128)(2,1)} %get-tuple-element.49.value_ref) | copy-start | bytes 786436 | tf_op jit(solution)/shard_map/cond
  31.7 15.7 %copy-start.4 = (bf16[1024,128]{1,0:T(8,128)(2,1)S(1)}, bf16[1024,128]{1,0:T(8,128)(2,1)}, u32[]{:S(2)}) copy-start(bf16[1024,128]{1,0:T(8,128)(2,1)} %get-tuple-element.58.query_ref) | copy-start | bytes 786436 | tf_op jit(solution)/shard_map/cond

commit v23 on v20

--- a/solution.py
+++ b/solution.py
@@ -99,12 +99,12 @@
     return jnp.concatenate([jnp.concatenate(reals, axis=1), jnp.concatenate(imags, axis=1)], axis=0)
 
 
-def pack_kernel(layout, staged, where_ref, key_ref, value_ref, filter_ref, bias_ref, out_ref, bias_out, key, value, taps, sems):
+def pack_kernel(layout, staged, where_ref, near_ref, key_ref, value_ref, filter_ref, bias_ref, out_ref, bias_out, key, value, taps, sems):
     rows, own, part, groups = layout
     count = out_ref.shape[0]
     blocks = count // groups
     homes = [
-        ((peer // blocks ^ where_ref[0]) * blocks + peer % blocks if staged else peer, peer * own)
+        ((peer % 2 ^ near_ref[0]) * (count // 2) + peer // 2 if staged else peer, peer * own)
         for peer in range(count)
     ]
     first = where_ref[0] * (part * LANES if part < rows else 0)
@@ -132,42 +132,43 @@
     fetches[-1].wait()
 
 
-def arrived(layout, staged, moved_ref, group, start, height):
+def arrived(layout, staged, near, moved_ref, group, start, height):
     rows, own, part, groups = layout
     if staged:
-        start += group * own * (rows + part)
-        return moved_ref[:, start : start + height]
+        far, second = moved_ref.shape[0] // groups, start + own * (rows + part)
+        span = pl.ds(group * far, far)
+        ours, other = moved_ref[span, start : start + height], moved_ref[span, second : second + height]
+        pair = [jnp.where(near == 0, ours, other), jnp.where(near == 0, other, ours)]
+        return jnp.stack(pair, axis=1).reshape(2 * far, height, LANES)
     blocks = moved_ref.shape[0] // groups
     return moved_ref[pl.ds(group * blocks, blocks), start : start + height]
 
 
-def driver_signals(layout, staged, moved_ref, chans):
+def driver_signals(layout, staged, near, moved_ref, chans):
     rows, own, part, groups = layout
     parts = [
-        arrived(layout, staged, moved_ref, group, chan * rows, rows) for chan in chans for group in range(groups)
+        arrived(layout, staged, near, moved_ref, group, chan * rows, rows) for chan in chans for group in range(groups)
     ]
     return [values.reshape(values.shape[0] * rows, LANES) for values in parts]
 
 
-def filter_signals(layout, staged, mine, moved_ref, chans):
+def filter_signals(layout, staged, near, moved_ref, chans):
     rows, own, part, groups = layout
     signals = []
     for chan in chans:
         pieces = [
-            arrived(layout, staged, moved_ref, group, own * rows + chan * part, part)
+            arrived(layout, staged, near, moved_ref, group, own * rows + chan * part, part)
             for group in range(groups if part < rows else 1)
         ]
-        if staged and len(pieces) == 2:
-            pieces = [jnp.where(mine == 0, pieces[0], pieces[1]), jnp.where(mine == 0, pieces[1], pieces[0])]
         signals.append(jnp.concatenate(pieces, axis=1).reshape(pieces[0].shape[0] * rows, LANES))
     return signals
 
 
 def conv_kernel(
-    layout, staged, pieces, where_ref, moved_ref, head_ref, twist_ref, tail_ref, back_tail_ref, back_head_ref, out_ref
+    layout, staged, pieces, near_ref, moved_ref, head_ref, twist_ref, tail_ref, back_tail_ref, back_head_ref, out_ref
 ):
     rows, own, part, groups = layout
-    mine = where_ref[0]
+    near = near_ref[0]
     blocks = out_ref.shape[0] // groups
     outer = blocks * rows
     scale = 1.0 / (outer * LANES)
@@ -175,7 +176,7 @@
     sets = [range(piece * own // pieces, (piece + 1) * own // pieces) for piece in range(pieces)]
     mixed = [
         head_stage(
-            filter_signals(layout, staged, mine, moved_ref, chans) + driver_signals(layout, staged, moved_ref, chans),
+            filter_signals(layout, staged, near, moved_ref, chans) + driver_signals(layout, staged, near, moved_ref, chans),
             head_ref[...],
             twist_ref[...],
         )
@@ -191,7 +192,6 @@
         for idx in range(len(chans) * groups):
             chan, group = divmod(idx, groups)
             start = (chans[0] + chan) * rows
-            group = group ^ mine if staged else group
             out_ref[pl.ds(group * blocks, blocks), start : start + rows] = result[
                 :, idx * LANES : (idx + 1) * LANES
             ].reshape(blocks, rows, LANES)
@@ -250,6 +250,7 @@
     size = tokens * chans * 4
     macs = 2 * 3 * own * seq_len * (2 * outer + 4 * LANES)
     where = lax.axis_index("groups").reshape(1).astype(jnp.int32)
+    near = (lax.axis_index("seq") % 2).reshape(1).astype(jnp.int32)
 
     def exchange(array):
         return lax.all_to_all(array, axes, 0, 0, tiled=True)
@@ -258,20 +259,22 @@
     packed, bias = call(
         functools.partial(pack_kernel, layout, staged),
         [((count, own * (rows + part), LANES), F32), ((1, chans), F32)],
-        [SMEM] + [HBM] * 4, size // 4, size * 3,
+        [SMEM] * 2 + [HBM] * 4, size // 4, size * 3,
         [pltpu.VMEM((tokens, chans), BF16), pltpu.VMEM((tokens, chans), BF16), pltpu.VMEM((part * LANES, chans), F32),
          pltpu.SemaphoreType.DMA((6,))],
-    )(where, *(pltpu.with_memory_space_constraint(source, pltpu.HBM) for source in sources))
+    )(where, near, *(pltpu.with_memory_space_constraint(source, pltpu.HBM) for source in sources))
     if staged:
-        kept, sent = packed[:blocks], packed[blocks:]
-        pair = jnp.concatenate([kept, lax.ppermute(sent, "groups", [(0, 1), (1, 0)])], axis=1)
-        moved = lax.all_to_all(pair, "seq", 0, 0, tiled=True)
+        kept, sent = packed[: count // 2], packed[count // 2 :]
+        swap = [(block, block ^ 1) for block in range(blocks)]
+        pair = jnp.concatenate([kept, lax.ppermute(sent, "seq", swap)], axis=1)
+        sides = [list(range(side, count, 2)) for side in range(2)]
+        moved = lax.all_to_all(pair, axes, 0, 0, axis_index_groups=sides, tiled=True)
     else:
         moved = exchange(packed)
     local = call(
         functools.partial(conv_kernel, layout, staged, min(own, 4)),
         [((count, own * rows, LANES), F32)], [SMEM] + [VMEM] * 6, 5 * macs, 3 * size,
-    )(where, moved, head, twist, tail, back_tail, back_head)[0]
+    )(near, moved, head, twist, tail, back_tail, back_head)[0]
     convolved = exchange(local).reshape(chans * rows, LANES)
     return pl.pallas_call(
         functools.partial(gate_kernel, rows),
@@ -285,7 +288,7 @@
 
 
 def shards(groups, blocks, cores, *args):
-    if cores == 1 or groups != 2:
+    if cores == 1 or blocks % 2:
         return convolve(groups, blocks, False, *args)
     return lax.cond(
         lax.axis_index("chan") % 2 == 1,

time: 48.6 us -> 47.5 us (0.977)
  blocking collectives: 35.2 us -> 34.1 us
    all_to_all x1, blocking collectives: 15.7 us -> 13.8 us  [exchange(): return lax.all_to_all(array, axes, 0, 0, tiled=True)]
    all_to_all x1, blocking collectives: 19.4 us -> 20.2 us  [convolve(): lax.all_to_all(pair, axes, 0, 0, axis_index_groups=sides, tiled=True)]
where the time goes in v23:
time: 47.5 us; the launch traced here: 47.3 us
  blocking collectives  34.1 us (72%)
  waiting for transfers between devices  5.76 us (12%)
  Pallas kernels  4.15 us (9%)
  starting transfers between devices  3.03 us (6%)
    all_to_all x1, blocking collectives, convolve(): lax.all_to_all(pair, axes, 0, 0, axis_index_groups=sides, tiled=True)  20.2 us
    all_to_all x1, blocking collectives, exchange(): return lax.all_to_all(array, axes, 0, 0, tiled=True)  13.8 us
    ppermute x1, waiting for transfers between devices, convolve(): pair = jnp.concatenate([kept, lax.ppermute(sent, 'seq', swap)], axis=1)  5.76 us
    ppermute x1, starting transfers between devices, convolve(): pair = jnp.concatenate([kept, lax.ppermute(sent, 'seq', swap)], axis=1)  3.03 us
    pallas_call x1, Pallas kernels, convolve(): call(functools.partial(conv_kernel, layout, staged, min(own, 4)), [((coun...  1.79 us
    pallas_call x1, Pallas kernels, convolve(): call(functools.partial(pack_kernel, layout, staged), [((count, own * (row...  1.48 us
  transfers between devices with their start and end apart: 1, of which 1 were waited for; matrix products, arithmetic and copies ran while one was open for 0% of the time, Pallas kernels for 0%

profile of v23, /device:TPU:0, one launch (start us, length us, event | category | flops | bytes accessed | tf_op | source)
XLA Modules:
  0.0 47.3 jit_solution(4874814537393519269)
XLA Ops:
  0.0 47.3 %conditional.1 = (bf16[1024,128]{1,0:T(8,128)(2,1)}) conditional(s32[]{:T(128)} %convert_element_type.3, (f32[128]{0:T(128)}, bf16[1024,128]{1,0:T(8,128)(2,1)}, bf16[1024,128]{1,0:T(8,128)(2,1)}, f32[1024,128]{1,0:T(8,128)}, bf16[128,192]{1,0:T(8,128)(2,1)}, /*index=5*/f32[64,256]{1,0:T(8,128)}, bf16[768,256]{1,0:T(8,128)(2,1)}, ...), branch_computations={%region_0.1_spmd, %region_1.2_spmd} | conditional | flops 1259143168 | bytes 19071420 | solution.py:293
  0.0 1.5 %branch_0_fun.3 = (f32[16,96,128]{2,1,0:T(8,128)S(1)}, f32[1,128]{1,0:T(1,128)S(1)}) custom-call(s32[1]{0:T(128)} %bitcast.1.where_ref, s32[1]{0:T(128)} %bitcast.near_ref, bf16[1024,128]{1,0:T(8,128)(2,1)} %get-tuple-element.48.key_ref, bf16[1024,128]{1,0:T(8,128)(2,1)} %get-tuple-element.49.value_ref, f32[1024,128]{1,0:T(8,128)} %get-tuple-element.50.filter_ref, ...), custom_call_target="tpu_custom_call" | custom-call | flops 131072 | bytes 1572864 | tf_op jit(solution)/shard_map/cond/branch_0_fun/pallas_call | solution.py:259
  1.5 0.1 fusion
  1.6 3.0 %collective-permute-start = (f32[8,96,128]{2,1,0:T(8,128)S(1)}, f32[8,96,128]{2,1,0:T(8,128)S(1)}, u32[]{:S(2)}, u32[]{:S(2)}) collective-permute-start(f32[8,96,128]{2,1,0:T(8,128)S(1)} %get-tuple-element.74), channel_id=1, source_target_pairs={{0,2},{2,0},{4,6},{6,4},{8,10},{10,8},{12,14},{14,12},{1,3},{3,1},... | collective-permute-start | bytes 1179656 | tf_op jit(solution)/shard_map/cond/branch_0_fun/ppermute | solution.py:269
  4.6 5.8 %collective-permute-done = f32[8,96,128]{2,1,0:T(8,128)S(1)} collective-permute-done((f32[8,96,128]{2,1,0:T(8,128)S(1)}, f32[8,96,128]{2,1,0:T(8,128)S(1)}, u32[]{:S(2)}, u32[]{:S(2)}) %collective-permute-start) | collective-permute-done | bytes 393248 | tf_op jit(solution)/shard_map/cond/branch_0_fun/ppermute | solution.py:269
  10.3 0.1 pad_maximum_fusion
  10.4 0.0 copy-start.6
  10.4 0.0 copy-start.8
  10.4 0.0 copy-start.10
  10.4 0.0 copy-start.12
  10.4 0.0 copy-start.14
  10.5 20.2 %all_to_all.16.moved_ref = f32[8,192,128]{2,1,0:T(8,128)S(1)} all-to-all(f32[8,192,128]{2,1,0:T(8,128)S(1)} %pad_maximum_fusion), channel_id=1, replica_groups={{0,4,8,12,16,20,24,28},{2,6,10,14,18,22,26,30},{1,5,9,13,17,21,25,29},{..., dimensions={0} | all-to-all | bytes 1572864 | tf_op jit(solution)/shard_map/cond/branch_0_fun/all_to_all | solution.py:271
  30.7 0.0 copy-done.6
  30.7 0.0 copy-done.8
  30.7 0.0 copy-done.10
  30.7 0.0 copy-done.12
  30.7 0.0 copy-done.14
  30.7 1.8 %branch_0_fun.4 = f32[16,64,128]{2,1,0:T(8,128)S(1)} custom-call(s32[1]{0:T(128)} %bitcast.near_ref, f32[8,192,128]{2,1,0:T(8,128)S(1)} %all_to_all.16.moved_ref, bf16[128,192]{1,0:T(8,128)(2,1)S(1)} %copy-done.14, f32[64,256]{1,0:T(8,128)S(1)} %copy-done.12, bf16[768,256]{1,0:T(8,128)(2,1)S(1)} %copy-done.8, bf16[768,256]{1,0:T(8,128)(2,1)S(1)} %copy-done.6, ...), custom_call_target="tpu_custom_call" | custom-call | flops 1258291200 | bytes 1572864 | tf_op jit(solution)/shard_map/cond/branch_0_fun/pallas_call | solution.py:274
  32.5 0.0 copy-start
  32.5 0.0 copy-start.2
  32.5 0.0 copy-start.4
  32.6 13.8 %all_to_all.17 = f32[16,64,128]{2,1,0:T(8,128)S(1)} all-to-all(f32[16,64,128]{2,1,0:T(8,128)S(1)} %branch_0_fun.4), channel_id=1, replica_groups=mesh['groups'=2,'seq'=8,'chan'=2] {'groups','seq'}, dimensions={0} | all-to-all | bytes 1048576 | tf_op jit(solution)/shard_map/cond/branch_0_fun/all_to_all | solution.py:256
  46.4 0.0 copy-done
  46.4 0.0 copy-done.2
  46.4 0.0 copy-done.4
  46.4 0.9 %branch_0_fun.5 = bf16[1024,128]{1,0:T(8,128)(2,1)} custom-call(f32[1024,128]{1,0:T(8,128)S(1)} %bitcast.8, bf16[1024,128]{1,0:T(8,128)(2,1)S(1)} %copy-done.4, bf16[1024,128]{1,0:T(8,128)(2,1)S(1)} %copy-done, bf16[1024,128]{1,0:T(8,128)(2,1)S(1)} %copy-done.2, f32[1,128]{1,0:T(1,128)S(1)} %get-tuple-element.59.bias_ref), custom_call_target="tpu_custom_call" | custom-call | flops 524288 | bytes 1572864 | tf_op jit(solution)/shard_map/cond/branch_0_fun/pallas_call | solution.py:279
Async XLA Ops:
  1.6 8.8 %collective-permute-start = (f32[8,96,128]{2,1,0:T(8,128)S(1)}, f32[8,96,128]{2,1,0:T(8,128)S(1)}, u32[]{:S(2)}, u32[]{:S(2)}) collective-permute-start(f32[8,96,128]{2,1,0:T(8,128)S(1)} %get-tuple-element.74), channel_id=1, source_target_pairs={{0,2},{2,0},{4,6},{6,4},{8,10},{10,8},{12,14},{14,12},{1,3},{3,1},... | collective-permute-start | bytes 1179656 | tf_op jit(solution)/shard_map/cond/branch_0_fun/ppermute | solution.py:269
  10.4 20.3 %copy-start.6 = (bf16[768,256]{1,0:T(8,128)(2,1)S(1)}, bf16[768,256]{1,0:T(8,128)(2,1)}, u32[]{:S(2)}) copy-start(bf16[768,256]{1,0:T(8,128)(2,1)} %get-tuple-element.56.back_tail_ref) | copy-start | bytes 1179652 | tf_op jit(solution)/shard_map/cond
  10.4 20.3 %copy-start.8 = (bf16[768,256]{1,0:T(8,128)(2,1)S(1)}, bf16[768,256]{1,0:T(8,128)(2,1)}, u32[]{:S(2)}) copy-start(bf16[768,256]{1,0:T(8,128)(2,1)} %get-tuple-element.55.tail_ref) | copy-start | bytes 1179652 | tf_op jit(solution)/shard_map/cond
  10.4 20.3 %copy-start.10 = (bf16[128,256]{1,0:T(8,128)(2,1)S(1)}, bf16[128,256]{1,0:T(8,128)(2,1)}, u32[]{:S(2)}) copy-start(bf16[128,256]{1,0:T(8,128)(2,1)} %get-tuple-element.57.back_head_ref) | copy-start | bytes 196612 | tf_op jit(solution)/shard_map/cond
  10.4 20.3 %copy-start.12 = (f32[64,256]{1,0:T(8,128)S(1)}, f32[64,256]{1,0:T(8,128)}, u32[]{:S(2)}) copy-start(f32[64,256]{1,0:T(8,128)} %get-tuple-element.54.twist_ref) | copy-start | bytes 196612 | tf_op jit(solution)/shard_map/cond
  10.4 20.3 %copy-start.14 = (bf16[128,192]{1,0:T(8,128)(2,1)S(1)}, bf16[128,192]{1,0:T(8,128)(2,1)}, u32[]{:S(2)}) copy-start(bf16[128,192]{1,0:T(8,128)(2,1)} %get-tuple-element.53.head_ref) | copy-start | bytes 147460 | tf_op jit(solution)/shard_map/cond
  32.5 13.9 %copy-start = (bf16[1024,128]{1,0:T(8,128)(2,1)S(1)}, bf16[1024,128]{1,0:T(8,128)(2,1)}, u32[]{:S(2)}) copy-start(bf16[1024,128]{1,0:T(8,128)(2,1)} %get-tuple-element.48.key_ref) | copy-start | bytes 786436 | tf_op jit(solution)/shard_map/cond
  32.5 13.9 %copy-start.2 = (bf16[1024,128]{1,0:T(8,128)(2,1)S(1)}, bf16[1024,128]{1,0:T(8,128)(2,1)}, u32[]{:S(2)}) copy-start(bf16[1024,128]{1,0:T(8,128)(2,1)} %get-tuple-element.49.value_ref) | copy-start | bytes 786436 | tf_op jit(solution)/shard_map/cond
  32.5 13.9 %copy-start.4 = (bf16[1024,128]{1,0:T(8,128)(2,1)S(1)}, bf16[1024,128]{1,0:T(8,128)(2,1)}, u32[]{:S(2)}) copy-start(bf16[1024,128]{1,0:T(8,128)(2,1)} %get-tuple-element.58.query_ref) | copy-start | bytes 786436 | tf_op jit(solution)/shard_map/cond

commit v24 on v23

--- a/solution.py
+++ b/solution.py
@@ -99,37 +99,43 @@
     return jnp.concatenate([jnp.concatenate(reals, axis=1), jnp.concatenate(imags, axis=1)], axis=0)
 
 
-def pack_kernel(layout, staged, where_ref, near_ref, key_ref, value_ref, filter_ref, bias_ref, out_ref, bias_out, key, value, taps, sems):
-    rows, own, part, groups = layout
+def pack_kernel(layout, staged, with_driver, with_filter, where_ref, near_ref, *refs):
+    rows, own, part, groups = layout
+    refs = list(refs)
+    sources = [refs.pop(0) for _ in range(3 * with_driver + with_filter)]
+    out_ref = refs.pop(0)
+    held = ([refs.pop(0)] if with_driver else []) + refs[:-1]
+    sems = refs[-1]
+    if with_driver:
+        held = held[1:3] + held[:1] + held[3:]
+    if with_filter:
+        first = where_ref[0] * (part * LANES if part < rows else 0)
+        sources[-1] = sources[-1].at[pl.ds(pl.multiple_of(first, part * LANES), part * LANES)]
+    fetches = [pltpu.make_async_copy(*pair, sems.at[idx]) for idx, pair in enumerate(zip(sources, held))]
+    for fetch in fetches:
+        fetch.start()
     count = out_ref.shape[0]
-    blocks = count // groups
     homes = [
         ((peer % 2 ^ near_ref[0]) * (count // 2) + peer // 2 if staged else peer, peer * own)
         for peer in range(count)
     ]
-    first = where_ref[0] * (part * LANES if part < rows else 0)
-    taken = filter_ref.at[pl.ds(pl.multiple_of(first, part * LANES), part * LANES)]
-    cuts = 2 if rows % 2 == 0 else 1
-    spans = [pl.ds(cut * rows // cuts * LANES, rows // cuts * LANES) for cut in range(cuts)]
-    pairs = [(source.at[span], held.at[span]) for span in spans for source, held in ((key_ref, key), (value_ref, value))]
-    pairs += [(taken, taps), (bias_ref, bias_out)]
-    fetches = [pltpu.make_async_copy(*pair, sems.at[idx]) for idx, pair in enumerate(pairs)]
-    for fetch in fetches:
-        fetch.start()
-    for row in range(rows):
-        if row % (rows // cuts) == 0:
-            for fetch in fetches[row // (rows // cuts) * 2 :][:2]:
-                fetch.wait()
-        span = pl.ds(row * LANES, LANES)
-        turned = (key[span, :].astype(F32) * value[span, :].astype(F32)).T
-        for place, chan in homes:
-            out_ref[place, pl.ds(row, own, stride=rows), :] = turned[chan : chan + own]
-    fetches[-2].wait()
-    for row in range(part):
-        turned = taps[pl.ds(row * LANES, LANES), :].T
-        for place, chan in homes:
-            out_ref[place, pl.ds(own * rows + row, own, stride=part), :] = turned[chan : chan + own]
-    fetches[-1].wait()
+    if with_driver:
+        fetches[0].wait()
+        fetches[1].wait()
+        for row in range(rows):
+            span = pl.ds(row * LANES, LANES)
+            turned = (held[0][span, :].astype(F32) * held[1][span, :].astype(F32)).T
+            for place, chan in homes:
+                out_ref[place, pl.ds(row, own, stride=rows), :] = turned[chan : chan + own]
+    if with_filter:
+        fetches[-1].wait()
+        base = own * rows * with_driver
+        for row in range(part):
+            turned = held[-1][pl.ds(row * LANES, LANES), :].T
+            for place, chan in homes:
+                out_ref[place, pl.ds(base + row, own, stride=part), :] = turned[chan : chan + own]
+    if with_driver:
+        fetches[2].wait()
 
 
 def arrived(layout, staged, near, moved_ref, group, start, height):
@@ -255,21 +261,30 @@
     def exchange(array):
         return lax.all_to_all(array, axes, 0, 0, tiled=True)
 
-    sources = (key_proj, value_proj, long_filter, skip_bias.reshape(1, chans))
-    packed, bias = call(
-        functools.partial(pack_kernel, layout, staged),
-        [((count, own * (rows + part), LANES), F32), ((1, chans), F32)],
-        [SMEM] * 2 + [HBM] * 4, size // 4, size * 3,
-        [pltpu.VMEM((tokens, chans), BF16), pltpu.VMEM((tokens, chans), BF16), pltpu.VMEM((part * LANES, chans), F32),
-         pltpu.SemaphoreType.DMA((6,))],
-    )(where, near, *(pltpu.with_memory_space_constraint(source, pltpu.HBM) for source in sources))
+    def pack(with_driver, with_filter):
+        sources = [key_proj, value_proj, skip_bias.reshape(1, chans)] * with_driver + [long_filter] * with_filter
+        tall = [(tokens, BF16), (tokens, BF16)] * with_driver + [(part * LANES, F32)] * with_filter
+        height = own * (rows * with_driver + part * with_filter)
+        return call(
+            functools.partial(pack_kernel, layout, staged, with_driver, with_filter),
+            [((count, height, LANES), F32)] + [((1, chans), F32)] * with_driver,
+            [SMEM] * 2 + [HBM] * len(sources), size // 4, size * 3,
+            [pltpu.VMEM((rows_held, chans), kind) for rows_held, kind in tall]
+            + [pltpu.SemaphoreType.DMA((len(sources),))],
+        )(where, near, *(pltpu.with_memory_space_constraint(source, pltpu.HBM) for source in sources))
+
     if staged:
-        kept, sent = packed[: count // 2], packed[count // 2 :]
         swap = [(block, block ^ 1) for block in range(blocks)]
-        pair = jnp.concatenate([kept, lax.ppermute(sent, "seq", swap)], axis=1)
+        packed, bias = pack(1, 0)
+        half = count // 2
+        driver_blocks = [packed[:half], lax.ppermute(packed[half:], "seq", swap)]
+        packed = pack(0, 1)[0]
+        filter_blocks = [packed[:half], lax.ppermute(packed[half:], "seq", swap)]
+        pair = jnp.concatenate([driver_blocks[0], filter_blocks[0], driver_blocks[1], filter_blocks[1]], axis=1)
         sides = [list(range(side, count, 2)) for side in range(2)]
         moved = lax.all_to_all(pair, axes, 0, 0, axis_index_groups=sides, tiled=True)
     else:
+        packed, bias = pack(1, 1)
         moved = exchange(packed)
     local = call(
         functools.partial(conv_kernel, layout, staged, min(own, 4)),

time: 47.5 us -> 47.3 us (level)
  Pallas kernels: 4.15 us -> 5.06 us
  waiting for transfers between devices: 5.76 us -> 4.95 us
  blocking collectives: 34.1 us -> 33.6 us
    pallas_call x1 -> x2, Pallas kernels: 1.48 us -> 2.39 us  [pack(): call(functools.partial(pack_kernel, layout, staged, with_driver, with_fil...]
    ppermute x1 -> x2, waiting for transfers between devices: 5.76 us -> 4.95 us  [the longest x1 4.95 us: convolve(): filter_blocks = [packed[:half], lax.ppermute(packed[half:], 'seq', swap)]]
    ppermute x1 -> x2, starting transfers between devices: 3.03 us -> 3.12 us  [the longest x1 3.03 us: convolve(): driver_blocks = [packed[:half], lax.ppermute(packed[half:], 'seq', swap)]]
  transfers between devices with their start and end apart: 1 -> 2, of which waited for: 1 -> 1; matrix products, arithmetic and copies ran while one was open for 0% -> 0% of each run, Pallas kernels for 0% -> 2%
where the time goes in v24:
time: 47.3 us; the launch traced here: 47.1 us
  blocking collectives  33.6 us (71%)
  Pallas kernels  5.06 us (11%)
  waiting for transfers between devices  4.95 us (10%)
  starting transfers between devices  3.12 us (7%)
    all_to_all x1, blocking collectives, convolve(): lax.all_to_all(pair, axes, 0, 0, axis_index_groups=sides, tiled=True)  19.9 us
    all_to_all x1, blocking collectives, exchange(): return lax.all_to_all(array, axes, 0, 0, tiled=True)  13.7 us
    ppermute x1, waiting for transfers between devices, convolve(): filter_blocks = [packed[:half], lax.ppermute(packed[half:], 'seq', swap)]  4.95 us
    ppermute x1, starting transfers between devices, convolve(): driver_blocks = [packed[:half], lax.ppermute(packed[half:], 'seq', swap)]  3.03 us
    pallas_call x2, Pallas kernels, pack(): call(functools.partial(pack_kernel, layout, staged, with_driver, with_fil...  2.39 us
    pallas_call x1, Pallas kernels, convolve(): call(functools.partial(conv_kernel, layout, staged, min(own, 4)), [((coun...  1.79 us
  transfers between devices with their start and end apart: 2, of which 1 were waited for; matrix products, arithmetic and copies ran while one was open for 0% of the time, Pallas kernels for 2%

profile of v24, /device:TPU:0, one launch (start us, length us, event | category | flops | bytes accessed | tf_op | source)
XLA Modules:
  0.0 47.1 jit_solution(6635554810045170188)
XLA Ops:
  0.0 47.1 %conditional.1 = (bf16[1024,128]{1,0:T(8,128)(2,1)}) conditional(s32[]{:T(128)} %convert_element_type.3, (f32[128]{0:T(128)}, bf16[1024,128]{1,0:T(8,128)(2,1)}, bf16[1024,128]{1,0:T(8,128)(2,1)}, f32[1024,128]{1,0:T(8,128)}, bf16[128,192]{1,0:T(8,128)(2,1)}, /*index=5*/f32[64,256]{1,0:T(8,128)}, bf16[768,256]{1,0:T(8,128)(2,1)}, ...), branch_computations={%region_0.1_spmd, %region_1.2_spmd} | conditional | flops 1259667456 | bytes 20644324 | solution.py:308
  0.0 1.3 %branch_0_fun.4 = (f32[16,64,128]{2,1,0:T(8,128)S(1)}, f32[1,128]{1,0:T(1,128)S(1)}) custom-call(s32[1]{0:T(128)} %bitcast.1.where_ref, s32[1]{0:T(128)} %bitcast.near_ref, bf16[1024,128]{1,0:T(8,128)(2,1)} %get-tuple-element.48.refs_0_.key_ref, bf16[1024,128]{1,0:T(8,128)(2,1)} %get-tuple-element.49.refs_1_.value_ref, f32[1,128]{1,0:T(1,128)} %bitcast.10), custom_call_target="tpu_custom_call" | custom-call | flops 131072 | bytes 1572864 | tf_op jit(solution)/shard_map/cond/branch_0_fun/pallas_call | solution.py:268
  1.4 3.0 %collective-permute-start = (f32[8,64,128]{2,1,0:T(8,128)S(1)}, f32[8,64,128]{2,1,0:T(8,128)S(1)}, u32[]{:S(2)}, u32[]{:S(2)}) collective-permute-start(f32[8,64,128]{2,1,0:T(8,128)S(1)} %get-tuple-element.74), channel_id=1, source_target_pairs={{0,2},{2,0},{4,6},{6,4},{8,10},{10,8},{12,14},{14,12},{1,3},{3,1},... | collective-permute-start | bytes 786440 | tf_op jit(solution)/shard_map/cond/branch_0_fun/ppermute | solution.py:280
  4.4 1.1 %branch_0_fun.5 = f32[16,32,128]{2,1,0:T(8,128)S(1)} custom-call(s32[1]{0:T(128)} %bitcast.1.where_ref, s32[1]{0:T(128)} %bitcast.near_ref, f32[1024,128]{1,0:T(8,128)} %get-tuple-element.52.refs_0_), custom_call_target="tpu_custom_call" | custom-call | flops 131072 | bytes 1572864 | tf_op jit(solution)/shard_map/cond/branch_0_fun/pallas_call | solution.py:268
  5.5 0.1 collective-permute-start.1
  5.6 4.9 %collective-permute-done.1 = f32[8,32,128]{2,1,0:T(8,128)S(1)} collective-permute-done((f32[8,32,128]{2,1,0:T(8,128)S(1)}, f32[8,32,128]{2,1,0:T(8,128)S(1)}, u32[]{:S(2)}, u32[]{:S(2)}) %collective-permute-start.1) | collective-permute-done | bytes 131104 | tf_op jit(solution)/shard_map/cond/branch_0_fun/ppermute | solution.py:282
  10.6 0.0 collective-permute-done
  10.6 0.1 pad_maximum_fusion
  10.6 0.0 copy-start.6
  10.6 0.0 copy-start.8
  10.6 0.0 copy-start.10
  10.7 0.0 copy-start.12
  10.7 0.0 copy-start.14
  10.7 19.9 %all_to_all.16.moved_ref = f32[8,192,128]{2,1,0:T(8,128)S(1)} all-to-all(f32[8,192,128]{2,1,0:T(8,128)S(1)} %pad_maximum_fusion), channel_id=1, replica_groups={{0,4,8,12,16,20,24,28},{2,6,10,14,18,22,26,30},{1,5,9,13,17,21,25,29},{..., dimensions={0} | all-to-all | bytes 1572864 | tf_op jit(solution)/shard_map/cond/branch_0_fun/all_to_all | solution.py:285
  30.6 0.0 copy-done.6
  30.6 0.0 copy-done.8
  30.6 0.0 copy-done.10
  30.6 0.0 copy-done.12
  30.6 0.0 copy-done.14
  30.7 1.8 %branch_0_fun.6 = f32[16,64,128]{2,1,0:T(8,128)S(1)} custom-call(s32[1]{0:T(128)} %bitcast.near_ref, f32[8,192,128]{2,1,0:T(8,128)S(1)} %all_to_all.16.moved_ref, bf16[128,192]{1,0:T(8,128)(2,1)S(1)} %copy-done.14, f32[64,256]{1,0:T(8,128)S(1)} %copy-done.12, bf16[768,256]{1,0:T(8,128)(2,1)S(1)} %copy-done.8, bf16[768,256]{1,0:T(8,128)(2,1)S(1)} %copy-done.6, ...), custom_call_target="tpu_custom_call" | custom-call | flops 1258291200 | bytes 1572864 | tf_op jit(solution)/shard_map/cond/branch_0_fun/pallas_call | solution.py:289
  32.5 0.0 copy-start
  32.5 0.0 copy-start.2
  32.5 0.0 copy-start.4
  32.5 13.7 %all_to_all.17 = f32[16,64,128]{2,1,0:T(8,128)S(1)} all-to-all(f32[16,64,128]{2,1,0:T(8,128)S(1)} %branch_0_fun.6), channel_id=1, replica_groups=mesh['groups'=2,'seq'=8,'chan'=2] {'groups','seq'}, dimensions={0} | all-to-all | bytes 1048576 | tf_op jit(solution)/shard_map/cond/branch_0_fun/all_to_all | solution.py:262
  46.2 0.0 copy-done
  46.2 0.0 copy-done.2
  46.2 0.0 copy-done.4
  46.2 0.9 %branch_0_fun.7 = bf16[1024,128]{1,0:T(8,128)(2,1)} custom-call(f32[1024,128]{1,0:T(8,128)S(1)} %bitcast.8, bf16[1024,128]{1,0:T(8,128)(2,1)S(1)} %copy-done.4, bf16[1024,128]{1,0:T(8,128)(2,1)S(1)} %copy-done, bf16[1024,128]{1,0:T(8,128)(2,1)S(1)} %copy-done.2, f32[1,128]{1,0:T(1,128)S(1)} %get-tuple-element.59.bias_ref), custom_call_target="tpu_custom_call" | custom-call | flops 524288 | bytes 1572864 | tf_op jit(solution)/shard_map/cond/branch_0_fun/pallas_call | solution.py:294
  (2 shorter events, 0.1 us)
Async XLA Ops:
  1.4 9.2 %collective-permute-start = (f32[8,64,128]{2,1,0:T(8,128)S(1)}, f32[8,64,128]{2,1,0:T(8,128)S(1)}, u32[]{:S(2)}, u32[]{:S(2)}) collective-permute-start(f32[8,64,128]{2,1,0:T(8,128)S(1)} %get-tuple-element.74), channel_id=1, source_target_pairs={{0,2},{2,0},{4,6},{6,4},{8,10},{10,8},{12,14},{14,12},{1,3},{3,1},... | collective-permute-start | bytes 786440 | tf_op jit(solution)/shard_map/cond/branch_0_fun/ppermute | solution.py:280
  5.5 5.0 %collective-permute-start.1 = (f32[8,32,128]{2,1,0:T(8,128)S(1)}, f32[8,32,128]{2,1,0:T(8,128)S(1)}, u32[]{:S(2)}, u32[]{:S(2)}) collective-permute-start(f32[8,32,128]{2,1,0:T(8,128)S(1)} %get-tuple-element.76), channel_id=1, source_target_pairs={{0,2},{2,0},{4,6},{6,4},{8,10},{10,8},{12,14},{14,12},{1,3},{3,1},... | collective-permute-start | bytes 393224 | tf_op jit(solution)/shard_map/cond/branch_0_fun/ppermute | solution.py:282
  10.6 20.0 %copy-start.6 = (bf16[768,256]{1,0:T(8,128)(2,1)S(1)}, bf16[768,256]{1,0:T(8,128)(2,1)}, u32[]{:S(2)}) copy-start(bf16[768,256]{1,0:T(8,128)(2,1)} %get-tuple-element.56.back_tail_ref) | copy-start | bytes 1179652 | tf_op jit(solution)/shard_map/cond
  10.6 20.0 %copy-start.8 = (bf16[768,256]{1,0:T(8,128)(2,1)S(1)}, bf16[768,256]{1,0:T(8,128)(2,1)}, u32[]{:S(2)}) copy-start(bf16[768,256]{1,0:T(8,128)(2,1)} %get-tuple-element.55.tail_ref) | copy-start | bytes 1179652 | tf_op jit(solution)/shard_map/cond
  10.6 20.0 %copy-start.10 = (bf16[128,256]{1,0:T(8,128)(2,1)S(1)}, bf16[128,256]{1,0:T(8,128)(2,1)}, u32[]{:S(2)}) copy-start(bf16[128,256]{1,0:T(8,128)(2,1)} %get-tuple-element.57.back_head_ref) | copy-start | bytes 196612 | tf_op jit(solution)/shard_map/cond
  10.7 20.0 %copy-start.12 = (f32[64,256]{1,0:T(8,128)S(1)}, f32[64,256]{1,0:T(8,128)}, u32[]{:S(2)}) copy-start(f32[64,256]{1,0:T(8,128)} %get-tuple-element.54.twist_ref) | copy-start | bytes 196612 | tf_op jit(solution)/shard_map/cond
  10.7 20.0 %copy-start.14 = (bf16[128,192]{1,0:T(8,128)(2,1)S(1)}, bf16[128,192]{1,0:T(8,128)(2,1)}, u32[]{:S(2)}) copy-start(bf16[128,192]{1,0:T(8,128)(2,1)} %get-tuple-element.53.head_ref) | copy-start | bytes 147460 | tf_op jit(solution)/shard_map/cond
  32.5 13.7 %copy-start = (bf16[1024,128]{1,0:T(8,128)(2,1)S(1)}, bf16[1024,128]{1,0:T(8,128)(2,1)}, u32[]{:S(2)}) copy-start(bf16[1024,128]{1,0:T(8,128)(2,1)} %get-tuple-element.48.refs_0_.key_ref) | copy-start | bytes 786436 | tf_op jit(solution)/shard_map/cond
  32.5 13.7 %copy-start.2 = (bf16[1024,128]{1,0:T(8,128)(2,1)S(1)}, bf16[1024,128]{1,0:T(8,128)(2,1)}, u32[]{:S(2)}) copy-start(bf16[1024,128]{1,0:T(8,128)(2,1)} %get-tuple-element.49.refs_1_.value_ref) | copy-start | bytes 786436 | tf_op jit(solution)/shard_map/cond
  32.5 13.7 %copy-start.4 = (bf16[1024,128]{1,0:T(8,128)(2,1)S(1)}, bf16[1024,128]{1,0:T(8,128)(2,1)}, u32[]{:S(2)}) copy-start(bf16[1024,128]{1,0:T(8,128)(2,1)} %get-tuple-element.58.query_ref) | copy-start | bytes 786436 | tf_op jit(solution)/shard_map/cond

commit v25 on v23

--- a/solution.py
+++ b/solution.py
@@ -104,7 +104,7 @@
     count = out_ref.shape[0]
     blocks = count // groups
     homes = [
-        ((peer % 2 ^ near_ref[0]) * (count // 2) + peer // 2 if staged else peer, peer * own)
+        (((peer // blocks + peer) % 2 ^ near_ref[0]) * (count // 2) + peer // 2 if staged else peer, peer * own)
         for peer in range(count)
     ]
     first = where_ref[0] * (part * LANES if part < rows else 0)
@@ -138,6 +138,7 @@
         far, second = moved_ref.shape[0] // groups, start + own * (rows + part)
         span = pl.ds(group * far, far)
         ours, other = moved_ref[span, start : start + height], moved_ref[span, second : second + height]
+        near = near ^ group % 2
         pair = [jnp.where(near == 0, ours, other), jnp.where(near == 0, other, ours)]
         return jnp.stack(pair, axis=1).reshape(2 * far, height, LANES)
     blocks = moved_ref.shape[0] // groups
@@ -250,7 +251,7 @@
     size = tokens * chans * 4
     macs = 2 * 3 * own * seq_len * (2 * outer + 4 * LANES)
     where = lax.axis_index("groups").reshape(1).astype(jnp.int32)
-    near = (lax.axis_index("seq") % 2).reshape(1).astype(jnp.int32)
+    near = ((lax.axis_index("groups") + lax.axis_index("seq")) % 2).reshape(1).astype(jnp.int32)
 
     def exchange(array):
         return lax.all_to_all(array, axes, 0, 0, tiled=True)
@@ -267,7 +268,7 @@
         kept, sent = packed[: count // 2], packed[count // 2 :]
         swap = [(block, block ^ 1) for block in range(blocks)]
         pair = jnp.concatenate([kept, lax.ppermute(sent, "seq", swap)], axis=1)
-        sides = [list(range(side, count, 2)) for side in range(2)]
+        sides = [[peer for peer in range(count) if (peer // blocks + peer) % 2 == side] for side in range(2)]
         moved = lax.all_to_all(pair, axes, 0, 0, axis_index_groups=sides, tiled=True)
     else:
         moved = exchange(packed)

time: 47.5 us -> 49 us (1.032)
  blocking collectives: 34.1 us -> 35.6 us
    all_to_all x1, blocking collectives: 20.2 us -> 22.2 us  [convolve(): lax.all_to_all(pair, axes, 0, 0, axis_index_groups=sides, tiled=True)]
where the time goes in v25:
time: 49 us; the launch traced here: 48.8 us
  blocking collectives  35.6 us (73%)
  waiting for transfers between devices  5.76 us (12%)
  Pallas kernels  4.14 us (8%)
  starting transfers between devices  3.03 us (6%)
    all_to_all x1, blocking collectives, convolve(): lax.all_to_all(pair, axes, 0, 0, axis_index_groups=sides, tiled=True)  22.2 us
    all_to_all x1, blocking collectives, exchange(): return lax.all_to_all(array, axes, 0, 0, tiled=True)  13.4 us
    ppermute x1, waiting for transfers between devices, convolve(): pair = jnp.concatenate([kept, lax.ppermute(sent, 'seq', swap)], axis=1)  5.76 us
    ppermute x1, starting transfers between devices, convolve(): pair = jnp.concatenate([kept, lax.ppermute(sent, 'seq', swap)], axis=1)  3.03 us
    pallas_call x1, Pallas kernels, convolve(): call(functools.partial(conv_kernel, layout, staged, min(own, 4)), [((coun...  1.78 us
    pallas_call x1, Pallas kernels, convolve(): call(functools.partial(pack_kernel, layout, staged), [((count, own * (row...  1.48 us
  transfers between devices with their start and end apart: 1, of which 1 were waited for; matrix products, arithmetic and copies ran while one was open for 0% of the time, Pallas kernels for 0%

profile of v25, /device:TPU:0, one launch (start us, length us, event | category | flops | bytes accessed | tf_op | source)
XLA Modules:
  0.0 48.8 jit_solution(6261792088206178141)
XLA Ops:
  0.0 48.8 %conditional.1 = (bf16[1024,128]{1,0:T(8,128)(2,1)}) conditional(s32[]{:T(128)} %convert_element_type.3, (f32[128]{0:T(128)}, bf16[1024,128]{1,0:T(8,128)(2,1)}, bf16[1024,128]{1,0:T(8,128)(2,1)}, f32[1024,128]{1,0:T(8,128)}, bf16[128,192]{1,0:T(8,128)(2,1)}, /*index=5*/f32[64,256]{1,0:T(8,128)}, bf16[768,256]{1,0:T(8,128)(2,1)}, ...), branch_computations={%region_0.1_spmd, %region_1.2_spmd} | conditional | flops 1259143168 | bytes 19071432 | solution.py:294
  0.0 1.5 %branch_0_fun.3 = (f32[16,96,128]{2,1,0:T(8,128)S(1)}, f32[1,128]{1,0:T(1,128)S(1)}) custom-call(s32[1]{0:T(128)} %bitcast.1.where_ref, s32[1]{0:T(128)} %bitcast.near_ref, bf16[1024,128]{1,0:T(8,128)(2,1)} %get-tuple-element.48.key_ref, bf16[1024,128]{1,0:T(8,128)(2,1)} %get-tuple-element.49.value_ref, f32[1024,128]{1,0:T(8,128)} %get-tuple-element.50.filter_ref, ...), custom_call_target="tpu_custom_call" | custom-call | flops 131072 | bytes 1572864 | tf_op jit(solution)/shard_map/cond/branch_0_fun/pallas_call | solution.py:260
  1.5 0.1 fusion
  1.5 3.0 %collective-permute-start = (f32[8,96,128]{2,1,0:T(8,128)S(1)}, f32[8,96,128]{2,1,0:T(8,128)S(1)}, u32[]{:S(2)}, u32[]{:S(2)}) collective-permute-start(f32[8,96,128]{2,1,0:T(8,128)S(1)} %get-tuple-element.74), channel_id=1, source_target_pairs={{0,2},{2,0},{4,6},{6,4},{8,10},{10,8},{12,14},{14,12},{1,3},{3,1},... | collective-permute-start | bytes 1179656 | tf_op jit(solution)/shard_map/cond/branch_0_fun/ppermute | solution.py:270
  4.6 5.8 %collective-permute-done = f32[8,96,128]{2,1,0:T(8,128)S(1)} collective-permute-done((f32[8,96,128]{2,1,0:T(8,128)S(1)}, f32[8,96,128]{2,1,0:T(8,128)S(1)}, u32[]{:S(2)}, u32[]{:S(2)}) %collective-permute-start) | collective-permute-done | bytes 393248 | tf_op jit(solution)/shard_map/cond/branch_0_fun/ppermute | solution.py:270
  10.3 0.1 pad_maximum_fusion
  10.4 0.0 copy-start.6
  10.4 0.0 copy-start.8
  10.4 0.0 copy-start.10
  10.4 0.0 copy-start.12
  10.4 0.0 copy-start.14
  10.5 22.2 %all_to_all.16.moved_ref = f32[8,192,128]{2,1,0:T(8,128)S(1)} all-to-all(f32[8,192,128]{2,1,0:T(8,128)S(1)} %pad_maximum_fusion), channel_id=1, replica_groups={{0,4,8,12,18,22,26,30},{2,6,10,14,16,20,24,28},{1,5,9,13,19,23,27,31},{..., dimensions={0} | all-to-all | bytes 1572864 | tf_op jit(solution)/shard_map/cond/branch_0_fun/all_to_all | solution.py:272
  32.6 0.0 copy-done.6
  32.6 0.0 copy-done.8
  32.6 0.0 copy-done.10
  32.6 0.0 copy-done.12
  32.6 0.0 copy-done.14
  32.7 1.8 %branch_0_fun.4 = f32[16,64,128]{2,1,0:T(8,128)S(1)} custom-call(s32[1]{0:T(128)} %bitcast.near_ref, f32[8,192,128]{2,1,0:T(8,128)S(1)} %all_to_all.16.moved_ref, bf16[128,192]{1,0:T(8,128)(2,1)S(1)} %copy-done.14, f32[64,256]{1,0:T(8,128)S(1)} %copy-done.12, bf16[768,256]{1,0:T(8,128)(2,1)S(1)} %copy-done.8, bf16[768,256]{1,0:T(8,128)(2,1)S(1)} %copy-done.6, ...), custom_call_target="tpu_custom_call" | custom-call | flops 1258291200 | bytes 1572864 | tf_op jit(solution)/shard_map/cond/branch_0_fun/pallas_call | solution.py:275
  34.4 0.0 copy-start
  34.5 0.0 copy-start.2
  34.5 0.0 copy-start.4
  34.5 13.4 %all_to_all.17 = f32[16,64,128]{2,1,0:T(8,128)S(1)} all-to-all(f32[16,64,128]{2,1,0:T(8,128)S(1)} %branch_0_fun.4), channel_id=1, replica_groups=mesh['groups'=2,'seq'=8,'chan'=2] {'groups','seq'}, dimensions={0} | all-to-all | bytes 1048576 | tf_op jit(solution)/shard_map/cond/branch_0_fun/all_to_all | solution.py:257
  47.9 0.0 copy-done
  47.9 0.0 copy-done.2
  47.9 0.0 copy-done.4
  47.9 0.9 %branch_0_fun.5 = bf16[1024,128]{1,0:T(8,128)(2,1)} custom-call(f32[1024,128]{1,0:T(8,128)S(1)} %bitcast.8, bf16[1024,128]{1,0:T(8,128)(2,1)S(1)} %copy-done.4, bf16[1024,128]{1,0:T(8,128)(2,1)S(1)} %copy-done, bf16[1024,128]{1,0:T(8,128)(2,1)S(1)} %copy-done.2, f32[1,128]{1,0:T(1,128)S(1)} %get-tuple-element.59.bias_ref), custom_call_target="tpu_custom_call" | custom-call | flops 524288 | bytes 1572864 | tf_op jit(solution)/shard_map/cond/branch_0_fun/pallas_call | solution.py:280
Async XLA Ops:
  1.5 8.8 %collective-permute-start = (f32[8,96,128]{2,1,0:T(8,128)S(1)}, f32[8,96,128]{2,1,0:T(8,128)S(1)}, u32[]{:S(2)}, u32[]{:S(2)}) collective-permute-start(f32[8,96,128]{2,1,0:T(8,128)S(1)} %get-tuple-element.74), channel_id=1, source_target_pairs={{0,2},{2,0},{4,6},{6,4},{8,10},{10,8},{12,14},{14,12},{1,3},{3,1},... | collective-permute-start | bytes 1179656 | tf_op jit(solution)/shard_map/cond/branch_0_fun/ppermute | solution.py:270
  10.4 22.2 %copy-start.6 = (bf16[768,256]{1,0:T(8,128)(2,1)S(1)}, bf16[768,256]{1,0:T(8,128)(2,1)}, u32[]{:S(2)}) copy-start(bf16[768,256]{1,0:T(8,128)(2,1)} %get-tuple-element.56.back_tail_ref) | copy-start | bytes 1179652 | tf_op jit(solution)/shard_map/cond
  10.4 22.2 %copy-start.8 = (bf16[768,256]{1,0:T(8,128)(2,1)S(1)}, bf16[768,256]{1,0:T(8,128)(2,1)}, u32[]{:S(2)}) copy-start(bf16[768,256]{1,0:T(8,128)(2,1)} %get-tuple-element.55.tail_ref) | copy-start | bytes 1179652 | tf_op jit(solution)/shard_map/cond
  10.4 22.2 %copy-start.10 = (bf16[128,256]{1,0:T(8,128)(2,1)S(1)}, bf16[128,256]{1,0:T(8,128)(2,1)}, u32[]{:S(2)}) copy-start(bf16[128,256]{1,0:T(8,128)(2,1)} %get-tuple-element.57.back_head_ref) | copy-start | bytes 196612 | tf_op jit(solution)/shard_map/cond
  10.4 22.2 %copy-start.12 = (f32[64,256]{1,0:T(8,128)S(1)}, f32[64,256]{1,0:T(8,128)}, u32[]{:S(2)}) copy-start(f32[64,256]{1,0:T(8,128)} %get-tuple-element.54.twist_ref) | copy-start | bytes 196612 | tf_op jit(solution)/shard_map/cond
  10.4 22.2 %copy-start.14 = (bf16[128,192]{1,0:T(8,128)(2,1)S(1)}, bf16[128,192]{1,0:T(8,128)(2,1)}, u32[]{:S(2)}) copy-start(bf16[128,192]{1,0:T(8,128)(2,1)} %get-tuple-element.53.head_ref) | copy-start | bytes 147460 | tf_op jit(solution)/shard_map/cond
  34.4 13.5 %copy-start = (bf16[1024,128]{1,0:T(8,128)(2,1)S(1)}, bf16[1024,128]{1,0:T(8,128)(2,1)}, u32[]{:S(2)}) copy-start(bf16[1024,128]{1,0:T(8,128)(2,1)} %get-tuple-element.48.key_ref) | copy-start | bytes 786436 | tf_op jit(solution)/shard_map/cond
  34.5 13.5 %copy-start.2 = (bf16[1024,128]{1,0:T(8,128)(2,1)S(1)}, bf16[1024,128]{1,0:T(8,128)(2,1)}, u32[]{:S(2)}) copy-start(bf16[1024,128]{1,0:T(8,128)(2,1)} %get-tuple-element.49.value_ref) | copy-start | bytes 786436 | tf_op jit(solution)/shard_map/cond
  34.5 13.4 %copy-start.4 = (bf16[1024,128]{1,0:T(8,128)(2,1)S(1)}, bf16[1024,128]{1,0:T(8,128)(2,1)}, u32[]{:S(2)}) copy-start(bf16[1024,128]{1,0:T(8,128)(2,1)} %get-tuple-element.58.query_ref) | copy-start | bytes 786436 | tf_op jit(solution)/shard_map/cond

commit v26 on v23

--- a/solution.py
+++ b/solution.py
@@ -109,7 +109,7 @@
     ]
     first = where_ref[0] * (part * LANES if part < rows else 0)
     taken = filter_ref.at[pl.ds(pl.multiple_of(first, part * LANES), part * LANES)]
-    cuts = 2 if rows % 2 == 0 else 1
+    cuts = 1
     spans = [pl.ds(cut * rows // cuts * LANES, rows // cuts * LANES) for cut in range(cuts)]
     pairs = [(source.at[span], held.at[span]) for span in spans for source, held in ((key_ref, key), (value_ref, value))]
     pairs += [(taken, taps), (bias_ref, bias_out)]
@@ -272,7 +272,7 @@
     else:
         moved = exchange(packed)
     local = call(
-        functools.partial(conv_kernel, layout, staged, min(own, 4)),
+        functools.partial(conv_kernel, layout, staged, min(own, 2)),
         [((count, own * rows, LANES), F32)], [SMEM] + [VMEM] * 6, 5 * macs, 3 * size,
     )(near, moved, head, twist, tail, back_tail, back_head)[0]
     convolved = exchange(local).reshape(chans * rows, LANES)

time: 47.5 us -> 47.5 us (level)
  no operation moved by 1% of the time
where the time goes in v26:
time: 47.5 us; the launch traced here: 47.3 us
  blocking collectives  34.1 us (72%)
  waiting for transfers between devices  5.76 us (12%)
  Pallas kernels  4.13 us (9%)
  starting transfers between devices  3.03 us (6%)
    all_to_all x1, blocking collectives, convolve(): lax.all_to_all(pair, axes, 0, 0, axis_index_groups=sides, tiled=True)  20.2 us
    all_to_all x1, blocking collectives, exchange(): return lax.all_to_all(array, axes, 0, 0, tiled=True)  13.8 us
    ppermute x1, waiting for transfers between devices, convolve(): pair = jnp.concatenate([kept, lax.ppermute(sent, 'seq', swap)], axis=1)  5.76 us
    ppermute x1, starting transfers between devices, convolve(): pair = jnp.concatenate([kept, lax.ppermute(sent, 'seq', swap)], axis=1)  3.03 us
    pallas_call x1, Pallas kernels, convolve(): call(functools.partial(conv_kernel, layout, staged, min(own, 2)), [((coun...  1.78 us
    pallas_call x1, Pallas kernels, convolve(): call(functools.partial(pack_kernel, layout, staged), [((count, own * (row...  1.47 us
  transfers between devices with their start and end apart: 1, of which 1 were waited for; matrix products, arithmetic and copies ran while one was open for 0% of the time, Pallas kernels for 0%

profile of v26, /device:TPU:0, one launch (start us, length us, event | category | flops | bytes accessed | tf_op | source)
XLA Modules:
  0.0 47.3 jit_solution(7485436412848304107)
XLA Ops:
  0.0 47.3 %conditional.1 = (bf16[1024,128]{1,0:T(8,128)(2,1)}) conditional(s32[]{:T(128)} %convert_element_type.3, (f32[128]{0:T(128)}, bf16[1024,128]{1,0:T(8,128)(2,1)}, bf16[1024,128]{1,0:T(8,128)(2,1)}, f32[1024,128]{1,0:T(8,128)}, bf16[128,192]{1,0:T(8,128)(2,1)}, /*index=5*/f32[64,256]{1,0:T(8,128)}, bf16[768,256]{1,0:T(8,128)(2,1)}, ...), branch_computations={%region_0.1_spmd, %region_1.2_spmd} | conditional | flops 1259143168 | bytes 19071420 | solution.py:293
  0.0 1.5 %branch_0_fun.3 = (f32[16,96,128]{2,1,0:T(8,128)S(1)}, f32[1,128]{1,0:T(1,128)S(1)}) custom-call(s32[1]{0:T(128)} %bitcast.1.where_ref, s32[1]{0:T(128)} %bitcast.near_ref, bf16[1024,128]{1,0:T(8,128)(2,1)} %get-tuple-element.48.key_ref, bf16[1024,128]{1,0:T(8,128)(2,1)} %get-tuple-element.49.value_ref, f32[1024,128]{1,0:T(8,128)} %get-tuple-element.50.filter_ref, ...), custom_call_target="tpu_custom_call" | custom-call | flops 131072 | bytes 1572864 | tf_op jit(solution)/shard_map/cond/branch_0_fun/pallas_call | solution.py:259
  1.5 0.1 fusion
  1.5 3.0 %collective-permute-start = (f32[8,96,128]{2,1,0:T(8,128)S(1)}, f32[8,96,128]{2,1,0:T(8,128)S(1)}, u32[]{:S(2)}, u32[]{:S(2)}) collective-permute-start(f32[8,96,128]{2,1,0:T(8,128)S(1)} %get-tuple-element.74), channel_id=1, source_target_pairs={{0,2},{2,0},{4,6},{6,4},{8,10},{10,8},{12,14},{14,12},{1,3},{3,1},... | collective-permute-start | bytes 1179656 | tf_op jit(solution)/shard_map/cond/branch_0_fun/ppermute | solution.py:269
  4.6 5.8 %collective-permute-done = f32[8,96,128]{2,1,0:T(8,128)S(1)} collective-permute-done((f32[8,96,128]{2,1,0:T(8,128)S(1)}, f32[8,96,128]{2,1,0:T(8,128)S(1)}, u32[]{:S(2)}, u32[]{:S(2)}) %collective-permute-start) | collective-permute-done | bytes 393248 | tf_op jit(solution)/shard_map/cond/branch_0_fun/ppermute | solution.py:269
  10.3 0.1 pad_maximum_fusion
  10.4 0.0 copy-start.6
  10.4 0.0 copy-start.8
  10.4 0.0 copy-start.10
  10.4 0.0 copy-start.12
  10.4 0.0 copy-start.14
  10.4 20.2 %all_to_all.16.moved_ref = f32[8,192,128]{2,1,0:T(8,128)S(1)} all-to-all(f32[8,192,128]{2,1,0:T(8,128)S(1)} %pad_maximum_fusion), channel_id=1, replica_groups={{0,4,8,12,16,20,24,28},{2,6,10,14,18,22,26,30},{1,5,9,13,17,21,25,29},{..., dimensions={0} | all-to-all | bytes 1572864 | tf_op jit(solution)/shard_map/cond/branch_0_fun/all_to_all | solution.py:271
  30.7 0.0 copy-done.6
  30.7 0.0 copy-done.8
  30.7 0.0 copy-done.10
  30.7 0.0 copy-done.12
  30.7 0.0 copy-done.14
  30.7 1.8 %branch_0_fun.4 = f32[16,64,128]{2,1,0:T(8,128)S(1)} custom-call(s32[1]{0:T(128)} %bitcast.near_ref, f32[8,192,128]{2,1,0:T(8,128)S(1)} %all_to_all.16.moved_ref, bf16[128,192]{1,0:T(8,128)(2,1)S(1)} %copy-done.14, f32[64,256]{1,0:T(8,128)S(1)} %copy-done.12, bf16[768,256]{1,0:T(8,128)(2,1)S(1)} %copy-done.8, bf16[768,256]{1,0:T(8,128)(2,1)S(1)} %copy-done.6, ...), custom_call_target="tpu_custom_call" | custom-call | flops 1258291200 | bytes 1572864 | tf_op jit(solution)/shard_map/cond/branch_0_fun/pallas_call | solution.py:274
  32.5 0.0 copy-start
  32.5 0.0 copy-start.2
  32.5 0.0 copy-start.4
  32.5 13.8 %all_to_all.17 = f32[16,64,128]{2,1,0:T(8,128)S(1)} all-to-all(f32[16,64,128]{2,1,0:T(8,128)S(1)} %branch_0_fun.4), channel_id=1, replica_groups=mesh['groups'=2,'seq'=8,'chan'=2] {'groups','seq'}, dimensions={0} | all-to-all | bytes 1048576 | tf_op jit(solution)/shard_map/cond/branch_0_fun/all_to_all | solution.py:256
  46.4 0.0 copy-done
  46.4 0.0 copy-done.2
  46.4 0.0 copy-done.4
  46.4 0.9 %branch_0_fun.5 = bf16[1024,128]{1,0:T(8,128)(2,1)} custom-call(f32[1024,128]{1,0:T(8,128)S(1)} %bitcast.8, bf16[1024,128]{1,0:T(8,128)(2,1)S(1)} %copy-done.4, bf16[1024,128]{1,0:T(8,128)(2,1)S(1)} %copy-done, bf16[1024,128]{1,0:T(8,128)(2,1)S(1)} %copy-done.2, f32[1,128]{1,0:T(1,128)S(1)} %get-tuple-element.59.bias_ref), custom_call_target="tpu_custom_call" | custom-call | flops 524288 | bytes 1572864 | tf_op jit(solution)/shard_map/cond/branch_0_fun/pallas_call | solution.py:279
Async XLA Ops:
  1.5 8.8 %collective-permute-start = (f32[8,96,128]{2,1,0:T(8,128)S(1)}, f32[8,96,128]{2,1,0:T(8,128)S(1)}, u32[]{:S(2)}, u32[]{:S(2)}) collective-permute-start(f32[8,96,128]{2,1,0:T(8,128)S(1)} %get-tuple-element.74), channel_id=1, source_target_pairs={{0,2},{2,0},{4,6},{6,4},{8,10},{10,8},{12,14},{14,12},{1,3},{3,1},... | collective-permute-start | bytes 1179656 | tf_op jit(solution)/shard_map/cond/branch_0_fun/ppermute | solution.py:269
  10.4 20.3 %copy-start.6 = (bf16[768,256]{1,0:T(8,128)(2,1)S(1)}, bf16[768,256]{1,0:T(8,128)(2,1)}, u32[]{:S(2)}) copy-start(bf16[768,256]{1,0:T(8,128)(2,1)} %get-tuple-element.56.back_tail_ref) | copy-start | bytes 1179652 | tf_op jit(solution)/shard_map/cond
  10.4 20.3 %copy-start.8 = (bf16[768,256]{1,0:T(8,128)(2,1)S(1)}, bf16[768,256]{1,0:T(8,128)(2,1)}, u32[]{:S(2)}) copy-start(bf16[768,256]{1,0:T(8,128)(2,1)} %get-tuple-element.55.tail_ref) | copy-start | bytes 1179652 | tf_op jit(solution)/shard_map/cond
  10.4 20.3 %copy-start.10 = (bf16[128,256]{1,0:T(8,128)(2,1)S(1)}, bf16[128,256]{1,0:T(8,128)(2,1)}, u32[]{:S(2)}) copy-start(bf16[128,256]{1,0:T(8,128)(2,1)} %get-tuple-element.57.back_head_ref) | copy-start | bytes 196612 | tf_op jit(solution)/shard_map/cond
  10.4 20.3 %copy-start.12 = (f32[64,256]{1,0:T(8,128)S(1)}, f32[64,256]{1,0:T(8,128)}, u32[]{:S(2)}) copy-start(f32[64,256]{1,0:T(8,128)} %get-tuple-element.54.twist_ref) | copy-start | bytes 196612 | tf_op jit(solution)/shard_map/cond
  10.4 20.3 %copy-start.14 = (bf16[128,192]{1,0:T(8,128)(2,1)S(1)}, bf16[128,192]{1,0:T(8,128)(2,1)}, u32[]{:S(2)}) copy-start(bf16[128,192]{1,0:T(8,128)(2,1)} %get-tuple-element.53.head_ref) | copy-start | bytes 147460 | tf_op jit(solution)/shard_map/cond
  32.5 13.9 %copy-start = (bf16[1024,128]{1,0:T(8,128)(2,1)S(1)}, bf16[1024,128]{1,0:T(8,128)(2,1)}, u32[]{:S(2)}) copy-start(bf16[1024,128]{1,0:T(8,128)(2,1)} %get-tuple-element.48.key_ref) | copy-start | bytes 786436 | tf_op jit(solution)/shard_map/cond
  32.5 13.9 %copy-start.2 = (bf16[1024,128]{1,0:T(8,128)(2,1)S(1)}, bf16[1024,128]{1,0:T(8,128)(2,1)}, u32[]{:S(2)}) copy-start(bf16[1024,128]{1,0:T(8,128)(2,1)} %get-tuple-element.49.value_ref) | copy-start | bytes 786436 | tf_op jit(solution)/shard_map/cond
  32.5 13.9 %copy-start.4 = (bf16[1024,128]{1,0:T(8,128)(2,1)S(1)}, bf16[1024,128]{1,0:T(8,128)(2,1)}, u32[]{:S(2)}) copy-start(bf16[1024,128]{1,0:T(8,128)(2,1)} %get-tuple-element.58.query_ref) | copy-start | bytes 786436 | tf_op jit(solution)/shard_map/cond

commit v27 on v23

--- a/solution.py
+++ b/solution.py
@@ -112,23 +112,23 @@
     cuts = 2 if rows % 2 == 0 else 1
     spans = [pl.ds(cut * rows // cuts * LANES, rows // cuts * LANES) for cut in range(cuts)]
     pairs = [(source.at[span], held.at[span]) for span in spans for source, held in ((key_ref, key), (value_ref, value))]
-    pairs += [(taken, taps), (bias_ref, bias_out)]
+    pairs = [(taken, taps)] + pairs + [(bias_ref, bias_out)]
     fetches = [pltpu.make_async_copy(*pair, sems.at[idx]) for idx, pair in enumerate(pairs)]
     for fetch in fetches:
         fetch.start()
+    fetches[0].wait()
+    for row in range(part):
+        turned = taps[pl.ds(row * LANES, LANES), :].T
+        for place, chan in homes:
+            out_ref[place, pl.ds(own * rows + row, own, stride=part), :] = turned[chan : chan + own]
     for row in range(rows):
         if row % (rows // cuts) == 0:
-            for fetch in fetches[row // (rows // cuts) * 2 :][:2]:
+            for fetch in fetches[1 + row // (rows // cuts) * 2 :][:2]:
                 fetch.wait()
         span = pl.ds(row * LANES, LANES)
         turned = (key[span, :].astype(F32) * value[span, :].astype(F32)).T
         for place, chan in homes:
             out_ref[place, pl.ds(row, own, stride=rows), :] = turned[chan : chan + own]
-    fetches[-2].wait()
-    for row in range(part):
-        turned = taps[pl.ds(row * LANES, LANES), :].T
-        for place, chan in homes:
-            out_ref[place, pl.ds(own * rows + row, own, stride=part), :] = turned[chan : chan + own]
     fetches[-1].wait()
 
 

time: 47.5 us -> 47.5 us (level)
  no operation moved by 1% of the time
where the time goes in v27:
time: 47.5 us; the launch traced here: 47.3 us
  blocking collectives  34.1 us (72%)
  waiting for transfers between devices  5.76 us (12%)
  Pallas kernels  4.13 us (9%)
  starting transfers between devices  3.03 us (6%)
    all_to_all x1, blocking collectives, convolve(): lax.all_to_all(pair, axes, 0, 0, axis_index_groups=sides, tiled=True)  20.2 us
    all_to_all x1, blocking collectives, exchange(): return lax.all_to_all(array, axes, 0, 0, tiled=True)  13.9 us
    ppermute x1, waiting for transfers between devices, convolve(): pair = jnp.concatenate([kept, lax.ppermute(sent, 'seq', swap)], axis=1)  5.76 us
    ppermute x1, starting transfers between devices, convolve(): pair = jnp.concatenate([kept, lax.ppermute(sent, 'seq', swap)], axis=1)  3.03 us
    pallas_call x1, Pallas kernels, convolve(): call(functools.partial(conv_kernel, layout, staged, min(own, 4)), [((coun...  1.78 us
    pallas_call x1, Pallas kernels, convolve(): call(functools.partial(pack_kernel, layout, staged), [((count, own * (row...  1.47 us
  transfers between devices with their start and end apart: 1, of which 1 were waited for; matrix products, arithmetic and copies ran while one was open for 0% of the time, Pallas kernels for 0%

profile of v27, /device:TPU:0, one launch (start us, length us, event | category | flops | bytes accessed | tf_op | source)
XLA Modules:
  0.0 47.3 jit_solution(3203383025762481364)
XLA Ops:
  0.0 47.3 %conditional.1 = (bf16[1024,128]{1,0:T(8,128)(2,1)}) conditional(s32[]{:T(128)} %convert_element_type.3, (f32[128]{0:T(128)}, bf16[1024,128]{1,0:T(8,128)(2,1)}, bf16[1024,128]{1,0:T(8,128)(2,1)}, f32[1024,128]{1,0:T(8,128)}, bf16[128,192]{1,0:T(8,128)(2,1)}, /*index=5*/f32[64,256]{1,0:T(8,128)}, bf16[768,256]{1,0:T(8,128)(2,1)}, ...), branch_computations={%region_0.1_spmd, %region_1.2_spmd} | conditional | flops 1259143168 | bytes 19071420 | solution.py:293
  0.0 1.5 %branch_0_fun.3 = (f32[16,96,128]{2,1,0:T(8,128)S(1)}, f32[1,128]{1,0:T(1,128)S(1)}) custom-call(s32[1]{0:T(128)} %bitcast.1.where_ref, s32[1]{0:T(128)} %bitcast.near_ref, bf16[1024,128]{1,0:T(8,128)(2,1)} %get-tuple-element.48.key_ref, bf16[1024,128]{1,0:T(8,128)(2,1)} %get-tuple-element.49.value_ref, f32[1024,128]{1,0:T(8,128)} %get-tuple-element.50.filter_ref, ...), custom_call_target="tpu_custom_call" | custom-call | flops 131072 | bytes 1572864 | tf_op jit(solution)/shard_map/cond/branch_0_fun/pallas_call | solution.py:259
  1.5 0.1 fusion
  1.5 3.0 %collective-permute-start = (f32[8,96,128]{2,1,0:T(8,128)S(1)}, f32[8,96,128]{2,1,0:T(8,128)S(1)}, u32[]{:S(2)}, u32[]{:S(2)}) collective-permute-start(f32[8,96,128]{2,1,0:T(8,128)S(1)} %get-tuple-element.74), channel_id=1, source_target_pairs={{0,2},{2,0},{4,6},{6,4},{8,10},{10,8},{12,14},{14,12},{1,3},{3,1},... | collective-permute-start | bytes 1179656 | tf_op jit(solution)/shard_map/cond/branch_0_fun/ppermute | solution.py:269
  4.6 5.8 %collective-permute-done = f32[8,96,128]{2,1,0:T(8,128)S(1)} collective-permute-done((f32[8,96,128]{2,1,0:T(8,128)S(1)}, f32[8,96,128]{2,1,0:T(8,128)S(1)}, u32[]{:S(2)}, u32[]{:S(2)}) %collective-permute-start) | collective-permute-done | bytes 393248 | tf_op jit(solution)/shard_map/cond/branch_0_fun/ppermute | solution.py:269
  10.3 0.1 pad_maximum_fusion
  10.4 0.0 copy-start.6
  10.4 0.0 copy-start.8
  10.4 0.0 copy-start.10
  10.4 0.0 copy-start.12
  10.4 0.0 copy-start.14
  10.4 20.2 %all_to_all.16.moved_ref = f32[8,192,128]{2,1,0:T(8,128)S(1)} all-to-all(f32[8,192,128]{2,1,0:T(8,128)S(1)} %pad_maximum_fusion), channel_id=1, replica_groups={{0,4,8,12,16,20,24,28},{2,6,10,14,18,22,26,30},{1,5,9,13,17,21,25,29},{..., dimensions={0} | all-to-all | bytes 1572864 | tf_op jit(solution)/shard_map/cond/branch_0_fun/all_to_all | solution.py:271
  30.7 0.0 copy-done.6
  30.7 0.0 copy-done.8
  30.7 0.0 copy-done.10
  30.7 0.0 copy-done.12
  30.7 0.0 copy-done.14
  30.7 1.8 %branch_0_fun.4 = f32[16,64,128]{2,1,0:T(8,128)S(1)} custom-call(s32[1]{0:T(128)} %bitcast.near_ref, f32[8,192,128]{2,1,0:T(8,128)S(1)} %all_to_all.16.moved_ref, bf16[128,192]{1,0:T(8,128)(2,1)S(1)} %copy-done.14, f32[64,256]{1,0:T(8,128)S(1)} %copy-done.12, bf16[768,256]{1,0:T(8,128)(2,1)S(1)} %copy-done.8, bf16[768,256]{1,0:T(8,128)(2,1)S(1)} %copy-done.6, ...), custom_call_target="tpu_custom_call" | custom-call | flops 1258291200 | bytes 1572864 | tf_op jit(solution)/shard_map/cond/branch_0_fun/pallas_call | solution.py:274
  32.5 0.0 copy-start
  32.5 0.0 copy-start.2
  32.5 0.0 copy-start.4
  32.5 13.9 %all_to_all.17 = f32[16,64,128]{2,1,0:T(8,128)S(1)} all-to-all(f32[16,64,128]{2,1,0:T(8,128)S(1)} %branch_0_fun.4), channel_id=1, replica_groups=mesh['groups'=2,'seq'=8,'chan'=2] {'groups','seq'}, dimensions={0} | all-to-all | bytes 1048576 | tf_op jit(solution)/shard_map/cond/branch_0_fun/all_to_all | solution.py:256
  46.4 0.0 copy-done
  46.4 0.0 copy-done.2
  46.4 0.0 copy-done.4
  46.4 0.9 %branch_0_fun.5 = bf16[1024,128]{1,0:T(8,128)(2,1)} custom-call(f32[1024,128]{1,0:T(8,128)S(1)} %bitcast.8, bf16[1024,128]{1,0:T(8,128)(2,1)S(1)} %copy-done.4, bf16[1024,128]{1,0:T(8,128)(2,1)S(1)} %copy-done, bf16[1024,128]{1,0:T(8,128)(2,1)S(1)} %copy-done.2, f32[1,128]{1,0:T(1,128)S(1)} %get-tuple-element.59.bias_ref), custom_call_target="tpu_custom_call" | custom-call | flops 524288 | bytes 1572864 | tf_op jit(solution)/shard_map/cond/branch_0_fun/pallas_call | solution.py:279
Async XLA Ops:
  1.5 8.8 %collective-permute-start = (f32[8,96,128]{2,1,0:T(8,128)S(1)}, f32[8,96,128]{2,1,0:T(8,128)S(1)}, u32[]{:S(2)}, u32[]{:S(2)}) collective-permute-start(f32[8,96,128]{2,1,0:T(8,128)S(1)} %get-tuple-element.74), channel_id=1, source_target_pairs={{0,2},{2,0},{4,6},{6,4},{8,10},{10,8},{12,14},{14,12},{1,3},{3,1},... | collective-permute-start | bytes 1179656 | tf_op jit(solution)/shard_map/cond/branch_0_fun/ppermute | solution.py:269
  10.4 20.3 %copy-start.6 = (bf16[768,256]{1,0:T(8,128)(2,1)S(1)}, bf16[768,256]{1,0:T(8,128)(2,1)}, u32[]{:S(2)}) copy-start(bf16[768,256]{1,0:T(8,128)(2,1)} %get-tuple-element.56.back_tail_ref) | copy-start | bytes 1179652 | tf_op jit(solution)/shard_map/cond
  10.4 20.3 %copy-start.8 = (bf16[768,256]{1,0:T(8,128)(2,1)S(1)}, bf16[768,256]{1,0:T(8,128)(2,1)}, u32[]{:S(2)}) copy-start(bf16[768,256]{1,0:T(8,128)(2,1)} %get-tuple-element.55.tail_ref) | copy-start | bytes 1179652 | tf_op jit(solution)/shard_map/cond
  10.4 20.3 %copy-start.10 = (bf16[128,256]{1,0:T(8,128)(2,1)S(1)}, bf16[128,256]{1,0:T(8,128)(2,1)}, u32[]{:S(2)}) copy-start(bf16[128,256]{1,0:T(8,128)(2,1)} %get-tuple-element.57.back_head_ref) | copy-start | bytes 196612 | tf_op jit(solution)/shard_map/cond
  10.4 20.3 %copy-start.12 = (f32[64,256]{1,0:T(8,128)S(1)}, f32[64,256]{1,0:T(8,128)}, u32[]{:S(2)}) copy-start(f32[64,256]{1,0:T(8,128)} %get-tuple-element.54.twist_ref) | copy-start | bytes 196612 | tf_op jit(solution)/shard_map/cond
  10.4 20.3 %copy-start.14 = (bf16[128,192]{1,0:T(8,128)(2,1)S(1)}, bf16[128,192]{1,0:T(8,128)(2,1)}, u32[]{:S(2)}) copy-start(bf16[128,192]{1,0:T(8,128)(2,1)} %get-tuple-element.53.head_ref) | copy-start | bytes 147460 | tf_op jit(solution)/shard_map/cond
  32.5 13.9 %copy-start = (bf16[1024,128]{1,0:T(8,128)(2,1)S(1)}, bf16[1024,128]{1,0:T(8,128)(2,1)}, u32[]{:S(2)}) copy-start(bf16[1024,128]{1,0:T(8,128)(2,1)} %get-tuple-element.48.key_ref) | copy-start | bytes 786436 | tf_op jit(solution)/shard_map/cond
  32.5 13.9 %copy-start.2 = (bf16[1024,128]{1,0:T(8,128)(2,1)S(1)}, bf16[1024,128]{1,0:T(8,128)(2,1)}, u32[]{:S(2)}) copy-start(bf16[1024,128]{1,0:T(8,128)(2,1)} %get-tuple-element.49.value_ref) | copy-start | bytes 786436 | tf_op jit(solution)/shard_map/cond
  32.5 13.9 %copy-start.4 = (bf16[1024,128]{1,0:T(8,128)(2,1)S(1)}, bf16[1024,128]{1,0:T(8,128)(2,1)}, u32[]{:S(2)}) copy-start(bf16[1024,128]{1,0:T(8,128)(2,1)} %get-tuple-element.58.query_ref) | copy-start | bytes 786436 | tf_op jit(solution)/shard_map/cond
